TPU v7x, 32 devices: a whole 2x2x4 slice. The times are simulated.
32 devices in a mesh: groups: 2 (over y), vocab: 4 (over z), ctx: 2 (over x), dp: 2 (over core).
Axes of the slice: x: 2, y: 2, z: 4, core: 2. Of those that a mesh axis runs over, the one named last changes fastest.
Arguments:
- hidden: bfloat16 [4096, 4, 2, 128], P('vocab', ('groups', 'dp'), None, 'ctx'), parts along dimension 1, may hold values from -36 to 36, as said below
- head_weight: bfloat16 [4096, 8192], P(None, ('vocab', 'ctx', 'dp')), may hold values from -3 to 3, as said below
- targets: int32 [4, 2, 128], P('groups'), parts along dimension 0, may hold values from 0 to 8191
- response_start: int32 [4], P('groups'), parts along dimension 0, may hold values from 0 to 63
- other_sums: float32 [4, 2], P('groups'), parts along dimension 0, may hold values from -12 to 12
- ref_logp: float32 [4, 2], P('groups'), parts along dimension 0, may hold values from -12 to 12
- loss_cotangent: float32 [4], P('groups'), parts along dimension 0, may hold values from 130 to 516
Outputs:
- grad_hidden: bfloat16 [4096, 4, 2, 128], P('vocab', ('groups', 'dp'), None, 'ctx'), parts along dimension 1
- grad_head: bfloat16 [8192, 8192], P('groups', ('vocab', 'ctx', 'dp')), parts along dimension 0
- pair_loss: float32 [4], P('groups'), parts along dimension 0
There are 2 independent parts, one for each index of `groups`. A program takes and returns all parts, laid end to end along the dimension named above; an argument that names none is the same for every part. Nothing has to cross between parts.
Inputs may be any that keep to these rules, and one draw needn't show every extreme that they name: `hidden`: entries of order one, a few of larger size. `head_weight`: entries of order 3 * 4096 ** -0.5.
All inputs are finite; a program needn't handle non-finite values.
Results may differ from a plain program's by a relative error of at most 0.0057.
Values may be sent and summed in bfloat16 or wider, within the bound.
No kernel may reach another device: no remote copies, remote signals or barrier semaphores. Data moves between devices by JAX's collectives and lax.ppermute only.
A program may use at most 128 MiB of HBM per device.

v0:
```python
import jax
import jax.numpy as jnp
from jax import lax
from jax.sharding import PartitionSpec as P

BETA = 0.1


def shards(hidden, head_weight, targets, response_start, other_sums, ref_logp, loss_cotangent):
    along_seq = lax.all_gather(hidden, "ctx", axis=3, tiled=True)
    all_pairs = lax.all_gather(along_seq, "dp", axis=1, tiled=True)
    width_part = all_pairs.shape[0]
    pair_count = all_pairs.shape[1]
    side_count = all_pairs.shape[2]
    seq_len = all_pairs.shape[3]
    row_count = pair_count * side_count * seq_len
    full_hidden = lax.all_gather(
        all_pairs.reshape(width_part, row_count), "vocab", axis=0, tiled=True
    )
    voc_width = head_weight.shape[1]
    first_column = lax.axis_index(("vocab", "ctx", "dp")) * voc_width
    logits = lax.dot_general(
        full_hidden, head_weight, (((0,), (0,)), ((), ())), preferred_element_type=jnp.float32
    )
    column = lax.broadcasted_iota(jnp.int32, logits.shape, 1) + first_column
    hit = column == targets.reshape(row_count)[:, None]
    local_pick = jnp.sum(jnp.where(hit, logits, jnp.zeros_like(logits)), axis=1)
    local_max = jnp.max(logits, axis=1)
    row_max = lax.pmax(local_max, ("vocab", "ctx", "dp"))
    shifted = jnp.exp(logits - row_max[:, None])
    sum_exp, picked = lax.psum((jnp.sum(shifted, axis=1), local_pick), ("vocab", "ctx", "dp"))
    token_logp = (picked - row_max - jnp.log(sum_exp)).reshape(pair_count, side_count, seq_len)
    position = lax.broadcasted_iota(jnp.int32, (pair_count, seq_len), 1)
    mask = (position >= response_start[:, None]).astype(jnp.float32)[:, None, :]
    seq_logp = other_sums + jnp.sum(mask * token_logp, axis=2)
    ratios = seq_logp - ref_logp
    margin = BETA * (ratios[:, 0] - ratios[:, 1])
    pair_loss = jax.nn.softplus(-margin)
    factor = -BETA * jax.nn.sigmoid(-margin) * loss_cotangent
    side_sign = jnp.array([1.0, -1.0], dtype=jnp.float32)
    row_weight = (factor[:, None, None] * side_sign[None, :, None] * mask).reshape(row_count)
    grad_logits = (
        row_weight[:, None] * (hit.astype(jnp.float32) - shifted / sum_exp[:, None])
    ).astype(jnp.bfloat16)
    grad_head = jnp.dot(full_hidden, grad_logits, preferred_element_type=jnp.float32).astype(
        jnp.bfloat16
    )
    summed = lax.psum_scatter(
        lax.dot_general(
            head_weight, grad_logits, (((1,), (1,)), ((), ())), preferred_element_type=jnp.float32
        ),
        "vocab",
        scatter_dimension=0,
        tiled=True,
    )
    summed = summed.reshape(width_part, pair_count, side_count, seq_len)
    summed = lax.psum_scatter(summed, "ctx", scatter_dimension=3, tiled=True)
    summed = lax.psum_scatter(summed, "dp", scatter_dimension=1, tiled=True)
    return (summed.astype(jnp.bfloat16), grad_head, pair_loss)


def solution(mesh):
    placed = (
        P("vocab", ("groups", "dp"), None, "ctx"),
        P(None, ("vocab", "ctx", "dp")),
        P("groups", None, None),
        P("groups"),
        P("groups", None),
        P("groups", None),
        P("groups"),
    )
    return jax.shard_map(
        shards,
        mesh=mesh,
        in_specs=placed,
        out_specs=(
            P("vocab", ("groups", "dp"), None, "ctx"),
            P("groups", ("vocab", "ctx", "dp")),
            P("groups"),
        ),
        check_vma=False,
    )
```

profile of v0, /device:TPU:0, one launch (start us, length us, event | category | flops | bytes accessed | tf_op | source)
XLA Modules:
  0.0 388.0 jit_solution(6864695013371004015)
XLA Ops:
  7.2 0.0 copy-start.4
  7.2 0.0 all-gather.3.cloned.1.call-start
  7.2 1.2 copy.25
  8.4 9.9 %all_gather.9 = bf16[1024,1,2,128]{0,2,1,3:T(2,128)(2,1)S(1)} all-gather(bf16[1024,1,2,64]{0,2,1,3:T(2,128)(2,1)S(1)} %copy.25), channel_id=1, replica_groups=mesh['groups'=2,'vocab'=4,'ctx'=2,'dp'=2] {'ctx'}, dimensions={3}, use_global_device_ids=true | all-gather | bytes 786432 | tf_op jit(solution)/shard_map/all_gather | solution.py:10
  18.4 1.2 copy.26
  19.5 0.0 all-gather.3.cloned.1.call-update
  19.5 0.0 all-gather.5.cloned.1.call-start
  19.6 10.7 %all-gather.3.cloned.1.call-done = bf16[1024,2,2,128]{3,0,2,1:T(8,128)(2,1)} async-done(((bf16[1024,1,2,128]{3,0,2,1:T(8,128)(2,1)}), bf16[1024,2,2,128]{3,0,2,1:T(8,128)(2,1)}) %all-gather.3.cloned.1.call-update) | async-done | bytes 1048592 | tf_op jit(solution)/shard_map/all_gather | solution.py:11
  30.2 2.3 copy.27
  32.5 0.0 all-gather.5.cloned.1.call-update
  32.5 0.0 reduce-scatter.4.cloned.1.call-start
  32.6 0.0 copy-done.4
  32.6 0.1 compare_convert_fusion.1
  32.7 0.0 copy-start
  32.7 0.0 copy-start.1
  32.7 0.0 copy-start.2
  32.7 0.0 copy-start.5
  32.7 0.0 copy-start.3
  32.7 81.9 %all-gather.5.cloned.1.call-done = bf16[4096,512]{0,1:T(8,128)(2,1)} async-done(((bf16[1024,512]{0,1:T(8,128)(2,1)}), bf16[4096,512]{0,1:T(8,128)(2,1)}) %all-gather.5.cloned.1.call-update) | async-done | bytes 4194320 | tf_op jit(solution)/shard_map/all_gather | solution.py:17
  114.6 5.9 %fusion.8 = (f32[512]{0:T(512)S(1)}, f32[512,512]{0,1:T(8,128)S(1)}) fusion(bf16[4096,512]{0,1:T(8,128)(2,1)} %all-gather.5.cloned.1.call-done, bf16[4096,512]{1,0:T(8,128)(2,1)} %param.9), kind=kOutput, calls=%fused_computation.22 | convolution fusion | flops 2147745280 | bytes 9439232 | tf_op jit(solution)/shard_map/dot_general | solution.py:22
  120.5 30.9 %pmax.7 = f32[512]{0:T(512)S(1)} all-reduce(f32[512]{0:T(512)S(1)} %get-tuple-element.27), channel_id=1, replica_groups=mesh['groups'=2,'vocab'=4,'ctx'=2,'dp'=2] {'vocab','ctx','dp'}, use_global_device_ids=true, to_apply=%region_3.4 | all-reduce | flops 512 | bytes 4096 | tf_op jit(solution)/shard_map/pmax | solution.py:29
  151.4 0.0 copy-done
  151.4 0.3 fusion.1
  151.6 29.5 %all-reduce = (f32[512]{0:T(512)S(1)}, f32[512]{0:T(512)S(1)}) all-reduce(f32[512]{0:T(512)S(1)} %get-tuple-element.22, f32[512]{0:T(512)S(1)} %get-tuple-element.21), channel_id=1, replica_groups=mesh['groups'=2,'vocab'=4,'ctx'=2,'dp'=2] {'vocab','ctx','dp'}, use_global_device_ids=true, to_apply=%region_5.6 | all-reduce | flops 1024 | bytes 8192 | tf_op jit(solution)/shard_map/psum | solution.py:31
  181.1 0.1 multiply_reduce_fusion
  181.2 0.0 copy-done.1
  181.2 0.0 copy-done.2
  181.2 0.2 negate_reduce_fusion
  181.4 0.0 copy-done.5
  181.4 0.0 copy-done.3
  181.5 0.1 broadcast_multiply_fusion.1
  181.5 0.1 broadcast_multiply_fusion
  181.6 8.0 %convolution_bitcast_fusion = f32[4096,512]{0,1:T(8,128)} fusion(bf16[4096,512]{1,0:T(8,128)(2,1)} %param.9, f32[512,512]{0,1:T(8,128)S(1)} %get-tuple-element.28, f32[512]{0:T(512)S(1)} %get-tuple-element.25, f32[512]{0:T(512)S(1)} %bitcast.19, f32[512]{0:T(512)S(1)} %pmax.7, s32[512]{0:T(512)S(1)} %bitcast.17, s32[512]{0:T(512)S(1)} %iota_add_fusion), kind=kOutput, calls=%fused_computation | convolution fusion | flops 2149318656 | bytes 13641728 | tf_op jit(solution)/shard_map/dot_general | solution.py:49
  189.6 0.0 reduce-scatter.4.cloned.1.call-update
  189.6 0.0 reduce-scatter.6.cloned.1.call-start
  189.7 141.8 %reduce-scatter.4.cloned.1.call-done = f32[1024,512]{0,1:T(8,128)} async-done(((f32[4096,512]{0,1:T(8,128)}), f32[1024,512]{0,1:T(8,128)}) %reduce-scatter.4.cloned.1.call-update) | async-done | bytes 2097168 | tf_op jit(solution)/shard_map/reduce_scatter | solution.py:48
  331.5 0.0 reduce-scatter.6.cloned.1.call-update
  331.5 0.0 reduce-scatter.8.cloned.1.call-start
  331.6 34.6 %reduce-scatter.6.cloned.1.call-done = f32[1024,2,2,64]{0,3,2,1:T(8,128)} async-done(((f32[1024,2,2,128]{0,3,2,1:T(8,128)}), f32[1024,2,2,64]{0,3,2,1:T(8,128)}) %reduce-scatter.6.cloned.1.call-update) | async-done | bytes 1048592 | tf_op jit(solution)/shard_map/reduce_scatter | solution.py:57
  366.2 0.0 reduce-scatter.8.cloned.1.call-update
  366.2 6.6 %fusion = bf16[4096,512]{0,1:T(8,128)(2,1)} fusion(bf16[4096,512]{0,1:T(8,128)(2,1)} %all-gather.5.cloned.1.call-done, f32[512,512]{0,1:T(8,128)S(1)} %get-tuple-element.28, f32[512]{0:T(512)S(1)} %get-tuple-element.25, f32[512]{0:T(512)S(1)} %bitcast.20, f32[512]{0:T(512)S(1)} %pmax.7, s32[512]{0:T(512)S(1)} %bitcast.18, s32[512]{0:T(512)S(1)} %iota_add_fusion), kind=kOutput, calls=%fused_computation.2 | convolution fusion | flops 2151415808 | bytes 9447424 | tf_op jit(solution)/shard_map/dot_general | solution.py:45
  372.8 6.4 %copy.28 = bf16[4096,512]{1,0:T(8,128)(2,1)} copy(bf16[4096,512]{0,1:T(8,128)(2,1)} %fusion) | data formatting | bytes 8388608
  379.2 0.5 compare_select_fusion.1
  379.7 0.0 reduce-scatter.8.cloned.1.call-done
  379.7 1.8 convert_element_type.25
  (4 shorter events, 0.0 us)
Async XLA Ops:
  7.2 25.4 %copy-start.4 = (s32[2]{0:T(128)S(1)}, s32[2]{0:T(128)}, u32[]{:S(2)}) copy-start(s32[2]{0:T(128)} %param.11) | copy-start | bytes 28
  7.2 23.1 %all-gather.3.cloned.1.call-start = ((), (), s32[]{:S(2)}) async-start(), calls=%async_computation.3 | async-start | bytes 1572864 | tf_op jit(solution)/shard_map/all_gather | solution.py:11
  19.5 95.1 %all-gather.5.cloned.1.call-start = ((), (), s32[]{:S(2)}) async-start(), calls=%async_computation.4 | async-start | bytes 5242880 | tf_op jit(solution)/shard_map/all_gather | solution.py:17
  32.5 299.0 %reduce-scatter.4.cloned.1.call-start = ((), (), s32[]{:S(2)}) async-start(), calls=%async_computation.5 | async-start | bytes 10485760 | tf_op jit(solution)/shard_map/reduce_scatter | solution.py:48
  32.7 118.7 %copy-start = (s32[2,2,128]{2,1,0:T(2,128)S(1)}, s32[2,2,128]{2,1,0:T(2,128)}, u32[]{:S(2)}) copy-start(s32[2,2,128]{2,1,0:T(2,128)} %param.10) | copy-start | bytes 6148
  32.7 148.5 %copy-start.1 = (f32[2,2]{1,0:T(2,128)S(1)}, f32[2,2]{1,0:T(2,128)}, u32[]{:S(2)}) copy-start(f32[2,2]{1,0:T(2,128)} %param.13) | copy-start | bytes 52
  32.7 148.5 %copy-start.2 = (f32[2,2]{1,0:T(2,128)S(1)}, f32[2,2]{1,0:T(2,128)}, u32[]{:S(2)}) copy-start(f32[2,2]{1,0:T(2,128)} %param.12) | copy-start | bytes 52
  32.7 148.7 %copy-start.5 = (f32[2]{0:T(128)S(1)}, f32[2]{0:T(128)}, u32[]{:S(2)}) copy-start(f32[2]{0:T(128)} %param.14) | copy-start | bytes 28
  32.7 148.7 %copy-start.3 = (f32[2]{0:T(128)S(1)}, f32[2]{0:T(128)}, u32[]{:S(2)}) copy-start(f32[2]{0:T(128)} %constant.32.clone) | copy-start | bytes 28
  189.6 176.5 %reduce-scatter.6.cloned.1.call-start = ((), (), s32[]{:S(2)}) async-start(), calls=%async_computation.6 | async-start | bytes 3145728 | tf_op jit(solution)/shard_map/reduce_scatter | solution.py:57
  331.5 48.2 %reduce-scatter.8.cloned.1.call-start = ((), (), s32[]{:S(2)}) async-start(), calls=%async_computation.7 | async-start | bytes 1572864 | tf_op jit(solution)/shard_map/reduce_scatter | solution.py:58
Sparse Core Ops, SparseCore 0:
  19.7 10.5 all-gather.2
  32.7 81.9 all-gather.4
  189.8 141.6 reduce-scatter.3
  333.6 32.5 reduce-scatter.5
  368.3 8.5 reduce-scatter.7
where the time goes:
time: 388 us
  waiting for transfers between devices  269 us (69%)
  blocking collectives  70.3 us (18%)
  matrix products  20.5 us (5%)
  between operations  13.9 us (4%)
  local copies, waits for them, and re-layouts  11.1 us (3%)
    reduce_scatter x1, waiting for transfers between devices, shards(): lax.psum_scatter(lax.dot_general(head_weight, grad_logits, (((1,), (1,)),...  142 us
    all_gather x1, waiting for transfers between devices, shards(): lax.all_gather(all_pairs.reshape(width_part, row_count), 'vocab', axis=0,...  81.9 us
    reduce_scatter x1, waiting for transfers between devices, shards(): summed = lax.psum_scatter(summed, 'ctx', scatter_dimension=3, tiled=True)  34.6 us
    pmax x1, blocking collectives, shards(): row_max = lax.pmax(local_max, ('vocab', 'ctx', 'dp'))  30.9 us
    psum x1, blocking collectives, shards(): lax.psum((jnp.sum(shifted, axis=1), local_pick), ('vocab', 'ctx', 'dp'))  29.5 us
    all_gather x1, waiting for transfers between devices, shards(): all_pairs = lax.all_gather(along_seq, 'dp', axis=1, tiled=True)  10.7 us
    all_gather x1, blocking collectives, shards(): along_seq = lax.all_gather(hidden, 'ctx', axis=3, tiled=True)  9.91 us
    dot_general x1, matrix products, shards(): lax.dot_general(head_weight, grad_logits, (((1,), (1,)), ((), ())), prefe...  8 us
  transfers between devices with their start and end apart: 5, of which 4 were waited for; matrix products, arithmetic and copies ran while one was open for 4% of the time, Pallas kernels for 0%

commit v1 on v0

v1 whole, which is shorter than its diff:
```python
import jax
import jax.numpy as jnp
from jax import lax
from jax.sharding import PartitionSpec as P

BETA = 0.1


def ring(count, shift):
    return [(i, (i + shift) % count) for i in range(count)]


def shards(hidden, head_weight, targets, response_start, other_sums, ref_logp, loss_cotangent):
    f32, bf16 = jnp.float32, jnp.bfloat16
    n_voc, n_ctx, n_dp = lax.axis_size("vocab"), lax.axis_size("ctx"), lax.axis_size("dp")
    me_voc, me_ctx, me_dp = lax.axis_index("vocab"), lax.axis_index("ctx"), lax.axis_index("dp")
    part, pairs_here, sides, window = hidden.shape
    rows = pairs_here * sides * window
    width, columns = head_weight.shape
    seq_len = window * n_ctx

    weights = [head_weight]
    for t in range(1, n_dp):
        weights.append(lax.ppermute(head_weight, "dp", ring(n_dp, -t)))
    owners = [(me_dp + t) % n_dp for t in range(n_dp)]
    x = lax.all_gather(
        hidden.reshape(part, rows), ("ctx", "vocab"), axis=0, tiled=True
    ).reshape(n_ctx, width, rows)
    x_pairs = [x]
    for t in range(1, n_dp):
        x_pairs.append(lax.ppermute(x, "dp", ring(n_dp, -t)))

    mine = lambda a: lax.dynamic_slice_in_dim(a, me_dp * pairs_here, pairs_here, 0)
    by_block = lambda a: a.reshape(pairs_here, sides, n_ctx, window).transpose(2, 0, 1, 3).reshape(n_ctx, rows)
    target = by_block(mine(targets))

    logits, hits = [], []
    for w, owner in zip(weights, owners):
        part_logits = lax.dot_general(x, w, (((1,), (0,)), ((), ())), preferred_element_type=f32)
        first = ((me_voc * n_ctx + me_ctx) * n_dp + owner) * columns
        column = lax.broadcasted_iota(jnp.int32, part_logits.shape, 2) + first
        logits.append(part_logits)
        hits.append(column == target[:, :, None])
    top = logits[0].max(axis=2)
    for l in logits[1:]:
        top = jnp.maximum(top, l.max(axis=2))
    total = sum(jnp.exp(l - top[:, :, None]).sum(axis=2) for l in logits)
    picked = sum(jnp.where(h, l, jnp.zeros_like(l)).sum(axis=2) for h, l in zip(hits, logits))
    for axis, count in (("ctx", n_ctx), ("vocab", n_voc)):
        stats = jnp.stack([top, total, picked])
        seen = [stats] + [lax.ppermute(stats, axis, ring(count, s)) for s in range(1, count)]
        top = seen[0][0]
        for s in seen[1:]:
            top = jnp.maximum(top, s[0])
        total = sum(s[1] * jnp.exp(s[0] - top) for s in seen)
        picked = sum(s[2] for s in seen)

    token_logp = (picked - top - jnp.log(total)).reshape(n_ctx, pairs_here, sides, window)
    position = (
        lax.broadcasted_iota(jnp.int32, (n_ctx, pairs_here, 1, window), 0) * window
        + lax.broadcasted_iota(jnp.int32, (n_ctx, pairs_here, 1, window), 3)
    )
    mask = (position >= mine(response_start)[None, :, None, None]).astype(f32)
    seq_logp = mine(other_sums) + jnp.sum(mask * token_logp, axis=(0, 3))
    ratios = seq_logp - mine(ref_logp)
    margin = BETA * (ratios[:, 0] - ratios[:, 1])
    loss_here = jax.nn.softplus(-margin)
    factor = -BETA * jax.nn.sigmoid(-margin) * mine(loss_cotangent)
    side_sign = jnp.array([1.0, -1.0], dtype=f32)
    row_weight = (factor[None, :, None, None] * side_sign[None, None, :, None] * mask).reshape(n_ctx, rows)
    grads = [
        (row_weight[:, :, None] * (h.astype(f32) - jnp.exp(l - top[:, :, None]) / total[:, :, None])).astype(bf16)
        for h, l in zip(hits, logits)
    ]

    summed = None
    for s in list(range(1, n_voc)) + [0]:
        start = ((me_voc + s) % n_voc) * part
        here = sum(
            lax.dot_general(
                lax.dynamic_slice_in_dim(w, start, part, 0), g, (((1,), (2,)), ((), ())), preferred_element_type=f32
            )
            for w, g in zip(weights, grads)
        )
        block = lambda t: lax.dynamic_index_in_dim(here, (me_ctx + t) % n_ctx, 1, keepdims=False)
        kept = block(0)
        for t in range(1, n_ctx):
            kept = kept + lax.ppermute(block(t).astype(bf16), "ctx", ring(n_ctx, t)).astype(f32)
        if s:
            kept = lax.ppermute(kept.astype(bf16), "vocab", ring(n_voc, s)).astype(f32)
        summed = kept if summed is None else summed + kept
    grad_hidden = summed.astype(bf16).reshape(hidden.shape)

    grad_head = lax.dot_general(x, grads[0], (((0, 2), (0, 1)), ((), ())), preferred_element_type=f32)
    losses = [loss_here]
    for t in range(1, n_dp):
        theirs = lax.ppermute(grads[t], "dp", ring(n_dp, t))
        xt = x_pairs[n_dp - t]
        grad_head = grad_head + lax.dot_general(
            xt, theirs, (((0, 2), (0, 1)), ((), ())), preferred_element_type=f32
        )
        losses.append(lax.ppermute(loss_here, "dp", ring(n_dp, t)))
    pair_loss = jnp.zeros((n_dp, pairs_here), f32)
    for t, loss in enumerate(losses):
        owner = (me_dp - t) % n_dp
        pair_loss = jnp.where(
            lax.broadcasted_iota(jnp.int32, (n_dp, 1), 0) == owner, loss[None, :], pair_loss
        )
    return (grad_hidden, grad_head.astype(bf16), pair_loss.reshape(n_dp * pairs_here))


def solution(mesh):
    placed = (
        P("vocab", ("groups", "dp"), None, "ctx"),
        P(None, ("vocab", "ctx", "dp")),
        P("groups", None, None),
        P("groups"),
        P("groups", None),
        P("groups", None),
        P("groups"),
    )
    return jax.shard_map(
        shards,
        mesh=mesh,
        in_specs=placed,
        out_specs=(
            P("vocab", ("groups", "dp"), None, "ctx"),
            P("groups", ("vocab", "ctx", "dp")),
            P("groups"),
        ),
        check_vma=False,
    )
```

time: 388 us -> 161 us (0.41)
  waiting for transfers between devices: 269 us -> 87 us
  blocking collectives: 70.3 us -> 0 us
  starting transfers between devices: 0.2 us -> 9.6 us
  matrix products: 20.5 us -> 29.1 us
    reduce_scatter x3 -> x0, waiting for transfers between devices: 176 us -> none  [the longest x1 142 us: shards(): lax.psum_scatter(lax.dot_general(head_weight, grad_logits, (((1,), (1,)),...]
    all_gather x2 -> x1, waiting for transfers between devices: 92.6 us -> 53 us  [shards(): lax.all_gather(hidden.reshape(part, rows), ('ctx', 'vocab'), axis=0, tile...]
    ppermute x0 -> x15, waiting for transfers between devices: none -> 33.9 us  [the longest x4 15.4 us: shards(): lax.ppermute(block(t).astype(bf16), 'ctx', ring(n_ctx, t)).astype(f32)]
    pmax x1 -> x0, blocking collectives: 30.9 us -> none  [shards(): row_max = lax.pmax(local_max, ('vocab', 'ctx', 'dp'))]
    psum x1 -> x0, blocking collectives: 29.5 us -> none  [shards(): lax.psum((jnp.sum(shifted, axis=1), local_pick), ('vocab', 'ctx', 'dp'))]
    all_gather x1 -> x0, blocking collectives: 9.91 us -> none  [shards(): along_seq = lax.all_gather(hidden, 'ctx', axis=3, tiled=True)]
    ppermute x0 -> x15, starting transfers between devices: none -> 9.56 us  [the longest x4 4.52 us: shards(): lax.ppermute(stats, axis, ring(count, s))]
    dot_general x3 -> x12, matrix products: 20.5 us -> 29.1 us  [the longest x8 10 us: shards(): lax.dot_general(lax.dynamic_slice_in_dim(w, start, part, 0), g, (((1,), (...]
  transfers between devices with their start and end apart: 5 -> 16, of which waited for: 4 -> 8; matrix products, arithmetic and copies ran while one was open for 4% -> 19% of each run, Pallas kernels for 0% -> 0%
where the time goes in v1:
time: 161 us
  waiting for transfers between devices  87 us (54%)
  matrix products  29.1 us (18%)
  between operations  16.5 us (10%)
  local copies, waits for them, and re-layouts  14.6 us (9%)
  starting transfers between devices  9.6 us (6%)
  other arithmetic  3.94 us (2%)
    all_gather x1, waiting for transfers between devices, shards(): lax.all_gather(hidden.reshape(part, rows), ('ctx', 'vocab'), axis=0, tile...  53 us
    ppermute x4, waiting for transfers between devices, shards(): lax.ppermute(block(t).astype(bf16), 'ctx', ring(n_ctx, t)).astype(f32)  15.4 us
    ppermute x3, waiting for transfers between devices, shards(): kept = lax.ppermute(kept.astype(bf16), 'vocab', ring(n_voc, s)).astype(f32)  12.4 us
    dot_general x8, matrix products, shards(): lax.dot_general(lax.dynamic_slice_in_dim(w, start, part, 0), g, (((1,), (...  10 us
    dot_general x1, matrix products, shards(): lax.dot_general(xt, theirs, (((0, 2), (0, 1)), ((), ())), preferred_eleme...  7.37 us
    dot_general x2, matrix products, shards(): lax.dot_general(x, w, (((1,), (0,)), ((), ())), preferred_element_type=f32)  7.1 us
    unnamed x13, local copies, waits for them, and re-layouts  6.44 us
    ppermute x4, waiting for transfers between devices, shards(): lax.ppermute(stats, axis, ring(count, s))  6.06 us
  transfers between devices with their start and end apart: 16, of which 8 were waited for; matrix products, arithmetic and copies ran while one was open for 19% of the time, Pallas kernels for 0%

profile of v1, /device:TPU:0, one launch (start us, length us, event | category | flops | bytes accessed | tf_op | source)
XLA Modules:
  0.0 160.6 jit_solution(3792866569413709848)
XLA Ops:
  7.2 0.0 copy-start
  7.2 0.0 all-gather.2.cloned.1.call-start
  7.2 0.5 collective-permute-start
  7.7 0.2 all-gather.2.cloned.1.call-update
  7.9 1.2 dynamic_slice.66
  9.2 0.1 reshape.283
  9.3 0.1 eq.51
  9.4 53.0 %all-gather.2.cloned.1.call-done = bf16[8192,128]{0,1:T(8,128)(2,1)} async-done(((bf16[1024,128]{0,1:T(8,128)(2,1)}), bf16[8192,128]{0,1:T(8,128)(2,1)}) %all-gather.2.cloned.1.call-update) | async-done | bytes 2097168 | tf_op jit(solution)/shard_map/all_gather | solution.py:26
  62.3 3.2 %copy.29 = bf16[8192,128]{1,0:T(8,128)(2,1)S(1)} copy(bf16[8192,128]{0,1:T(8,128)(2,1)} %all-gather.2.cloned.1.call-done) | data formatting | bytes 4194304 | tf_op jit(solution)/shard_map/all_gather | solution.py:26
  65.6 3.5 %fusion.67 = (f32[2,128]{1,0:T(2,128)S(1)}, f32[2,128,512]{2,1,0:T(8,128)S(1)}) fusion(bf16[2,4096,128]{2,1,0:T(8,128)(2,1)S(1)} %bitcast.172, bf16[4096,512]{1,0:T(8,128)(2,1)} %param.9), kind=kOutput, calls=%fused_computation.118 | convolution fusion | flops 1073872640 | bytes 6816768 | tf_op jit(solution)/shard_map/dot_general | solution.py:39
  69.1 0.0 copy-start.4
  69.1 0.0 copy-start.2
  69.1 0.0 copy-start.3
  69.1 0.0 copy-start.5
  69.2 0.0 collective-permute-done
  69.2 3.6 %fusion.68 = (f32[2,128]{1,0:T(2,128)S(1)}, f32[2,128,512]{2,1,0:T(8,128)S(1)}) fusion(bf16[2,4096,128]{2,1,0:T(8,128)(2,1)S(1)} %bitcast.173, bf16[4096,512]{1,0:T(8,128)(2,1)} %collective-permute-done), kind=kOutput, calls=%fused_computation.119 | convolution fusion | flops 1073872640 | bytes 6816768 | tf_op jit(solution)/shard_map/dot_general | solution.py:39
  72.7 0.4 exponential_reduce_fusion.1
  73.2 0.6 collective-permute-start.1
  73.8 0.7 compare_convert_fusion.2
  74.5 2.3 %collective-permute-done.1 = f32[3,2,128]{2,1,0:T(2,128)S(1)} collective-permute-done((f32[3,2,128]{2,1,0:T(2,128)S(1)}, f32[3,2,128]{2,1,0:T(2,128)S(1)}, u32[]{:S(2)}, u32[]{:S(2)}) %collective-permute-start.1) | collective-permute-done | bytes 3104 | tf_op jit(solution)/shard_map/ppermute | solution.py:51
  76.9 1.9 %collective-permute-start.4 = (f32[3,2,128]{2,1,0:T(2,128)S(1)}, f32[3,2,128]{2,1,0:T(2,128)S(1)}, u32[]{:S(2)}, u32[]{:S(2)}) collective-permute-start(f32[3,2,128]{2,1,0:T(2,128)S(1)} %pad_maximum_fusion.1), channel_id=1, source_target_pairs={{0,12},{4,0},{8,4},{12,8},{1,13},{5,1},{9,5},{13,9},{2,14},{6,2},{... | collective-permute-start | bytes 9224 | tf_op jit(solution)/shard_map/ppermute | solution.py:51
  78.7 1.1 collective-permute-start.3
  79.9 0.9 collective-permute-start.2
  80.8 0.1 mul.203
  80.9 0.1 mul.182
  80.9 0.6 dynamic_slice.69
  81.5 0.0 collective-permute-start.13
  81.5 0.0 collective-permute-done.4
  81.5 1.7 %collective-permute-done.3 = f32[3,2,128]{2,1,0:T(2,128)S(1)} collective-permute-done((f32[3,2,128]{2,1,0:T(2,128)S(1)}, f32[3,2,128]{2,1,0:T(2,128)S(1)}, u32[]{:S(2)}, u32[]{:S(2)}) %collective-permute-start.3) | collective-permute-done | bytes 3104 | tf_op jit(solution)/shard_map/ppermute | solution.py:51
  83.2 2.0 %collective-permute-done.2 = f32[3,2,128]{2,1,0:T(2,128)S(1)} collective-permute-done((f32[3,2,128]{2,1,0:T(2,128)S(1)}, f32[3,2,128]{2,1,0:T(2,128)S(1)}, u32[]{:S(2)}, u32[]{:S(2)}) %collective-permute-start.2) | collective-permute-done | bytes 3104 | tf_op jit(solution)/shard_map/ppermute | solution.py:51
  85.3 0.1 reduce_sum.59
  85.4 0.1 reduce_sum.60
  85.5 0.6 fusion.66
  88.3 0.1 mul.200
  88.3 0.1 mul.201
  88.4 0.8 collective-permute-start.14
  89.3 0.4 fusion.33
  89.7 1.7 %fusion.7 = f32[1024,2,128]{2,0,1:T(8,128)S(1)} fusion(bf16[2,128,512]{2,1,0:T(8,128)(2,1)S(1)} %get-tuple-element.23, bf16[4096,512]{1,0:T(8,128)(2,1)} %param.9, s32[]{:T(128)S(6)} %select_n.129), kind=kOutput, calls=%fused_computation.12 | convolution fusion | flops 268435456 | bytes 2359300 | tf_op jit(solution)/shard_map/dot_general | solution.py:80
  91.4 1.7 %convolution_add_fusion = f32[1024,2,128]{2,0,1:T(8,128)S(1)} fusion(f32[1024,2,128]{2,0,1:T(8,128)S(1)} %fusion.7, bf16[2,128,512]{2,1,0:T(8,128)(2,1)S(1)} %get-tuple-element.22, bf16[4096,512]{1,0:T(8,128)(2,1)} %collective-permute-done, s32[]{:T(128)S(6)} %select_n.129), kind=kOutput, calls=%fused_computation.7 | convolution fusion | flops 268697600 | bytes 3407876 | tf_op jit(solution)/shard_map/dot_general | solution.py:80
  93.2 0.6 collective-permute-start.11
  93.8 0.5 fusion.10
  94.3 1.7 %convolution_add_fusion.1 = f32[1024,2,128]{2,0,1:T(8,128)S(1)} fusion(f32[1024,2,128]{2,0,1:T(8,128)S(1)} %fusion.10, bf16[2,128,512]{2,1,0:T(8,128)(2,1)S(1)} %get-tuple-element.22, bf16[4096,512]{1,0:T(8,128)(2,1)} %collective-permute-done, s32[]{:T(128)S(6)} %select_n.127), kind=kOutput, calls=%fused_computation.8 | convolution fusion | flops 268697600 | bytes 3407876 | tf_op jit(solution)/shard_map/dot_general | solution.py:80
  96.0 1.5 collective-permute-start.9
  97.6 0.5 fusion.13
  98.1 1.7 %convolution_add_fusion.2 = f32[1024,2,128]{2,0,1:T(8,128)S(1)} fusion(f32[1024,2,128]{2,0,1:T(8,128)S(1)} %fusion.13, bf16[2,128,512]{2,1,0:T(8,128)(2,1)S(1)} %get-tuple-element.22, bf16[4096,512]{1,0:T(8,128)(2,1)} %collective-permute-done, s32[]{:T(128)S(6)} %select_n.125), kind=kOutput, calls=%fused_computation.9 | convolution fusion | flops 268697600 | bytes 3407876 | tf_op jit(solution)/shard_map/dot_general | solution.py:80
  99.8 0.6 collective-permute-start.7
  100.4 0.5 fusion.16
  100.9 1.7 %convolution_add_fusion.3 = f32[1024,2,128]{2,0,1:T(8,128)S(1)} fusion(f32[1024,2,128]{2,0,1:T(8,128)S(1)} %fusion.16, bf16[2,128,512]{2,1,0:T(8,128)(2,1)S(1)} %get-tuple-element.22, bf16[4096,512]{1,0:T(8,128)(2,1)} %collective-permute-done, s32[]{:T(128)S(6)} %select_n.114), kind=kOutput, calls=%fused_computation.10 | convolution fusion | flops 268697600 | bytes 3407876 | tf_op jit(solution)/shard_map/dot_general | solution.py:80
  102.7 5.3 %collective-permute-done.9 = bf16[1024,128]{1,0:T(8,128)(2,1)S(1)} collective-permute-done((bf16[1024,128]{1,0:T(8,128)(2,1)S(1)}, bf16[1024,128]{1,0:T(8,128)(2,1)S(1)}, u32[]{:S(2)}, u32[]{:S(2)}) %collective-permute-start.9) | collective-permute-done | bytes 262176 | tf_op jit(solution)/shard_map/ppermute | solution.py:88
  108.0 0.6 collective-permute-start.5
  108.5 0.1 fusion.36
  108.6 5.0 %collective-permute-done.7 = bf16[1024,128]{1,0:T(8,128)(2,1)S(1)} collective-permute-done((bf16[1024,128]{1,0:T(8,128)(2,1)S(1)}, bf16[1024,128]{1,0:T(8,128)(2,1)S(1)}, u32[]{:S(2)}, u32[]{:S(2)}) %collective-permute-start.7) | collective-permute-done | bytes 262176 | tf_op jit(solution)/shard_map/ppermute | solution.py:88
  113.6 0.1 fusion.37
  113.6 5.1 %collective-permute-done.5 = bf16[1024,128]{1,0:T(8,128)(2,1)S(1)} collective-permute-done((bf16[1024,128]{1,0:T(8,128)(2,1)S(1)}, bf16[1024,128]{1,0:T(8,128)(2,1)S(1)}, u32[]{:S(2)}, u32[]{:S(2)}) %collective-permute-start.5) | collective-permute-done | bytes 262176 | tf_op jit(solution)/shard_map/ppermute | solution.py:88
  118.8 0.0 collective-permute-start.8
  118.8 0.1 fusion.38
  118.8 0.4 collective-permute-start.6
  119.2 4.6 %fusion.69 = f32[512,4096,1]{1,0,2:T(8,128)} fusion(bf16[2,128,512]{2,1,0:T(8,128)(2,1)S(1)} %get-tuple-element.23, bf16[2,4096,128]{2,1,0:T(8,128)(2,1)S(1)} %bitcast.175), kind=kOutput, calls=%fused_computation.120 | convolution fusion | flops 1073741824 | bytes 10747904 | tf_op jit(solution)/shard_map/dot_general | solution.py:94
  123.8 1.1 compare_select_fusion.3
  124.9 12.4 %collective-permute-done.8 = bf16[1024,128]{1,0:T(8,128)(2,1)S(1)} collective-permute-done((bf16[1024,128]{1,0:T(8,128)(2,1)S(1)}, bf16[1024,128]{1,0:T(8,128)(2,1)S(1)}, u32[]{:S(2)}, u32[]{:S(2)}) %collective-permute-start.8) | collective-permute-done | bytes 262176 | tf_op jit(solution)/shard_map/ppermute | solution.py:90
  137.3 0.9 fusion.35
  138.2 1.8 %copy.34 = bf16[1024,128]{0,1:T(8,128)(2,1)} copy(bf16[1024,128]{1,0:T(8,128)(2,1)} %fusion.35) | data formatting | bytes 524288 | tf_op jit(solution)/shard_map/convert_element_type | solution.py:92
  140.0 7.4 %fusion.1 = bf16[4096,512]{0,1:T(8,128)(2,1)} fusion(bf16[2,128,512]{2,1,0:T(8,128)(2,1)} %collective-permute-done.12, bf16[2,4096,128]{2,1,0:T(8,128)(2,1)} %collective-permute-done.13, f32[512,4096,1]{1,0,2:T(8,128)} %fusion.69), kind=kOutput, calls=%fused_computation.2 | convolution fusion | flops 1077936128 | bytes 14942208 | tf_op jit(solution)/shard_map/dot_general | solution.py:99
  147.4 6.4 %copy.37 = bf16[4096,512]{1,0:T(8,128)(2,1)} copy(bf16[4096,512]{0,1:T(8,128)(2,1)} %fusion.1) | data formatting | bytes 8388608
  (35 shorter events, 0.3 us)
Async XLA Ops:
  7.2 2.0 %copy-start = (s32[2,2,128]{2,1,0:T(2,128)S(1)}, s32[2,2,128]{2,1,0:T(2,128)}, u32[]{:S(2)}) copy-start(s32[2,2,128]{2,1,0:T(2,128)} %param.10) | copy-start | bytes 6148
  7.2 55.2 %all-gather.2.cloned.1.call-start = ((), (), s32[]{:S(2)}) async-start(), calls=%async_computation | async-start | bytes 2359296 | tf_op jit(solution)/shard_map/all_gather | solution.py:26
  7.2 61.9 %collective-permute-start = (bf16[4096,512]{1,0:T(8,128)(2,1)}, bf16[4096,512]{1,0:T(8,128)(2,1)}, u32[]{:S(2)}, u32[]{:S(2)}) collective-permute-start(bf16[4096,512]{1,0:T(8,128)(2,1)} %param.9), channel_id=1, source_target_pairs={{0,1},{1,0},{2,3},{3,2},{4,5},{5,4},{6,7},{7,6},{8,9},{9,8},{10,11... | collective-permute-start | bytes 12582920 | tf_op jit(solution)/shard_map/ppermute | solution.py:24
  69.1 11.8 %copy-start.4 = (f32[2]{0:T(128)S(1)}, f32[2]{0:T(128)}, u32[]{:S(2)}) copy-start(f32[2]{0:T(128)} %param.14) | copy-start | bytes 28
  69.1 16.4 %copy-start.2 = (f32[2,2]{1,0:T(2,128)S(1)}, f32[2,2]{1,0:T(2,128)}, u32[]{:S(2)}) copy-start(f32[2,2]{1,0:T(2,128)} %param.12) | copy-start | bytes 52
  69.1 16.4 %copy-start.3 = (f32[2,2]{1,0:T(2,128)S(1)}, f32[2,2]{1,0:T(2,128)}, u32[]{:S(2)}) copy-start(f32[2,2]{1,0:T(2,128)} %param.13) | copy-start | bytes 52
  69.1 19.1 %copy-start.5 = (f32[2]{0:T(128)S(1)}, f32[2]{0:T(128)}, u32[]{:S(2)}) copy-start(f32[2]{0:T(128)} %constant.127.clone) | copy-start | bytes 28
  73.2 3.7 %collective-permute-start.1 = (f32[3,2,128]{2,1,0:T(2,128)S(1)}, f32[3,2,128]{2,1,0:T(2,128)S(1)}, u32[]{:S(2)}, u32[]{:S(2)}) collective-permute-start(f32[3,2,128]{2,1,0:T(2,128)S(1)} %pad_maximum_fusion), channel_id=1, source_target_pairs={{0,2},{2,0},{1,3},{3,1},{4,6},{6,4},{5,7},{7,5},{8,10},{10,8},{9,1... | collective-permute-start | bytes 9224 | tf_op jit(solution)/shard_map/ppermute | solution.py:51
  76.9 4.7 %collective-permute-start.4 = (f32[3,2,128]{2,1,0:T(2,128)S(1)}, f32[3,2,128]{2,1,0:T(2,128)S(1)}, u32[]{:S(2)}, u32[]{:S(2)}) collective-permute-start(f32[3,2,128]{2,1,0:T(2,128)S(1)} %pad_maximum_fusion.1), channel_id=1, source_target_pairs={{0,12},{4,0},{8,4},{12,8},{1,13},{5,1},{9,5},{13,9},{2,14},{6,2},{... | collective-permute-start | bytes 9224 | tf_op jit(solution)/shard_map/ppermute | solution.py:51
  78.7 4.5 %collective-permute-start.3 = (f32[3,2,128]{2,1,0:T(2,128)S(1)}, f32[3,2,128]{2,1,0:T(2,128)S(1)}, u32[]{:S(2)}, u32[]{:S(2)}) collective-permute-start(f32[3,2,128]{2,1,0:T(2,128)S(1)} %pad_maximum_fusion.1), channel_id=1, source_target_pairs={{0,8},{4,12},{8,0},{12,4},{1,9},{5,13},{9,1},{13,5},{2,10},{6,14},... | collective-permute-start | bytes 9224 | tf_op jit(solution)/shard_map/ppermute | solution.py:51
  79.9 5.4 %collective-permute-start.2 = (f32[3,2,128]{2,1,0:T(2,128)S(1)}, f32[3,2,128]{2,1,0:T(2,128)S(1)}, u32[]{:S(2)}, u32[]{:S(2)}) collective-permute-start(f32[3,2,128]{2,1,0:T(2,128)S(1)} %pad_maximum_fusion.1), channel_id=1, source_target_pairs={{0,4},{4,8},{8,12},{12,0},{1,5},{5,9},{9,13},{13,1},{2,6},{6,10},{... | collective-permute-start | bytes 9224 | tf_op jit(solution)/shard_map/ppermute | solution.py:51
  81.5 58.5 %collective-permute-start.13 = (bf16[2,4096,128]{2,1,0:T(8,128)(2,1)S(1)}, bf16[2,4096,128]{2,1,0:T(8,128)(2,1)}, u32[]{:S(2)}, u32[]{:S(2)}) collective-permute-start(bf16[2,4096,128]{2,1,0:T(8,128)(2,1)S(1)} %bitcast.174), channel_id=1, source_target_pairs={{0,1},{1,0},{2,3},{3,2},{4,5},{5,4},{6,7},{7,6},{8,9},{9,8},{10,11... | collective-permute-start | bytes 6291464 | tf_op jit(solution)/shard_map/ppermute | solution.py:31
  88.4 5.4 %copy-start.1 = (bf16[4096,512]{1,0:T(8,128)(2,1)S(1)}, bf16[4096,512]{1,0:T(8,128)(2,1)}, u32[]{:S(2)}) copy-start(bf16[4096,512]{1,0:T(8,128)(2,1)} %param.9) | copy-start | bytes 12582916
  88.4 30.4 %collective-permute-start.14 = (f32[1]{0:T(128)}, f32[1]{0:T(128)}, u32[]{:S(2)}, u32[]{:S(2)}) collective-permute-start(f32[1]{0:T(128)} %select_n.131), channel_id=1, source_target_pairs={{0,1},{1,0},{2,3},{3,2},{4,5},{5,4},{6,7},{7,6},{8,9},{9,8},{10,11... | collective-permute-start | bytes 20 | tf_op jit(solution)/shard_map/ppermute | solution.py:102
  93.2 30.6 %collective-permute-start.11 = (bf16[1024,128]{1,0:T(8,128)(2,1)S(1)}, bf16[1024,128]{1,0:T(8,128)(2,1)S(1)}, u32[]{:S(2)}, u32[]{:S(2)}) collective-permute-start(bf16[1024,128]{1,0:T(8,128)(2,1)S(1)} %fusion.42), channel_id=1, source_target_pairs={{0,2},{2,0},{1,3},{3,1},{4,6},{6,4},{5,7},{7,5},{8,10},{10,8},{9,1... | collective-permute-start | bytes 786440 | tf_op jit(solution)/shard_map/ppermute | solution.py:88
  96.0 11.9 %collective-permute-start.9 = (bf16[1024,128]{1,0:T(8,128)(2,1)S(1)}, bf16[1024,128]{1,0:T(8,128)(2,1)S(1)}, u32[]{:S(2)}, u32[]{:S(2)}) collective-permute-start(bf16[1024,128]{1,0:T(8,128)(2,1)S(1)} %fusion.41), channel_id=1, source_target_pairs={{0,2},{2,0},{1,3},{3,1},{4,6},{6,4},{5,7},{7,5},{8,10},{10,8},{9,1... | collective-permute-start | bytes 786440 | tf_op jit(solution)/shard_map/ppermute | solution.py:88
  99.8 13.7 %collective-permute-start.7 = (bf16[1024,128]{1,0:T(8,128)(2,1)S(1)}, bf16[1024,128]{1,0:T(8,128)(2,1)S(1)}, u32[]{:S(2)}, u32[]{:S(2)}) collective-permute-start(bf16[1024,128]{1,0:T(8,128)(2,1)S(1)} %fusion.40), channel_id=1, source_target_pairs={{0,2},{2,0},{1,3},{3,1},{4,6},{6,4},{5,7},{7,5},{8,10},{10,8},{9,1... | collective-permute-start | bytes 786440 | tf_op jit(solution)/shard_map/ppermute | solution.py:88
  108.0 10.8 %collective-permute-start.5 = (bf16[1024,128]{1,0:T(8,128)(2,1)S(1)}, bf16[1024,128]{1,0:T(8,128)(2,1)S(1)}, u32[]{:S(2)}, u32[]{:S(2)}) collective-permute-start(bf16[1024,128]{1,0:T(8,128)(2,1)S(1)} %fusion.39), channel_id=1, source_target_pairs={{0,2},{2,0},{1,3},{3,1},{4,6},{6,4},{5,7},{7,5},{8,10},{10,8},{9,1... | collective-permute-start | bytes 786440 | tf_op jit(solution)/shard_map/ppermute | solution.py:88
  113.6 11.4 %collective-permute-start.10 = (bf16[1024,128]{1,0:T(8,128)(2,1)S(1)}, bf16[1024,128]{1,0:T(8,128)(2,1)S(1)}, u32[]{:S(2)}, u32[]{:S(2)}) collective-permute-start(bf16[1024,128]{1,0:T(8,128)(2,1)S(1)} %fusion.36), channel_id=1, source_target_pairs={{0,12},{4,0},{8,4},{12,8},{1,13},{5,1},{9,5},{13,9},{2,14},{6,2},{... | collective-permute-start | bytes 786440 | tf_op jit(solution)/shard_map/ppermute | solution.py:90
  118.8 18.6 %collective-permute-start.8 = (bf16[1024,128]{1,0:T(8,128)(2,1)S(1)}, bf16[1024,128]{1,0:T(8,128)(2,1)S(1)}, u32[]{:S(2)}, u32[]{:S(2)}) collective-permute-start(bf16[1024,128]{1,0:T(8,128)(2,1)S(1)} %fusion.37), channel_id=1, source_target_pairs={{0,8},{4,12},{8,0},{12,4},{1,9},{5,13},{9,1},{13,5},{2,10},{6,14},... | collective-permute-start | bytes 786440 | tf_op jit(solution)/shard_map/ppermute | solution.py:90
  118.8 18.5 %collective-permute-start.6 = (bf16[1024,128]{1,0:T(8,128)(2,1)S(1)}, bf16[1024,128]{1,0:T(8,128)(2,1)S(1)}, u32[]{:S(2)}, u32[]{:S(2)}) collective-permute-start(bf16[1024,128]{1,0:T(8,128)(2,1)S(1)} %fusion.38), channel_id=1, source_target_pairs={{0,4},{4,8},{8,12},{12,0},{1,5},{5,9},{9,13},{13,1},{2,6},{6,10},{... | collective-permute-start | bytes 786440 | tf_op jit(solution)/shard_map/ppermute | solution.py:90
  123.8 16.2 %collective-permute-start.12 = (bf16[2,128,512]{2,1,0:T(8,128)(2,1)S(1)}, bf16[2,128,512]{2,1,0:T(8,128)(2,1)}, u32[]{:S(2)}, u32[]{:S(2)}) collective-permute-start(bf16[2,128,512]{2,1,0:T(8,128)(2,1)S(1)} %get-tuple-element.22), channel_id=1, source_target_pairs={{0,1},{1,0},{2,3},{3,2},{4,5},{5,4},{6,7},{7,6},{8,9},{9,8},{10,11... | collective-permute-start | bytes 786440 | tf_op jit(solution)/shard_map/ppermute | solution.py:97
Sparse Core Ops, SparseCore 0:
  10.2 52.1 all-gather.1

commit v2 on v0

v2 whole, which is shorter than its diff:
```python
import functools

import jax
import jax.numpy as jnp
from jax import lax
from jax.experimental import pallas as pl
from jax.experimental.pallas import tpu as pltpu
from jax.sharding import PartitionSpec as P

BETA = 0.1
F32, BF16 = jnp.float32, jnp.bfloat16
VMEM_BYTES = 32 * 1024 * 1024


def ring(count, shift):
    return [(i, (i + shift) % count) for i in range(count)]


def whole(shape):
    return pl.BlockSpec(shape, lambda *_: (0,) * len(shape))


def params():
    return pltpu.CompilerParams(vmem_limit_bytes=VMEM_BYTES)


def cost(flops, moved):
    return pl.CostEstimate(flops=int(flops), bytes_accessed=int(moved), transcendentals=0)


def size_of(*arrays):
    return sum(a.size * a.dtype.itemsize for a in arrays)


def logits_kernel(steps, has_acc, with_stats, columns, meta, *refs):
    count = sum(len(s) for s in steps)
    chunks, refs = refs[:count], refs[count:]
    w_own, w_far = refs[:2]
    refs = refs[2:]
    acc = None
    if has_acc:
        acc, refs = refs[0], refs[1:]
    if with_stats:
        target, refs = refs[0], refs[1:]
    out = refs[0]
    step = pl.program_id(0)

    @pl.when(step == 0)
    def _():
        if has_acc:
            out[...] = acc[...]
        else:
            out[...] = jnp.zeros_like(out)

    first_chunk = 0
    for i, blocks in enumerate(steps):
        here = [(t, chunks[first_chunk + j]) for j, t in enumerate(blocks)]
        first_chunk += len(blocks)

        @pl.when(step == i)
        def _():
            for t, chunk in here:
                x = chunk[...]
                out[t, :, :columns] += jnp.dot(x, w_own[...], preferred_element_type=F32)
                out[t, :, columns:] += jnp.dot(x, w_far[...], preferred_element_type=F32)

    if with_stats:
        stats = refs[1]

        @pl.when(step == len(steps) - 1)
        def _():
            n_blocks, rows, _ = out.shape
            for t in range(n_blocks):
                own, far = out[t, :, :columns], out[t, :, columns:]
                top = jnp.max(jnp.maximum(own, far), axis=1, keepdims=True)
                total = jnp.sum(jnp.exp(own - top) + jnp.exp(far - top), axis=1, keepdims=True)
                column = lax.broadcasted_iota(jnp.int32, own.shape, 1)
                wanted = target[t * rows:(t + 1) * rows, :]
                zero = jnp.zeros_like(own)
                picked = jnp.sum(
                    jnp.where(column + meta[len(steps)] == wanted, own, zero)
                    + jnp.where(column + meta[len(steps) + 1] == wanted, far, zero),
                    axis=1,
                    keepdims=True,
                )
                lane = lax.broadcasted_iota(jnp.int32, (rows, 128), 1)
                packed = jnp.where(lane == 0, top, jnp.where(lane == 1, total, picked))
                stats[:, t * rows:(t + 1) * rows] = packed.T[:8, :]


def logits_call(steps, chunks, k_ids, weights, acc, target, firsts, part, columns):
    n_blocks = max(max(s) for s in steps) + 1 if acc is None else acc.shape[0]
    rows = chunks[0].shape[0]
    meta = jnp.stack(list(k_ids) + list(firsts)).astype(jnp.int32)
    with_stats = target is not None
    out_shape = [jax.ShapeDtypeStruct((n_blocks, rows, 2 * columns), F32)]
    if with_stats:
        out_shape.append(jax.ShapeDtypeStruct((8, n_blocks * rows), F32))
    operands = list(chunks) + list(weights)
    specs = [whole(c.shape) for c in chunks]
    specs += [pl.BlockSpec((part, columns), lambda i, meta: (meta[i], 0))] * 2
    if acc is not None:
        operands.append(acc)
        specs.append(whole(acc.shape))
    if with_stats:
        operands.append(target)
        specs.append(whole(target.shape))
    return pl.pallas_call(
        functools.partial(logits_kernel, steps, acc is not None, with_stats, columns),
        out_shape=out_shape,
        grid_spec=pltpu.PrefetchScalarGridSpec(
            num_scalar_prefetch=1,
            grid=(len(steps),),
            in_specs=specs,
            out_specs=[whole(s.shape) for s in out_shape],
        ),
        compiler_params=params(),
        cost_estimate=cost(
            2 * len(chunks) * rows * part * 2 * columns,
            size_of(*chunks) + len(steps) * 4 * part * columns + n_blocks * rows * columns * 16,
        ),
    )(meta, *operands)


def spread(grads_own, grads_far, w_own, w_far, send, kept):
    n_blocks, rows, columns = grads_own.shape
    flat = (n_blocks * rows, columns)
    over = (((1,), (1,)), ((), ()))
    here = lax.dot_general(grads_own[...].reshape(flat), w_own[...], over, preferred_element_type=F32)
    here += lax.dot_general(grads_far[...].reshape(flat), w_far[...], over, preferred_element_type=F32)
    kept[...] = here[:rows]
    for t in range(1, n_blocks):
        send[t - 1] = here[t * rows:(t + 1) * rows].astype(BF16)


def grads_kernel(n_stats, columns, meta, logits, target, info, scalars, *refs):
    stats, refs = refs[:n_stats], refs[n_stats:]
    w_own, w_far, grads_own, grads_far, send, kept, loss = refs
    n_blocks, rows, _ = logits.shape
    top = stats[0][0:1, :]
    for s in stats[1:]:
        top = jnp.maximum(top, s[0:1, :])
    total = jnp.zeros_like(top)
    picked = jnp.zeros_like(top)
    for s in stats:
        total += s[1:2, :] * jnp.exp(s[0:1, :] - top)
        picked += s[2:3, :]
    signed_mask = info[0:1, :]
    token_logp = picked - top - jnp.log(total)
    margin = BETA * (jnp.sum(signed_mask * token_logp, axis=1, keepdims=True) + scalars[0:1, :])
    loss[...] = jnp.maximum(-margin, 0.0) + jnp.log1p(jnp.exp(-jnp.abs(margin)))
    factor = -BETA * (1.0 / (1.0 + jnp.exp(margin))) * scalars[1:2, :]
    weight = factor[:, 0:1] * signed_mask
    lines = lax.broadcasted_iota(jnp.int32, (128, top.shape[1]), 0)
    packed = jnp.where(lines == 0, top, jnp.where(lines == 1, weight, 1.0 / total)).T
    for t in range(n_blocks):
        at = slice(t * rows, (t + 1) * rows)
        top_t, weight_t, inverse_t = packed[at, 0:1], packed[at, 1:2], packed[at, 2:3]
        wanted = target[at, :]
        for j, grads in enumerate((grads_own, grads_far)):
            l = logits[t, :, j * columns:(j + 1) * columns]
            column = lax.broadcasted_iota(jnp.int32, l.shape, 1) + meta[1 + j]
            hit = jnp.where(column == wanted, 1.0, 0.0)
            grads[t] = (weight_t * (hit - jnp.exp(l - top_t) * inverse_t)).astype(BF16)
    spread(grads_own, grads_far, w_own, w_far, send, kept)


def spread_kernel(meta, grads_own, grads_far, w_own, w_far, send, kept):
    spread(grads_own, grads_far, w_own, w_far, send, kept)


def spread_shapes(n_blocks, rows, part):
    return [
        jax.ShapeDtypeStruct((n_blocks - 1, rows, part), BF16),
        jax.ShapeDtypeStruct((rows, part), F32),
    ]


def grads_call(logits, target, info, scalars, stats, weights, k_id, firsts, part, columns):
    n_blocks, rows, _ = logits.shape
    meta = jnp.stack([k_id] + list(firsts)).astype(jnp.int32)
    grads = jax.ShapeDtypeStruct((n_blocks, rows, columns), BF16)
    out_shape = [grads, grads] + spread_shapes(n_blocks, rows, part) + [jax.ShapeDtypeStruct((1, 128), F32)]
    small = [logits, target, info, scalars] + list(stats)
    return pl.pallas_call(
        functools.partial(grads_kernel, len(stats), columns),
        out_shape=out_shape,
        grid_spec=pltpu.PrefetchScalarGridSpec(
            num_scalar_prefetch=1,
            grid=(1,),
            in_specs=[whole(a.shape) for a in small]
            + [pl.BlockSpec((part, columns), lambda i, meta: (meta[0], 0))] * 2,
            out_specs=[whole(s.shape) for s in out_shape],
        ),
        compiler_params=params(),
        cost_estimate=cost(4 * n_blocks * rows * part * columns, size_of(logits) + 4 * part * columns),
    )(meta, *small, *weights)


def spread_call(grads_own, grads_far, weights, k_id, part, columns):
    n_blocks, rows, _ = grads_own.shape
    out_shape = spread_shapes(n_blocks, rows, part)
    return pl.pallas_call(
        spread_kernel,
        out_shape=out_shape,
        grid_spec=pltpu.PrefetchScalarGridSpec(
            num_scalar_prefetch=1,
            grid=(1,),
            in_specs=[whole(grads_own.shape)] * 2
            + [pl.BlockSpec((part, columns), lambda i, meta: (meta[0], 0))] * 2,
            out_specs=[whole(s.shape) for s in out_shape],
        ),
        compiler_params=params(),
        cost_estimate=cost(4 * n_blocks * rows * part * columns, 4 * part * columns),
    )(k_id.reshape(1).astype(jnp.int32), grads_own, grads_far, *weights)


def head_kernel(n_pairs, meta, *refs):
    xs, grads, out = refs[:n_pairs], refs[n_pairs:2 * n_pairs], refs[2 * n_pairs]
    total = None
    for x, g in zip(xs, grads):
        n_blocks, rows, columns = g.shape
        product = lax.dot_general(
            x[...].reshape(n_blocks * rows, x.shape[3]),
            g[...].reshape(n_blocks * rows, columns),
            (((0,), (0,)), ((), ())),
            preferred_element_type=F32,
        )
        total = product if total is None else total + product
    out[...] = total.astype(BF16)


def head_call(xs, grads, k_ids):
    n_blocks, n_parts, rows, part = xs[0].shape
    columns = grads[0].shape[2]
    return pl.pallas_call(
        functools.partial(head_kernel, len(xs)),
        out_shape=jax.ShapeDtypeStruct((n_parts * part, columns), BF16),
        grid_spec=pltpu.PrefetchScalarGridSpec(
            num_scalar_prefetch=1,
            grid=(n_parts,),
            in_specs=[pl.BlockSpec((n_blocks, 1, rows, part), lambda i, meta: (0, i, 0, 0))] * len(xs)
            + [whole(g.shape) for g in grads],
            out_specs=pl.BlockSpec((part, columns), lambda i, meta: (meta[i], 0)),
        ),
        compiler_params=params(),
        cost_estimate=cost(
            2 * len(xs) * n_blocks * rows * n_parts * part * columns,
            size_of(*xs, *grads) + 2 * n_parts * part * columns,
        ),
    )(jnp.stack(k_ids).astype(jnp.int32), *xs, *grads)


def shards(hidden, head_weight, targets, response_start, other_sums, ref_logp, loss_cotangent):
    n_voc, n_ctx, n_dp = lax.axis_size("vocab"), lax.axis_size("ctx"), lax.axis_size("dp")
    me_voc, me_ctx, me_dp = lax.axis_index("vocab"), lax.axis_index("ctx"), lax.axis_index("dp")
    part, _, sides, window = hidden.shape
    rows = sides * window
    columns = head_weight.shape[1]

    weights = (head_weight, lax.ppermute(head_weight, "dp", ring(n_dp, 1)))
    firsts = [
        ((me_voc * n_ctx + me_ctx) * n_dp + owner) * columns for owner in (me_dp, (me_dp + 1) % n_dp)
    ]
    part_of = [(me_voc - s) % n_voc for s in range(n_voc)]

    own = hidden.transpose(1, 2, 3, 0).reshape(rows, part)
    order = [0]
    for s in range(1, n_voc // 2 + 1):
        order += [s] if 2 * s == n_voc else [s, n_voc - s]
    chunk = {(0, 0): own}
    for t in range(1, n_ctx):
        chunk[t, 0] = lax.ppermute(own, "ctx", ring(n_ctx, t))
    source = own
    for i, s in enumerate(order[1:]):
        chunk[0, s] = lax.ppermute(source, "vocab", ring(n_voc, s))
        if i % 2:
            held = lax.optimization_barrier((source, chunk[0, order[i]], chunk[0, s]))
            source, chunk[0, order[i]], chunk[0, s] = held
    for s in order[1:]:
        for t in range(1, n_ctx):
            chunk[t, s] = lax.ppermute(chunk[0, s], "ctx", ring(n_ctx, t))

    blocks_of = [(me_ctx - t) % n_ctx for t in range(n_ctx)]
    by_block = lambda a: jnp.concatenate(
        [lax.dynamic_slice_in_dim(a, b * window, window, 1).reshape(rows) for b in blocks_of]
    )
    mine = lambda a: lax.dynamic_index_in_dim(a, me_dp, 0, keepdims=False)
    target = by_block(mine(targets))[:, None]
    position = lax.broadcasted_iota(jnp.int32, (sides, window * n_ctx), 1)
    side_sign = jnp.array([1.0, -1.0], dtype=F32)[:, None]
    signed_mask = jnp.where(position >= mine(response_start), side_sign, 0.0)
    info = jnp.broadcast_to(by_block(signed_mask)[None, :], (8, n_ctx * rows))
    ratio = mine(other_sums) - mine(ref_logp)
    scalars = jnp.stack([ratio[0] - ratio[1], mine(loss_cotangent)])
    scalars = jnp.broadcast_to(jnp.pad(scalars, (0, 6))[:, None], (8, 128))

    call = functools.partial(logits_call, part=part, columns=columns)
    early = order[:3]
    last = order[-1]
    everything = list(range(n_ctx))
    first_steps = [everything] + [[0] for _ in early[1:]]
    logits, = call(
        first_steps,
        [chunk[t, s] for s, ts in zip(early, first_steps) for t in ts],
        [part_of[s] for s in early],
        weights, None, None, firsts,
    )
    middle_steps = [everything[1:] for _ in early[1:]] + [everything for _ in order[3:-1]] + [[0]]
    logits, = call(
        middle_steps,
        [chunk[t, s] for s, ts in zip(order[1:], middle_steps) for t in ts],
        [part_of[s] for s in order[1:]],
        weights, logits, None, firsts,
    )
    logits, stats = call(
        [everything[1:]],
        [chunk[t, last] for t in everything[1:]],
        [part_of[last]],
        weights, logits, target, firsts,
    )

    others = [lax.ppermute(stats, "ctx", ring(n_ctx, t)) for t in range(1, n_ctx)]
    top = stats[0]
    for o in others:
        top = jnp.maximum(top, o[0])
    def turn(o, t):
        return jnp.roll(o.reshape(8, n_ctx, rows), t, axis=1).reshape(8, n_ctx * rows)
    others = [turn(o, t) for t, o in enumerate(others, 1)]
    top = stats[0]
    for o in others:
        top = jnp.maximum(top, o[0])
    total = sum(o[1] * jnp.exp(o[0] - top) for o in [stats] + others)
    picked = sum(o[2] for o in [stats] + others)
    stats = jnp.pad(jnp.stack([top, total, picked]), ((0, 5), (0, 0)))
    all_stats = [stats] + [lax.ppermute(stats, "vocab", ring(n_voc, s)) for s in range(1, n_voc)]

    goes_to = [(me_voc + s) % n_voc for s in range(n_voc)]
    leave = order[::-1]
    grads_own, grads_far, send, kept, loss = grads_call(
        logits, target, info, scalars, all_stats, weights, goes_to[leave[0]], firsts, part, columns
    )
    theirs = lax.ppermute(grads_far, "dp", ring(n_dp, 1))
    summed = None
    for i, s in enumerate(leave):
        if i:
            send, kept = spread_call(grads_own, grads_far, weights, goes_to[s], part, columns)
        for t in range(1, n_ctx):
            kept = kept + lax.ppermute(send[t - 1], "ctx", ring(n_ctx, -t)).astype(F32)
        if s:
            kept = lax.ppermute(kept.astype(BF16), "vocab", ring(n_voc, s)).astype(F32)
        summed = kept if summed is None else summed + kept
    grad_hidden = summed.astype(BF16).reshape(1, sides, window, part).transpose(3, 0, 1, 2)

    stacked = jnp.stack([jnp.stack([chunk[t, s] for s in range(n_voc)]) for t in range(n_ctx)])
    far_stacked = lax.ppermute(stacked, "dp", ring(n_dp, 1))
    grad_head = head_call([stacked, far_stacked], [grads_own, theirs], part_of)

    far_loss = lax.ppermute(loss, "dp", ring(n_dp, 1))
    pair = lax.broadcasted_iota(jnp.int32, (n_dp,), 0)
    pair_loss = jnp.where(pair == me_dp, loss[0, :n_dp], far_loss[0, :n_dp])
    return (grad_hidden, grad_head, pair_loss)


def solution(mesh):
    placed = (
        P("vocab", ("groups", "dp"), None, "ctx"),
        P(None, ("vocab", "ctx", "dp")),
        P("groups", None, None),
        P("groups"),
        P("groups", None),
        P("groups", None),
        P("groups"),
    )
    return jax.shard_map(
        shards,
        mesh=mesh,
        in_specs=placed,
        out_specs=(
            P("vocab", ("groups", "dp"), None, "ctx"),
            P("groups", ("vocab", "ctx", "dp")),
            P("groups"),
        ),
        check_vma=False,
    )
```

time: 388 us -> 131 us (0.34)
  waiting for transfers between devices: 269 us -> 52.3 us
  blocking collectives: 70.3 us -> 0 us
  Pallas kernels: 0 us -> 26.8 us
  starting transfers between devices: 0.2 us -> 25.6 us
  matrix products: 20.5 us -> 0 us
  between operations: 13.9 us -> 2.16 us
  local copies, waits for them, and re-layouts: 11.1 us -> 15.9 us
  other arithmetic: 3.1 us -> 7.02 us
    reduce_scatter x3 -> x0, waiting for transfers between devices: 176 us -> none  [the longest x1 142 us: shards(): lax.psum_scatter(lax.dot_general(head_weight, grad_logits, (((1,), (1,)),...]
    all_gather x2 -> x0, waiting for transfers between devices: 92.6 us -> none  [the longest x1 81.9 us: shards(): lax.all_gather(all_pairs.reshape(width_part, row_count), 'vocab', axis=0,...]
    ppermute x0 -> x22, waiting for transfers between devices: none -> 52.3 us  [the longest x3 16.9 us: shards(): chunk[0, s] = lax.ppermute(source, 'vocab', ring(n_voc, s))]
    pmax x1 -> x0, blocking collectives: 30.9 us -> none  [shards(): row_max = lax.pmax(local_max, ('vocab', 'ctx', 'dp'))]
    psum x1 -> x0, blocking collectives: 29.5 us -> none  [shards(): lax.psum((jnp.sum(shifted, axis=1), local_pick), ('vocab', 'ctx', 'dp'))]
    pallas_call x0 -> x8, Pallas kernels: none -> 26.8 us  [the longest x3 10.7 us: logits_call(): pl.pallas_call(functools.partial(logits_kernel, steps, acc is not None, w...]
    ppermute x0 -> x22, starting transfers between devices: none -> 25.6 us  [the longest x3 6.04 us: shards(): chunk[0, s] = lax.ppermute(source, 'vocab', ring(n_voc, s))]
    dot_general x3 -> x0, matrix products: 20.5 us -> none  [the longest x1 8 us: shards(): lax.dot_general(head_weight, grad_logits, (((1,), (1,)), ((), ())), prefe...]
  transfers between devices with their start and end apart: 5 -> 22, of which waited for: 4 -> 13; matrix products, arithmetic and copies ran while one was open for 4% -> 8% of each run, Pallas kernels for 0% -> 21%
where the time goes in v2:
time: 131 us; the launch traced here: 130 us
  waiting for transfers between devices  52.3 us (40%)
  Pallas kernels  26.8 us (20%)
  starting transfers between devices  25.6 us (20%)
  local copies, waits for them, and re-layouts  15.9 us (12%)
  other arithmetic  7.02 us (5%)
  between operations  2.16 us (2%)
    ppermute x3, waiting for transfers between devices, shards(): chunk[0, s] = lax.ppermute(source, 'vocab', ring(n_voc, s))  16.9 us
    ppermute x3, waiting for transfers between devices, shards(): kept = lax.ppermute(kept.astype(BF16), 'vocab', ring(n_voc, s)).astype(F32)  14.6 us
    ppermute x4, waiting for transfers between devices, shards(): kept = kept + lax.ppermute(send[t - 1], 'ctx', ring(n_ctx, -t)).astype(F32)  14.4 us
    unnamed x30, local copies, waits for them, and re-layouts  11.9 us
    pallas_call x3, Pallas kernels, logits_call(): pl.pallas_call(functools.partial(logits_kernel, steps, acc is not None, w...  10.7 us
    pallas_call x3, Pallas kernels, spread_call(): pl.pallas_call(spread_kernel, out_shape=out_shape, grid_spec=pltpu.Prefet...  6.69 us
    pallas_call x1, Pallas kernels, head_call(): pl.pallas_call(functools.partial(head_kernel, len(xs)), out_shape=jax.Sha...  6.42 us
    ppermute x3, starting transfers between devices, shards(): chunk[0, s] = lax.ppermute(source, 'vocab', ring(n_voc, s))  6.04 us
  transfers between devices with their start and end apart: 22, of which 13 were waited for; matrix products, arithmetic and copies ran while one was open for 8% of the time, Pallas kernels for 21%

profile of v2, /device:TPU:0, one launch (start us, length us, event | category | flops | bytes accessed | tf_op | source)
XLA Modules:
  0.0 129.8 jit_solution(7569948688439358921)
XLA Ops:
  0.6 0.5 collective-permute-start.4
  1.1 2.6 %collective-permute-start = (bf16[128,1024]{1,0:T(8,128)(2,1)}, bf16[128,1024]{1,0:T(8,128)(2,1)S(1)}, u32[]{:S(2)}, u32[]{:S(2)}) collective-permute-start(bf16[128,1024]{1,0:T(8,128)(2,1)} %bitcast.49), channel_id=1, source_target_pairs={{0,4},{4,8},{8,12},{12,0},{1,5},{5,9},{9,13},{13,1},{2,6},{6,10},{... | collective-permute-start | bytes 786440 | tf_op jit(solution)/shard_map/ppermute | solution.py:276
  3.8 2.1 %collective-permute-start.1 = (bf16[128,1024]{1,0:T(8,128)(2,1)}, bf16[128,1024]{1,0:T(8,128)(2,1)S(1)}, u32[]{:S(2)}, u32[]{:S(2)}) collective-permute-start(bf16[128,1024]{1,0:T(8,128)(2,1)} %bitcast.50), channel_id=1, source_target_pairs={{0,12},{4,0},{8,4},{12,8},{1,13},{5,1},{9,5},{13,9},{2,14},{6,2},{... | collective-permute-start | bytes 786440 | tf_op jit(solution)/shard_map/ppermute | solution.py:276
  5.9 1.6 %collective-permute-start.7 = (bf16[128,1024]{1,0:T(8,128)(2,1)}, bf16[128,1024]{1,0:T(8,128)(2,1)S(1)}, u32[]{:S(2)}, u32[]{:S(2)}) collective-permute-start(bf16[128,1024]{1,0:T(8,128)(2,1)} %bitcast.51), channel_id=1, source_target_pairs={{0,2},{2,0},{1,3},{3,1},{4,6},{6,4},{5,7},{7,5},{8,10},{10,8},{9,1... | collective-permute-start | bytes 786440 | tf_op jit(solution)/shard_map/ppermute | solution.py:273
  7.5 1.2 dynamic_slice.31
  8.8 0.6 iota_compare_fusion.1
  9.4 0.7 broadcast_select_fusion
  10.2 0.8 constant_dynamic-slice_fusion.5
  11.1 2.2 %collective-permute-done.refs_2_ = bf16[128,1024]{1,0:T(8,128)(2,1)S(1)} collective-permute-done((bf16[128,1024]{1,0:T(8,128)(2,1)}, bf16[128,1024]{1,0:T(8,128)(2,1)S(1)}, u32[]{:S(2)}, u32[]{:S(2)}) %collective-permute-start) | collective-permute-done | bytes 262176 | tf_op jit(solution)/shard_map/ppermute | solution.py:276
  13.2 4.8 %collective-permute-done.1.refs_3_ = bf16[128,1024]{1,0:T(8,128)(2,1)S(1)} collective-permute-done((bf16[128,1024]{1,0:T(8,128)(2,1)}, bf16[128,1024]{1,0:T(8,128)(2,1)S(1)}, u32[]{:S(2)}, u32[]{:S(2)}) %collective-permute-start.1) | collective-permute-done | bytes 262176 | tf_op jit(solution)/shard_map/ppermute | solution.py:276
  18.0 1.3 collective-permute-start.2
  19.3 0.7 fusion.1
  20.3 1.6 %collective-permute-start.5 = (bf16[128,1024]{1,0:T(8,128)(2,1)S(1)}, bf16[128,1024]{1,0:T(8,128)(2,1)S(1)}, u32[]{:S(2)}, u32[]{:S(2)}) collective-permute-start(bf16[128,1024]{1,0:T(8,128)(2,1)S(1)} %collective-permute-done.refs_2_), channel_id=1, source_target_pairs={{0,2},{2,0},{1,3},{3,1},{4,6},{6,4},{5,7},{7,5},{8,10},{10,8},{9,1... | collective-permute-start | bytes 786440 | tf_op jit(solution)/shard_map/ppermute | solution.py:282
  21.9 0.5 collective-permute-start.6
  22.4 10.0 %collective-permute-done.2.refs_2_ = bf16[128,1024]{1,0:T(8,128)(2,1)S(1)} collective-permute-done((bf16[128,1024]{1,0:T(8,128)(2,1)}, bf16[128,1024]{1,0:T(8,128)(2,1)S(1)}, u32[]{:S(2)}, u32[]{:S(2)}) %collective-permute-start.2) | collective-permute-done | bytes 262176 | tf_op jit(solution)/shard_map/ppermute | solution.py:276
  32.4 1.5 %collective-permute-start.3 = (bf16[128,1024]{1,0:T(8,128)(2,1)S(1)}, bf16[128,1024]{1,0:T(8,128)(2,1)S(1)}, u32[]{:S(2)}, u32[]{:S(2)}) collective-permute-start(bf16[128,1024]{1,0:T(8,128)(2,1)S(1)} %collective-permute-done.2.refs_2_), channel_id=1, source_target_pairs={{0,2},{2,0},{1,3},{3,1},{4,6},{6,4},{5,7},{7,5},{8,10},{10,8},{9,1... | collective-permute-start | bytes 786440 | tf_op jit(solution)/shard_map/ppermute | solution.py:282
  34.0 0.1 stack.104.meta
  34.1 0.1 copy.13.refs_4_.target
  34.3 0.6 fusion.3
  34.9 1.1 maximum_bitcast_fusion
  36.0 3.4 %collective-permute-done.3.refs_0_ = bf16[128,1024]{1,0:T(8,128)(2,1)S(1)} collective-permute-done((bf16[128,1024]{1,0:T(8,128)(2,1)S(1)}, bf16[128,1024]{1,0:T(8,128)(2,1)S(1)}, u32[]{:S(2)}, u32[]{:S(2)}) %collective-permute-start.3) | collective-permute-done | bytes 262176 | tf_op jit(solution)/shard_map/ppermute | solution.py:282
  39.5 0.1 maximum_bitcast_fusion.1
  39.6 0.7 copy-done.8
  40.3 0.2 pad_maximum_fusion.refs_0_
  40.6 1.9 %copy-done = bf16[4096,512]{1,0:T(8,128)(2,1)S(1)} copy-done((bf16[4096,512]{1,0:T(8,128)(2,1)S(1)}, bf16[4096,512]{1,0:T(8,128)(2,1)}, u32[]{:S(2)}) %copy-start) | copy-done | bytes 4194328
  42.5 0.9 copy-done.7
  43.5 0.9 copy-done.9
  44.4 4.2 %shard_map.103.refs_5_ = f32[2,128,1024]{2,1,0:T(8,128)S(1)} custom-call(s32[5]{0:T(128)S(1)} %stack.106.meta, bf16[128,1024]{1,0:T(8,128)(2,1)S(1)} %bitcast.54, bf16[128,1024]{1,0:T(8,128)(2,1)S(1)} %copy-done.9, bf16[128,1024]{1,0:T(8,128)(2,1)S(1)} %collective-permute-done.refs_2_, bf16[128,1024]{1,0:T(8,128)(2,1)S(1)} %copy-done.7, ...), custom_call_target="tpu_custom_call" | custom-call | flops 1073741824 | bytes 9437184 | tf_op jit(solution)/shard_map/pallas_call | solution.py:108
  48.6 4.0 %shard_map.104.refs_3_ = f32[2,128,1024]{2,1,0:T(8,128)S(1)} custom-call(s32[5]{0:T(128)S(1)} %stack.104.meta, bf16[128,1024]{1,0:T(8,128)(2,1)S(1)} %collective-permute-done.5.refs_0_, bf16[128,1024]{1,0:T(8,128)(2,1)S(1)} %collective-permute-done.6.refs_1_, bf16[128,1024]{1,0:T(8,128)(2,1)S(1)} %collective-permute-done.2.refs_2_, ...), custom_call_target="tpu_custom_call" | custom-call | flops 805306368 | bytes 9175040 | tf_op jit(solution)/shard_map/pallas_call | solution.py:108
  52.6 2.5 %shard_map.105 = (f32[2,128,1024]{2,1,0:T(8,128)S(1)}, f32[8,256]{1,0:T(8,128)S(1)}) custom-call(s32[3]{0:T(128)S(1)} %add_add_fusion.1.meta, bf16[128,1024]{1,0:T(8,128)(2,1)S(1)} %collective-permute-done.3.refs_0_, bf16[4096,512]{1,0:T(8,128)(2,1)S(1)} %copy-done, bf16[4096,512]{1,0:T(8,128)(2,1)} %collective-permute-done.4.refs_5_.refs_4_.refs_2_.w_far, ...), custom_call_target="tpu_custom_call" | custom-call | flops 268435456 | bytes 4456448 | tf_op jit(solution)/shard_map/pallas_call | solution.py:108
  55.1 1.0 copy-done.3
  56.1 1.5 %collective-permute-start.8 = (f32[8,256]{1,0:T(8,128)S(1)}, f32[8,256]{1,0:T(8,128)S(1)}, u32[]{:S(2)}, u32[]{:S(2)}) collective-permute-start(f32[8,256]{1,0:T(8,128)S(1)} %get-tuple-element.23), channel_id=1, source_target_pairs={{0,2},{2,0},{1,3},{3,1},{4,6},{6,4},{5,7},{7,5},{8,10},{10,8},{9,1... | collective-permute-start | bytes 24584 | tf_op jit(solution)/shard_map/ppermute | solution.py:323
  57.7 0.6 dynamic_slice.36
  59.5 0.2 collective-permute-done.8
  59.8 1.2 collective-permute-start.9
  61.0 2.7 %collective-permute-start.10 = (f32[8,256]{1,0:T(8,128)S(1)}, f32[8,256]{1,0:T(8,128)S(1)}, u32[]{:S(2)}, u32[]{:S(2)}) collective-permute-start(f32[8,256]{1,0:T(8,128)S(1)} %select_maximum_fusion.refs_0_), channel_id=1, source_target_pairs={{0,8},{4,12},{8,0},{12,4},{1,9},{5,13},{9,1},{13,5},{2,10},{6,14},... | collective-permute-start | bytes 24584 | tf_op jit(solution)/shard_map/ppermute | solution.py:336
  63.8 0.3 collective-permute-start.11
  64.0 0.7 fusion
  64.8 0.6 collective-permute-done.9.refs_1_
  65.3 0.3 collective-permute-done.10.refs_2_
  65.6 1.8 %collective-permute-done.11.refs_3_ = f32[8,256]{1,0:T(8,128)S(1)} collective-permute-done((f32[8,256]{1,0:T(8,128)S(1)}, f32[8,256]{1,0:T(8,128)S(1)}, u32[]{:S(2)}, u32[]{:S(2)}) %collective-permute-start.11) | collective-permute-done | bytes 8224 | tf_op jit(solution)/shard_map/ppermute | solution.py:336
  67.5 2.2 %copy-done.1 = bf16[4096,512]{1,0:T(8,128)(2,1)S(1)} copy-done((bf16[4096,512]{1,0:T(8,128)(2,1)S(1)}, bf16[4096,512]{1,0:T(8,128)(2,1)}, u32[]{:S(2)}) %copy-start.1) | copy-done | bytes 4194328
  69.7 1.2 copy-done.4
  70.9 3.0 %shard_map.106 = (bf16[2,128,512]{2,1,0:T(8,128)(2,1)S(1)}, bf16[2,128,512]{2,1,0:T(8,128)(2,1)S(1)}, bf16[1,128,1024]{2,1,0:T(8,128)(2,1)S(1)}, f32[128,1024]{1,0:T(8,128)S(1)}, f32[1,128]{1,0:T(1,128)S(1)}) custom-call(s32[3]{0:T(128)S(1)} %add_add_fusion.meta, f32[2,128,1024]{2,1,0:T(8,128)S(1)} %copy-done.4, s32[256,1]{1,0:T(8,128)S(1)} %copy.13.refs_4_.target, ...), custom_call_target="tpu_custom_call" | custom-call | flops 536870912 | bytes 3145728 | tf_op jit(solution)/shard_map/pallas_call | solution.py:185
  73.9 2.8 %shard_map.108 = (bf16[1,128,1024]{2,1,0:T(8,128)(2,1)}, f32[128,1024]{1,0:T(8,128)S(1)}) custom-call(s32[1]{0:T(128)} %bitcast.20.meta, bf16[2,128,512]{2,1,0:T(8,128)(2,1)S(1)} %get-tuple-element.26.grads_own.refs_2_, bf16[2,128,512]{2,1,0:T(8,128)(2,1)S(1)} %get-tuple-element.27.grads_far, bf16[4096,512]{1,0:T(8,128)(2,1)S(1)} %copy-done.1, ...), custom_call_target="tpu_custom_call" | custom-call | flops 536870912 | bytes 2097152 | tf_op jit(solution)/shard_map/pallas_call | solution.py:203
  76.7 0.8 copy-done.10
  77.5 1.6 %collective-permute-start.16 = (bf16[128,1024]{1,0:T(8,128)(2,1)}, bf16[128,1024]{1,0:T(8,128)(2,1)}, u32[]{:S(2)}, u32[]{:S(2)}) collective-permute-start(bf16[128,1024]{1,0:T(8,128)(2,1)} %bitcast.21), channel_id=1, source_target_pairs={{0,2},{2,0},{1,3},{3,1},{4,6},{6,4},{5,7},{7,5},{8,10},{10,8},{9,1... | collective-permute-start | bytes 786440 | tf_op jit(solution)/shard_map/ppermute | solution.py:349
  79.2 2.2 %copy-done.2 = bf16[4096,512]{1,0:T(8,128)(2,1)S(1)} copy-done((bf16[4096,512]{1,0:T(8,128)(2,1)S(1)}, bf16[4096,512]{1,0:T(8,128)(2,1)}, u32[]{:S(2)}) %copy-start.2) | copy-done | bytes 4194328
  81.4 2.0 %shard_map.107 = (bf16[1,128,1024]{2,1,0:T(8,128)(2,1)S(1)}, f32[128,1024]{1,0:T(8,128)S(1)}) custom-call(s32[1]{0:T(128)} %bitcast.18.meta, bf16[2,128,512]{2,1,0:T(8,128)(2,1)S(1)} %get-tuple-element.26.grads_own.refs_2_, bf16[2,128,512]{2,1,0:T(8,128)(2,1)S(1)} %get-tuple-element.27.grads_far, bf16[4096,512]{1,0:T(8,128)(2,1)S(1)} %copy-done.2, ...), custom_call_target="tpu_custom_call" | custom-call | flops 536870912 | bytes 2097152 | tf_op jit(solution)/shard_map/pallas_call | solution.py:203
  83.4 0.5 collective-permute-start.14
  83.8 2.0 %shard_map.109 = (bf16[1,128,1024]{2,1,0:T(8,128)(2,1)S(1)}, f32[128,1024]{1,0:T(8,128)S(1)}) custom-call(s32[1]{0:T(128)} %bitcast.9.meta, bf16[2,128,512]{2,1,0:T(8,128)(2,1)S(1)} %get-tuple-element.26.grads_own.refs_2_, bf16[2,128,512]{2,1,0:T(8,128)(2,1)S(1)} %get-tuple-element.27.grads_far, bf16[4096,512]{1,0:T(8,128)(2,1)S(1)} %copy-done.2, ...), custom_call_target="tpu_custom_call" | custom-call | flops 536870912 | bytes 2097152 | tf_op jit(solution)/shard_map/pallas_call | solution.py:203
  85.8 1.7 %collective-permute-start.18 = (bf16[128,1024]{1,0:T(8,128)(2,1)S(1)}, bf16[128,1024]{1,0:T(8,128)(2,1)S(1)}, u32[]{:S(2)}, u32[]{:S(2)}) collective-permute-start(bf16[128,1024]{1,0:T(8,128)(2,1)S(1)} %bitcast.59), channel_id=1, source_target_pairs={{0,2},{2,0},{1,3},{3,1},{4,6},{6,4},{5,7},{7,5},{8,10},{10,8},{9,1... | collective-permute-start | bytes 786440 | tf_op jit(solution)/shard_map/ppermute | solution.py:349
  87.5 0.4 collective-permute-start.12
  87.9 1.0 add_convert_fusion.1
  88.9 3.6 %collective-permute-done.14 = bf16[128,1024]{1,0:T(8,128)(2,1)S(1)} collective-permute-done((bf16[128,1024]{1,0:T(8,128)(2,1)S(1)}, bf16[128,1024]{1,0:T(8,128)(2,1)S(1)}, u32[]{:S(2)}, u32[]{:S(2)}) %collective-permute-start.14) | collective-permute-done | bytes 262176 | tf_op jit(solution)/shard_map/ppermute | solution.py:349
  92.6 10.8 %collective-permute-done.12 = bf16[128,1024]{1,0:T(8,128)(2,1)S(1)} collective-permute-done((bf16[128,1024]{1,0:T(8,128)(2,1)S(1)}, bf16[128,1024]{1,0:T(8,128)(2,1)S(1)}, u32[]{:S(2)}, u32[]{:S(2)}) %collective-permute-start.12) | collective-permute-done | bytes 262176 | tf_op jit(solution)/shard_map/ppermute | solution.py:349
  103.4 0.3 collective-permute-start.17
  103.8 3.5 %collective-permute-start.15 = (bf16[128,1024]{1,0:T(8,128)(2,1)S(1)}, bf16[128,1024]{1,0:T(8,128)(2,1)S(1)}, u32[]{:S(2)}, u32[]{:S(2)}) collective-permute-start(bf16[128,1024]{1,0:T(8,128)(2,1)S(1)} %add_convert_fusion.2), channel_id=1, source_target_pairs={{0,12},{4,0},{8,4},{12,8},{1,13},{5,1},{9,5},{13,9},{2,14},{6,2},{... | collective-permute-start | bytes 786440 | tf_op jit(solution)/shard_map/ppermute | solution.py:351
  107.3 0.5 compare_select_fusion
  107.8 6.4 %shard_map.110 = bf16[4096,512]{1,0:T(8,128)(2,1)} custom-call(s32[4]{0:T(128)S(1)} %pad_add_fusion.1.meta, bf16[2,4,128,1024]{3,2,1,0:T(8,128)(2,1)S(1)} %pad_maximum_fusion.refs_0_, bf16[2,4,128,1024]{3,2,1,0:T(8,128)(2,1)} %collective-permute-done.19.refs_1_, bf16[2,128,512]{2,1,0:T(8,128)(2,1)S(1)} %get-tuple-element.26.grads_own.refs_2_, ...), custom_call_target="tpu_custom_call" | custom-call | flops 2147483648 | bytes 8912896 | tf_op jit(solution)/shard_map/pallas_call | solution.py:236
  114.3 0.1 collective-permute-done.17
  114.4 3.3 %collective-permute-done.15 = bf16[128,1024]{1,0:T(8,128)(2,1)S(1)} collective-permute-done((bf16[128,1024]{1,0:T(8,128)(2,1)S(1)}, bf16[128,1024]{1,0:T(8,128)(2,1)S(1)}, u32[]{:S(2)}, u32[]{:S(2)}) %collective-permute-start.15) | collective-permute-done | bytes 262176 | tf_op jit(solution)/shard_map/ppermute | solution.py:351
  117.7 11.2 %collective-permute-done.13 = bf16[128,1024]{1,0:T(8,128)(2,1)S(1)} collective-permute-done((bf16[128,1024]{1,0:T(8,128)(2,1)S(1)}, bf16[128,1024]{1,0:T(8,128)(2,1)S(1)}, u32[]{:S(2)}, u32[]{:S(2)}) %collective-permute-start.13) | collective-permute-done | bytes 262176 | tf_op jit(solution)/shard_map/ppermute | solution.py:351
  128.9 0.9 add_convert_fusion
  (53 shorter events, 1.1 us)
Async XLA Ops:
  0.6 39.9 %collective-permute-start.4 = (bf16[4096,512]{1,0:T(8,128)(2,1)}, bf16[4096,512]{1,0:T(8,128)(2,1)}, u32[]{:S(2)}, u32[]{:S(2)}) collective-permute-start(bf16[4096,512]{1,0:T(8,128)(2,1)} %w_own.5), channel_id=1, source_target_pairs={{0,1},{1,0},{2,3},{3,2},{4,5},{5,4},{6,7},{7,6},{8,9},{9,8},{10,11... | collective-permute-start | bytes 12582920 | tf_op jit(solution)/shard_map/ppermute | solution.py:261
  1.1 12.1 %collective-permute-start = (bf16[128,1024]{1,0:T(8,128)(2,1)}, bf16[128,1024]{1,0:T(8,128)(2,1)S(1)}, u32[]{:S(2)}, u32[]{:S(2)}) collective-permute-start(bf16[128,1024]{1,0:T(8,128)(2,1)} %bitcast.49), channel_id=1, source_target_pairs={{0,4},{4,8},{8,12},{12,0},{1,5},{5,9},{9,13},{13,1},{2,6},{6,10},{... | collective-permute-start | bytes 786440 | tf_op jit(solution)/shard_map/ppermute | solution.py:276
  3.8 14.2 %collective-permute-start.1 = (bf16[128,1024]{1,0:T(8,128)(2,1)}, bf16[128,1024]{1,0:T(8,128)(2,1)S(1)}, u32[]{:S(2)}, u32[]{:S(2)}) collective-permute-start(bf16[128,1024]{1,0:T(8,128)(2,1)} %bitcast.50), channel_id=1, source_target_pairs={{0,12},{4,0},{8,4},{12,8},{1,13},{5,1},{9,5},{13,9},{2,14},{6,2},{... | collective-permute-start | bytes 786440 | tf_op jit(solution)/shard_map/ppermute | solution.py:276
  5.9 30.1 %collective-permute-start.7 = (bf16[128,1024]{1,0:T(8,128)(2,1)}, bf16[128,1024]{1,0:T(8,128)(2,1)S(1)}, u32[]{:S(2)}, u32[]{:S(2)}) collective-permute-start(bf16[128,1024]{1,0:T(8,128)(2,1)} %bitcast.51), channel_id=1, source_target_pairs={{0,2},{2,0},{1,3},{3,1},{4,6},{6,4},{5,7},{7,5},{8,10},{10,8},{9,1... | collective-permute-start | bytes 786440 | tf_op jit(solution)/shard_map/ppermute | solution.py:273
  18.0 21.5 %copy-start.6 = (bf16[128,1024]{1,0:T(8,128)(2,1)}, bf16[128,1024]{1,0:T(8,128)(2,1)S(1)}, u32[]{:S(2)}) copy-start(bf16[128,1024]{1,0:T(8,128)(2,1)S(1)} %collective-permute-done.1.refs_3_) | copy-start | bytes 786436
  18.0 14.4 %collective-permute-start.2 = (bf16[128,1024]{1,0:T(8,128)(2,1)}, bf16[128,1024]{1,0:T(8,128)(2,1)S(1)}, u32[]{:S(2)}, u32[]{:S(2)}) collective-permute-start(bf16[128,1024]{1,0:T(8,128)(2,1)} %bitcast.52), channel_id=1, source_target_pairs={{0,8},{4,12},{8,0},{12,4},{1,9},{5,13},{9,1},{13,5},{2,10},{6,14},... | collective-permute-start | bytes 786440 | tf_op jit(solution)/shard_map/ppermute | solution.py:276
  20.3 15.7 %collective-permute-start.5 = (bf16[128,1024]{1,0:T(8,128)(2,1)S(1)}, bf16[128,1024]{1,0:T(8,128)(2,1)S(1)}, u32[]{:S(2)}, u32[]{:S(2)}) collective-permute-start(bf16[128,1024]{1,0:T(8,128)(2,1)S(1)} %collective-permute-done.refs_2_), channel_id=1, source_target_pairs={{0,2},{2,0},{1,3},{3,1},{4,6},{6,4},{5,7},{7,5},{8,10},{10,8},{9,1... | collective-permute-start | bytes 786440 | tf_op jit(solution)/shard_map/ppermute | solution.py:282
  21.9 14.1 %collective-permute-start.6 = (bf16[128,1024]{1,0:T(8,128)(2,1)S(1)}, bf16[128,1024]{1,0:T(8,128)(2,1)S(1)}, u32[]{:S(2)}, u32[]{:S(2)}) collective-permute-start(bf16[128,1024]{1,0:T(8,128)(2,1)S(1)} %collective-permute-done.1.refs_3_), channel_id=1, source_target_pairs={{0,2},{2,0},{1,3},{3,1},{4,6},{6,4},{5,7},{7,5},{8,10},{10,8},{9,1... | collective-permute-start | bytes 786440 | tf_op jit(solution)/shard_map/ppermute | solution.py:282
  32.4 7.0 %collective-permute-start.3 = (bf16[128,1024]{1,0:T(8,128)(2,1)S(1)}, bf16[128,1024]{1,0:T(8,128)(2,1)S(1)}, u32[]{:S(2)}, u32[]{:S(2)}) collective-permute-start(bf16[128,1024]{1,0:T(8,128)(2,1)S(1)} %collective-permute-done.2.refs_2_), channel_id=1, source_target_pairs={{0,2},{2,0},{1,3},{3,1},{4,6},{6,4},{5,7},{7,5},{8,10},{10,8},{9,1... | collective-permute-start | bytes 786440 | tf_op jit(solution)/shard_map/ppermute | solution.py:282
  39.4 1.1 copy-start.5
  39.6 0.7 copy-start.8
  40.3 2.2 %copy-start = (bf16[4096,512]{1,0:T(8,128)(2,1)S(1)}, bf16[4096,512]{1,0:T(8,128)(2,1)}, u32[]{:S(2)}) copy-start(bf16[4096,512]{1,0:T(8,128)(2,1)} %w_own.5) | copy-start | bytes 12582916
  40.5 63.3 %collective-permute-start.19 = (bf16[2,4,128,1024]{3,2,1,0:T(8,128)(2,1)S(1)}, bf16[2,4,128,1024]{3,2,1,0:T(8,128)(2,1)}, u32[]{:S(2)}, u32[]{:S(2)}) collective-permute-start(bf16[2,4,128,1024]{3,2,1,0:T(8,128)(2,1)S(1)} %pad_maximum_fusion.refs_0_), channel_id=1, source_target_pairs={{0,1},{1,0},{2,3},{3,2},{4,5},{5,4},{6,7},{7,6},{8,9},{9,8},{10,11... | collective-permute-start | bytes 6291464 | tf_op jit(solution)/shard_map/ppermute | solution.py:356
  42.5 0.9 copy-start.7
  43.5 0.9 copy-start.9
  52.6 5.1 %copy-start.14 = (f32[2]{0:T(128)S(1)}, f32[2]{0:T(128)}, u32[]{:S(2)}) copy-start(f32[2]{0:T(128)} %param.14) | copy-start | bytes 28
  55.1 1.0 copy-start.3
  56.1 3.7 %collective-permute-start.8 = (f32[8,256]{1,0:T(8,128)S(1)}, f32[8,256]{1,0:T(8,128)S(1)}, u32[]{:S(2)}, u32[]{:S(2)}) collective-permute-start(f32[8,256]{1,0:T(8,128)S(1)} %get-tuple-element.23), channel_id=1, source_target_pairs={{0,2},{2,0},{1,3},{3,1},{4,6},{6,4},{5,7},{7,5},{8,10},{10,8},{9,1... | collective-permute-start | bytes 24584 | tf_op jit(solution)/shard_map/ppermute | solution.py:323
  59.8 5.5 %collective-permute-start.9 = (f32[8,256]{1,0:T(8,128)S(1)}, f32[8,256]{1,0:T(8,128)S(1)}, u32[]{:S(2)}, u32[]{:S(2)}) collective-permute-start(f32[8,256]{1,0:T(8,128)S(1)} %select_maximum_fusion.refs_0_), channel_id=1, source_target_pairs={{0,4},{4,8},{8,12},{12,0},{1,5},{5,9},{9,13},{13,1},{2,6},{6,10},{... | collective-permute-start | bytes 24584 | tf_op jit(solution)/shard_map/ppermute | solution.py:336
  61.0 4.6 %collective-permute-start.10 = (f32[8,256]{1,0:T(8,128)S(1)}, f32[8,256]{1,0:T(8,128)S(1)}, u32[]{:S(2)}, u32[]{:S(2)}) collective-permute-start(f32[8,256]{1,0:T(8,128)S(1)} %select_maximum_fusion.refs_0_), channel_id=1, source_target_pairs={{0,8},{4,12},{8,0},{12,4},{1,9},{5,13},{9,1},{13,5},{2,10},{6,14},... | collective-permute-start | bytes 24584 | tf_op jit(solution)/shard_map/ppermute | solution.py:336
  63.8 3.7 %collective-permute-start.11 = (f32[8,256]{1,0:T(8,128)S(1)}, f32[8,256]{1,0:T(8,128)S(1)}, u32[]{:S(2)}, u32[]{:S(2)}) collective-permute-start(f32[8,256]{1,0:T(8,128)S(1)} %select_maximum_fusion.refs_0_), channel_id=1, source_target_pairs={{0,12},{4,0},{8,4},{12,8},{1,13},{5,1},{9,5},{13,9},{2,14},{6,2},{... | collective-permute-start | bytes 24584 | tf_op jit(solution)/shard_map/ppermute | solution.py:336
  67.5 2.2 %copy-start.1 = (bf16[4096,512]{1,0:T(8,128)(2,1)S(1)}, bf16[4096,512]{1,0:T(8,128)(2,1)}, u32[]{:S(2)}) copy-start(bf16[4096,512]{1,0:T(8,128)(2,1)} %w_own.5) | copy-start | bytes 12582916
  69.7 1.2 copy-start.4
  73.9 2.8 %copy-start.12 = (bf16[1,128,1024]{2,1,0:T(8,128)(2,1)}, bf16[1,128,1024]{2,1,0:T(8,128)(2,1)S(1)}, u32[]{:S(2)}) copy-start(bf16[1,128,1024]{2,1,0:T(8,128)(2,1)S(1)} %get-tuple-element.25) | copy-start | bytes 786436
  76.7 0.8 copy-start.10
  77.5 10.0 %collective-permute-start.16 = (bf16[128,1024]{1,0:T(8,128)(2,1)}, bf16[128,1024]{1,0:T(8,128)(2,1)}, u32[]{:S(2)}, u32[]{:S(2)}) collective-permute-start(bf16[128,1024]{1,0:T(8,128)(2,1)} %bitcast.21), channel_id=1, source_target_pairs={{0,2},{2,0},{1,3},{3,1},{4,6},{6,4},{5,7},{7,5},{8,10},{10,8},{9,1... | collective-permute-start | bytes 786440 | tf_op jit(solution)/shard_map/ppermute | solution.py:349
  79.2 28.7 %collective-permute-start.20 = (bf16[2,128,512]{2,1,0:T(8,128)(2,1)S(1)}, bf16[2,128,512]{2,1,0:T(8,128)(2,1)S(1)}, u32[]{:S(2)}, u32[]{:S(2)}) collective-permute-start(bf16[2,128,512]{2,1,0:T(8,128)(2,1)S(1)} %get-tuple-element.27.grads_far), channel_id=1, source_target_pairs={{0,1},{1,0},{2,3},{3,2},{4,5},{5,4},{6,7},{7,6},{8,9},{9,8},{10,11... | collective-permute-start | bytes 786440 | tf_op jit(solution)/shard_map/ppermute | solution.py:343
  79.2 2.2 %copy-start.2 = (bf16[4096,512]{1,0:T(8,128)(2,1)S(1)}, bf16[4096,512]{1,0:T(8,128)(2,1)}, u32[]{:S(2)}) copy-start(bf16[4096,512]{1,0:T(8,128)(2,1)} %w_own.5) | copy-start | bytes 12582916
  83.3 4.2 %copy-start.13 = (bf16[1,128,1024]{2,1,0:T(8,128)(2,1)S(1)}, bf16[1,128,1024]{2,1,0:T(8,128)(2,1)}, u32[]{:S(2)}) copy-start(bf16[1,128,1024]{2,1,0:T(8,128)(2,1)} %copy-done.12) | copy-start | bytes 786436
  83.4 4.5 %copy-start.11 = (f32[128,1024]{1,0:T(8,128)S(1)}, f32[128,1024]{1,0:T(8,128)}, u32[]{:S(2)}) copy-start(f32[128,1024]{1,0:T(8,128)} %copy-done.10) | copy-start | bytes 1572868
  83.4 9.2 %collective-permute-start.14 = (bf16[128,1024]{1,0:T(8,128)(2,1)S(1)}, bf16[128,1024]{1,0:T(8,128)(2,1)S(1)}, u32[]{:S(2)}, u32[]{:S(2)}) collective-permute-start(bf16[128,1024]{1,0:T(8,128)(2,1)S(1)} %bitcast.60), channel_id=1, source_target_pairs={{0,2},{2,0},{1,3},{3,1},{4,6},{6,4},{5,7},{7,5},{8,10},{10,8},{9,1... | collective-permute-start | bytes 786440 | tf_op jit(solution)/shard_map/ppermute | solution.py:349
  85.8 28.5 %collective-permute-start.18 = (bf16[128,1024]{1,0:T(8,128)(2,1)S(1)}, bf16[128,1024]{1,0:T(8,128)(2,1)S(1)}, u32[]{:S(2)}, u32[]{:S(2)}) collective-permute-start(bf16[128,1024]{1,0:T(8,128)(2,1)S(1)} %bitcast.59), channel_id=1, source_target_pairs={{0,2},{2,0},{1,3},{3,1},{4,6},{6,4},{5,7},{7,5},{8,10},{10,8},{9,1... | collective-permute-start | bytes 786440 | tf_op jit(solution)/shard_map/ppermute | solution.py:349
  87.5 15.9 %collective-permute-start.12 = (bf16[128,1024]{1,0:T(8,128)(2,1)S(1)}, bf16[128,1024]{1,0:T(8,128)(2,1)S(1)}, u32[]{:S(2)}, u32[]{:S(2)}) collective-permute-start(bf16[128,1024]{1,0:T(8,128)(2,1)S(1)} %bitcast.58), channel_id=1, source_target_pairs={{0,2},{2,0},{1,3},{3,1},{4,6},{6,4},{5,7},{7,5},{8,10},{10,8},{9,1... | collective-permute-start | bytes 786440 | tf_op jit(solution)/shard_map/ppermute | solution.py:349
  92.5 14.8 %collective-permute-start.21 = (f32[1,128]{1,0:T(1,128)S(1)}, f32[1,128]{1,0:T(1,128)S(1)}, u32[]{:S(2)}, u32[]{:S(2)}) collective-permute-start(f32[1,128]{1,0:T(1,128)S(1)} %get-tuple-element.34), channel_id=1, source_target_pairs={{0,1},{1,0},{2,3},{3,2},{4,5},{5,4},{6,7},{7,6},{8,9},{9,8},{10,11... | collective-permute-start | bytes 1544 | tf_op jit(solution)/shard_map/ppermute | solution.py:359
  103.4 11.0 %collective-permute-start.17 = (bf16[128,1024]{1,0:T(8,128)(2,1)S(1)}, bf16[128,1024]{1,0:T(8,128)(2,1)S(1)}, u32[]{:S(2)}, u32[]{:S(2)}) collective-permute-start(bf16[128,1024]{1,0:T(8,128)(2,1)S(1)} %add_convert_fusion.1), channel_id=1, source_target_pairs={{0,4},{4,8},{8,12},{12,0},{1,5},{5,9},{9,13},{13,1},{2,6},{6,10},{... | collective-permute-start | bytes 786440 | tf_op jit(solution)/shard_map/ppermute | solution.py:351
  103.8 13.9 %collective-permute-start.15 = (bf16[128,1024]{1,0:T(8,128)(2,1)S(1)}, bf16[128,1024]{1,0:T(8,128)(2,1)S(1)}, u32[]{:S(2)}, u32[]{:S(2)}) collective-permute-start(bf16[128,1024]{1,0:T(8,128)(2,1)S(1)} %add_convert_fusion.2), channel_id=1, source_target_pairs={{0,12},{4,0},{8,4},{12,8},{1,13},{5,1},{9,5},{13,9},{2,14},{6,2},{... | collective-permute-start | bytes 786440 | tf_op jit(solution)/shard_map/ppermute | solution.py:351
  107.3 21.6 %collective-permute-start.13 = (bf16[128,1024]{1,0:T(8,128)(2,1)S(1)}, bf16[128,1024]{1,0:T(8,128)(2,1)S(1)}, u32[]{:S(2)}, u32[]{:S(2)}) collective-permute-start(bf16[128,1024]{1,0:T(8,128)(2,1)S(1)} %add_convert_fusion.3), channel_id=1, source_target_pairs={{0,8},{4,12},{8,0},{12,4},{1,9},{5,13},{9,1},{13,5},{2,10},{6,14},... | collective-permute-start | bytes 786440 | tf_op jit(solution)/shard_map/ppermute | solution.py:351

commit v3 on v0

v3 whole, which is shorter than its diff:
```python
import functools

import jax
import jax.numpy as jnp
from jax import lax
from jax.experimental import pallas as pl
from jax.experimental.pallas import tpu as pltpu
from jax.sharding import PartitionSpec as P

BETA = 0.1
F32, BF16 = jnp.float32, jnp.bfloat16
VMEM_BYTES = 16 * 1024 * 1024
IN_VMEM = pl.BlockSpec(memory_space=pltpu.VMEM)
IN_SMEM = pl.BlockSpec(memory_space=pltpu.SMEM)


def ring(count, shift):
    return [(i, (i + shift) % count) for i in range(count)]


def params():
    return pltpu.CompilerParams(vmem_limit_bytes=VMEM_BYTES)


def cost(flops, moved):
    return pl.CostEstimate(flops=int(flops), bytes_accessed=int(moved), transcendentals=0)


def shape_of(shape, kind):
    return jax.ShapeDtypeStruct(shape, kind)


def row_stats(own, far, wanted, first_own, first_far):
    top = jnp.max(jnp.maximum(own, far), axis=1, keepdims=True)
    total = jnp.sum(jnp.exp(own - top) + jnp.exp(far - top), axis=1, keepdims=True)
    column = lax.broadcasted_iota(jnp.int32, own.shape, 1)
    zero = jnp.zeros_like(own)
    picked = jnp.sum(
        jnp.where(column + first_own == wanted, own, zero) + jnp.where(column + first_far == wanted, far, zero),
        axis=1,
        keepdims=True,
    )
    lane = lax.broadcasted_iota(jnp.int32, (own.shape[0], 128), 1)
    return jnp.where(lane == 0, top, jnp.where(lane == 1, total, picked)).T[:8, :]


def logits_kernel(plan, columns, part, meta, w_own, w_far, *refs):
    refs = list(refs)
    chunks = {(t, i): refs.pop(0) for t, slots, _, _ in plan for i in range(len(slots))}
    accs = {t: refs.pop(0) for t, _, has_acc, _ in plan if has_acc}
    wanted = {t: refs.pop(0) for t, _, _, done in plan if done}
    for t, slots, has_acc, done in plan:
        out = refs.pop(0)
        halves = []
        for j, w in enumerate((w_own, w_far)):
            at = slice(j * columns, (j + 1) * columns)
            total = accs[t][:, at] if has_acc else None
            for i, slot in enumerate(slots):
                start = pl.multiple_of(meta[slot] * part, part)
                product = jnp.dot(chunks[t, i][...], w[pl.ds(start, part), :], preferred_element_type=F32)
                total = product if total is None else total + product
            out[:, at] = total
            halves.append(total)
        if done:
            stats = refs.pop(0)
            stats[...] = row_stats(halves[0], halves[1], wanted[t][...], meta[-2 + meta.shape[0]], meta[-1 + meta.shape[0]])


def logits_call(plan, meta, weights, part):
    columns = weights[0].shape[1]
    chunks = [c for _, slots, _, _ in plan for _, c in slots]
    accs = [acc for _, _, acc, _ in plan if acc is not None]
    wanted = [w for _, _, _, w in plan if w is not None]
    rows = chunks[0].shape[0]
    out_shape = []
    for _, _, _, w in plan:
        out_shape.append(shape_of((rows, 2 * columns), F32))
        if w is not None:
            out_shape.append(shape_of((8, rows), F32))
    kernel_plan = [(t, [slot for slot, _ in slots], acc is not None, w is not None) for t, slots, acc, w in plan]
    operands = list(weights) + chunks + accs + wanted
    return pl.pallas_call(
        functools.partial(logits_kernel, kernel_plan, columns, part),
        out_shape=out_shape,
        in_specs=[IN_SMEM] + [IN_VMEM] * len(operands),
        out_specs=[IN_VMEM] * len(out_shape),
        compiler_params=params(),
        cost_estimate=cost(4 * len(chunks) * rows * part * columns, len(chunks) * (2 * rows * part + 4 * part * columns)),
    )(meta, *operands)


def spread(start, part, grads_own, grads_far, w_own, w_far, send, kept):
    n_blocks, rows, columns = grads_own.shape
    flat = (n_blocks * rows, columns)
    over = (((1,), (1,)), ((), ()))
    here = lax.dot_general(
        grads_own[...].reshape(flat), w_own[pl.ds(start, part), :], over, preferred_element_type=F32
    )
    here += lax.dot_general(
        grads_far[...].reshape(flat), w_far[pl.ds(start, part), :], over, preferred_element_type=F32
    )
    kept[...] = here[:rows]
    for t in range(1, n_blocks):
        send[t - 1][...] = here[t * rows:(t + 1) * rows].astype(BF16)


def grads_kernel(n_blocks, n_stats, columns, part, meta, *refs):
    refs = list(refs)
    logits = [refs.pop(0) for _ in range(n_blocks)]
    target, info, scalars = refs.pop(0), refs.pop(0), refs.pop(0)
    stats = [refs.pop(0) for _ in range(n_stats)]
    w_own, w_far, grads_own, grads_far, loss, kept = refs[:6]
    send = refs[6:]
    rows = logits[0].shape[0]
    top = stats[0][0:1, :]
    for s in stats[1:]:
        top = jnp.maximum(top, s[0:1, :])
    total = jnp.zeros_like(top)
    picked = jnp.zeros_like(top)
    for s in stats:
        total += s[1:2, :] * jnp.exp(s[0:1, :] - top)
        picked += s[2:3, :]
    signed_mask = info[0:1, :]
    token_logp = picked - top - jnp.log(total)
    margin = BETA * (jnp.sum(signed_mask * token_logp, axis=1, keepdims=True) + scalars[0:1, :])
    loss[...] = jnp.maximum(-margin, 0.0) + jnp.log1p(jnp.exp(-jnp.abs(margin)))
    factor = -BETA * (1.0 / (1.0 + jnp.exp(margin))) * scalars[1:2, :]
    weight = factor[:, 0:1] * signed_mask
    lines = lax.broadcasted_iota(jnp.int32, (128, top.shape[1]), 0)
    packed = jnp.where(lines == 0, top, jnp.where(lines == 1, weight, 1.0 / total)).T
    for t in range(n_blocks):
        at = slice(t * rows, (t + 1) * rows)
        top_t, weight_t, inverse_t = packed[at, 0:1], packed[at, 1:2], packed[at, 2:3]
        wanted = target[at, :]
        for j, grads in enumerate((grads_own, grads_far)):
            l = logits[t][:, j * columns:(j + 1) * columns]
            column = lax.broadcasted_iota(jnp.int32, l.shape, 1) + meta[1 + j]
            hit = jnp.where(column == wanted, 1.0, 0.0)
            grads[t] = (weight_t * (hit - jnp.exp(l - top_t) * inverse_t)).astype(BF16)
    start = pl.multiple_of(meta[0] * part, part)
    spread(start, part, grads_own, grads_far, w_own, w_far, send, kept)


def spread_kernel(part, meta, grads_own, grads_far, w_own, w_far, kept, *send):
    start = pl.multiple_of(meta[0] * part, part)
    spread(start, part, grads_own, grads_far, w_own, w_far, send, kept)


def spread_shapes(n_blocks, rows, part):
    return [shape_of((rows, part), F32)] + [shape_of((rows, part), BF16)] * (n_blocks - 1)


def grads_call(logits, target, info, scalars, stats, weights, k_id, firsts, part):
    n_blocks, rows, columns = len(logits), logits[0].shape[0], weights[0].shape[1]
    meta = jnp.stack([k_id] + list(firsts)).astype(jnp.int32)
    grads = shape_of((n_blocks, rows, columns), BF16)
    out_shape = [grads, grads, shape_of((1, 128), F32)] + spread_shapes(n_blocks, rows, part)
    operands = list(logits) + [target, info, scalars] + list(stats) + list(weights)
    return pl.pallas_call(
        functools.partial(grads_kernel, n_blocks, len(stats), columns, part),
        out_shape=out_shape,
        in_specs=[IN_SMEM] + [IN_VMEM] * len(operands),
        out_specs=[IN_VMEM] * len(out_shape),
        compiler_params=params(),
        cost_estimate=cost(4 * n_blocks * rows * part * columns, 8 * part * columns),
    )(meta, *operands)


def spread_call(grads_own, grads_far, weights, k_id, part):
    n_blocks, rows, columns = grads_own.shape
    out_shape = spread_shapes(n_blocks, rows, part)
    return pl.pallas_call(
        functools.partial(spread_kernel, part),
        out_shape=out_shape,
        in_specs=[IN_SMEM] + [IN_VMEM] * 4,
        out_specs=[IN_VMEM] * len(out_shape),
        compiler_params=params(),
        cost_estimate=cost(4 * n_blocks * rows * part * columns, 4 * part * columns),
    )(k_id.reshape(1).astype(jnp.int32), grads_own, grads_far, *weights)


def head_kernel(near_keys, far_keys, n_parts, part, meta, *refs):
    refs = list(refs)
    grads = [refs.pop(0), refs.pop(0)]
    near = {k: refs.pop(0) for k in near_keys}
    stacks = [refs.pop(0) for _ in far_keys]
    far = {k: stack.at[i] for stack, keys in zip(stacks, far_keys) for i, k in enumerate(keys)}
    out, slots, sems = refs
    n_blocks, rows, columns = grads[0].shape
    right = jnp.concatenate([g[...].reshape(n_blocks * rows, columns) for g in grads])
    copies = []
    for i in range(n_parts):
        left = jnp.concatenate([x[t, i][...] for x in (near, far) for t in range(n_blocks)])
        product = lax.dot_general(left, right, (((0,), (0,)), ((), ())), preferred_element_type=F32)
        if i >= 2:
            copies[i - 2].wait()
        slots[i % 2] = product.astype(BF16)
        start = pl.multiple_of(meta[i] * part, part)
        copies.append(pltpu.make_async_copy(slots.at[i % 2], out.at[pl.ds(start, part), :], sems.at[i % 2]))
        copies[-1].start()
    for copy in copies[-2:]:
        copy.wait()


def head_call(near, far, grads, meta):
    n_blocks, rows, columns = grads[0].shape
    n_parts = len(near) // n_blocks
    part = near[0, 0].shape[1]
    operands = list(grads) + list(near.values()) + [stack for _, stack in far]
    return pl.pallas_call(
        functools.partial(head_kernel, list(near), [keys for keys, _ in far], n_parts, part),
        out_shape=shape_of((n_parts * part, columns), BF16),
        in_specs=[IN_SMEM] + [IN_VMEM] * len(operands),
        out_specs=pl.BlockSpec(memory_space=pl.ANY),
        scratch_shapes=[pltpu.VMEM((2, part, columns), BF16), pltpu.SemaphoreType.DMA((2,))],
        compiler_params=params(),
        cost_estimate=cost(
            4 * n_blocks * rows * n_parts * part * columns,
            4 * n_blocks * n_parts * rows * part + 2 * n_parts * part * columns,
        ),
    )(meta, *operands)


def shards(hidden, head_weight, targets, response_start, other_sums, ref_logp, loss_cotangent):
    n_voc, n_ctx, n_dp = lax.axis_size("vocab"), lax.axis_size("ctx"), lax.axis_size("dp")
    me_voc, me_ctx, me_dp = lax.axis_index("vocab"), lax.axis_index("ctx"), lax.axis_index("dp")
    part, _, sides, window = hidden.shape
    rows = sides * window
    columns = head_weight.shape[1]

    weights = (head_weight, lax.ppermute(head_weight, "dp", ring(n_dp, 1)))
    firsts = [
        ((me_voc * n_ctx + me_ctx) * n_dp + owner) * columns for owner in (me_dp, (me_dp + 1) % n_dp)
    ]
    part_of = [(me_voc - s) % n_voc for s in range(n_voc)]
    meta = jnp.stack(part_of + firsts).astype(jnp.int32)

    blocks_of = [(me_ctx - t) % n_ctx for t in range(n_ctx)]
    block = lambda a, b: lax.dynamic_slice_in_dim(a, b * window, window, 1).reshape(rows)
    mine = lambda a: lax.dynamic_index_in_dim(a, me_dp, 0, keepdims=False)
    wanted = [block(mine(targets), b)[:, None] for b in blocks_of]
    target = jnp.concatenate(wanted)
    position = lax.broadcasted_iota(jnp.int32, (sides, window * n_ctx), 1)
    side_sign = jnp.array([1.0, -1.0], dtype=F32)[:, None]
    signed_mask = jnp.where(position >= mine(response_start), side_sign, 0.0)
    info = jnp.concatenate([block(signed_mask, b) for b in blocks_of])
    info = jnp.broadcast_to(info[None, :], (8, n_ctx * rows))
    ratio = mine(other_sums) - mine(ref_logp)
    scalars = jnp.stack([ratio[0] - ratio[1], mine(loss_cotangent)])
    scalars = jnp.broadcast_to(jnp.pad(scalars, (0, 6))[:, None], (8, 128))

    own = hidden.transpose(1, 2, 3, 0).reshape(rows, part)
    order = [0]
    for s in range(1, n_voc // 2 + 1):
        order += [s] if 2 * s == n_voc else [s, n_voc - s]
    near, rest = order[1:3], order[3:]
    chunk = {(0, 0): own}
    for s in near:
        chunk[0, s] = lax.ppermute(own, "vocab", ring(n_voc, s))
    for t in range(1, n_ctx):
        chunk[t, 0] = lax.ppermute(own, "ctx", ring(n_ctx, t))
    held = lax.optimization_barrier([own] + [chunk[0, s] for s in near])
    for s, c in zip(near, held[1:]):
        chunk[0, s] = c
    for s in rest:
        chunk[0, s] = lax.ppermute(held[0], "vocab", ring(n_voc, s))
    for s in near:
        for t in range(1, n_ctx):
            chunk[t, s] = lax.ppermute(chunk[0, s], "ctx", ring(n_ctx, t))

    beyond = list(range(1, n_ctx))
    call = functools.partial(logits_call, meta=meta, weights=weights, part=part)
    logits = call(
        [(0, [(s, chunk[0, s]) for s in [0] + near], None, None)] + [(t, [(0, chunk[t, 0])], None, None) for t in beyond]
    )
    held = lax.optimization_barrier([chunk[0, s] for s in rest] + list(logits))
    for s, c in zip(rest, held):
        chunk[0, s] = c
    logits = held[len(rest):]
    for s in rest:
        for t in beyond:
            chunk[t, s] = lax.ppermute(chunk[0, s], "ctx", ring(n_ctx, t))
    done = call(
        [(0, [(s, chunk[0, s]) for s in rest], logits[0], wanted[0])]
        + [(t, [(s, chunk[t, s]) for s in near], logits[t], None) for t in beyond]
    )
    logits = [done[0]] + list(done[2:])
    stats = [done[1]]

    late = [(t, s) for t in beyond for s in rest]
    soon = [k for k in chunk if k not in late]
    far_soon = lax.ppermute(jnp.stack([chunk[k] for k in soon]), "dp", ring(n_dp, 1))
    done = call([(t, [(s, chunk[t, s]) for s in rest], logits[t], wanted[t]) for t in beyond])
    logits = [logits[0]] + list(done[0::2])
    stats = stats + list(done[1::2])

    others = [lax.ppermute(jnp.stack(stats), "ctx", ring(n_ctx, t)) for t in beyond]
    merged = []
    for b in range(n_ctx):
        seen = [stats[b]] + [o[(b - t) % n_ctx] for t, o in zip(beyond, others)]
        top = seen[0][0]
        for o in seen[1:]:
            top = jnp.maximum(top, o[0])
        total = sum(o[1] * jnp.exp(o[0] - top) for o in seen)
        picked = sum(o[2] for o in seen)
        merged.append(jnp.pad(jnp.stack([top, total, picked]), ((0, 5), (0, 0))))
    merged = jnp.concatenate(merged, axis=1)
    held = lax.optimization_barrier([merged] + [chunk[k] for k in late])
    merged = held[0]
    far_late = lax.ppermute(jnp.stack(held[1:]), "dp", ring(n_dp, 1))
    all_stats = [merged] + [lax.ppermute(merged, "vocab", ring(n_voc, s)) for s in range(1, n_voc)]

    goes_to = [(me_voc + s) % n_voc for s in range(n_voc)]
    leave = order[::-1]
    grads_own, grads_far, loss, kept, *send = grads_call(
        logits, target, info, scalars, all_stats, weights, goes_to[leave[0]], firsts, part
    )
    theirs = lax.ppermute(grads_far, "dp", ring(n_dp, 1))

    arrived, landed = [], []
    for i, s in enumerate(leave):
        if i:
            kept, *send = spread_call(grads_own, grads_far, weights, goes_to[s], part)
            held = lax.optimization_barrier(list(arrived) + list(send))
            arrived, send = held[:len(arrived)], held[len(arrived):]
            leaving = together(before, arrived).astype(BF16)
            leaving, *send = lax.optimization_barrier([leaving] + list(send))
            by = ring(n_voc, leave[i - 1])
            if i == 1:
                half = rows // 2
                landed = [lax.ppermute(leaving[:half], "vocab", by), lax.ppermute(leaving[half:], "vocab", by)]
            else:
                landed.append(lax.ppermute(leaving, "vocab", by))
            if i > 1:
                landed[i - 2], *send = lax.optimization_barrier([landed[i - 2]] + list(send))
        arrived = [lax.ppermute(c, "ctx", ring(n_ctx, -t)) for t, c in zip(beyond, send)]
        before = kept
    grad_head = head_call(chunk, [(soon, far_soon), (late, far_late)], [grads_own, theirs], meta)
    before, grad_head = lax.optimization_barrier((before, grad_head))
    landed = [jnp.concatenate(landed[:2])] + landed[2:]
    summed = together(before, arrived + landed)
    grad_hidden = summed.astype(BF16).reshape(1, sides, window, part).transpose(3, 0, 1, 2)

    far_loss = lax.ppermute(loss, "dp", ring(n_dp, 1))
    pair = lax.broadcasted_iota(jnp.int32, (n_dp,), 0)
    pair_loss = jnp.where(pair == me_dp, loss[0, :n_dp], far_loss[0, :n_dp])
    return (grad_hidden, grad_head, pair_loss)


def together(kept, arrived):
    for a in arrived:
        kept = kept + a.astype(F32)
    return kept


def solution(mesh):
    placed = (
        P("vocab", ("groups", "dp"), None, "ctx"),
        P(None, ("vocab", "ctx", "dp")),
        P("groups", None, None),
        P("groups"),
        P("groups", None),
        P("groups", None),
        P("groups"),
    )
    return jax.shard_map(
        shards,
        mesh=mesh,
        in_specs=placed,
        out_specs=(
            P("vocab", ("groups", "dp"), None, "ctx"),
            P("groups", ("vocab", "ctx", "dp")),
            P("groups"),
        ),
        check_vma=False,
    )
```

time: 388 us -> 105 us (0.27)
  waiting for transfers between devices: 269 us -> 28.5 us
  blocking collectives: 70.3 us -> 0 us
  Pallas kernels: 0 us -> 27.6 us
  starting transfers between devices: 0.2 us -> 25.3 us
  matrix products: 20.5 us -> 0 us
  between operations: 13.9 us -> 2.06 us
  local copies, waits for them, and re-layouts: 11.1 us -> 15.3 us
    reduce_scatter x3 -> x0, waiting for transfers between devices: 176 us -> none  [the longest x1 142 us: shards(): lax.psum_scatter(lax.dot_general(head_weight, grad_logits, (((1,), (1,)),...]
    all_gather x2 -> x0, waiting for transfers between devices: 92.6 us -> none  [the longest x1 81.9 us: shards(): lax.all_gather(all_pairs.reshape(width_part, row_count), 'vocab', axis=0,...]
    pmax x1 -> x0, blocking collectives: 30.9 us -> none  [shards(): row_max = lax.pmax(local_max, ('vocab', 'ctx', 'dp'))]
    psum x1 -> x0, blocking collectives: 29.5 us -> none  [shards(): lax.psum((jnp.sum(shifted, axis=1), local_pick), ('vocab', 'ctx', 'dp'))]
    ppermute x0 -> x24, waiting for transfers between devices: none -> 28.5 us  [the longest x1 6.85 us: shards(): lax.ppermute(leaving[half:], 'vocab', by)]
    pallas_call x0 -> x8, Pallas kernels: none -> 27.6 us  [the longest x3 9.89 us: logits_call(): pl.pallas_call(functools.partial(logits_kernel, kernel_plan, columns, par...]
    ppermute x0 -> x24, starting transfers between devices: none -> 25.3 us  [the longest x4 5.27 us: shards(): lax.ppermute(c, 'ctx', ring(n_ctx, -t))]
    dot_general x3 -> x0, matrix products: 20.5 us -> none  [the longest x1 8 us: shards(): lax.dot_general(head_weight, grad_logits, (((1,), (1,)), ((), ())), prefe...]
  transfers between devices with their start and end apart: 5 -> 24, of which waited for: 4 -> 10; matrix products, arithmetic and copies ran while one was open for 4% -> 15% of each run, Pallas kernels for 0% -> 24%
where the time goes in v3:
time: 105 us; the launch traced here: 104 us
  waiting for transfers between devices  28.5 us (27%)
  Pallas kernels  27.6 us (26%)
  starting transfers between devices  25.3 us (24%)
  local copies, waits for them, and re-layouts  15.3 us (15%)
  other arithmetic  5.39 us (5%)
  between operations  2.06 us (2%)
    pallas_call x3, Pallas kernels, logits_call(): pl.pallas_call(functools.partial(logits_kernel, kernel_plan, columns, par...  9.89 us
    unnamed x14, local copies, waits for them, and re-layouts  9.66 us
    pallas_call x3, Pallas kernels, spread_call(): pl.pallas_call(functools.partial(spread_kernel, part), out_shape=out_shap...  8.77 us
    ppermute x1, waiting for transfers between devices, shards(): lax.ppermute(leaving[half:], 'vocab', by)  6.85 us
    pallas_call x1, Pallas kernels, head_call(): pl.pallas_call(functools.partial(head_kernel, list(near), [keys for keys,...  5.53 us
    ppermute x4, starting transfers between devices, shards(): lax.ppermute(c, 'ctx', ring(n_ctx, -t))  5.27 us
    ppermute x1, waiting for transfers between devices, shards(): lax.ppermute(leaving[:half], 'vocab', by)  5.2 us
    ppermute x2, starting transfers between devices, shards(): chunk[0, s] = lax.ppermute(own, 'vocab', ring(n_voc, s))  4.75 us
  transfers between devices with their start and end apart: 24, of which 10 were waited for; matrix products, arithmetic and copies ran while one was open for 15% of the time, Pallas kernels for 24%

profile of v3, /device:TPU:0, one launch (start us, length us, event | category | flops | bytes accessed | tf_op | source)
XLA Modules:
  0.0 104.1 jit_solution(7503360562327344812)
XLA Ops:
  0.6 0.5 collective-permute-start
  1.2 2.6 %collective-permute-start.1 = (bf16[128,1024]{1,0:T(8,128)(2,1)}, bf16[128,1024]{1,0:T(8,128)(2,1)S(1)}, u32[]{:S(2)}, u32[]{:S(2)}) collective-permute-start(bf16[128,1024]{1,0:T(8,128)(2,1)} %bitcast.72), channel_id=1, source_target_pairs={{0,4},{4,8},{8,12},{12,0},{1,5},{5,9},{9,13},{13,1},{2,6},{6,10},{... | collective-permute-start | bytes 786440 | tf_op jit(solution)/shard_map/ppermute | solution.py:259
  3.8 2.1 %collective-permute-start.2 = (bf16[128,1024]{1,0:T(8,128)(2,1)}, bf16[128,1024]{1,0:T(8,128)(2,1)S(1)}, u32[]{:S(2)}, u32[]{:S(2)}) collective-permute-start(bf16[128,1024]{1,0:T(8,128)(2,1)} %bitcast.73), channel_id=1, source_target_pairs={{0,12},{4,0},{8,4},{12,8},{1,13},{5,1},{9,5},{13,9},{2,14},{6,2},{... | collective-permute-start | bytes 786440 | tf_op jit(solution)/shard_map/ppermute | solution.py:259
  5.9 1.6 %collective-permute-start.4 = (bf16[128,1024]{1,0:T(8,128)(2,1)}, bf16[128,1024]{1,0:T(8,128)(2,1)S(1)}, u32[]{:S(2)}, u32[]{:S(2)}) collective-permute-start(bf16[128,1024]{1,0:T(8,128)(2,1)} %bitcast.74), channel_id=1, source_target_pairs={{0,2},{2,0},{1,3},{3,1},{4,6},{6,4},{5,7},{7,5},{8,10},{10,8},{9,1... | collective-permute-start | bytes 786440 | tf_op jit(solution)/shard_map/ppermute | solution.py:261
  7.5 0.8 constant_dynamic-slice_fusion.4
  8.4 0.1 broadcast_in_dim_reshape.6
  8.4 0.1 broadcast_in_dim_reshape.7
  8.5 1.3 %dynamic_slice.32 = s32[1]{0:T(128)} dynamic-slice(s32[2]{0:T(128)} %param.11, s32[]{:T(128)S(6)} %select_n.85), dynamic_slice_sizes={1} | dynamic-slice | bytes 12 | tf_op jit(solution)/shard_map/jit(dynamic_index_in_dim)/dynamic_slice | solution.py:240
  9.8 1.2 %dynamic_slice.37 = f32[1]{0:T(128)} dynamic-slice(f32[2]{0:T(128)} %param.14, s32[]{:T(128)S(6)} %select_n.85), dynamic_slice_sizes={1} | dynamic-slice | bytes 12 | tf_op jit(solution)/shard_map/jit(dynamic_index_in_dim)/dynamic_slice | solution.py:240
  11.1 0.7 fusion.1
  11.8 0.6 fusion.13
  13.6 0.7 iota_compare_fusion.1
  14.3 0.6 fusion
  14.9 0.7 broadcast_select_fusion
  15.8 0.1 copy.15.refs_5_
  15.9 0.1 copy.16.refs_2_
  16.0 0.1 copy.17.refs_2_
  16.2 0.1 reshape.63
  16.3 0.1 stack.84.meta
  16.4 1.7 %constant_dynamic-update-slice_fusion = bf16[7,128,1024]{2,1,0:T(8,128)(2,1)} fusion(bf16[1,128,1024]{2,1,0:T(8,128)(2,1)} %bitcast.75), kind=kLoop, calls=%fused_computation.10 | loop fusion | bytes 524288
  18.1 1.2 %collective-permute-start.3 = (bf16[128,1024]{1,0:T(8,128)(2,1)}, bf16[128,1024]{1,0:T(8,128)(2,1)S(1)}, u32[]{:S(2)}, u32[]{:S(2)}) collective-permute-start(bf16[128,1024]{1,0:T(8,128)(2,1)} %bitcast.76), channel_id=1, source_target_pairs={{0,8},{4,12},{8,0},{12,4},{1,9},{5,13},{9,1},{13,5},{2,10},{6,14},... | collective-permute-start | bytes 786440 | tf_op jit(solution)/shard_map/ppermute | solution.py:266
  19.3 1.5 %collective-permute-start.5 = (bf16[128,1024]{1,0:T(8,128)(2,1)S(1)}, bf16[128,1024]{1,0:T(8,128)(2,1)S(1)}, u32[]{:S(2)}, u32[]{:S(2)}) collective-permute-start(bf16[128,1024]{1,0:T(8,128)(2,1)S(1)} %collective-permute-done.1.refs_1_.refs_3_), channel_id=1, source_target_pairs={{0,2},{2,0},{1,3},{3,1},{4,6},{6,4},{5,7},{7,5},{8,10},{10,8},{9,1... | collective-permute-start | bytes 786440 | tf_op jit(solution)/shard_map/ppermute | solution.py:269
  20.8 0.5 collective-permute-start.6
  21.3 0.7 bitcast_dynamic-update-slice_fusion.5
  22.0 0.7 bitcast_dynamic-update-slice_fusion.4
  22.8 0.7 bitcast_dynamic-update-slice_fusion.3
  23.5 2.2 %copy-done = bf16[4096,512]{1,0:T(8,128)(2,1)S(1)} copy-done((bf16[4096,512]{1,0:T(8,128)(2,1)S(1)}, bf16[4096,512]{1,0:T(8,128)(2,1)}, u32[]{:S(2)}) %copy-start) | copy-done | bytes 4194328
  25.7 3.5 %shard_map.103 = (f32[128,1024]{1,0:T(8,128)S(1)}, f32[128,1024]{1,0:T(8,128)S(1)}) custom-call(s32[6]{0:T(128)S(1)} %stack.84.meta, bf16[4096,512]{1,0:T(8,128)(2,1)S(1)} %copy-done, bf16[4096,512]{1,0:T(8,128)(2,1)} %collective-permute-done.w_far.refs_10_, bf16[128,1024]{1,0:T(8,128)(2,1)S(1)} %bitcast.77, ...), custom_call_target="tpu_custom_call" | custom-call | flops 1073741824 | bytes 9437184 | tf_op jit(solution)/shard_map/pallas_call | solution.py:82
  29.2 3.5 %collective-permute-done.3.refs_0_.refs_6_ = bf16[128,1024]{1,0:T(8,128)(2,1)S(1)} collective-permute-done((bf16[128,1024]{1,0:T(8,128)(2,1)}, bf16[128,1024]{1,0:T(8,128)(2,1)S(1)}, u32[]{:S(2)}, u32[]{:S(2)}) %collective-permute-start.3) | collective-permute-done | bytes 262176 | tf_op jit(solution)/shard_map/ppermute | solution.py:266
  32.7 1.2 %collective-permute-start.7 = (bf16[128,1024]{1,0:T(8,128)(2,1)S(1)}, bf16[128,1024]{1,0:T(8,128)(2,1)S(1)}, u32[]{:S(2)}, u32[]{:S(2)}) collective-permute-start(bf16[128,1024]{1,0:T(8,128)(2,1)S(1)} %collective-permute-done.3.refs_0_.refs_6_), channel_id=1, source_target_pairs={{0,2},{2,0},{1,3},{3,1},{4,6},{6,4},{5,7},{7,5},{8,10},{10,8},{9,1... | collective-permute-start | bytes 786440 | tf_op jit(solution)/shard_map/ppermute | solution.py:282
  33.9 3.3 %shard_map.104 = (f32[128,1024]{1,0:T(8,128)S(1)}, f32[8,128]{1,0:T(8,128)S(1)}, f32[128,1024]{1,0:T(8,128)S(1)}) custom-call(s32[6]{0:T(128)S(1)} %stack.84.meta, bf16[4096,512]{1,0:T(8,128)(2,1)S(1)} %copy-done, bf16[4096,512]{1,0:T(8,128)(2,1)} %collective-permute-done.w_far.refs_10_, bf16[128,1024]{1,0:T(8,128)(2,1)S(1)} %collective-permute-done.3.refs_0_.refs_6_, ...), custom_call_target="tpu_custom_call" | custom-call | flops 805306368 | bytes 7077888 | tf_op jit(solution)/shard_map/pallas_call | solution.py:82
  37.2 0.7 bitcast_dynamic-update-slice_fusion.2
  38.0 2.1 %collective-permute-done.7.refs_0_.refs_9_ = bf16[128,1024]{1,0:T(8,128)(2,1)S(1)} collective-permute-done((bf16[128,1024]{1,0:T(8,128)(2,1)S(1)}, bf16[128,1024]{1,0:T(8,128)(2,1)S(1)}, u32[]{:S(2)}, u32[]{:S(2)}) %collective-permute-start.7) | collective-permute-done | bytes 262176 | tf_op jit(solution)/shard_map/ppermute | solution.py:282
  40.1 3.1 %shard_map.105 = (f32[128,1024]{1,0:T(8,128)S(1)}, f32[8,128]{1,0:T(8,128)S(1)}) custom-call(s32[6]{0:T(128)S(1)} %stack.84.meta, bf16[4096,512]{1,0:T(8,128)(2,1)S(1)} %copy-done, bf16[4096,512]{1,0:T(8,128)(2,1)} %collective-permute-done.w_far.refs_10_, bf16[128,1024]{1,0:T(8,128)(2,1)S(1)} %collective-permute-done.7.refs_0_.refs_9_, ...), custom_call_target="tpu_custom_call" | custom-call | flops 268435456 | bytes 2359296 | tf_op jit(solution)/shard_map/pallas_call | solution.py:82
  43.1 0.9 collective-permute-start.8
  44.1 0.7 bitcast_dynamic-update-slice_fusion.1
  44.8 2.0 %collective-permute-done.8 = f32[2,8,128]{2,1,0:T(8,128)S(1)} collective-permute-done((f32[2,8,128]{2,1,0:T(8,128)S(1)}, f32[2,8,128]{2,1,0:T(8,128)S(1)}, u32[]{:S(2)}, u32[]{:S(2)}) %collective-permute-start.8) | collective-permute-done | bytes 8224 | tf_op jit(solution)/shard_map/ppermute | solution.py:297
  46.9 3.3 %collective-permute-start.10 = (f32[8,256]{1,0:T(8,128)S(1)}, f32[8,256]{1,0:T(8,128)S(1)}, u32[]{:S(2)}, u32[]{:S(2)}) collective-permute-start(f32[8,256]{1,0:T(8,128)S(1)} %pad_maximum_fusion.1.refs_5_), channel_id=1, source_target_pairs={{0,8},{4,12},{8,0},{12,4},{1,9},{5,13},{9,1},{13,5},{2,10},{6,14},... | collective-permute-start | bytes 24584 | tf_op jit(solution)/shard_map/ppermute | solution.py:311
  50.2 0.5 collective-permute-start.11
  50.7 0.7 bitcast_dynamic-update-slice_fusion
  51.5 0.9 collective-permute-done.9.refs_6_
  52.4 1.5 %collective-permute-done.11.refs_8_ = f32[8,256]{1,0:T(8,128)S(1)} collective-permute-done((f32[8,256]{1,0:T(8,128)S(1)}, f32[8,256]{1,0:T(8,128)S(1)}, u32[]{:S(2)}, u32[]{:S(2)}) %collective-permute-start.11) | collective-permute-done | bytes 8224 | tf_op jit(solution)/shard_map/ppermute | solution.py:311
  53.9 3.4 %shard_map.106 = (bf16[2,128,512]{2,1,0:T(8,128)(2,1)S(1)}, bf16[2,128,512]{2,1,0:T(8,128)(2,1)S(1)}, f32[1,128]{1,0:T(1,128)S(1)}, f32[128,1024]{1,0:T(8,128)S(1)}, bf16[128,1024]{1,0:T(8,128)(2,1)S(1)}) custom-call(s32[3]{0:T(128)S(1)} %pad_add_fusion.1.meta, f32[128,1024]{1,0:T(8,128)S(1)} %get-tuple-element.55.refs_0_, ...), custom_call_target="tpu_custom_call" | custom-call | flops 536870912 | bytes 4194304 | tf_op jit(solution)/shard_map/pallas_call | solution.py:159
  57.3 1.7 %collective-permute-start.15 = (bf16[128,1024]{1,0:T(8,128)(2,1)S(1)}, bf16[128,1024]{1,0:T(8,128)(2,1)}, u32[]{:S(2)}, u32[]{:S(2)}) collective-permute-start(bf16[128,1024]{1,0:T(8,128)(2,1)S(1)} %get-tuple-element.67), channel_id=1, source_target_pairs={{0,2},{2,0},{1,3},{3,1},{4,6},{6,4},{5,7},{7,5},{8,10},{10,8},{9,1... | collective-permute-start | bytes 786440 | tf_op jit(solution)/shard_map/ppermute | solution.py:336
  59.0 2.2 %copy-done.2 = bf16[4096,512]{1,0:T(8,128)(2,1)S(1)} copy-done((bf16[4096,512]{1,0:T(8,128)(2,1)S(1)}, bf16[4096,512]{1,0:T(8,128)(2,1)}, u32[]{:S(2)}) %copy-start.2) | copy-done | bytes 4194328
  61.2 2.9 %shard_map.109 = (f32[128,1024]{1,0:T(8,128)S(1)}, bf16[128,1024]{1,0:T(8,128)(2,1)S(1)}) custom-call(s32[1]{0:T(128)} %bitcast.28.meta, bf16[2,128,512]{2,1,0:T(8,128)(2,1)S(1)} %get-tuple-element.61.grads_own.refs_0_, bf16[2,128,512]{2,1,0:T(8,128)(2,1)S(1)} %get-tuple-element.62.grads_far, bf16[4096,512]{1,0:T(8,128)(2,1)S(1)} %copy-done.2, ...), custom_call_target="tpu_custom_call" | custom-call | flops 536870912 | bytes 2097152 | tf_op jit(solution)/shard_map/pallas_call | solution.py:172
  64.2 1.0 add_convert_fusion.3
  65.2 1.4 %collective-permute-start.18 = (bf16[128,1024]{1,0:T(8,128)(2,1)S(1)}, bf16[128,1024]{1,0:T(8,128)(2,1)S(1)}, u32[]{:S(2)}, u32[]{:S(2)}) collective-permute-start(bf16[128,1024]{1,0:T(8,128)(2,1)S(1)} %get-tuple-element.74), channel_id=1, source_target_pairs={{0,2},{2,0},{1,3},{3,1},{4,6},{6,4},{5,7},{7,5},{8,10},{10,8},{9,1... | collective-permute-start | bytes 786440 | tf_op jit(solution)/shard_map/ppermute | solution.py:336
  66.6 2.9 %shard_map.110 = (f32[128,1024]{1,0:T(8,128)S(1)}, bf16[128,1024]{1,0:T(8,128)(2,1)S(1)}) custom-call(s32[1]{0:T(128)} %bitcast.29.meta, bf16[2,128,512]{2,1,0:T(8,128)(2,1)S(1)} %get-tuple-element.61.grads_own.refs_0_, bf16[2,128,512]{2,1,0:T(8,128)(2,1)S(1)} %get-tuple-element.62.grads_far, bf16[4096,512]{1,0:T(8,128)(2,1)S(1)} %copy-done.2, ...), custom_call_target="tpu_custom_call" | custom-call | flops 536870912 | bytes 2097152 | tf_op jit(solution)/shard_map/pallas_call | solution.py:172
  69.5 1.3 %collective-permute-start.17 = (bf16[64,1024]{1,0:T(8,128)(2,1)S(1)}, bf16[64,1024]{1,0:T(8,128)(2,1)S(1)}, u32[]{:S(2)}, u32[]{:S(2)}) collective-permute-start(bf16[64,1024]{1,0:T(8,128)(2,1)S(1)} %get-tuple-element.96), channel_id=1, source_target_pairs={{0,8},{4,12},{8,0},{12,4},{1,9},{5,13},{9,1},{13,5},{2,10},{6,14},... | collective-permute-start | bytes 393224 | tf_op jit(solution)/shard_map/ppermute | solution.py:331
  70.9 0.7 collective-permute-done.18
  71.7 5.2 %collective-permute-done.17 = bf16[64,1024]{1,0:T(8,128)(2,1)S(1)} collective-permute-done((bf16[64,1024]{1,0:T(8,128)(2,1)S(1)}, bf16[64,1024]{1,0:T(8,128)(2,1)S(1)}, u32[]{:S(2)}, u32[]{:S(2)}) %collective-permute-start.17) | collective-permute-done | bytes 131104 | tf_op jit(solution)/shard_map/ppermute | solution.py:331
  76.9 0.7 collective-permute-start.19
  77.6 0.5 collective-permute-start.12
  78.1 2.9 %shard_map.107 = (f32[128,1024]{1,0:T(8,128)S(1)}, bf16[128,1024]{1,0:T(8,128)(2,1)S(1)}) custom-call(s32[1]{0:T(128)} %bitcast.meta, bf16[2,128,512]{2,1,0:T(8,128)(2,1)S(1)} %get-tuple-element.61.grads_own.refs_0_, bf16[2,128,512]{2,1,0:T(8,128)(2,1)S(1)} %get-tuple-element.62.grads_far, bf16[4096,512]{1,0:T(8,128)(2,1)S(1)} %copy-done.2, ...), custom_call_target="tpu_custom_call" | custom-call | flops 536870912 | bytes 2097152 | tf_op jit(solution)/shard_map/pallas_call | solution.py:172
  81.0 2.2 %collective-permute-done.19 = bf16[128,1024]{1,0:T(8,128)(2,1)S(1)} collective-permute-done((bf16[128,1024]{1,0:T(8,128)(2,1)S(1)}, bf16[128,1024]{1,0:T(8,128)(2,1)S(1)}, u32[]{:S(2)}, u32[]{:S(2)}) %collective-permute-start.19) | collective-permute-done | bytes 262176 | tf_op jit(solution)/shard_map/ppermute | solution.py:336
  83.3 6.8 %collective-permute-done.16 = bf16[64,1024]{1,0:T(8,128)(2,1)S(1)} collective-permute-done((bf16[64,1024]{1,0:T(8,128)(2,1)S(1)}, bf16[64,1024]{1,0:T(8,128)(2,1)S(1)}, u32[]{:S(2)}, u32[]{:S(2)}) %collective-permute-start.16) | collective-permute-done | bytes 131104 | tf_op jit(solution)/shard_map/ppermute | solution.py:331
  90.2 1.9 %collective-permute-start.21 = (bf16[128,1024]{1,0:T(8,128)(2,1)S(1)}, bf16[128,1024]{1,0:T(8,128)(2,1)S(1)}, u32[]{:S(2)}, u32[]{:S(2)}) collective-permute-start(bf16[128,1024]{1,0:T(8,128)(2,1)S(1)} %add_convert_fusion.2), channel_id=1, source_target_pairs={{0,12},{4,0},{8,4},{12,8},{1,13},{5,1},{9,5},{13,9},{2,14},{6,2},{... | collective-permute-start | bytes 786440 | tf_op jit(solution)/shard_map/ppermute | solution.py:333
  92.0 0.2 collective-permute-start.22
  92.2 1.5 %collective-permute-start.20 = (bf16[128,1024]{1,0:T(8,128)(2,1)S(1)}, bf16[128,1024]{1,0:T(8,128)(2,1)S(1)}, u32[]{:S(2)}, u32[]{:S(2)}) collective-permute-start(bf16[128,1024]{1,0:T(8,128)(2,1)S(1)} %get-tuple-element.84), channel_id=1, source_target_pairs={{0,2},{2,0},{1,3},{3,1},{4,6},{6,4},{5,7},{7,5},{8,10},{10,8},{9,1... | collective-permute-start | bytes 786440 | tf_op jit(solution)/shard_map/ppermute | solution.py:336
  93.7 0.5 compare_select_fusion
  94.2 5.5 %shard_map.108 = bf16[4096,512]{1,0:T(8,128)(2,1)} custom-call(s32[6]{0:T(128)S(1)} %stack.84.meta, bf16[2,128,512]{2,1,0:T(8,128)(2,1)S(1)} %get-tuple-element.61.grads_own.refs_0_, bf16[2,128,512]{2,1,0:T(8,128)(2,1)S(1)} %collective-permute-done.12.refs_1_, bf16[128,1024]{1,0:T(8,128)(2,1)S(1)} %bitcast.78, ...), custom_call_target="tpu_custom_call" | custom-call | flops 2147483648 | bytes 8388608 | tf_op jit(solution)/shard_map/pallas_call | solution.py:210
  99.7 3.5 %collective-permute-done.22 = bf16[128,1024]{1,0:T(8,128)(2,1)S(1)} collective-permute-done((bf16[128,1024]{1,0:T(8,128)(2,1)S(1)}, bf16[128,1024]{1,0:T(8,128)(2,1)S(1)}, u32[]{:S(2)}, u32[]{:S(2)}) %collective-permute-start.22) | collective-permute-done | bytes 262176 | tf_op jit(solution)/shard_map/ppermute | solution.py:333
  103.2 0.9 add_convert_fusion
  (39 shorter events, 0.6 us)
Async XLA Ops:
  0.6 22.9 %copy-start.3 = (bf16[1024,1,2,64]{0,3,2,1:T(8,128)(2,1)S(1)}, bf16[1024,1,2,64]{0,3,2,1:T(8,128)(2,1)}, u32[]{:S(2)}) copy-start(bf16[1024,1,2,64]{0,3,2,1:T(8,128)(2,1)} %param.8) | copy-start | bytes 786436
  0.6 22.9 %collective-permute-start = (bf16[4096,512]{1,0:T(8,128)(2,1)}, bf16[4096,512]{1,0:T(8,128)(2,1)}, u32[]{:S(2)}, u32[]{:S(2)}) collective-permute-start(bf16[4096,512]{1,0:T(8,128)(2,1)} %w_own.11), channel_id=1, source_target_pairs={{0,1},{1,0},{2,3},{3,2},{4,5},{5,4},{6,7},{7,6},{8,9},{9,8},{10,11... | collective-permute-start | bytes 12582920 | tf_op jit(solution)/shard_map/ppermute | solution.py:231
  1.2 16.9 %collective-permute-start.1 = (bf16[128,1024]{1,0:T(8,128)(2,1)}, bf16[128,1024]{1,0:T(8,128)(2,1)S(1)}, u32[]{:S(2)}, u32[]{:S(2)}) collective-permute-start(bf16[128,1024]{1,0:T(8,128)(2,1)} %bitcast.72), channel_id=1, source_target_pairs={{0,4},{4,8},{8,12},{12,0},{1,5},{5,9},{9,13},{13,1},{2,6},{6,10},{... | collective-permute-start | bytes 786440 | tf_op jit(solution)/shard_map/ppermute | solution.py:259
  3.8 14.3 %collective-permute-start.2 = (bf16[128,1024]{1,0:T(8,128)(2,1)}, bf16[128,1024]{1,0:T(8,128)(2,1)S(1)}, u32[]{:S(2)}, u32[]{:S(2)}) collective-permute-start(bf16[128,1024]{1,0:T(8,128)(2,1)} %bitcast.73), channel_id=1, source_target_pairs={{0,12},{4,0},{8,4},{12,8},{1,13},{5,1},{9,5},{13,9},{2,14},{6,2},{... | collective-permute-start | bytes 786440 | tf_op jit(solution)/shard_map/ppermute | solution.py:259
  5.9 16.9 %collective-permute-start.4 = (bf16[128,1024]{1,0:T(8,128)(2,1)}, bf16[128,1024]{1,0:T(8,128)(2,1)S(1)}, u32[]{:S(2)}, u32[]{:S(2)}) collective-permute-start(bf16[128,1024]{1,0:T(8,128)(2,1)} %bitcast.74), channel_id=1, source_target_pairs={{0,2},{2,0},{1,3},{3,1},{4,6},{6,4},{5,7},{7,5},{8,10},{10,8},{9,1... | collective-permute-start | bytes 786440 | tf_op jit(solution)/shard_map/ppermute | solution.py:261
  18.1 14.6 %collective-permute-start.3 = (bf16[128,1024]{1,0:T(8,128)(2,1)}, bf16[128,1024]{1,0:T(8,128)(2,1)S(1)}, u32[]{:S(2)}, u32[]{:S(2)}) collective-permute-start(bf16[128,1024]{1,0:T(8,128)(2,1)} %bitcast.76), channel_id=1, source_target_pairs={{0,8},{4,12},{8,0},{12,4},{1,9},{5,13},{9,1},{13,5},{2,10},{6,14},... | collective-permute-start | bytes 786440 | tf_op jit(solution)/shard_map/ppermute | solution.py:266
  19.3 14.6 %collective-permute-start.5 = (bf16[128,1024]{1,0:T(8,128)(2,1)S(1)}, bf16[128,1024]{1,0:T(8,128)(2,1)S(1)}, u32[]{:S(2)}, u32[]{:S(2)}) collective-permute-start(bf16[128,1024]{1,0:T(8,128)(2,1)S(1)} %collective-permute-done.1.refs_1_.refs_3_), channel_id=1, source_target_pairs={{0,2},{2,0},{1,3},{3,1},{4,6},{6,4},{5,7},{7,5},{8,10},{10,8},{9,1... | collective-permute-start | bytes 786440 | tf_op jit(solution)/shard_map/ppermute | solution.py:269
  20.8 13.1 %collective-permute-start.6 = (bf16[128,1024]{1,0:T(8,128)(2,1)S(1)}, bf16[128,1024]{1,0:T(8,128)(2,1)S(1)}, u32[]{:S(2)}, u32[]{:S(2)}) collective-permute-start(bf16[128,1024]{1,0:T(8,128)(2,1)S(1)} %collective-permute-done.2.refs_2_.refs_4_), channel_id=1, source_target_pairs={{0,2},{2,0},{1,3},{3,1},{4,6},{6,4},{5,7},{7,5},{8,10},{10,8},{9,1... | collective-permute-start | bytes 786440 | tf_op jit(solution)/shard_map/ppermute | solution.py:269
  23.5 2.2 %copy-start = (bf16[4096,512]{1,0:T(8,128)(2,1)S(1)}, bf16[4096,512]{1,0:T(8,128)(2,1)}, u32[]{:S(2)}) copy-start(bf16[4096,512]{1,0:T(8,128)(2,1)} %w_own.11) | copy-start | bytes 12582916
  32.7 7.3 %collective-permute-start.7 = (bf16[128,1024]{1,0:T(8,128)(2,1)S(1)}, bf16[128,1024]{1,0:T(8,128)(2,1)S(1)}, u32[]{:S(2)}, u32[]{:S(2)}) collective-permute-start(bf16[128,1024]{1,0:T(8,128)(2,1)S(1)} %collective-permute-done.3.refs_0_.refs_6_), channel_id=1, source_target_pairs={{0,2},{2,0},{1,3},{3,1},{4,6},{6,4},{5,7},{7,5},{8,10},{10,8},{9,1... | collective-permute-start | bytes 786440 | tf_op jit(solution)/shard_map/ppermute | solution.py:282
  40.1 13.9 %copy-start.1 = (bf16[4096,512]{1,0:T(8,128)(2,1)S(1)}, bf16[4096,512]{1,0:T(8,128)(2,1)}, u32[]{:S(2)}) copy-start(bf16[4096,512]{1,0:T(8,128)(2,1)} %w_own.11) | copy-start | bytes 12582916
  43.1 3.7 %collective-permute-start.8 = (f32[2,8,128]{2,1,0:T(8,128)S(1)}, f32[2,8,128]{2,1,0:T(8,128)S(1)}, u32[]{:S(2)}, u32[]{:S(2)}) collective-permute-start(f32[2,8,128]{2,1,0:T(8,128)S(1)} %pad_maximum_fusion), channel_id=1, source_target_pairs={{0,2},{2,0},{1,3},{3,1},{4,6},{6,4},{5,7},{7,5},{8,10},{10,8},{9,1... | collective-permute-start | bytes 24584 | tf_op jit(solution)/shard_map/ppermute | solution.py:297
  46.9 5.5 %collective-permute-start.9 = (f32[8,256]{1,0:T(8,128)S(1)}, f32[8,256]{1,0:T(8,128)S(1)}, u32[]{:S(2)}, u32[]{:S(2)}) collective-permute-start(f32[8,256]{1,0:T(8,128)S(1)} %pad_maximum_fusion.1.refs_5_), channel_id=1, source_target_pairs={{0,4},{4,8},{8,12},{12,0},{1,5},{5,9},{9,13},{13,1},{2,6},{6,10},{... | collective-permute-start | bytes 24584 | tf_op jit(solution)/shard_map/ppermute | solution.py:311
  46.9 5.4 %collective-permute-start.10 = (f32[8,256]{1,0:T(8,128)S(1)}, f32[8,256]{1,0:T(8,128)S(1)}, u32[]{:S(2)}, u32[]{:S(2)}) collective-permute-start(f32[8,256]{1,0:T(8,128)S(1)} %pad_maximum_fusion.1.refs_5_), channel_id=1, source_target_pairs={{0,8},{4,12},{8,0},{12,4},{1,9},{5,13},{9,1},{13,5},{2,10},{6,14},... | collective-permute-start | bytes 24584 | tf_op jit(solution)/shard_map/ppermute | solution.py:311
  50.2 3.7 %collective-permute-start.11 = (f32[8,256]{1,0:T(8,128)S(1)}, f32[8,256]{1,0:T(8,128)S(1)}, u32[]{:S(2)}, u32[]{:S(2)}) collective-permute-start(f32[8,256]{1,0:T(8,128)S(1)} %pad_maximum_fusion.1.refs_5_), channel_id=1, source_target_pairs={{0,12},{4,0},{8,4},{12,8},{1,13},{5,1},{9,5},{13,9},{2,14},{6,2},{... | collective-permute-start | bytes 24584 | tf_op jit(solution)/shard_map/ppermute | solution.py:311
  51.5 42.7 %collective-permute-start.13 = (bf16[7,128,1024]{2,1,0:T(8,128)(2,1)}, bf16[7,128,1024]{2,1,0:T(8,128)(2,1)}, u32[]{:S(2)}, u32[]{:S(2)}) collective-permute-start(bf16[7,128,1024]{2,1,0:T(8,128)(2,1)} %bitcast_dynamic-update-slice_fusion), channel_id=1, source_target_pairs={{0,1},{1,0},{2,3},{3,2},{4,5},{5,4},{6,7},{7,6},{8,9},{9,8},{10,11... | collective-permute-start | bytes 5505032 | tf_op jit(solution)/shard_map/ppermute | solution.py:292
  57.3 6.8 %collective-permute-start.15 = (bf16[128,1024]{1,0:T(8,128)(2,1)S(1)}, bf16[128,1024]{1,0:T(8,128)(2,1)}, u32[]{:S(2)}, u32[]{:S(2)}) collective-permute-start(bf16[128,1024]{1,0:T(8,128)(2,1)S(1)} %get-tuple-element.67), channel_id=1, source_target_pairs={{0,2},{2,0},{1,3},{3,1},{4,6},{6,4},{5,7},{7,5},{8,10},{10,8},{9,1... | collective-permute-start | bytes 786440 | tf_op jit(solution)/shard_map/ppermute | solution.py:336
  59.0 2.2 %copy-start.2 = (bf16[4096,512]{1,0:T(8,128)(2,1)S(1)}, bf16[4096,512]{1,0:T(8,128)(2,1)}, u32[]{:S(2)}) copy-start(bf16[4096,512]{1,0:T(8,128)(2,1)} %w_own.11) | copy-start | bytes 12582916
  65.2 6.4 %collective-permute-start.18 = (bf16[128,1024]{1,0:T(8,128)(2,1)S(1)}, bf16[128,1024]{1,0:T(8,128)(2,1)S(1)}, u32[]{:S(2)}, u32[]{:S(2)}) collective-permute-start(bf16[128,1024]{1,0:T(8,128)(2,1)S(1)} %get-tuple-element.74), channel_id=1, source_target_pairs={{0,2},{2,0},{1,3},{3,1},{4,6},{6,4},{5,7},{7,5},{8,10},{10,8},{9,1... | collective-permute-start | bytes 786440 | tf_op jit(solution)/shard_map/ppermute | solution.py:336
  69.5 7.3 %collective-permute-start.17 = (bf16[64,1024]{1,0:T(8,128)(2,1)S(1)}, bf16[64,1024]{1,0:T(8,128)(2,1)S(1)}, u32[]{:S(2)}, u32[]{:S(2)}) collective-permute-start(bf16[64,1024]{1,0:T(8,128)(2,1)S(1)} %get-tuple-element.96), channel_id=1, source_target_pairs={{0,8},{4,12},{8,0},{12,4},{1,9},{5,13},{9,1},{13,5},{2,10},{6,14},... | collective-permute-start | bytes 393224 | tf_op jit(solution)/shard_map/ppermute | solution.py:331
  76.9 6.4 %collective-permute-start.19 = (bf16[128,1024]{1,0:T(8,128)(2,1)S(1)}, bf16[128,1024]{1,0:T(8,128)(2,1)S(1)}, u32[]{:S(2)}, u32[]{:S(2)}) collective-permute-start(bf16[128,1024]{1,0:T(8,128)(2,1)S(1)} %get-tuple-element.79), channel_id=1, source_target_pairs={{0,2},{2,0},{1,3},{3,1},{4,6},{6,4},{5,7},{7,5},{8,10},{10,8},{9,1... | collective-permute-start | bytes 786440 | tf_op jit(solution)/shard_map/ppermute | solution.py:336
  77.6 14.6 %collective-permute-start.14 = (bf16[1,128,1024]{2,1,0:T(8,128)(2,1)S(1)}, bf16[1,128,1024]{2,1,0:T(8,128)(2,1)S(1)}, u32[]{:S(2)}, u32[]{:S(2)}) collective-permute-start(bf16[1,128,1024]{2,1,0:T(8,128)(2,1)S(1)} %bitcast.79), channel_id=1, source_target_pairs={{0,1},{1,0},{2,3},{3,2},{4,5},{5,4},{6,7},{7,6},{8,9},{9,8},{10,11... | collective-permute-start | bytes 786440 | tf_op jit(solution)/shard_map/ppermute | solution.py:310
  77.6 16.6 %collective-permute-start.12 = (bf16[2,128,512]{2,1,0:T(8,128)(2,1)S(1)}, bf16[2,128,512]{2,1,0:T(8,128)(2,1)S(1)}, u32[]{:S(2)}, u32[]{:S(2)}) collective-permute-start(bf16[2,128,512]{2,1,0:T(8,128)(2,1)S(1)} %get-tuple-element.62.grads_far), channel_id=1, source_target_pairs={{0,1},{1,0},{2,3},{3,2},{4,5},{5,4},{6,7},{7,6},{8,9},{9,8},{10,11... | collective-permute-start | bytes 786440 | tf_op jit(solution)/shard_map/ppermute | solution.py:318
  78.1 14.0 %collective-permute-start.23 = (f32[1,128]{1,0:T(1,128)S(1)}, f32[1,128]{1,0:T(1,128)S(1)}, u32[]{:S(2)}, u32[]{:S(2)}) collective-permute-start(f32[1,128]{1,0:T(1,128)S(1)} %get-tuple-element.90), channel_id=1, source_target_pairs={{0,1},{1,0},{2,3},{3,2},{4,5},{5,4},{6,7},{7,6},{8,9},{9,8},{10,11... | collective-permute-start | bytes 1544 | tf_op jit(solution)/shard_map/ppermute | solution.py:344
  83.2 6.9 %collective-permute-start.16 = (bf16[64,1024]{1,0:T(8,128)(2,1)S(1)}, bf16[64,1024]{1,0:T(8,128)(2,1)S(1)}, u32[]{:S(2)}, u32[]{:S(2)}) collective-permute-start(bf16[64,1024]{1,0:T(8,128)(2,1)S(1)} %get-tuple-element.95), channel_id=1, source_target_pairs={{0,8},{4,12},{8,0},{12,4},{1,9},{5,13},{9,1},{13,5},{2,10},{6,14},... | collective-permute-start | bytes 393224 | tf_op jit(solution)/shard_map/ppermute | solution.py:331
  90.2 9.6 %collective-permute-start.21 = (bf16[128,1024]{1,0:T(8,128)(2,1)S(1)}, bf16[128,1024]{1,0:T(8,128)(2,1)S(1)}, u32[]{:S(2)}, u32[]{:S(2)}) collective-permute-start(bf16[128,1024]{1,0:T(8,128)(2,1)S(1)} %add_convert_fusion.2), channel_id=1, source_target_pairs={{0,12},{4,0},{8,4},{12,8},{1,13},{5,1},{9,5},{13,9},{2,14},{6,2},{... | collective-permute-start | bytes 786440 | tf_op jit(solution)/shard_map/ppermute | solution.py:333
  92.0 11.2 %collective-permute-start.22 = (bf16[128,1024]{1,0:T(8,128)(2,1)S(1)}, bf16[128,1024]{1,0:T(8,128)(2,1)S(1)}, u32[]{:S(2)}, u32[]{:S(2)}) collective-permute-start(bf16[128,1024]{1,0:T(8,128)(2,1)S(1)} %add_convert_fusion.1), channel_id=1, source_target_pairs={{0,4},{4,8},{8,12},{12,0},{1,5},{5,9},{9,13},{13,1},{2,6},{6,10},{... | collective-permute-start | bytes 786440 | tf_op jit(solution)/shard_map/ppermute | solution.py:333
  92.2 11.1 %collective-permute-start.20 = (bf16[128,1024]{1,0:T(8,128)(2,1)S(1)}, bf16[128,1024]{1,0:T(8,128)(2,1)S(1)}, u32[]{:S(2)}, u32[]{:S(2)}) collective-permute-start(bf16[128,1024]{1,0:T(8,128)(2,1)S(1)} %get-tuple-element.84), channel_id=1, source_target_pairs={{0,2},{2,0},{1,3},{3,1},{4,6},{6,4},{5,7},{7,5},{8,10},{10,8},{9,1... | collective-permute-start | bytes 786440 | tf_op jit(solution)/shard_map/ppermute | solution.py:336

commit v4 on v3

v4 whole, which is shorter than its diff:
```python
import functools

import jax
import jax.numpy as jnp
from jax import lax
from jax.experimental import pallas as pl
from jax.experimental.pallas import tpu as pltpu
from jax.sharding import PartitionSpec as P

BETA = 0.1
F32, BF16 = jnp.float32, jnp.bfloat16
VMEM_BYTES = 16 * 1024 * 1024
IN_VMEM = pl.BlockSpec(memory_space=pltpu.VMEM)
IN_SMEM = pl.BlockSpec(memory_space=pltpu.SMEM)
IN_PLACE = pl.BlockSpec(memory_space=pl.ANY)
PAIRS_OUT = [(0, 1), (1, 0), (2, 3), (3, 2)]
PAIR_IN = [(1, 2), (2, 1)]
TO_ENDS = [(1, 0), (2, 3)]
FROM_ENDS = [(0, 1), (3, 2)]


def ring(count, shift):
    return [(i, (i + shift) % count) for i in range(count)]


def params():
    return pltpu.CompilerParams(vmem_limit_bytes=VMEM_BYTES)


def cost(flops, moved):
    return pl.CostEstimate(flops=int(flops), bytes_accessed=int(moved), transcendentals=0)


def shape_of(shape, kind):
    return jax.ShapeDtypeStruct(shape, kind)


def fetch(w_own, w_far, start, part, slots, i, sems):
    copies = []
    for j, w in enumerate((w_own, w_far)):
        copies.append(pltpu.make_async_copy(w.at[pl.ds(start, part), :], slots.at[i, j], sems.at[i, j]))
        copies[-1].start()
    return copies


def row_stats(own, far, wanted, first_own, first_far):
    top = jnp.max(jnp.maximum(own, far), axis=1, keepdims=True)
    total = jnp.sum(jnp.exp(own - top) + jnp.exp(far - top), axis=1, keepdims=True)
    column = lax.broadcasted_iota(jnp.int32, own.shape, 1)
    zero = jnp.zeros_like(own)
    picked = jnp.sum(
        jnp.where(column + first_own == wanted, own, zero) + jnp.where(column + first_far == wanted, far, zero),
        axis=1,
        keepdims=True,
    )
    lane = lax.broadcasted_iota(jnp.int32, (own.shape[0], 128), 1)
    return jnp.where(lane == 0, top, jnp.where(lane == 1, total, picked)).T[:8, :]


def logits_kernel(plan, columns, part, n_voc, meta, w_own, w_far, *refs):
    refs = list(refs)
    chunks = {(t, i): refs.pop(0) for t, parts, _, _ in plan for i in parts}
    accs = {t: refs.pop(0) for t, _, has_acc, _ in plan if has_acc}
    wanted = {t: refs.pop(0) for t, _, _, done in plan if done}
    slots, sems = refs[-2:]
    used = sorted({i for _, parts, _, _ in plan for i in parts})
    coming = [fetch(w_own, w_far, pl.multiple_of(meta[i] * part, part), part, slots, n, sems) for n, i in enumerate(used)]
    outs = {}
    stats = {}
    for t, _, _, done in plan:
        outs[t] = refs.pop(0)
        if done:
            stats[t] = refs.pop(0)
    for n, i in enumerate(used):
        for copy in coming[n]:
            copy.wait()
        for t, parts, has_acc, _ in plan:
            if i not in parts:
                continue
            x = chunks[t, i][...]
            for j in range(2):
                at = slice(j * columns, (j + 1) * columns)
                product = jnp.dot(x, slots[n, j], preferred_element_type=F32)
                if i != parts[0]:
                    product += outs[t][:, at]
                elif has_acc:
                    product += accs[t][:, at]
                outs[t][:, at] = product
    for t in stats:
        own, far = outs[t][:, :columns], outs[t][:, columns:]
        stats[t][...] = row_stats(own, far, wanted[t][...], meta[n_voc], meta[n_voc + 1])


def logits_call(plan, meta, weights, part, n_voc):
    columns = weights[0].shape[1]
    chunks = [c for _, parts, _, _ in plan for c in parts.values()]
    accs = [acc for _, _, acc, _ in plan if acc is not None]
    wanted = [w for _, _, _, w in plan if w is not None]
    rows = chunks[0].shape[0]
    out_shape = []
    for _, _, _, w in plan:
        out_shape.append(shape_of((rows, 2 * columns), F32))
        if w is not None:
            out_shape.append(shape_of((8, rows), F32))
    kernel_plan = [(t, sorted(parts), acc is not None, w is not None) for t, parts, acc, w in plan]
    chunks = [parts[i] for _, parts, _, _ in plan for i in sorted(parts)]
    n_used = len({i for _, parts, _, _ in plan for i in parts})
    operands = chunks + accs + wanted
    return pl.pallas_call(
        functools.partial(logits_kernel, kernel_plan, columns, part, n_voc),
        out_shape=out_shape,
        in_specs=[IN_SMEM, IN_PLACE, IN_PLACE] + [IN_VMEM] * len(operands),
        out_specs=[IN_VMEM] * len(out_shape),
        scratch_shapes=[pltpu.VMEM((n_used, 2, part, columns), BF16), pltpu.SemaphoreType.DMA((n_used, 2))],
        compiler_params=params(),
        cost_estimate=cost(4 * len(chunks) * rows * part * columns, n_used * 4 * part * columns),
    )(meta, *weights, *operands)


def spread(flipped_own, flipped_far, w_own, w_far, kept, send):
    rows = kept.shape[1]
    here = jnp.dot(w_own, flipped_own, preferred_element_type=F32)
    here += jnp.dot(w_far, flipped_far, preferred_element_type=F32)
    kept[...] = here[:, :rows]
    for t, out in enumerate(send, 1):
        out[...] = here[:, t * rows:(t + 1) * rows].astype(BF16)


def grads_kernel(n_blocks, n_stats, columns, part, window, meta, start, sums, refer, cotangent, w_own, w_far, *refs):
    refs = list(refs)
    logits = [refs.pop(0) for _ in range(n_blocks)]
    target = refs.pop(0)
    stats = [refs.pop(0) for _ in range(n_stats)]
    slots, sems = refs[-2:]
    grads_own, grads_far, flipped_own, flipped_far, loss, kept = refs[:6]
    send = refs[6:-2]
    coming = fetch(w_own, w_far, pl.multiple_of(meta[0] * part, part), part, slots, 0, sems)
    rows = logits[0].shape[0]
    pair, me_ctx = meta[3], meta[4]
    top = stats[0][0:1, :]
    for s in stats[1:]:
        top = jnp.maximum(top, s[0:1, :])
    total = jnp.zeros_like(top)
    picked = jnp.zeros_like(top)
    for s in stats:
        total += s[1:2, :] * jnp.exp(s[0:1, :] - top)
        picked += s[2:3, :]
    row = lax.broadcasted_iota(jnp.int32, (1, rows), 1)
    masks = []
    for t in range(n_blocks):
        block = lax.rem(me_ctx + (n_blocks - t), n_blocks)
        seen = lax.rem(row, window) + block * window >= start[pair]
        masks.append(jnp.where(seen, jnp.where(row < window, 1.0, -1.0), 0.0))
    signed_mask = jnp.concatenate(masks, axis=1)
    token_logp = picked - top - jnp.log(total)
    offset = (sums[pair, 0] - refer[pair, 0]) - (sums[pair, 1] - refer[pair, 1])
    zeros = jnp.zeros((1, 128), F32)
    margin = BETA * (jnp.sum(signed_mask * token_logp, axis=1, keepdims=True) + (zeros + offset))
    loss[...] = jnp.maximum(-margin, 0.0) + jnp.log1p(jnp.exp(-jnp.abs(margin)))
    factor = -BETA * (1.0 / (1.0 + jnp.exp(margin))) * cotangent[pair]
    weight = factor[:, 0:1] * signed_mask
    lines = lax.broadcasted_iota(jnp.int32, (128, top.shape[1]), 0)
    packed = jnp.where(lines == 0, top, jnp.where(lines == 1, weight, 1.0 / total)).T
    for t in range(n_blocks):
        at = slice(t * rows, (t + 1) * rows)
        top_t, weight_t, inverse_t = packed[at, 0:1], packed[at, 1:2], packed[at, 2:3]
        wanted = target[at, :]
        for j, (grads, flipped) in enumerate(((grads_own, flipped_own), (grads_far, flipped_far))):
            l = logits[t][:, j * columns:(j + 1) * columns]
            column = lax.broadcasted_iota(jnp.int32, l.shape, 1) + meta[1 + j]
            hit = jnp.where(column == wanted, 1.0, 0.0)
            g = weight_t * (hit - jnp.exp(l - top_t) * inverse_t)
            grads[t] = g.astype(BF16)
            flipped[:, at] = g.T.astype(BF16)
    for copy in coming:
        copy.wait()
    spread(flipped_own[...], flipped_far[...], slots[0, 0], slots[0, 1], kept, send)


def spread_kernel(part, meta, w_own, w_far, flipped_own, flipped_far, kept, *rest):
    send, slots, sems = rest[:-2], rest[-2], rest[-1]
    coming = fetch(w_own, w_far, pl.multiple_of(meta[0] * part, part), part, slots, 0, sems)
    for copy in coming:
        copy.wait()
    spread(flipped_own[...], flipped_far[...], slots[0, 0], slots[0, 1], kept, send)


def spread_shapes(n_blocks, rows, part):
    return [shape_of((part, rows), F32)] + [shape_of((part, rows), BF16)] * (n_blocks - 1)


def weight_slots(part, columns):
    return [pltpu.VMEM((1, 2, part, columns), BF16), pltpu.SemaphoreType.DMA((1, 2))]


def grads_call(logits, target, stats, small, weights, meta, part, window):
    n_blocks, rows, columns = len(logits), logits[0].shape[0], weights[0].shape[1]
    grads = shape_of((n_blocks, rows, columns), BF16)
    flipped = shape_of((columns, n_blocks * rows), BF16)
    out_shape = [grads, grads, flipped, flipped, shape_of((1, 128), F32)] + spread_shapes(n_blocks, rows, part)
    operands = list(logits) + [target] + list(stats)
    return pl.pallas_call(
        functools.partial(grads_kernel, n_blocks, len(stats), columns, part, window),
        out_shape=out_shape,
        in_specs=[IN_SMEM] * 5 + [IN_PLACE] * 2 + [IN_VMEM] * len(operands),
        out_specs=[IN_VMEM] * len(out_shape),
        scratch_shapes=weight_slots(part, columns),
        compiler_params=params(),
        cost_estimate=cost(4 * n_blocks * rows * part * columns, 8 * part * columns),
    )(meta, *small, *weights, *operands)


def spread_call(flipped_own, flipped_far, weights, k_id, part, rows):
    columns, n_rows = flipped_own.shape
    out_shape = spread_shapes(n_rows // rows, rows, part)
    return pl.pallas_call(
        functools.partial(spread_kernel, part),
        out_shape=out_shape,
        in_specs=[IN_SMEM] + [IN_PLACE] * 2 + [IN_VMEM] * 2,
        out_specs=[IN_VMEM] * len(out_shape),
        scratch_shapes=weight_slots(part, columns),
        compiler_params=params(),
        cost_estimate=cost(4 * n_rows * part * columns, 4 * part * columns),
    )(k_id.reshape(1).astype(jnp.int32), *weights, flipped_own, flipped_far)


def add_kernel(turned, kept, *refs):
    total = kept[...]
    for a in refs[:-1]:
        total += a[...].astype(F32)
    refs[-1][...] = (total.T if turned else total).astype(BF16)


def add_call(kept, arrived, turned=False):
    shape = kept.shape[::-1] if turned else kept.shape
    return pl.pallas_call(
        functools.partial(add_kernel, turned),
        out_shape=shape_of(shape, BF16),
        in_specs=[IN_VMEM] * (1 + len(arrived)),
        out_specs=IN_VMEM,
        compiler_params=params(),
        cost_estimate=cost(kept.size, 4 * kept.size),
    )(kept, *arrived)


def head_kernel(near_keys, far_keys, n_parts, part, meta, *refs):
    refs = list(refs)
    grads = [refs.pop(0), refs.pop(0)]
    near = {k: refs.pop(0) for k in near_keys}
    stacks = [refs.pop(0) for _ in far_keys]
    far = {k: stack.at[i] for stack, keys in zip(stacks, far_keys) for i, k in enumerate(keys)}
    out, slots, sems = refs
    n_blocks, rows, columns = grads[0].shape
    right = jnp.concatenate([g[...].reshape(n_blocks * rows, columns) for g in grads])
    copies = []
    for i in range(n_parts):
        left = jnp.concatenate([x[t, i][...] for x in (near, far) for t in range(n_blocks)])
        product = lax.dot_general(left, right, (((0,), (0,)), ((), ())), preferred_element_type=F32)
        if i >= 2:
            copies[i - 2].wait()
        slots[i % 2] = product.astype(BF16)
        start = pl.multiple_of(meta[i] * part, part)
        copies.append(pltpu.make_async_copy(slots.at[i % 2], out.at[pl.ds(start, part), :], sems.at[i % 2]))
        copies[-1].start()
    for copy in copies[-2:]:
        copy.wait()


def head_call(near, far, grads, meta):
    n_blocks, rows, columns = grads[0].shape
    n_parts = len(near) // n_blocks
    part = near[0, 0].shape[1]
    operands = list(grads) + list(near.values()) + [stack for _, stack in far]
    return pl.pallas_call(
        functools.partial(head_kernel, list(near), [keys for keys, _ in far], n_parts, part),
        out_shape=shape_of((n_parts * part, columns), BF16),
        in_specs=[IN_SMEM] + [IN_VMEM] * len(operands),
        out_specs=pl.BlockSpec(memory_space=pl.ANY),
        scratch_shapes=[pltpu.VMEM((2, part, columns), BF16), pltpu.SemaphoreType.DMA((2,))],
        compiler_params=params(),
        cost_estimate=cost(
            4 * n_blocks * rows * n_parts * part * columns,
            4 * n_blocks * n_parts * rows * part + 2 * n_parts * part * columns,
        ),
    )(meta, *operands)


def together(*groups):
    flat = lax.optimization_barrier([a for group in groups for a in group])
    out = []
    for group in groups:
        out.append(flat[:len(group)])
        flat = flat[len(group):]
    return out


def shards(hidden, head_weight, targets, response_start, other_sums, ref_logp, loss_cotangent):
    n_voc, n_ctx, n_dp = lax.axis_size("vocab"), lax.axis_size("ctx"), lax.axis_size("dp")
    me_voc, me_ctx, me_dp = lax.axis_index("vocab"), lax.axis_index("ctx"), lax.axis_index("dp")
    part, _, sides, window = hidden.shape
    rows = sides * window
    columns = head_weight.shape[1]
    line = n_voc == 4
    beyond = list(range(1, n_ctx))
    dp_swap = lambda a: lax.ppermute(a, "dp", ring(n_dp, 1))
    along = lambda a, by: lax.ppermute(a, "vocab", by)

    if line:
        table = [[0, 1, 2, 3], [1, 0, 2, 3], [2, 3, 1, 0], [3, 2, 1, 0]]
        part_of = [sum(jnp.where(me_voc == z, table[z][i], 0) for z in range(n_voc)) for i in range(n_voc)]
    else:
        part_of = [(me_voc - s) % n_voc for s in range(n_voc)]
    firsts = [
        ((me_voc * n_ctx + me_ctx) * n_dp + owner) * columns for owner in (me_dp, (me_dp + 1) % n_dp)
    ]
    meta = jnp.stack(part_of + firsts).astype(jnp.int32)

    weights = (head_weight, dp_swap(head_weight))

    own = hidden.transpose(1, 2, 3, 0).reshape(rows, part)
    chunk = {(0, 0): own}
    logits = [None] * n_ctx
    stats = [None] * n_ctx
    call = functools.partial(logits_call, meta=meta, weights=weights, part=part, n_voc=n_voc)
    cross = lambda a: [lax.ppermute(a, "ctx", ring(n_ctx, t)) for t in beyond]
    inner = last = None
    for step in range(n_voc):
        over = cross(chunk[0, step])
        came = []
        if line:
            if step == 0:
                came = [along(own, PAIRS_OUT), along(own, PAIR_IN)]
            elif step == 1:
                came = [along(inner, TO_ENDS), along(chunk[0, 1], PAIR_IN)]
            elif step == 2:
                came = [along(last, TO_ENDS)]
        elif step + 1 < n_voc:
            came = [along(own, ring(n_voc, step + 1))]
        if step:
            plan = [(0, {i: chunk[0, i] for i in ([0, 1] if step == 1 else [step])}, logits[0], None)]
            plan += [(t, {step - 1: chunk[t, step - 1]}, logits[t], None) for t in beyond]
            if step == n_voc - 1:
                plan[0] = plan[0][:3] + (wanted[0],)
            done = list(call(plan))
            if step == n_voc - 1:
                stats[0] = done.pop(1)
            logits = list(done)
        else:
            held, raw = together(came[:1], [targets])
            pair = lax.broadcasted_iota(jnp.int32, targets.shape, 0)
            mine = jnp.sum(jnp.where(pair == me_dp, raw[0], 0), axis=0)
            blocks = [mine[:, b * window:(b + 1) * window].reshape(rows) for b in range(n_ctx)]
            wanted = []
            for t in range(n_ctx):
                at = (me_ctx - t) % n_ctx
                wanted.append(sum(jnp.where(at == b, blocks[b], 0) for b in range(n_ctx))[:, None])
            target = jnp.concatenate(wanted)
        ready = [a for a in logits if a is not None]
        over, came, ready = together(over, came, ready)
        if ready:
            logits = ready
        for t, a in zip(beyond, over):
            chunk[t, step] = a
        if not line:
            if came:
                chunk[0, step + 1] = came[0]
        elif step == 0:
            chunk[0, 1], inner = came
        elif step == 1:
            chunk[0, 2] = inner + came[0]
            last = came[1]
        elif step == 2:
            chunk[0, 3] = last + came[0]

    final = n_voc - 1
    done = call([(t, {final: chunk[t, final]}, logits[t], wanted[t]) for t in beyond])
    logits = [logits[0]] + list(done[0::2])
    stats = [stats[0]] + list(done[1::2])

    late = [(t, final) for t in beyond]
    soon = [k for k in chunk if k not in late]
    far_soon = dp_swap(jnp.stack([chunk[k] for k in soon]))

    others = cross(jnp.stack(stats))
    merged = []
    for b in range(n_ctx):
        seen = [stats[b]] + [o[(b - t) % n_ctx] for t, o in zip(beyond, others)]
        top = seen[0][0]
        for o in seen[1:]:
            top = jnp.maximum(top, o[0])
        total = sum(o[1] * jnp.exp(o[0] - top) for o in seen)
        picked = sum(o[2] for o in seen)
        merged.append(jnp.pad(jnp.stack([top, total, picked]), ((0, 5), (0, 0))))
    merged = jnp.concatenate(merged, axis=1)
    all_stats = [merged] + [along(merged, ring(n_voc, s)) for s in range(1, n_voc)]

    meta_grads = jnp.stack([part_of[final]] + firsts + [me_dp, me_ctx]).astype(jnp.int32)
    small = (response_start, other_sums, ref_logp, loss_cotangent)
    grads_own, grads_far, flipped_own, flipped_far, loss, kept, *send = grads_call(
        logits, target, all_stats, small, weights, meta_grads, part, window
    )
    theirs = dp_swap(grads_far)
    far_late = dp_swap(jnp.stack(together([chunk[k] for k in late], [kept])[0]))
    back = lambda cs: [lax.ppermute(c, "ctx", ring(n_ctx, -t)) for t, c in zip(beyond, cs)]
    landed = []
    for step in range(n_voc):
        slot = final - step
        over = back(send)
        came = []
        if line:
            if step == 1:
                sum_3 = (kept_before, arrived)
                came = [along(add_call(*sum_3), FROM_ENDS)]
            elif step == 2:
                sum_2 = (kept_before, arrived)
                came = [along(add_call(*sum_2), FROM_ENDS), along(add_call(sum_3[0], sum_3[1] + landed), PAIR_IN)]
            elif step == 3:
                came = [
                    along(add_call(kept_before, arrived + landed[1:]), PAIRS_OUT),
                    along(add_call(sum_2[0], sum_2[1] + landed[:1]), PAIR_IN),
                ]
        elif step:
            came = [along(add_call(kept_before, arrived), ring(n_voc, -(slot + 1)))]
        kept_before = kept
        if step < n_voc - 1:
            kept, *send = spread_call(flipped_own, flipped_far, weights, part_of[slot - 1], part, rows)
            arrived, came, send = together(over, came, send)
        else:
            grad_head = head_call(chunk, [(soon, far_soon), (late, far_late)], [grads_own, theirs], meta)
            arrived, came, (grad_head,) = together(over, came, [grad_head])
        landed = came if line else landed + came
    summed = add_call(kept_before, arrived + landed, turned=True)
    grad_hidden = summed.reshape(1, sides, window, part).transpose(3, 0, 1, 2)

    far_loss = dp_swap(loss)
    pair = lax.broadcasted_iota(jnp.int32, (n_dp,), 0)
    pair_loss = jnp.where(pair == me_dp, loss[0, :n_dp], far_loss[0, :n_dp])
    return (grad_hidden, grad_head, pair_loss)


def solution(mesh):
    placed = (
        P("vocab", ("groups", "dp"), None, "ctx"),
        P(None, ("vocab", "ctx", "dp")),
        P("groups", None, None),
        P("groups"),
        P("groups", None),
        P("groups", None),
        P("groups"),
    )
    return jax.shard_map(
        shards,
        mesh=mesh,
        in_specs=placed,
        out_specs=(
            P("vocab", ("groups", "dp"), None, "ctx"),
            P("groups", ("vocab", "ctx", "dp")),
            P("groups"),
        ),
        check_vma=False,
    )
```

time: 105 us -> 100 us (0.952)
  other arithmetic: 5.39 us -> 0.87 us
  local copies, waits for them, and re-layouts: 15.3 us -> 11.4 us
  starting transfers between devices: 25.3 us -> 28.7 us
    ppermute x20 -> x23, starting transfers between devices: 20 us -> 25.7 us  [the longest x13 19.3 us: shards(): along = lambda a, by: lax.ppermute(a, 'vocab', by)]
    ppermute x4, waiting for transfers between devices: 2.97 us -> 6.85 us  [shards(): lax.ppermute(c, 'ctx', ring(n_ctx, -t))]
    dynamic_slice x4 -> x0, local copies, waits for them, and re-layouts: 3.43 us -> none  [the longest x2 2.53 us: shards(): mine = lambda a: lax.dynamic_index_in_dim(a, me_dp, 0, keepdims=False)]
    ppermute x20 -> x23, waiting for transfers between devices: 25.6 us -> 22.7 us  [the longest x13 17.3 us: shards(): along = lambda a, by: lax.ppermute(a, 'vocab', by)]
    pallas_call x3, Pallas kernels: 8.77 us -> 6.21 us  [spread_call(): pl.pallas_call(functools.partial(spread_kernel, part), out_shape=out_shap...]
    ppermute x4, starting transfers between devices: 5.27 us -> 2.95 us  [shards(): lax.ppermute(c, 'ctx', ring(n_ctx, -t))]
    convert_element_type x4 -> x0, other arithmetic: 2.02 us -> none  [the longest x3 1.12 us: shards(): leaving = together(before, arrived).astype(BF16)]
    pallas_call x3 -> x4, Pallas kernels: 9.89 us -> 11.4 us  [logits_call(): pl.pallas_call(functools.partial(logits_kernel, kernel_plan, columns, par...]
  transfers between devices with their start and end apart: 24 -> 27, of which waited for: 10 -> 15; matrix products, arithmetic and copies ran while one was open for 15% -> 2% of each run, Pallas kernels for 24% -> 27%
where the time goes in v4:
time: 100 us; the launch traced here: 98.5 us
  waiting for transfers between devices  29.5 us (30%)
  starting transfers between devices  28.7 us (29%)
  Pallas kernels  27 us (27%)
  local copies, waits for them, and re-layouts  11.4 us (11%)
  between operations  1.05 us (1%)
    ppermute x13, starting transfers between devices, shards(): along = lambda a, by: lax.ppermute(a, 'vocab', by)  19.3 us
    ppermute x13, waiting for transfers between devices, shards(): along = lambda a, by: lax.ppermute(a, 'vocab', by)  17.3 us
    pallas_call x4, Pallas kernels, logits_call(): pl.pallas_call(functools.partial(logits_kernel, kernel_plan, columns, par...  11.4 us
    unnamed x31, local copies, waits for them, and re-layouts  10.7 us
    ppermute x4, waiting for transfers between devices, shards(): lax.ppermute(c, 'ctx', ring(n_ctx, -t))  6.85 us
    pallas_call x3, Pallas kernels, spread_call(): pl.pallas_call(functools.partial(spread_kernel, part), out_shape=out_shap...  6.21 us
    ppermute x5, starting transfers between devices, shards(): cross = lambda a: [lax.ppermute(a, 'ctx', ring(n_ctx, t)) for t in beyond]  5.74 us
    pallas_call x1, Pallas kernels, head_call(): pl.pallas_call(functools.partial(head_kernel, list(near), [keys for keys,...  5.53 us
  transfers between devices with their start and end apart: 27, of which 15 were waited for; matrix products, arithmetic and copies ran while one was open for 2% of the time, Pallas kernels for 27%

profile of v4, /device:TPU:0, one launch (start us, length us, event | category | flops | bytes accessed | tf_op | source)
XLA Modules:
  0.0 98.5 jit_solution(14732847248062254280)
XLA Ops:
  0.6 0.5 collective-permute-start
  1.2 0.7 collective-permute-start.3
  1.8 5.5 %collective-permute-start.2 = (bf16[128,1024]{1,0:T(8,128)(2,1)}, bf16[128,1024]{1,0:T(8,128)(2,1)S(1)}, u32[]{:S(2)}, u32[]{:S(2)}) collective-permute-start(bf16[128,1024]{1,0:T(8,128)(2,1)} %bitcast.70), channel_id=1, source_target_pairs={{0,4},{4,0},{8,12},{12,8},{1,5},{5,1},{9,13},{13,9},{2,6},{6,2},{1... | collective-permute-start | bytes 786440 | tf_op jit(solution)/shard_map/ppermute | solution.py:306
  7.3 1.5 %collective-permute-start.1 = (bf16[128,1024]{1,0:T(8,128)(2,1)}, bf16[128,1024]{1,0:T(8,128)(2,1)S(1)}, u32[]{:S(2)}, u32[]{:S(2)}) collective-permute-start(bf16[128,1024]{1,0:T(8,128)(2,1)} %bitcast.71), channel_id=1, source_target_pairs={{0,2},{2,0},{1,3},{3,1},{4,6},{6,4},{5,7},{7,5},{8,10},{10,8},{9,1... | collective-permute-start | bytes 786440 | tf_op jit(solution)/shard_map/ppermute | solution.py:325
  8.8 0.1 stack.84.meta
  8.9 1.0 constant_dynamic-update-slice_fusion
  9.9 4.3 %collective-permute-done.2.refs_1_.refs_4_ = bf16[128,1024]{1,0:T(8,128)(2,1)S(1)} collective-permute-done((bf16[128,1024]{1,0:T(8,128)(2,1)}, bf16[128,1024]{1,0:T(8,128)(2,1)S(1)}, u32[]{:S(2)}, u32[]{:S(2)}) %collective-permute-start.2) | collective-permute-done | bytes 262176 | tf_op jit(solution)/shard_map/ppermute | solution.py:306
  14.2 1.5 %collective-permute-done.1.refs_2_.refs_3_ = bf16[128,1024]{1,0:T(8,128)(2,1)S(1)} collective-permute-done((bf16[128,1024]{1,0:T(8,128)(2,1)}, bf16[128,1024]{1,0:T(8,128)(2,1)S(1)}, u32[]{:S(2)}, u32[]{:S(2)}) %collective-permute-start.1) | collective-permute-done | bytes 262176 | tf_op jit(solution)/shard_map/ppermute | solution.py:325
  15.7 0.7 collective-permute-start.6
  16.3 1.6 %collective-permute-start.4 = (bf16[128,1024]{1,0:T(8,128)(2,1)S(1)}, bf16[128,1024]{1,0:T(8,128)(2,1)S(1)}, u32[]{:S(2)}, u32[]{:S(2)}) collective-permute-start(bf16[128,1024]{1,0:T(8,128)(2,1)S(1)} %collective-permute-done.2.refs_1_.refs_4_), channel_id=1, source_target_pairs={{0,2},{2,0},{1,3},{3,1},{4,6},{6,4},{5,7},{7,5},{8,10},{10,8},{9,1... | collective-permute-start | bytes 786440 | tf_op jit(solution)/shard_map/ppermute | solution.py:325
  17.9 1.3 %collective-permute-start.5 = (bf16[128,1024]{1,0:T(8,128)(2,1)S(1)}, bf16[128,1024]{1,0:T(8,128)(2,1)S(1)}, u32[]{:S(2)}, u32[]{:S(2)}) collective-permute-start(bf16[128,1024]{1,0:T(8,128)(2,1)S(1)} %collective-permute-done.3), channel_id=1, source_target_pairs={{4,0},{8,12},{5,1},{9,13},{6,2},{10,14},{7,3},{11,15},{20,16},{24,... | collective-permute-start | bytes 786440 | tf_op jit(solution)/shard_map/ppermute | solution.py:306
  19.3 2.2 %copy-done = bf16[4096,512]{1,0:T(8,128)(2,1)S(1)} copy-done((bf16[4096,512]{1,0:T(8,128)(2,1)S(1)}, bf16[4096,512]{1,0:T(8,128)(2,1)}, u32[]{:S(2)}) %copy-start) | copy-done | bytes 4194328
  21.4 3.0 %shard_map.94 = (f32[128,1024]{1,0:T(8,128)S(1)}, f32[128,1024]{1,0:T(8,128)S(1)}) custom-call(s32[6]{0:T(128)S(1)} %stack.84.meta, bf16[4096,512]{1,0:T(8,128)(2,1)S(1)} %copy-done, bf16[4096,512]{1,0:T(8,128)(2,1)} %collective-permute-done.w_far, bf16[128,1024]{1,0:T(8,128)(2,1)S(1)} %bitcast.73, ...), custom_call_target="tpu_custom_call" | custom-call | flops 805306368 | bytes 4194304 | tf_op jit(solution)/shard_map/pallas_call | solution.py:109
  24.5 2.3 %collective-permute-done.5 = bf16[128,1024]{1,0:T(8,128)(2,1)S(1)} collective-permute-done((bf16[128,1024]{1,0:T(8,128)(2,1)S(1)}, bf16[128,1024]{1,0:T(8,128)(2,1)S(1)}, u32[]{:S(2)}, u32[]{:S(2)}) %collective-permute-start.5) | collective-permute-done | bytes 262176 | tf_op jit(solution)/shard_map/ppermute | solution.py:306
  26.9 0.6 collective-permute-start.7
  27.5 1.3 %collective-permute-start.8 = (bf16[128,1024]{1,0:T(8,128)(2,1)S(1)}, bf16[128,1024]{1,0:T(8,128)(2,1)S(1)}, u32[]{:S(2)}, u32[]{:S(2)}) collective-permute-start(bf16[128,1024]{1,0:T(8,128)(2,1)S(1)} %collective-permute-done.6), channel_id=1, source_target_pairs={{4,0},{8,12},{5,1},{9,13},{6,2},{10,14},{7,3},{11,15},{20,16},{24,... | collective-permute-start | bytes 786440 | tf_op jit(solution)/shard_map/ppermute | solution.py:306
  28.8 0.1 select_reduce_fusion
  28.9 2.8 %shard_map.95 = (f32[128,1024]{1,0:T(8,128)S(1)}, f32[128,1024]{1,0:T(8,128)S(1)}) custom-call(s32[6]{0:T(128)S(1)} %stack.84.meta, bf16[4096,512]{1,0:T(8,128)(2,1)S(1)} %copy-done, bf16[4096,512]{1,0:T(8,128)(2,1)} %collective-permute-done.w_far, bf16[128,1024]{1,0:T(8,128)(2,1)S(1)} %get-tuple-element.110.refs_0_.refs_6_, ...), custom_call_target="tpu_custom_call" | custom-call | flops 536870912 | bytes 4194304 | tf_op jit(solution)/shard_map/pallas_call | solution.py:109
  31.7 0.8 copy-done.5
  32.5 0.8 collective-permute-done.7.refs_1_.refs_7_
  33.3 2.4 %collective-permute-done.8 = bf16[128,1024]{1,0:T(8,128)(2,1)S(1)} collective-permute-done((bf16[128,1024]{1,0:T(8,128)(2,1)S(1)}, bf16[128,1024]{1,0:T(8,128)(2,1)S(1)}, u32[]{:S(2)}, u32[]{:S(2)}) %collective-permute-start.8) | collective-permute-done | bytes 262176 | tf_op jit(solution)/shard_map/ppermute | solution.py:306
  35.8 1.2 %copy-done.11 = bf16[7,128,1024]{2,1,0:T(8,128)(2,1)} copy-done((bf16[7,128,1024]{2,1,0:T(8,128)(2,1)}, bf16[7,128,1024]{2,1,0:T(8,128)(2,1)S(1)}, u32[]{:S(2)}) %copy-start.11) | copy-done | bytes 1835032
  37.1 1.5 %collective-permute-start.9 = (bf16[128,1024]{1,0:T(8,128)(2,1)S(1)}, bf16[128,1024]{1,0:T(8,128)(2,1)S(1)}, u32[]{:S(2)}, u32[]{:S(2)}) collective-permute-start(bf16[128,1024]{1,0:T(8,128)(2,1)S(1)} %get-tuple-element.108.refs_0_.refs_8_), channel_id=1, source_target_pairs={{0,2},{2,0},{1,3},{3,1},{4,6},{6,4},{5,7},{7,5},{8,10},{10,8},{9,1... | collective-permute-start | bytes 786440 | tf_op jit(solution)/shard_map/ppermute | solution.py:325
  38.6 0.1 add.124
  38.7 0.1 add.121
  38.8 0.1 copy.14.refs_4_
  38.9 0.1 copy.15.refs_2_
  39.1 2.2 %copy-done.1 = bf16[4096,512]{1,0:T(8,128)(2,1)S(1)} copy-done((bf16[4096,512]{1,0:T(8,128)(2,1)S(1)}, bf16[4096,512]{1,0:T(8,128)(2,1)}, u32[]{:S(2)}) %copy-start.1) | copy-done | bytes 4194328
  41.3 1.0 %copy-done.6 = f32[128,1024]{1,0:T(8,128)S(1)} copy-done((f32[128,1024]{1,0:T(8,128)S(1)}, f32[128,1024]{1,0:T(8,128)}, u32[]{:S(2)}) %copy-start.6) | copy-done | bytes 524312
  42.3 3.0 %shard_map.96 = (f32[128,1024]{1,0:T(8,128)S(1)}, f32[8,128]{1,0:T(8,128)S(1)}, f32[128,1024]{1,0:T(8,128)S(1)}) custom-call(s32[6]{0:T(128)S(1)} %stack.84.meta, bf16[4096,512]{1,0:T(8,128)(2,1)S(1)} %copy-done.1, bf16[4096,512]{1,0:T(8,128)(2,1)} %collective-permute-done.w_far, bf16[128,1024]{1,0:T(8,128)(2,1)S(1)} %get-tuple-element.108.refs_0_.refs_8_, ...), custom_call_target="tpu_custom_call" | custom-call | flops 536870912 | bytes 4194304 | tf_op jit(solution)/shard_map/pallas_call | solution.py:109
  45.4 2.6 %shard_map.97 = (f32[128,1024]{1,0:T(8,128)S(1)}, f32[8,128]{1,0:T(8,128)S(1)}) custom-call(s32[6]{0:T(128)S(1)} %stack.84.meta, bf16[4096,512]{1,0:T(8,128)(2,1)S(1)} %copy-done.1, bf16[4096,512]{1,0:T(8,128)(2,1)} %collective-permute-done.w_far, bf16[128,1024]{1,0:T(8,128)(2,1)S(1)} %collective-permute-done.9.refs_0_.refs_9_, ...), custom_call_target="tpu_custom_call" | custom-call | flops 268435456 | bytes 2097152 | tf_op jit(solution)/shard_map/pallas_call | solution.py:109
  48.0 0.6 collective-permute-start.10
  48.6 0.1 stack.81.meta
  48.7 3.0 %collective-permute-done.10 = f32[2,8,128]{2,1,0:T(8,128)S(1)} collective-permute-done((f32[2,8,128]{2,1,0:T(8,128)S(1)}, f32[2,8,128]{2,1,0:T(8,128)S(1)}, u32[]{:S(2)}, u32[]{:S(2)}) %collective-permute-start.10) | collective-permute-done | bytes 8224 | tf_op jit(solution)/shard_map/ppermute | solution.py:325
  51.8 2.2 %collective-permute-start.13 = (f32[8,256]{1,0:T(8,128)S(1)}, f32[8,256]{1,0:T(8,128)S(1)}, u32[]{:S(2)}, u32[]{:S(2)}) collective-permute-start(f32[8,256]{1,0:T(8,128)S(1)} %pad_maximum_fusion.1.refs_3_), channel_id=1, source_target_pairs={{0,12},{4,0},{8,4},{12,8},{1,13},{5,1},{9,5},{13,9},{2,14},{6,2},{... | collective-permute-start | bytes 24584 | tf_op jit(solution)/shard_map/ppermute | solution.py:306
  54.0 0.6 collective-permute-start.11
  54.7 0.1 copy.16.refs_2_
  54.8 0.7 collective-permute-done.13.refs_6_
  55.5 3.1 %collective-permute-done.12.refs_5_ = f32[8,256]{1,0:T(8,128)S(1)} collective-permute-done((f32[8,256]{1,0:T(8,128)S(1)}, f32[8,256]{1,0:T(8,128)S(1)}, u32[]{:S(2)}, u32[]{:S(2)}) %collective-permute-start.12) | collective-permute-done | bytes 8224 | tf_op jit(solution)/shard_map/ppermute | solution.py:306
  58.6 0.9 collective-permute-done.11.refs_4_
  59.5 2.2 %copy-done.2 = bf16[4096,512]{1,0:T(8,128)(2,1)S(1)} copy-done((bf16[4096,512]{1,0:T(8,128)(2,1)S(1)}, bf16[4096,512]{1,0:T(8,128)(2,1)}, u32[]{:S(2)}) %copy-start.2) | copy-done | bytes 4194328
  61.7 2.6 %shard_map.98 = (bf16[2,128,512]{2,1,0:T(8,128)(2,1)S(1)}, bf16[2,128,512]{2,1,0:T(8,128)(2,1)S(1)}, bf16[512,256]{1,0:T(8,128)(2,1)S(1)}, bf16[512,256]{1,0:T(8...) custom-call(s32[5]{0:T(128)S(1)} %stack.81.meta, s32[2]{0:T(128)S(1)} %copy-done.9, ...), custom_call_target="tpu_custom_call" | custom-call | flops 536870912 | bytes 4194304 | tf_op jit(solution)/shard_map/pallas_call | solution.py:202
  64.3 0.6 collective-permute-start.14
  64.9 2.2 %shard_map.100 = (f32[1024,128]{1,0:T(8,128)S(1)}, bf16[1024,128]{1,0:T(8,128)(2,1)S(1)}) custom-call(s32[1]{0:T(128)} %bitcast.10.meta, bf16[4096,512]{1,0:T(8,128)(2,1)S(1)} %copy-done.2, bf16[4096,512]{1,0:T(8,128)(2,1)} %collective-permute-done.w_far, bf16[512,256]{1,0:T(8,128)(2,1)S(1)} %get-tuple-element.80.flipped_own, ...), custom_call_target="tpu_custom_call" | custom-call | flops 536870912 | bytes 2097152 | tf_op jit(solution)/shard_map/pallas_call | solution.py:216
  67.1 3.7 %collective-permute-done.14.refs_0_ = bf16[1024,128]{1,0:T(8,128)(2,1)S(1)} collective-permute-done((bf16[1024,128]{1,0:T(8,128)(2,1)S(1)}, bf16[1024,128]{1,0:T(8,128)(2,1)S(1)}, u32[]{:S(2)}, u32[]{:S(2)}) %collective-permute-start.14) | collective-permute-done | bytes 262176 | tf_op jit(solution)/shard_map/ppermute | solution.py:404
  70.8 1.3 %collective-permute-start.16 = (bf16[1024,128]{1,0:T(8,128)(2,1)S(1)}, bf16[1024,128]{1,0:T(8,128)(2,1)S(1)}, u32[]{:S(2)}, u32[]{:S(2)}) collective-permute-start(bf16[1024,128]{1,0:T(8,128)(2,1)S(1)} %shard_map.101), channel_id=1, source_target_pairs={{0,4},{12,8},{1,5},{13,9},{2,6},{14,10},{3,7},{15,11},{16,20},{28,... | collective-permute-start | bytes 786440 | tf_op jit(solution)/shard_map/ppermute | solution.py:306
  72.1 0.6 collective-permute-start.15
  72.7 2.0 %shard_map.102 = (f32[1024,128]{1,0:T(8,128)S(1)}, bf16[1024,128]{1,0:T(8,128)(2,1)S(1)}) custom-call(s32[1]{0:T(128)} %bitcast.9.meta, bf16[4096,512]{1,0:T(8,128)(2,1)S(1)} %copy-done.3, bf16[4096,512]{1,0:T(8,128)(2,1)} %collective-permute-done.w_far, bf16[512,256]{1,0:T(8,128)(2,1)S(1)} %get-tuple-element.80.flipped_own, ...), custom_call_target="tpu_custom_call" | custom-call | flops 536870912 | bytes 2097152 | tf_op jit(solution)/shard_map/pallas_call | solution.py:216
  74.8 1.2 %collective-permute-done.16.refs_1_ = bf16[1024,128]{1,0:T(8,128)(2,1)S(1)} collective-permute-done((bf16[1024,128]{1,0:T(8,128)(2,1)S(1)}, bf16[1024,128]{1,0:T(8,128)(2,1)S(1)}, u32[]{:S(2)}, u32[]{:S(2)}) %collective-permute-start.16) | collective-permute-done | bytes 262176 | tf_op jit(solution)/shard_map/ppermute | solution.py:306
  76.0 2.6 %collective-permute-done.15.refs_0_ = bf16[1024,128]{1,0:T(8,128)(2,1)S(1)} collective-permute-done((bf16[1024,128]{1,0:T(8,128)(2,1)S(1)}, bf16[1024,128]{1,0:T(8,128)(2,1)S(1)}, u32[]{:S(2)}, u32[]{:S(2)}) %collective-permute-start.15) | collective-permute-done | bytes 262176 | tf_op jit(solution)/shard_map/ppermute | solution.py:404
  78.6 1.8 %collective-permute-start.18 = (bf16[1024,128]{1,0:T(8,128)(2,1)S(1)}, bf16[1024,128]{1,0:T(8,128)(2,1)S(1)}, u32[]{:S(2)}, u32[]{:S(2)}) collective-permute-start(bf16[1024,128]{1,0:T(8,128)(2,1)S(1)} %shard_map.103), channel_id=1, source_target_pairs={{0,4},{12,8},{1,5},{13,9},{2,6},{14,10},{3,7},{15,11},{16,20},{28,... | collective-permute-start | bytes 786440 | tf_op jit(solution)/shard_map/ppermute | solution.py:306
  80.5 0.6 collective-permute-start.17
  81.1 0.1 shard_map.104
  81.1 0.7 collective-permute-start.19
  81.9 2.4 %collective-permute-done.18.refs_1_ = bf16[1024,128]{1,0:T(8,128)(2,1)S(1)} collective-permute-done((bf16[1024,128]{1,0:T(8,128)(2,1)S(1)}, bf16[1024,128]{1,0:T(8,128)(2,1)S(1)}, u32[]{:S(2)}, u32[]{:S(2)}) %collective-permute-start.18) | collective-permute-done | bytes 262176 | tf_op jit(solution)/shard_map/ppermute | solution.py:306
  84.3 2.0 %shard_map.99 = (f32[1024,128]{1,0:T(8,128)S(1)}, bf16[1024,128]{1,0:T(8,128)(2,1)S(1)}) custom-call(s32[1]{0:T(128)} %bitcast.meta, bf16[4096,512]{1,0:T(8,128)(2,1)S(1)} %copy-done.3, bf16[4096,512]{1,0:T(8,128)(2,1)} %collective-permute-done.w_far, bf16[512,256]{1,0:T(8,128)(2,1)S(1)} %get-tuple-element.80.flipped_own, ...), custom_call_target="tpu_custom_call" | custom-call | flops 536870912 | bytes 2097152 | tf_op jit(solution)/shard_map/pallas_call | solution.py:216
  86.3 0.5 collective-permute-done.17.refs_0_
  87.0 0.1 shard_map.105
  87.1 2.5 %collective-permute-start.21 = (bf16[1024,128]{1,0:T(8,128)(2,1)S(1)}, bf16[1024,128]{1,0:T(8,128)(2,1)S(1)}, u32[]{:S(2)}, u32[]{:S(2)}) collective-permute-start(bf16[1024,128]{1,0:T(8,128)(2,1)S(1)} %shard_map.105), channel_id=1, source_target_pairs={{0,4},{4,0},{8,12},{12,8},{1,5},{5,1},{9,13},{13,9},{2,6},{6,2},{1... | collective-permute-start | bytes 786440 | tf_op jit(solution)/shard_map/ppermute | solution.py:306
  89.7 1.1 %collective-permute-start.20 = (bf16[1024,128]{1,0:T(8,128)(2,1)S(1)}, bf16[1024,128]{1,0:T(8,128)(2,1)S(1)}, u32[]{:S(2)}, u32[]{:S(2)}) collective-permute-start(bf16[1024,128]{1,0:T(8,128)(2,1)S(1)} %get-tuple-element.94), channel_id=1, source_target_pairs={{0,2},{2,0},{1,3},{3,1},{4,6},{6,4},{5,7},{7,5},{8,10},{10,8},{9,1... | collective-permute-start | bytes 786440 | tf_op jit(solution)/shard_map/ppermute | solution.py:404
  90.8 0.7 collective-permute-start.22
  91.5 0.5 bitcast_select_fusion
  92.0 5.5 %shard_map.107 = bf16[4096,512]{1,0:T(8,128)(2,1)} custom-call(s32[6]{0:T(128)S(1)} %stack.84.meta, bf16[2,128,512]{2,1,0:T(8,128)(2,1)S(1)} %get-tuple-element.99.refs_0_, bf16[2,128,512]{2,1,0:T(8,128)(2,1)S(1)} %collective-permute-done.23.refs_1_, bf16[128,1024]{1,0:T(8,128)(2,1)S(1)} %bitcast.74, ...), custom_call_target="tpu_custom_call" | custom-call | flops 2147483648 | bytes 8388608 | tf_op jit(solution)/shard_map/pallas_call | solution.py:274
  97.6 0.9 shard_map.108
  (54 shorter events, 0.9 us)
Async XLA Ops:
  0.6 18.6 %copy-start.4 = (bf16[1024,1,2,64]{0,3,2,1:T(8,128)(2,1)S(1)}, bf16[1024,1,2,64]{0,3,2,1:T(8,128)(2,1)}, u32[]{:S(2)}) copy-start(bf16[1024,1,2,64]{0,3,2,1:T(8,128)(2,1)} %param.7) | copy-start | bytes 786436
  0.6 18.6 %collective-permute-start = (bf16[4096,512]{1,0:T(8,128)(2,1)}, bf16[4096,512]{1,0:T(8,128)(2,1)}, u32[]{:S(2)}, u32[]{:S(2)}) collective-permute-start(bf16[4096,512]{1,0:T(8,128)(2,1)} %w_own.15), channel_id=1, source_target_pairs={{0,1},{1,0},{2,3},{3,2},{4,5},{5,4},{6,7},{7,6},{8,9},{9,8},{10,11... | collective-permute-start | bytes 12582920 | tf_op jit(solution)/shard_map/ppermute | solution.py:305
  1.2 8.7 %collective-permute-start.3 = (bf16[128,1024]{1,0:T(8,128)(2,1)}, bf16[128,1024]{1,0:T(8,128)(2,1)S(1)}, u32[]{:S(2)}, u32[]{:S(2)}) collective-permute-start(bf16[128,1024]{1,0:T(8,128)(2,1)} %bitcast.69), channel_id=1, source_target_pairs={{4,8},{8,4},{5,9},{9,5},{6,10},{10,6},{7,11},{11,7},{20,24},{24,20... | collective-permute-start | bytes 786440 | tf_op jit(solution)/shard_map/ppermute | solution.py:306
  1.8 12.4 %collective-permute-start.2 = (bf16[128,1024]{1,0:T(8,128)(2,1)}, bf16[128,1024]{1,0:T(8,128)(2,1)S(1)}, u32[]{:S(2)}, u32[]{:S(2)}) collective-permute-start(bf16[128,1024]{1,0:T(8,128)(2,1)} %bitcast.70), channel_id=1, source_target_pairs={{0,4},{4,0},{8,12},{12,8},{1,5},{5,1},{9,13},{13,9},{2,6},{6,2},{1... | collective-permute-start | bytes 786440 | tf_op jit(solution)/shard_map/ppermute | solution.py:306
  7.3 8.3 %collective-permute-start.1 = (bf16[128,1024]{1,0:T(8,128)(2,1)}, bf16[128,1024]{1,0:T(8,128)(2,1)S(1)}, u32[]{:S(2)}, u32[]{:S(2)}) collective-permute-start(bf16[128,1024]{1,0:T(8,128)(2,1)} %bitcast.71), channel_id=1, source_target_pairs={{0,2},{2,0},{1,3},{3,1},{4,6},{6,4},{5,7},{7,5},{8,10},{10,8},{9,1... | collective-permute-start | bytes 786440 | tf_op jit(solution)/shard_map/ppermute | solution.py:325
  15.7 11.1 %collective-permute-start.6 = (bf16[128,1024]{1,0:T(8,128)(2,1)S(1)}, bf16[128,1024]{1,0:T(8,128)(2,1)S(1)}, u32[]{:S(2)}, u32[]{:S(2)}) collective-permute-start(bf16[128,1024]{1,0:T(8,128)(2,1)S(1)} %collective-permute-done.2.refs_1_.refs_4_), channel_id=1, source_target_pairs={{4,8},{8,4},{5,9},{9,5},{6,10},{10,6},{7,11},{11,7},{20,24},{24,20... | collective-permute-start | bytes 786440 | tf_op jit(solution)/shard_map/ppermute | solution.py:306
  16.3 10.4 %collective-permute-start.4 = (bf16[128,1024]{1,0:T(8,128)(2,1)S(1)}, bf16[128,1024]{1,0:T(8,128)(2,1)S(1)}, u32[]{:S(2)}, u32[]{:S(2)}) collective-permute-start(bf16[128,1024]{1,0:T(8,128)(2,1)S(1)} %collective-permute-done.2.refs_1_.refs_4_), channel_id=1, source_target_pairs={{0,2},{2,0},{1,3},{3,1},{4,6},{6,4},{5,7},{7,5},{8,10},{10,8},{9,1... | collective-permute-start | bytes 786440 | tf_op jit(solution)/shard_map/ppermute | solution.py:325
  17.9 8.9 %collective-permute-start.5 = (bf16[128,1024]{1,0:T(8,128)(2,1)S(1)}, bf16[128,1024]{1,0:T(8,128)(2,1)S(1)}, u32[]{:S(2)}, u32[]{:S(2)}) collective-permute-start(bf16[128,1024]{1,0:T(8,128)(2,1)S(1)} %collective-permute-done.3), channel_id=1, source_target_pairs={{4,0},{8,12},{5,1},{9,13},{6,2},{10,14},{7,3},{11,15},{20,16},{24,... | collective-permute-start | bytes 786440 | tf_op jit(solution)/shard_map/ppermute | solution.py:306
  19.2 2.2 %copy-start = (bf16[4096,512]{1,0:T(8,128)(2,1)S(1)}, bf16[4096,512]{1,0:T(8,128)(2,1)}, u32[]{:S(2)}) copy-start(bf16[4096,512]{1,0:T(8,128)(2,1)} %w_own.15) | copy-start | bytes 12582916
  21.4 7.3 %copy-start.12 = (s32[2,2,128]{2,1,0:T(2,128)S(1)}, s32[2,2,128]{2,1,0:T(2,128)}, u32[]{:S(2)}) copy-start(s32[2,2,128]{2,1,0:T(2,128)} %param.9) | copy-start | bytes 6148
  26.9 6.4 %collective-permute-start.7 = (bf16[128,1024]{1,0:T(8,128)(2,1)S(1)}, bf16[128,1024]{1,0:T(8,128)(2,1)S(1)}, u32[]{:S(2)}, u32[]{:S(2)}) collective-permute-start(bf16[128,1024]{1,0:T(8,128)(2,1)S(1)} %get-tuple-element.110.refs_0_.refs_6_), channel_id=1, source_target_pairs={{0,2},{2,0},{1,3},{3,1},{4,6},{6,4},{5,7},{7,5},{8,10},{10,8},{9,1... | collective-permute-start | bytes 786440 | tf_op jit(solution)/shard_map/ppermute | solution.py:325
  27.5 8.3 %collective-permute-start.8 = (bf16[128,1024]{1,0:T(8,128)(2,1)S(1)}, bf16[128,1024]{1,0:T(8,128)(2,1)S(1)}, u32[]{:S(2)}, u32[]{:S(2)}) collective-permute-start(bf16[128,1024]{1,0:T(8,128)(2,1)S(1)} %collective-permute-done.6), channel_id=1, source_target_pairs={{4,0},{8,12},{5,1},{9,13},{6,2},{10,14},{7,3},{11,15},{20,16},{24,... | collective-permute-start | bytes 786440 | tf_op jit(solution)/shard_map/ppermute | solution.py:306
  31.7 0.8 copy-start.5
  35.8 1.2 %copy-start.11 = (bf16[7,128,1024]{2,1,0:T(8,128)(2,1)}, bf16[7,128,1024]{2,1,0:T(8,128)(2,1)S(1)}, u32[]{:S(2)}) copy-start(bf16[7,128,1024]{2,1,0:T(8,128)(2,1)S(1)} %get-tuple-element.107) | copy-start | bytes 5505028
  37.1 8.3 %collective-permute-start.9 = (bf16[128,1024]{1,0:T(8,128)(2,1)S(1)}, bf16[128,1024]{1,0:T(8,128)(2,1)S(1)}, u32[]{:S(2)}, u32[]{:S(2)}) collective-permute-start(bf16[128,1024]{1,0:T(8,128)(2,1)S(1)} %get-tuple-element.108.refs_0_.refs_8_), channel_id=1, source_target_pairs={{0,2},{2,0},{1,3},{3,1},{4,6},{6,4},{5,7},{7,5},{8,10},{10,8},{9,1... | collective-permute-start | bytes 786440 | tf_op jit(solution)/shard_map/ppermute | solution.py:325
  39.0 53.0 %collective-permute-start.24 = (bf16[7,128,1024]{2,1,0:T(8,128)(2,1)}, bf16[7,128,1024]{2,1,0:T(8,128)(2,1)}, u32[]{:S(2)}, u32[]{:S(2)}) collective-permute-start(bf16[7,128,1024]{2,1,0:T(8,128)(2,1)} %copy-done.11), channel_id=1, source_target_pairs={{0,1},{1,0},{2,3},{3,2},{4,5},{5,4},{6,7},{7,6},{8,9},{9,8},{10,11... | collective-permute-start | bytes 5505032 | tf_op jit(solution)/shard_map/ppermute | solution.py:305
  39.1 2.2 %copy-start.1 = (bf16[4096,512]{1,0:T(8,128)(2,1)S(1)}, bf16[4096,512]{1,0:T(8,128)(2,1)}, u32[]{:S(2)}) copy-start(bf16[4096,512]{1,0:T(8,128)(2,1)} %w_own.15) | copy-start | bytes 12582916
  41.3 1.0 %copy-start.6 = (f32[128,1024]{1,0:T(8,128)S(1)}, f32[128,1024]{1,0:T(8,128)}, u32[]{:S(2)}) copy-start(f32[128,1024]{1,0:T(8,128)} %copy-done.5) | copy-start | bytes 1572868
  45.4 14.1 %copy-start.7 = (f32[2,2]{1,0:T(2,128)S(1)}, f32[2,2]{1,0:T(2,128)}, u32[]{:S(2)}) copy-start(f32[2,2]{1,0:T(2,128)} %sums.1) | copy-start | bytes 52
  45.4 14.1 %copy-start.8 = (f32[2,2]{1,0:T(2,128)S(1)}, f32[2,2]{1,0:T(2,128)}, u32[]{:S(2)}) copy-start(f32[2,2]{1,0:T(2,128)} %refer.1) | copy-start | bytes 52
  45.4 14.1 %copy-start.9 = (s32[2]{0:T(128)S(1)}, s32[2]{0:T(128)}, u32[]{:S(2)}) copy-start(s32[2]{0:T(128)} %start.1) | copy-start | bytes 28
  45.4 14.1 %copy-start.10 = (f32[2]{0:T(128)S(1)}, f32[2]{0:T(128)}, u32[]{:S(2)}) copy-start(f32[2]{0:T(128)} %cotangent.1) | copy-start | bytes 28
  48.0 3.7 %collective-permute-start.10 = (f32[2,8,128]{2,1,0:T(8,128)S(1)}, f32[2,8,128]{2,1,0:T(8,128)S(1)}, u32[]{:S(2)}, u32[]{:S(2)}) collective-permute-start(f32[2,8,128]{2,1,0:T(8,128)S(1)} %pad_maximum_fusion), channel_id=1, source_target_pairs={{0,2},{2,0},{1,3},{3,1},{4,6},{6,4},{5,7},{7,5},{8,10},{10,8},{9,1... | collective-permute-start | bytes 24584 | tf_op jit(solution)/shard_map/ppermute | solution.py:325
  51.8 3.7 %collective-permute-start.13 = (f32[8,256]{1,0:T(8,128)S(1)}, f32[8,256]{1,0:T(8,128)S(1)}, u32[]{:S(2)}, u32[]{:S(2)}) collective-permute-start(f32[8,256]{1,0:T(8,128)S(1)} %pad_maximum_fusion.1.refs_3_), channel_id=1, source_target_pairs={{0,12},{4,0},{8,4},{12,8},{1,13},{5,1},{9,5},{13,9},{2,14},{6,2},{... | collective-permute-start | bytes 24584 | tf_op jit(solution)/shard_map/ppermute | solution.py:306
  54.0 4.5 %collective-permute-start.12 = (f32[8,256]{1,0:T(8,128)S(1)}, f32[8,256]{1,0:T(8,128)S(1)}, u32[]{:S(2)}, u32[]{:S(2)}) collective-permute-start(f32[8,256]{1,0:T(8,128)S(1)} %pad_maximum_fusion.1.refs_3_), channel_id=1, source_target_pairs={{0,8},{4,12},{8,0},{12,4},{1,9},{5,13},{9,1},{13,5},{2,10},{6,14},... | collective-permute-start | bytes 24584 | tf_op jit(solution)/shard_map/ppermute | solution.py:306
  54.0 5.4 %collective-permute-start.11 = (f32[8,256]{1,0:T(8,128)S(1)}, f32[8,256]{1,0:T(8,128)S(1)}, u32[]{:S(2)}, u32[]{:S(2)}) collective-permute-start(f32[8,256]{1,0:T(8,128)S(1)} %pad_maximum_fusion.1.refs_3_), channel_id=1, source_target_pairs={{0,4},{4,8},{8,12},{12,0},{1,5},{5,9},{9,13},{13,1},{2,6},{6,10},{... | collective-permute-start | bytes 24584 | tf_op jit(solution)/shard_map/ppermute | solution.py:306
  59.5 2.2 %copy-start.2 = (bf16[4096,512]{1,0:T(8,128)(2,1)S(1)}, bf16[4096,512]{1,0:T(8,128)(2,1)}, u32[]{:S(2)}) copy-start(bf16[4096,512]{1,0:T(8,128)(2,1)} %w_own.15) | copy-start | bytes 12582916
  64.3 6.4 %collective-permute-start.14 = (bf16[1024,128]{1,0:T(8,128)(2,1)S(1)}, bf16[1024,128]{1,0:T(8,128)(2,1)S(1)}, u32[]{:S(2)}, u32[]{:S(2)}) collective-permute-start(bf16[1024,128]{1,0:T(8,128)(2,1)S(1)} %get-tuple-element.83), channel_id=1, source_target_pairs={{0,2},{2,0},{1,3},{3,1},{4,6},{6,4},{5,7},{7,5},{8,10},{10,8},{9,1... | collective-permute-start | bytes 786440 | tf_op jit(solution)/shard_map/ppermute | solution.py:404
  64.9 7.8 %copy-start.3 = (bf16[4096,512]{1,0:T(8,128)(2,1)S(1)}, bf16[4096,512]{1,0:T(8,128)(2,1)}, u32[]{:S(2)}) copy-start(bf16[4096,512]{1,0:T(8,128)(2,1)} %w_own.15) | copy-start | bytes 12582916
  70.8 5.2 %collective-permute-start.16 = (bf16[1024,128]{1,0:T(8,128)(2,1)S(1)}, bf16[1024,128]{1,0:T(8,128)(2,1)S(1)}, u32[]{:S(2)}, u32[]{:S(2)}) collective-permute-start(bf16[1024,128]{1,0:T(8,128)(2,1)S(1)} %shard_map.101), channel_id=1, source_target_pairs={{0,4},{12,8},{1,5},{13,9},{2,6},{14,10},{3,7},{15,11},{16,20},{28,... | collective-permute-start | bytes 786440 | tf_op jit(solution)/shard_map/ppermute | solution.py:306
  72.1 6.4 %collective-permute-start.15 = (bf16[1024,128]{1,0:T(8,128)(2,1)S(1)}, bf16[1024,128]{1,0:T(8,128)(2,1)S(1)}, u32[]{:S(2)}, u32[]{:S(2)}) collective-permute-start(bf16[1024,128]{1,0:T(8,128)(2,1)S(1)} %get-tuple-element.85), channel_id=1, source_target_pairs={{0,2},{2,0},{1,3},{3,1},{4,6},{6,4},{5,7},{7,5},{8,10},{10,8},{9,1... | collective-permute-start | bytes 786440 | tf_op jit(solution)/shard_map/ppermute | solution.py:404
  78.6 5.7 %collective-permute-start.18 = (bf16[1024,128]{1,0:T(8,128)(2,1)S(1)}, bf16[1024,128]{1,0:T(8,128)(2,1)S(1)}, u32[]{:S(2)}, u32[]{:S(2)}) collective-permute-start(bf16[1024,128]{1,0:T(8,128)(2,1)S(1)} %shard_map.103), channel_id=1, source_target_pairs={{0,4},{12,8},{1,5},{13,9},{2,6},{14,10},{3,7},{15,11},{16,20},{28,... | collective-permute-start | bytes 786440 | tf_op jit(solution)/shard_map/ppermute | solution.py:306
  80.5 6.4 %collective-permute-start.17 = (bf16[1024,128]{1,0:T(8,128)(2,1)S(1)}, bf16[1024,128]{1,0:T(8,128)(2,1)S(1)}, u32[]{:S(2)}, u32[]{:S(2)}) collective-permute-start(bf16[1024,128]{1,0:T(8,128)(2,1)S(1)} %get-tuple-element.89), channel_id=1, source_target_pairs={{0,2},{2,0},{1,3},{3,1},{4,6},{6,4},{5,7},{7,5},{8,10},{10,8},{9,1... | collective-permute-start | bytes 786440 | tf_op jit(solution)/shard_map/ppermute | solution.py:404
  81.1 5.8 %collective-permute-start.19 = (bf16[1024,128]{1,0:T(8,128)(2,1)S(1)}, bf16[1024,128]{1,0:T(8,128)(2,1)S(1)}, u32[]{:S(2)}, u32[]{:S(2)}) collective-permute-start(bf16[1024,128]{1,0:T(8,128)(2,1)S(1)} %shard_map.104), channel_id=1, source_target_pairs={{4,8},{8,4},{5,9},{9,5},{6,10},{10,6},{7,11},{11,7},{20,24},{24,20... | collective-permute-start | bytes 786440 | tf_op jit(solution)/shard_map/ppermute | solution.py:306
  81.8 9.0 %collective-permute-start.25 = (bf16[1,128,1024]{2,1,0:T(8,128)(2,1)S(1)}, bf16[1,128,1024]{2,1,0:T(8,128)(2,1)S(1)}, u32[]{:S(2)}, u32[]{:S(2)}) collective-permute-start(bf16[1,128,1024]{2,1,0:T(8,128)(2,1)S(1)} %bitcast.75), channel_id=1, source_target_pairs={{0,1},{1,0},{2,3},{3,2},{4,5},{5,4},{6,7},{7,6},{8,9},{9,8},{10,11... | collective-permute-start | bytes 786440 | tf_op jit(solution)/shard_map/ppermute | solution.py:305
  84.3 7.7 %collective-permute-start.23 = (bf16[2,128,512]{2,1,0:T(8,128)(2,1)S(1)}, bf16[2,128,512]{2,1,0:T(8,128)(2,1)S(1)}, u32[]{:S(2)}, u32[]{:S(2)}) collective-permute-start(bf16[2,128,512]{2,1,0:T(8,128)(2,1)S(1)} %get-tuple-element.100), channel_id=1, source_target_pairs={{0,1},{1,0},{2,3},{3,2},{4,5},{5,4},{6,7},{7,6},{8,9},{9,8},{10,11... | collective-permute-start | bytes 786440 | tf_op jit(solution)/shard_map/ppermute | solution.py:305
  86.9 2.8 %collective-permute-start.26 = (f32[1,128]{1,0:T(1,128)S(1)}, f32[1,128]{1,0:T(1,128)S(1)}, u32[]{:S(2)}, u32[]{:S(2)}) collective-permute-start(f32[1,128]{1,0:T(1,128)S(1)} %get-tuple-element.106), channel_id=1, source_target_pairs={{0,1},{1,0},{2,3},{3,2},{4,5},{5,4},{6,7},{7,6},{8,9},{9,8},{10,11... | collective-permute-start | bytes 1544 | tf_op jit(solution)/shard_map/ppermute | solution.py:305
  87.1 10.4 %collective-permute-start.21 = (bf16[1024,128]{1,0:T(8,128)(2,1)S(1)}, bf16[1024,128]{1,0:T(8,128)(2,1)S(1)}, u32[]{:S(2)}, u32[]{:S(2)}) collective-permute-start(bf16[1024,128]{1,0:T(8,128)(2,1)S(1)} %shard_map.105), channel_id=1, source_target_pairs={{0,4},{4,0},{8,12},{12,8},{1,5},{5,1},{9,13},{13,9},{2,6},{6,2},{1... | collective-permute-start | bytes 786440 | tf_op jit(solution)/shard_map/ppermute | solution.py:306
  89.7 8.0 %collective-permute-start.20 = (bf16[1024,128]{1,0:T(8,128)(2,1)S(1)}, bf16[1024,128]{1,0:T(8,128)(2,1)S(1)}, u32[]{:S(2)}, u32[]{:S(2)}) collective-permute-start(bf16[1024,128]{1,0:T(8,128)(2,1)S(1)} %get-tuple-element.94), channel_id=1, source_target_pairs={{0,2},{2,0},{1,3},{3,1},{4,6},{6,4},{5,7},{7,5},{8,10},{10,8},{9,1... | collective-permute-start | bytes 786440 | tf_op jit(solution)/shard_map/ppermute | solution.py:404
  90.8 6.8 %collective-permute-start.22 = (bf16[1024,128]{1,0:T(8,128)(2,1)S(1)}, bf16[1024,128]{1,0:T(8,128)(2,1)S(1)}, u32[]{:S(2)}, u32[]{:S(2)}) collective-permute-start(bf16[1024,128]{1,0:T(8,128)(2,1)S(1)} %shard_map.106), channel_id=1, source_target_pairs={{4,8},{8,4},{5,9},{9,5},{6,10},{10,6},{7,11},{11,7},{20,24},{24,20... | collective-permute-start | bytes 786440 | tf_op jit(solution)/shard_map/ppermute | solution.py:306

commit v5 on v4

v5 whole, which is shorter than its diff:
```python
import functools

import jax
import jax.numpy as jnp
from jax import lax
from jax.experimental import pallas as pl
from jax.experimental.pallas import tpu as pltpu
from jax.sharding import PartitionSpec as P

BETA = 0.1
F32, BF16 = jnp.float32, jnp.bfloat16
VMEM_BYTES = 16 * 1024 * 1024
IN_VMEM = pl.BlockSpec(memory_space=pltpu.VMEM)
IN_SMEM = pl.BlockSpec(memory_space=pltpu.SMEM)
IN_PLACE = pl.BlockSpec(memory_space=pl.ANY)
PAIRS_OUT = [(0, 1), (1, 0), (2, 3), (3, 2)]
PAIR_IN = [(1, 2), (2, 1)]
TO_ENDS = [(1, 0), (2, 3)]
FROM_ENDS = [(0, 1), (3, 2)]
SWAP_HALVES = [(0, 2), (2, 0), (1, 3), (3, 1)]


def ring(count, shift):
    return [(i, (i + shift) % count) for i in range(count)]


def params():
    return pltpu.CompilerParams(vmem_limit_bytes=VMEM_BYTES)


def cost(flops, moved):
    return pl.CostEstimate(flops=int(flops), bytes_accessed=int(moved), transcendentals=0)


def shape_of(shape, kind):
    return jax.ShapeDtypeStruct(shape, kind)


def hold_kernel(w, out, sem):
    copy = pltpu.make_async_copy(w, out, sem)
    copy.start()
    copy.wait()


def hold(w):
    return pl.pallas_call(
        hold_kernel,
        out_shape=shape_of(w.shape, w.dtype),
        in_specs=[IN_PLACE],
        out_specs=IN_VMEM,
        scratch_shapes=[pltpu.SemaphoreType.DMA],
        compiler_params=params(),
        cost_estimate=cost(1, 4 * w.size),
    )(w)


def row_stats(own, far, wanted, first_own, first_far):
    top = jnp.max(jnp.maximum(own, far), axis=1, keepdims=True)
    total = jnp.sum(jnp.exp(own - top) + jnp.exp(far - top), axis=1, keepdims=True)
    column = lax.broadcasted_iota(jnp.int32, own.shape, 1)
    zero = jnp.zeros_like(own)
    picked = jnp.sum(
        jnp.where(column + first_own == wanted, own, zero) + jnp.where(column + first_far == wanted, far, zero),
        axis=1,
        keepdims=True,
    )
    lane = lax.broadcasted_iota(jnp.int32, (own.shape[0], 128), 1)
    return jnp.where(lane == 0, top, jnp.where(lane == 1, total, picked)).T[:8, :]


def logits_kernel(plan, columns, part, n_voc, meta, w_own, w_far, *refs):
    refs = list(refs)
    chunks = {(t, i): refs.pop(0) for t, parts, _, _ in plan for i in parts}
    accs = {t: refs.pop(0) for t, _, has_acc, _ in plan if has_acc}
    wanted = {t: refs.pop(0) for t, _, _, done in plan if done}
    used = sorted({i for _, parts, _, _ in plan for i in parts})
    outs = {}
    stats = {}
    for t, _, _, done in plan:
        outs[t] = refs.pop(0)
        if done:
            stats[t] = refs.pop(0)
    for i in used:
        at_part = pl.ds(pl.multiple_of(meta[i] * part, part), part)
        for t, parts, has_acc, _ in plan:
            if i not in parts:
                continue
            x = chunks[t, i][...]
            for j, w in enumerate((w_own, w_far)):
                at = slice(j * columns, (j + 1) * columns)
                product = jnp.dot(x, w[at_part, :], preferred_element_type=F32)
                if i != parts[0]:
                    product += outs[t][:, at]
                elif has_acc:
                    product += accs[t][:, at]
                outs[t][:, at] = product
    for t in stats:
        own, far = outs[t][:, :columns], outs[t][:, columns:]
        stats[t][...] = row_stats(own, far, wanted[t][...], meta[n_voc], meta[n_voc + 1])


def logits_call(plan, meta, weights, part, n_voc):
    columns = weights[0].shape[1]
    chunks = [c for _, parts, _, _ in plan for c in parts.values()]
    accs = [acc for _, _, acc, _ in plan if acc is not None]
    wanted = [w for _, _, _, w in plan if w is not None]
    rows = chunks[0].shape[0]
    out_shape = []
    for _, _, _, w in plan:
        out_shape.append(shape_of((rows, 2 * columns), F32))
        if w is not None:
            out_shape.append(shape_of((8, rows), F32))
    kernel_plan = [(t, sorted(parts), acc is not None, w is not None) for t, parts, acc, w in plan]
    chunks = [parts[i] for _, parts, _, _ in plan for i in sorted(parts)]
    operands = list(weights) + chunks + accs + wanted
    return pl.pallas_call(
        functools.partial(logits_kernel, kernel_plan, columns, part, n_voc),
        out_shape=out_shape,
        in_specs=[IN_SMEM] + [IN_VMEM] * len(operands),
        out_specs=[IN_VMEM] * len(out_shape),
        compiler_params=params(),
        cost_estimate=cost(4 * len(chunks) * rows * part * columns, len(chunks) * 4 * part * columns),
    )(meta, *operands)


def spread(flipped_own, flipped_far, w_own, w_far, kept, send):
    rows = kept.shape[1]
    here = jnp.dot(w_own, flipped_own, preferred_element_type=F32)
    here += jnp.dot(w_far, flipped_far, preferred_element_type=F32)
    kept[...] = here[:, :rows]
    for t, out in enumerate(send, 1):
        out[...] = here[:, t * rows:(t + 1) * rows].astype(BF16)


def grads_kernel(n_blocks, n_stats, columns, part, window, meta, start, sums, refer, cotangent, w_own, w_far, *refs):
    refs = list(refs)
    logits = [refs.pop(0) for _ in range(n_blocks)]
    target = refs.pop(0)
    stats = [refs.pop(0) for _ in range(n_stats)]
    grads_own, grads_far, flipped_own, flipped_far, loss, kept = refs[:6]
    send = refs[6:]
    rows = logits[0].shape[0]
    pair, me_ctx = meta[3], meta[4]
    top = stats[0][0:1, :]
    for s in stats[1:]:
        top = jnp.maximum(top, s[0:1, :])
    total = jnp.zeros_like(top)
    picked = jnp.zeros_like(top)
    for s in stats:
        total += s[1:2, :] * jnp.exp(s[0:1, :] - top)
        picked += s[2:3, :]
    row = lax.broadcasted_iota(jnp.int32, (1, rows), 1)
    masks = []
    for t in range(n_blocks):
        block = lax.rem(me_ctx + (n_blocks - t), n_blocks)
        seen = lax.rem(row, window) + block * window >= start[pair]
        masks.append(jnp.where(seen, jnp.where(row < window, 1.0, -1.0), 0.0))
    signed_mask = jnp.concatenate(masks, axis=1)
    token_logp = picked - top - jnp.log(total)
    offset = (sums[pair, 0] - refer[pair, 0]) - (sums[pair, 1] - refer[pair, 1])
    zeros = jnp.zeros((1, 128), F32)
    margin = BETA * (jnp.sum(signed_mask * token_logp, axis=1, keepdims=True) + (zeros + offset))
    loss[...] = jnp.maximum(-margin, 0.0) + jnp.log1p(jnp.exp(-jnp.abs(margin)))
    factor = -BETA * (1.0 / (1.0 + jnp.exp(margin))) * cotangent[pair]
    weight = factor[:, 0:1] * signed_mask
    lines = lax.broadcasted_iota(jnp.int32, (128, top.shape[1]), 0)
    packed = jnp.where(lines == 0, top, jnp.where(lines == 1, weight, 1.0 / total)).T
    for t in range(n_blocks):
        at = slice(t * rows, (t + 1) * rows)
        top_t, weight_t, inverse_t = packed[at, 0:1], packed[at, 1:2], packed[at, 2:3]
        wanted = target[at, :]
        for j, (grads, flipped) in enumerate(((grads_own, flipped_own), (grads_far, flipped_far))):
            l = logits[t][:, j * columns:(j + 1) * columns]
            column = lax.broadcasted_iota(jnp.int32, l.shape, 1) + meta[1 + j]
            hit = jnp.where(column == wanted, 1.0, 0.0)
            g = weight_t * (hit - jnp.exp(l - top_t) * inverse_t)
            grads[t] = g.astype(BF16)
            flipped[:, at] = g.T.astype(BF16)
    at_part = pl.ds(pl.multiple_of(meta[0] * part, part), part)
    spread(flipped_own[...], flipped_far[...], w_own[at_part, :], w_far[at_part, :], kept, send)


def spread_kernel(part, n_parts, meta, w_own, w_far, flipped_own, flipped_far, *outs):
    each = len(outs) // n_parts
    for i in range(n_parts):
        kept, *send = outs[i * each:(i + 1) * each]
        at_part = pl.ds(pl.multiple_of(meta[i] * part, part), part)
        spread(flipped_own[...], flipped_far[...], w_own[at_part, :], w_far[at_part, :], kept, send)


def spread_shapes(n_blocks, rows, part):
    return [shape_of((part, rows), F32)] + [shape_of((part, rows), BF16)] * (n_blocks - 1)


def grads_call(logits, target, stats, small, weights, meta, part, window):
    n_blocks, rows, columns = len(logits), logits[0].shape[0], weights[0].shape[1]
    grads = shape_of((n_blocks, rows, columns), BF16)
    flipped = shape_of((columns, n_blocks * rows), BF16)
    out_shape = [grads, grads, flipped, flipped, shape_of((1, 128), F32)] + spread_shapes(n_blocks, rows, part)
    operands = list(logits) + [target] + list(stats)
    return pl.pallas_call(
        functools.partial(grads_kernel, n_blocks, len(stats), columns, part, window),
        out_shape=out_shape,
        in_specs=[IN_SMEM] * 5 + [IN_VMEM] * (2 + len(operands)),
        out_specs=[IN_VMEM] * len(out_shape),
        compiler_params=params(),
        cost_estimate=cost(4 * n_blocks * rows * part * columns, 8 * part * columns),
    )(meta, *small, *weights, *operands)


def spread_call(flipped_own, flipped_far, weights, k_ids, part, rows):
    columns, n_rows = flipped_own.shape
    n_parts = len(k_ids)
    out_shape = spread_shapes(n_rows // rows, rows, part) * n_parts
    outs = pl.pallas_call(
        functools.partial(spread_kernel, part, n_parts),
        out_shape=out_shape,
        in_specs=[IN_SMEM] + [IN_VMEM] * 4,
        out_specs=[IN_VMEM] * len(out_shape),
        compiler_params=params(),
        cost_estimate=cost(4 * n_parts * n_rows * part * columns, 4 * n_parts * part * columns),
    )(jnp.stack(k_ids).astype(jnp.int32), *weights, flipped_own, flipped_far)
    each = len(outs) // n_parts
    return [(outs[i * each], list(outs[i * each + 1:(i + 1) * each])) for i in range(n_parts)]


def add_kernel(turned, kept, *refs):
    total = kept[...]
    for a in refs[:-1]:
        total += a[...].astype(F32)
    refs[-1][...] = (total.T if turned else total).astype(BF16)


def add_call(kept, arrived, turned=False):
    shape = kept.shape[::-1] if turned else kept.shape
    return pl.pallas_call(
        functools.partial(add_kernel, turned),
        out_shape=shape_of(shape, BF16),
        in_specs=[IN_VMEM] * (1 + len(arrived)),
        out_specs=IN_VMEM,
        compiler_params=params(),
        cost_estimate=cost(kept.size, 4 * kept.size),
    )(kept, *arrived)


def head_kernel(slots_here, near_keys, far_keys, part, has_out, meta, *refs):
    refs = list(refs)
    grads = [refs.pop(0), refs.pop(0)]
    near = {k: refs.pop(0) for k in near_keys}
    stacks = [refs.pop(0) for _ in far_keys]
    far = {k: stack.at[i] for stack, keys in zip(stacks, far_keys) for i, k in enumerate(keys)}
    out, ready, sems = refs[has_out:]
    n_blocks, rows, columns = grads[0].shape
    right = jnp.concatenate([g[...].reshape(n_blocks * rows, columns) for g in grads])
    copies = []
    for n, i in enumerate(slots_here):
        left = jnp.concatenate([x[t, i][...] for x in (near, far) for t in range(n_blocks)])
        product = lax.dot_general(left, right, (((0,), (0,)), ((), ())), preferred_element_type=F32)
        if n >= 2:
            copies[n - 2].wait()
        ready[n % 2] = product.astype(BF16)
        start = pl.multiple_of(meta[i] * part, part)
        copies.append(pltpu.make_async_copy(ready.at[n % 2], out.at[pl.ds(start, part), :], sems.at[n % 2]))
        copies[-1].start()
    for copy in copies[-2:]:
        copy.wait()


def head_call(slots_here, near, far, grads, meta, out=None):
    n_blocks, rows, columns = grads[0].shape
    n_parts = len(near) // n_blocks
    part = near[0, 0].shape[1]
    near = {k: c for k, c in near.items() if k[1] in slots_here}
    far = [(keys, stack) for keys, stack in far if any(k[1] in slots_here for k in keys)]
    operands = list(grads) + list(near.values()) + [stack for _, stack in far]
    here = [] if out is None else [out]
    return pl.pallas_call(
        functools.partial(head_kernel, slots_here, list(near), [keys for keys, _ in far], part, len(here)),
        out_shape=shape_of((n_parts * part, columns), BF16),
        in_specs=[IN_SMEM] + [IN_VMEM] * len(operands) + [IN_PLACE] * len(here),
        out_specs=IN_PLACE,
        scratch_shapes=[pltpu.VMEM((2, part, columns), BF16), pltpu.SemaphoreType.DMA((2,))],
        input_output_aliases={1 + len(operands): 0} if here else {},
        compiler_params=params(),
        cost_estimate=cost(
            4 * n_blocks * rows * len(slots_here) * part * columns,
            4 * n_blocks * len(slots_here) * rows * part + 2 * len(slots_here) * part * columns,
        ),
    )(meta, *operands, *here)


def together(*groups):
    flat = lax.optimization_barrier([a for group in groups for a in group])
    out = []
    for group in groups:
        out.append(flat[:len(group)])
        flat = flat[len(group):]
    return out


def shards(hidden, head_weight, targets, response_start, other_sums, ref_logp, loss_cotangent):
    n_voc, n_ctx, n_dp = lax.axis_size("vocab"), lax.axis_size("ctx"), lax.axis_size("dp")
    me_voc, me_ctx, me_dp = lax.axis_index("vocab"), lax.axis_index("ctx"), lax.axis_index("dp")
    part, _, sides, window = hidden.shape
    rows = sides * window
    columns = head_weight.shape[1]
    line = n_voc == 4
    beyond = list(range(1, n_ctx))
    dp_swap = lambda a: lax.ppermute(a, "dp", ring(n_dp, 1))
    along = lambda a, by: lax.ppermute(a, "vocab", by)

    if line:
        table = [[0, 1, 2, 3], [1, 0, 2, 3], [2, 3, 1, 0], [3, 2, 1, 0]]
        part_of = [sum(jnp.where(me_voc == z, table[z][i], 0) for z in range(n_voc)) for i in range(n_voc)]
    else:
        part_of = [(me_voc - s) % n_voc for s in range(n_voc)]
    firsts = [
        ((me_voc * n_ctx + me_ctx) * n_dp + owner) * columns for owner in (me_dp, (me_dp + 1) % n_dp)
    ]
    meta = jnp.stack(part_of + firsts).astype(jnp.int32)

    weights = (hold(head_weight), dp_swap(head_weight))

    pair = lax.broadcasted_iota(jnp.int32, targets.shape, 0)

    def by_block(all_targets):
        mine = jnp.sum(jnp.where(pair == me_dp, all_targets, 0), axis=0)
        blocks = [mine[:, b * window:(b + 1) * window].reshape(rows) for b in range(n_ctx)]
        wanted = []
        for t in range(n_ctx):
            at = (me_ctx - t) % n_ctx
            wanted.append(sum(jnp.where(at == b, blocks[b], 0) for b in range(n_ctx))[:, None])
        return wanted

    own = hidden.transpose(1, 2, 3, 0).reshape(rows, part)
    final = n_voc - 1
    call = functools.partial(logits_call, meta=meta, weights=weights, part=part, n_voc=n_voc)
    cross = lambda a: [lax.ppermute(a, "ctx", ring(n_ctx, t)) for t in beyond]
    chunk = {}

    def arrive(i, near, over):
        chunk[0, i] = near
        for t, a in zip(beyond, over):
            chunk[t, i] = a

    def more_logits(i, logits):
        if logits is None:
            return call([(0, {j: chunk[0, j] for j in (0, 1)}, None, None)] + [(t, {0: chunk[t, 0]}, None, None) for t in beyond])
        return call(
            [(0, {i: chunk[0, i]}, logits[0], None)] + [(t, {i - 1: chunk[t, i - 1]}, logits[t], None) for t in beyond]
        )

    arrive(0, own, cross(own))
    if line:
        first = along(own, PAIRS_OUT)
        inner = along(own, PAIR_IN)
        over = cross(first)
        outer, inner_last = along(inner, TO_ENDS), along(first, PAIR_IN)
        arrive(1, first, over)
        over, (inner, outer, inner_last), logits = together(over, [inner, outer, inner_last], more_logits(1, None))
        arrive(1, first, over)
        arrive(2, inner + outer, cross(inner + outer))
        outer = along(inner_last, TO_ENDS)
        (inner_last, outer), logits = together([inner_last, outer], more_logits(2, logits))
        last = inner_last + outer
    else:
        near = [own] + [along(own, ring(n_voc, i)) for i in range(1, n_voc)]
        logits = None
        for i in range(1, final):
            arrive(i, near[i], cross(near[i]))
            (near[i + 1],), logits = together([near[i + 1]], more_logits(i, logits))
        last = near[final]
    arrive(final, last, cross(last))
    (raw_targets,), _ = together([targets], logits)
    wanted = by_block(raw_targets)
    target = jnp.concatenate(wanted)

    done = call(
        [(0, {final: chunk[0, final]}, logits[0], wanted[0])]
        + [(t, {final - 1: chunk[t, final - 1]}, logits[t], None) for t in beyond]
    )
    logits, stats = [done[0]] + list(done[2:]), [done[1]]
    done = call([(t, {final: chunk[t, final]}, logits[t], wanted[t]) for t in beyond])
    logits = [logits[0]] + list(done[0::2])
    stats = stats + list(done[1::2])

    late = [(t, final) for t in beyond]
    soon = [k for k in chunk if k not in late]
    far_soon = dp_swap(jnp.stack(together([chunk[k] for k in soon], [stats[0]])[0]))

    def merge(seen):
        merged = []
        for b in range(n_ctx):
            these = [s[(b - t) % n_ctx] for t, s in seen]
            top = these[0][0]
            for s in these[1:]:
                top = jnp.maximum(top, s[0])
            total = sum(s[1] * jnp.exp(s[0] - top) for s in these)
            picked = sum(s[2] for s in these)
            merged.append(jnp.pad(jnp.stack([top, total, picked]), ((0, 5), (0, 0))))
        return jnp.concatenate(merged, axis=1)

    stats = jnp.stack(stats)
    if line and n_ctx == 2:
        corner = [(2 * a + c, 2 * b + (1 - c)) for a, b in PAIRS_OUT for c in range(2)]
        diagonal = lax.ppermute(stats, ("vocab", "ctx"), corner)
        merged = merge([(0, stats), (1, cross(stats)[0]), (0, along(stats, PAIRS_OUT)), (1, diagonal)])
        all_stats = [merged, along(merged, SWAP_HALVES)]
    else:
        merged = merge([(0, stats)] + list(zip(beyond, cross(stats))))
        all_stats = [merged] + [along(merged, ring(n_voc, s)) for s in range(1, n_voc)]

    meta_grads = jnp.stack([part_of[final]] + firsts + [me_dp, me_ctx]).astype(jnp.int32)
    small = (response_start, other_sums, ref_logp, loss_cotangent)
    grads_own, grads_far, flipped_own, flipped_far, loss, kept, *send = grads_call(
        logits, target, all_stats, small, weights, meta_grads, part, window
    )
    theirs = dp_swap(grads_far)
    far_late = dp_swap(jnp.stack(together([chunk[k] for k in late], [kept])[0]))
    back = lambda cs: [lax.ppermute(c, "ctx", ring(n_ctx, -t)) for t, c in zip(beyond, cs)]
    shares = {final: (kept, list(send))}
    leave = list(range(final))[::-1]
    for i, share in zip(leave, spread_call(flipped_own, flipped_far, weights, [part_of[i] for i in leave], part, rows)):
        shares[i] = share

    over = {}
    for i in range(n_voc)[::-1]:
        send = shares[i][1]
        if i + 2 in over:
            over[i + 2], send = together(over[i + 2], send)
        over[i] = back(send)
    near_over = lambda i, *more: add_call(shares[i][0], over[i] + list(more))
    head = functools.partial(head_call, near=chunk, far=[(soon, far_soon), (late, far_late)], grads=[grads_own, theirs], meta=meta)
    early, rest = list(range(n_voc // 2)), list(range(n_voc // 2, n_voc))
    grad_head = head(early)
    if line:
        up_3 = along(near_over(3), FROM_ENDS)
        up_2 = along(near_over(2), FROM_ENDS)
        up_3 = along(near_over(3, up_3), PAIR_IN)
        (up_3,), (grad_head,) = together([up_3], [grad_head])
        landed = [along(near_over(1, up_3), PAIRS_OUT), along(near_over(2, up_2), PAIR_IN)]
    else:
        landed = [along(near_over(i), ring(n_voc, -i)) for i in range(1, n_voc)]
    grad_head = head(rest, out=grad_head)
    (kept,), (grad_head,) = together([shares[0][0]], [grad_head])
    summed = add_call(kept, over[0] + landed, turned=True)
    grad_hidden = summed.reshape(1, sides, window, part).transpose(3, 0, 1, 2)

    far_loss = dp_swap(loss)
    owner = lax.broadcasted_iota(jnp.int32, (n_dp,), 0)
    pair_loss = jnp.where(owner == me_dp, loss[0, :n_dp], far_loss[0, :n_dp])
    return (grad_hidden, grad_head, pair_loss)


def solution(mesh):
    placed = (
        P("vocab", ("groups", "dp"), None, "ctx"),
        P(None, ("vocab", "ctx", "dp")),
        P("groups", None, None),
        P("groups"),
        P("groups", None),
        P("groups", None),
        P("groups"),
    )
    return jax.shard_map(
        shards,
        mesh=mesh,
        in_specs=placed,
        out_specs=(
            P("vocab", ("groups", "dp"), None, "ctx"),
            P("groups", ("vocab", "ctx", "dp")),
            P("groups"),
        ),
        check_vma=False,
    )
```

time: 100 us -> 120 us (1.20)
  local copies, waits for them, and re-layouts: 11.4 us -> 30 us
  waiting for transfers between devices: 29.5 us -> 18 us
  starting transfers between devices: 28.7 us -> 39.7 us
  other arithmetic: 0.87 us -> 2.48 us
    unnamed x31 -> x54, local copies, waits for them, and re-layouts: 10.7 us -> 28 us
    ppermute x5, waiting for transfers between devices: 5.34 us -> 0.4 us  [shards(): cross = lambda a: [lax.ppermute(a, 'ctx', ring(n_ctx, t)) for t in beyond]]
    ppermute x13 -> x12, starting transfers between devices: 19.3 us -> 24.1 us  [shards(): along = lambda a, by: lax.ppermute(a, 'vocab', by)]
    ppermute x4, waiting for transfers between devices: 6.85 us -> 2.33 us  [shards(): lax.ppermute(c, 'ctx', ring(n_ctx, -t))]
    ppermute x4, starting transfers between devices: 2.95 us -> 6.57 us  [shards(): lax.ppermute(c, 'ctx', ring(n_ctx, -t))]
    ppermute x0 -> x1, starting transfers between devices: none -> 2.55 us  [shards(): diagonal = lax.ppermute(stats, ('vocab', 'ctx'), corner)]
    ppermute x13 -> x12, waiting for transfers between devices: 17.3 us -> 14.8 us  [shards(): along = lambda a, by: lax.ppermute(a, 'vocab', by)]
    pallas_call x4, Pallas kernels: 11.7 us -> 10.3 us  [the longest x2 6.07 us: head_call(): pl.pallas_call(functools.partial(head_kernel, slots_here, list(near), [ke...]
  transfers between devices with their start and end apart: 27 -> 27, of which waited for: 15 -> 11; matrix products, arithmetic and copies ran while one was open for 2% -> 8% of each run, Pallas kernels for 27% -> 22%
where the time goes in v5:
time: 120 us; the launch traced here: 119 us
  starting transfers between devices  39.7 us (33%)
  local copies, waits for them, and re-layouts  30 us (25%)
  Pallas kernels  27.4 us (23%)
  waiting for transfers between devices  18 us (15%)
  other arithmetic  2.48 us (2%)
    unnamed x54, local copies, waits for them, and re-layouts  28 us
    ppermute x12, starting transfers between devices, shards(): along = lambda a, by: lax.ppermute(a, 'vocab', by)  24.1 us
    ppermute x12, waiting for transfers between devices, shards(): along = lambda a, by: lax.ppermute(a, 'vocab', by)  14.8 us
    pallas_call x4, Pallas kernels, logits_call(): pl.pallas_call(functools.partial(logits_kernel, kernel_plan, columns, par...  12.3 us
    ppermute x4, starting transfers between devices, shards(): lax.ppermute(c, 'ctx', ring(n_ctx, -t))  6.57 us
    pallas_call x2, Pallas kernels, head_call(): pl.pallas_call(functools.partial(head_kernel, slots_here, list(near), [ke...  6.07 us
    ppermute x5, starting transfers between devices, shards(): cross = lambda a: [lax.ppermute(a, 'ctx', ring(n_ctx, t)) for t in beyond]  5.37 us
    pallas_call x1, Pallas kernels, spread_call(): pl.pallas_call(functools.partial(spread_kernel, part, n_parts), out_shape...  3.98 us
  transfers between devices with their start and end apart: 27, of which 11 were waited for; matrix products, arithmetic and copies ran while one was open for 8% of the time, Pallas kernels for 22%

profile of v5, /device:TPU:0, one launch (start us, length us, event | category | flops | bytes accessed | tf_op | source)
XLA Modules:
  0.0 118.7 jit_solution(16881280907994160695)
XLA Ops:
  1.1 0.7 collective-permute-start.3
  1.8 5.5 %collective-permute-start.1 = (bf16[128,1024]{1,0:T(8,128)(2,1)}, bf16[128,1024]{1,0:T(8,128)(2,1)S(1)}, u32[]{:S(2)}, u32[]{:S(2)}) collective-permute-start(bf16[128,1024]{1,0:T(8,128)(2,1)} %bitcast.154), channel_id=1, source_target_pairs={{0,4},{4,0},{8,12},{12,8},{1,5},{5,1},{9,13},{13,9},{2,6},{6,2},{1... | collective-permute-start | bytes 786440 | tf_op jit(solution)/shard_map/ppermute | solution.py:310
  7.3 1.5 %collective-permute-start.6 = (bf16[128,1024]{1,0:T(8,128)(2,1)}, bf16[128,1024]{1,0:T(8,128)(2,1)S(1)}, u32[]{:S(2)}, u32[]{:S(2)}) collective-permute-start(bf16[128,1024]{1,0:T(8,128)(2,1)} %bitcast.155), channel_id=1, source_target_pairs={{0,2},{2,0},{1,3},{3,1},{4,6},{6,4},{5,7},{7,5},{8,10},{10,8},{9,1... | collective-permute-start | bytes 786440 | tf_op jit(solution)/shard_map/ppermute | solution.py:338
  8.8 1.3 %collective-permute-start.4 = (bf16[128,1024]{1,0:T(8,128)(2,1)S(1)}, bf16[128,1024]{1,0:T(8,128)(2,1)S(1)}, u32[]{:S(2)}, u32[]{:S(2)}) collective-permute-start(bf16[128,1024]{1,0:T(8,128)(2,1)S(1)} %collective-permute-done.3), channel_id=1, source_target_pairs={{4,0},{8,12},{5,1},{9,13},{6,2},{10,14},{7,3},{11,15},{20,16},{24,... | collective-permute-start | bytes 786440 | tf_op jit(solution)/shard_map/ppermute | solution.py:310
  10.1 4.1 %collective-permute-done.1.refs_1_.refs_4_ = bf16[128,1024]{1,0:T(8,128)(2,1)S(1)} collective-permute-done((bf16[128,1024]{1,0:T(8,128)(2,1)}, bf16[128,1024]{1,0:T(8,128)(2,1)S(1)}, u32[]{:S(2)}, u32[]{:S(2)}) %collective-permute-start.1) | collective-permute-done | bytes 262176 | tf_op jit(solution)/shard_map/ppermute | solution.py:310
  14.2 0.7 collective-permute-start.5
  14.8 1.6 %collective-permute-start.2 = (bf16[128,1024]{1,0:T(8,128)(2,1)S(1)}, bf16[128,1024]{1,0:T(8,128)(2,1)S(1)}, u32[]{:S(2)}, u32[]{:S(2)}) collective-permute-start(bf16[128,1024]{1,0:T(8,128)(2,1)S(1)} %collective-permute-done.1.refs_1_.refs_4_), channel_id=1, source_target_pairs={{0,2},{2,0},{1,3},{3,1},{4,6},{6,4},{5,7},{7,5},{8,10},{10,8},{9,1... | collective-permute-start | bytes 786440 | tf_op jit(solution)/shard_map/ppermute | solution.py:338
  16.4 2.2 %copy-done.6 = bf16[4096,512]{1,0:T(8,128)(2,1)S(1)} copy-done((bf16[4096,512]{1,0:T(8,128)(2,1)S(1)}, bf16[4096,512]{1,0:T(8,128)(2,1)}, u32[]{:S(2)}) %copy-start.6) | copy-done | bytes 4194328
  18.9 2.0 %copy-done = bf16[4096,512]{1,0:T(8,128)(2,1)} copy-done((bf16[4096,512]{1,0:T(8,128)(2,1)}, bf16[4096,512]{1,0:T(8,128)(2,1)S(1)}, u32[]{:S(2)}) %copy-start) | copy-done | bytes 4194328
  21.0 2.2 %copy-done.1 = bf16[4096,512]{1,0:T(8,128)(2,1)S(1)} copy-done((bf16[4096,512]{1,0:T(8,128)(2,1)S(1)}, bf16[4096,512]{1,0:T(8,128)(2,1)}, u32[]{:S(2)}) %copy-start.1) | copy-done | bytes 4194328
  23.2 3.2 %shard_map.95 = (f32[128,1024]{1,0:T(8,128)S(1)}, f32[128,1024]{1,0:T(8,128)S(1)}) custom-call(s32[6]{0:T(128)S(1)} %stack.97.meta, bf16[4096,512]{1,0:T(8,128)(2,1)S(1)} %copy-done.1, bf16[4096,512]{1,0:T(8,128)(2,1)} %collective-permute-done.w_far, bf16[128,1024]{1,0:T(8,128)(2,1)S(1)} %bitcast.156, ...), custom_call_target="tpu_custom_call" | custom-call | flops 805306368 | bytes 6291456 | tf_op jit(solution)/shard_map/pallas_call | solution.py:116
  26.4 1.3 %collective-permute-start.7 = (bf16[128,1024]{1,0:T(8,128)(2,1)S(1)}, bf16[128,1024]{1,0:T(8,128)(2,1)}, u32[]{:S(2)}, u32[]{:S(2)}) collective-permute-start(bf16[128,1024]{1,0:T(8,128)(2,1)S(1)} %collective-permute-done.5), channel_id=1, source_target_pairs={{4,0},{8,12},{5,1},{9,13},{6,2},{10,14},{7,3},{11,15},{20,16},{24,... | collective-permute-start | bytes 786440 | tf_op jit(solution)/shard_map/ppermute | solution.py:310
  27.9 0.6 collective-permute-start.8
  28.5 2.2 %copy-done.2 = bf16[4096,512]{1,0:T(8,128)(2,1)S(1)} copy-done((bf16[4096,512]{1,0:T(8,128)(2,1)S(1)}, bf16[4096,512]{1,0:T(8,128)(2,1)}, u32[]{:S(2)}) %copy-start.2) | copy-done | bytes 4194328
  30.6 2.9 %shard_map.96 = (f32[128,1024]{1,0:T(8,128)S(1)}, f32[128,1024]{1,0:T(8,128)S(1)}) custom-call(s32[6]{0:T(128)S(1)} %stack.97.meta, bf16[4096,512]{1,0:T(8,128)(2,1)S(1)} %copy-done.2, bf16[4096,512]{1,0:T(8,128)(2,1)} %collective-permute-done.w_far, bf16[128,1024]{1,0:T(8,128)(2,1)S(1)} %add.150.refs_0_.refs_2_, ...), custom_call_target="tpu_custom_call" | custom-call | flops 536870912 | bytes 4194304 | tf_op jit(solution)/shard_map/pallas_call | solution.py:116
  33.6 0.8 copy-done.14
  34.4 3.5 %collective-permute-done.7 = bf16[128,1024]{1,0:T(8,128)(2,1)} collective-permute-done((bf16[128,1024]{1,0:T(8,128)(2,1)S(1)}, bf16[128,1024]{1,0:T(8,128)(2,1)}, u32[]{:S(2)}, u32[]{:S(2)}) %collective-permute-start.7) | collective-permute-done | bytes 262176 | tf_op jit(solution)/shard_map/ppermute | solution.py:310
  38.3 1.1 add.151.refs_0_.refs_4_
  39.4 0.6 collective-permute-start.9
  40.0 2.2 %copy-done.3 = bf16[4096,512]{1,0:T(8,128)(2,1)S(1)} copy-done((bf16[4096,512]{1,0:T(8,128)(2,1)S(1)}, bf16[4096,512]{1,0:T(8,128)(2,1)}, u32[]{:S(2)}) %copy-start.3) | copy-done | bytes 4194328
  42.2 1.0 copy-done.15
  43.2 3.3 %shard_map.97 = (f32[128,1024]{1,0:T(8,128)S(1)}, f32[8,128]{1,0:T(8,128)S(1)}, f32[128,1024]{1,0:T(8,128)S(1)}) custom-call(s32[6]{0:T(128)S(1)} %stack.97.meta, bf16[4096,512]{1,0:T(8,128)(2,1)S(1)} %copy-done.3, bf16[4096,512]{1,0:T(8,128)(2,1)} %collective-permute-done.w_far, bf16[128,1024]{1,0:T(8,128)(2,1)S(1)} %add.151.refs_0_.refs_4_, ...), custom_call_target="tpu_custom_call" | custom-call | flops 536870912 | bytes 4194304 | tf_op jit(solution)/shard_map/pallas_call | solution.py:116
  46.5 0.8 bitcast_dynamic-update-slice_fusion.6
  47.3 0.7 bitcast_dynamic-update-slice_fusion.5
  48.0 0.7 bitcast_dynamic-update-slice_fusion.4
  48.7 0.7 bitcast_dynamic-update-slice_fusion.3
  49.5 0.7 bitcast_dynamic-update-slice_fusion.2
  50.2 0.7 bitcast_dynamic-update-slice_fusion.1
  50.9 0.7 bitcast_dynamic-update-slice_fusion
  51.9 2.2 %copy-done.4 = bf16[4096,512]{1,0:T(8,128)(2,1)S(1)} copy-done((bf16[4096,512]{1,0:T(8,128)(2,1)S(1)}, bf16[4096,512]{1,0:T(8,128)(2,1)}, u32[]{:S(2)}) %copy-start.4) | copy-done | bytes 4194328
  54.1 1.0 copy-done.17
  55.1 2.9 %shard_map.98 = (f32[128,1024]{1,0:T(8,128)S(1)}, f32[8,128]{1,0:T(8,128)S(1)}) custom-call(s32[6]{0:T(128)S(1)} %stack.97.meta, bf16[4096,512]{1,0:T(8,128)(2,1)S(1)} %copy-done.4, bf16[4096,512]{1,0:T(8,128)(2,1)} %collective-permute-done.w_far, bf16[128,1024]{1,0:T(8,128)(2,1)} %collective-permute-done.9.refs_0_.refs_5_, f32[128,1024]{1,0:T(8,128)S(1)} %copy-done.17, ...), custom_call_target="tpu_custom_call" | custom-call | flops 268435456 | bytes 2097152 | tf_op jit(solution)/shard_map/pallas_call | solution.py:116
  58.0 0.8 copy-done.12
  58.8 2.6 %collective-permute-start.12 = (f32[2,8,128]{2,1,0:T(8,128)S(1)}, f32[2,8,128]{2,1,0:T(8,128)S(1)}, u32[]{:S(2)}, u32[]{:S(2)}) collective-permute-start(f32[2,8,128]{2,1,0:T(8,128)S(1)} %pad_maximum_fusion), channel_id=1, source_target_pairs={{0,6},{2,4},{4,2},{6,0},{8,14},{10,12},{12,10},{14,8},{1,7},{3,5},... | collective-permute-start | bytes 24584 | tf_op jit(solution)/shard_map/ppermute | solution.py:406
  61.8 1.1 collective-permute-start.10
  63.4 1.7 %collective-permute-done.11 = f32[2,8,128]{2,1,0:T(8,128)S(1)} collective-permute-done((f32[2,8,128]{2,1,0:T(8,128)S(1)}, f32[2,8,128]{2,1,0:T(8,128)S(1)}, u32[]{:S(2)}, u32[]{:S(2)}) %collective-permute-start.11) | collective-permute-done | bytes 8224 | tf_op jit(solution)/shard_map/ppermute | solution.py:310
  65.5 1.6 %collective-permute-start.13 = (f32[8,256]{1,0:T(8,128)S(1)}, f32[8,256]{1,0:T(8,128)}, u32[]{:S(2)}, u32[]{:S(2)}) collective-permute-start(f32[8,256]{1,0:T(8,128)S(1)} %pad_maximum_fusion.1.refs_3_), channel_id=1, source_target_pairs={{0,8},{8,0},{4,12},{12,4},{1,9},{9,1},{5,13},{13,5},{2,10},{10,2},... | collective-permute-start | bytes 24584 | tf_op jit(solution)/shard_map/ppermute | solution.py:310
  67.7 0.7 copy.17.refs_2_
  68.4 1.8 %collective-permute-done.13.refs_4_ = f32[8,256]{1,0:T(8,128)} collective-permute-done((f32[8,256]{1,0:T(8,128)S(1)}, f32[8,256]{1,0:T(8,128)}, u32[]{:S(2)}, u32[]{:S(2)}) %collective-permute-start.13) | collective-permute-done | bytes 8224 | tf_op jit(solution)/shard_map/ppermute | solution.py:310
  70.2 2.2 %copy-done.5 = bf16[4096,512]{1,0:T(8,128)(2,1)S(1)} copy-done((bf16[4096,512]{1,0:T(8,128)(2,1)S(1)}, bf16[4096,512]{1,0:T(8,128)(2,1)}, u32[]{:S(2)}) %copy-start.5) | copy-done | bytes 4194328
  72.4 1.0 copy-done.11
  73.5 1.0 copy-done.13
  74.5 0.7 copy-done.18
  75.2 0.7 copy-done.19
  75.9 0.7 copy-done.20
  76.5 0.7 copy-done.21
  77.2 3.5 %shard_map.99 = (bf16[2,128,512]{2,1,0:T(8,128)(2,1)S(1)}, bf16[2,128,512]{2,1,0:T(8,128)(2,1)S(1)}, bf16[512,256]{1,0:T(8,128)(2,1)S(1)}, bf16[512,256]{1,0:T(8...) custom-call(s32[5]{0:T(128)S(1)} %stack.96.meta, s32[2]{0:T(128)S(1)} %copy-done.20, ...), custom_call_target="tpu_custom_call" | custom-call | flops 536870912 | bytes 4194304 | tf_op jit(solution)/shard_map/pallas_call | solution.py:201
  80.7 1.2 collective-permute-start.17
  81.9 4.0 %shard_map.100 = (f32[1024,128]{1,0:T(8,128)S(1)}, bf16[1024,128]{1,0:T(8,128)(2,1)S(1)}, f32[1024,128]{1,0:T(8,128)S(1)}, bf16[1024,128]{1,0:T(8,128)(2,1)S(1)}...) custom-call(s32[3]{0:T(128)S(1)} %pad_add_fusion.1.meta, bf16[4096,512]{1,0:T(8,128)(2,1)S(1)} %copy-done.5, ...), custom_call_target="tpu_custom_call" | custom-call | flops 1610612736 | bytes 6291456 | tf_op jit(solution)/shard_map/pallas_call | solution.py:215
  85.9 1.0 collective-permute-start.20
  86.9 1.0 collective-permute-done.17.refs_0_
  88.0 3.4 %collective-permute-start.18 = (bf16[1024,128]{1,0:T(8,128)(2,1)S(1)}, bf16[1024,128]{1,0:T(8,128)(2,1)S(1)}, u32[]{:S(2)}, u32[]{:S(2)}) collective-permute-start(bf16[1024,128]{1,0:T(8,128)(2,1)S(1)} %shard_map.101), channel_id=1, source_target_pairs={{0,4},{12,8},{1,5},{13,9},{2,6},{14,10},{3,7},{15,11},{16,20},{28,... | collective-permute-start | bytes 786440 | tf_op jit(solution)/shard_map/ppermute | solution.py:310
  91.4 1.3 %collective-permute-done.20.refs_0_ = bf16[1024,128]{1,0:T(8,128)(2,1)S(1)} collective-permute-done((bf16[1024,128]{1,0:T(8,128)(2,1)S(1)}, bf16[1024,128]{1,0:T(8,128)(2,1)S(1)}, u32[]{:S(2)}, u32[]{:S(2)}) %collective-permute-start.20) | collective-permute-done | bytes 262176 | tf_op jit(solution)/shard_map/ppermute | solution.py:420
  92.8 3.6 %collective-permute-start.24 = (bf16[1024,128]{1,0:T(8,128)(2,1)S(1)}, bf16[1024,128]{1,0:T(8,128)(2,1)S(1)}, u32[]{:S(2)}, u32[]{:S(2)}) collective-permute-start(bf16[1024,128]{1,0:T(8,128)(2,1)S(1)} %shard_map.106), channel_id=1, source_target_pairs={{0,4},{12,8},{1,5},{13,9},{2,6},{14,10},{3,7},{15,11},{16,20},{28,... | collective-permute-start | bytes 786440 | tf_op jit(solution)/shard_map/ppermute | solution.py:310
  97.0 0.7 collective-permute-start.19
  97.7 2.1 %collective-permute-start.22 = (bf16[1024,128]{1,0:T(8,128)(2,1)S(1)}, bf16[1024,128]{1,0:T(8,128)(2,1)S(1)}, u32[]{:S(2)}, u32[]{:S(2)}) collective-permute-start(bf16[1024,128]{1,0:T(8,128)(2,1)S(1)} %get-tuple-element.95), channel_id=1, source_target_pairs={{0,2},{2,0},{1,3},{3,1},{4,6},{6,4},{5,7},{7,5},{8,10},{10,8},{9,1... | collective-permute-start | bytes 786440 | tf_op jit(solution)/shard_map/ppermute | solution.py:420
  99.8 1.1 collective-permute-done.24.refs_1_
  101.6 2.3 %collective-permute-start.21 = (bf16[1024,128]{1,0:T(8,128)(2,1)S(1)}, bf16[1024,128]{1,0:T(8,128)(2,1)S(1)}, u32[]{:S(2)}, u32[]{:S(2)}) collective-permute-start(bf16[1024,128]{1,0:T(8,128)(2,1)S(1)} %get-tuple-element.93), channel_id=1, source_target_pairs={{0,2},{2,0},{1,3},{3,1},{4,6},{6,4},{5,7},{7,5},{8,10},{10,8},{9,1... | collective-permute-start | bytes 786440 | tf_op jit(solution)/shard_map/ppermute | solution.py:420
  103.9 2.8 %shard_map.103.refs_8_ = bf16[4096,512]{1,0:T(8,128)(2,1)} custom-call(s32[6]{0:T(128)S(1)} %stack.97.meta, bf16[2,128,512]{2,1,0:T(8,128)(2,1)S(1)} %get-tuple-element.75.refs_0_, bf16[2,128,512]{2,1,0:T(8,128)(2,1)S(1)} %collective-permute-done.14.refs_1_, bf16[128,1024]{1,0:T(8,128)(2,1)S(1)} %bitcast.158, ...), custom_call_target="tpu_custom_call" | custom-call | flops 1073741824 | bytes 4194304 | tf_op jit(solution)/shard_map/pallas_call | solution.py:277
  106.7 0.7 collective-permute-start.25
  107.5 4.3 %collective-permute-start.23 = (bf16[1024,128]{1,0:T(8,128)(2,1)S(1)}, bf16[1024,128]{1,0:T(8,128)(2,1)S(1)}, u32[]{:S(2)}, u32[]{:S(2)}) collective-permute-start(bf16[1024,128]{1,0:T(8,128)(2,1)S(1)} %shard_map.105), channel_id=1, source_target_pairs={{0,4},{4,0},{8,12},{12,8},{1,5},{5,1},{9,13},{13,9},{2,6},{6,2},{1... | collective-permute-start | bytes 786440 | tf_op jit(solution)/shard_map/ppermute | solution.py:310
  112.3 3.3 %shard_map.104 = bf16[4096,512]{1,0:T(8,128)(2,1)} custom-call(s32[6]{0:T(128)S(1)} %stack.97.meta, bf16[2,128,512]{2,1,0:T(8,128)(2,1)S(1)} %get-tuple-element.75.refs_0_, bf16[2,128,512]{2,1,0:T(8,128)(2,1)S(1)} %collective-permute-done.14.refs_1_, bf16[128,1024]{1,0:T(8,128)(2,1)S(1)} %add.150.refs_0_.refs_2_, ...), custom_call_target="tpu_custom_call", output_to_operand_aliasing={{}: (9, {})} | custom-call | flops 1073741824 | bytes 4194304 | tf_op jit(solution)/shard_map/pallas_call | solution.py:277
  115.6 2.2 %collective-permute-done.23.refs_1_ = bf16[1024,128]{1,0:T(8,128)(2,1)S(1)} collective-permute-done((bf16[1024,128]{1,0:T(8,128)(2,1)S(1)}, bf16[1024,128]{1,0:T(8,128)(2,1)S(1)}, u32[]{:S(2)}, u32[]{:S(2)}) %collective-permute-start.23) | collective-permute-done | bytes 262176 | tf_op jit(solution)/shard_map/ppermute | solution.py:310
  117.8 0.9 shard_map.108
  (80 shorter events, 5.5 us)
Async XLA Ops:
  0.6 20.4 %collective-permute-start = (bf16[4096,512]{1,0:T(8,128)(2,1)}, bf16[4096,512]{1,0:T(8,128)(2,1)}, u32[]{:S(2)}, u32[]{:S(2)}) collective-permute-start(bf16[4096,512]{1,0:T(8,128)(2,1)} %w.1), channel_id=1, source_target_pairs={{0,1},{1,0},{2,3},{3,2},{4,5},{5,4},{6,7},{7,6},{8,9},{9,8},{10,11... | collective-permute-start | bytes 12582920 | tf_op jit(solution)/shard_map/ppermute | solution.py:309
  1.1 7.6 %collective-permute-start.3 = (bf16[128,1024]{1,0:T(8,128)(2,1)}, bf16[128,1024]{1,0:T(8,128)(2,1)S(1)}, u32[]{:S(2)}, u32[]{:S(2)}) collective-permute-start(bf16[128,1024]{1,0:T(8,128)(2,1)} %bitcast.153), channel_id=1, source_target_pairs={{4,8},{8,4},{5,9},{9,5},{6,10},{10,6},{7,11},{11,7},{20,24},{24,20... | collective-permute-start | bytes 786440 | tf_op jit(solution)/shard_map/ppermute | solution.py:310
  1.8 12.4 %collective-permute-start.1 = (bf16[128,1024]{1,0:T(8,128)(2,1)}, bf16[128,1024]{1,0:T(8,128)(2,1)S(1)}, u32[]{:S(2)}, u32[]{:S(2)}) collective-permute-start(bf16[128,1024]{1,0:T(8,128)(2,1)} %bitcast.154), channel_id=1, source_target_pairs={{0,4},{4,0},{8,12},{12,8},{1,5},{5,1},{9,13},{13,9},{2,6},{6,2},{1... | collective-permute-start | bytes 786440 | tf_op jit(solution)/shard_map/ppermute | solution.py:310
  7.3 13.7 %collective-permute-start.6 = (bf16[128,1024]{1,0:T(8,128)(2,1)}, bf16[128,1024]{1,0:T(8,128)(2,1)S(1)}, u32[]{:S(2)}, u32[]{:S(2)}) collective-permute-start(bf16[128,1024]{1,0:T(8,128)(2,1)} %bitcast.155), channel_id=1, source_target_pairs={{0,2},{2,0},{1,3},{3,1},{4,6},{6,4},{5,7},{7,5},{8,10},{10,8},{9,1... | collective-permute-start | bytes 786440 | tf_op jit(solution)/shard_map/ppermute | solution.py:338
  8.8 17.6 %collective-permute-start.4 = (bf16[128,1024]{1,0:T(8,128)(2,1)S(1)}, bf16[128,1024]{1,0:T(8,128)(2,1)S(1)}, u32[]{:S(2)}, u32[]{:S(2)}) collective-permute-start(bf16[128,1024]{1,0:T(8,128)(2,1)S(1)} %collective-permute-done.3), channel_id=1, source_target_pairs={{4,0},{8,12},{5,1},{9,13},{6,2},{10,14},{7,3},{11,15},{20,16},{24,... | collective-permute-start | bytes 786440 | tf_op jit(solution)/shard_map/ppermute | solution.py:310
  14.2 12.2 %collective-permute-start.5 = (bf16[128,1024]{1,0:T(8,128)(2,1)S(1)}, bf16[128,1024]{1,0:T(8,128)(2,1)S(1)}, u32[]{:S(2)}, u32[]{:S(2)}) collective-permute-start(bf16[128,1024]{1,0:T(8,128)(2,1)S(1)} %collective-permute-done.1.refs_1_.refs_4_), channel_id=1, source_target_pairs={{4,8},{8,4},{5,9},{9,5},{6,10},{10,6},{7,11},{11,7},{20,24},{24,20... | collective-permute-start | bytes 786440 | tf_op jit(solution)/shard_map/ppermute | solution.py:310
  14.8 11.6 %collective-permute-start.2 = (bf16[128,1024]{1,0:T(8,128)(2,1)S(1)}, bf16[128,1024]{1,0:T(8,128)(2,1)S(1)}, u32[]{:S(2)}, u32[]{:S(2)}) collective-permute-start(bf16[128,1024]{1,0:T(8,128)(2,1)S(1)} %collective-permute-done.1.refs_1_.refs_4_), channel_id=1, source_target_pairs={{0,2},{2,0},{1,3},{3,1},{4,6},{6,4},{5,7},{7,5},{8,10},{10,8},{9,1... | collective-permute-start | bytes 786440 | tf_op jit(solution)/shard_map/ppermute | solution.py:338
  16.4 2.2 %copy-start.6 = (bf16[4096,512]{1,0:T(8,128)(2,1)S(1)}, bf16[4096,512]{1,0:T(8,128)(2,1)}, u32[]{:S(2)}) copy-start(bf16[4096,512]{1,0:T(8,128)(2,1)} %w.1) | copy-start | bytes 12582916
  18.6 2.4 %copy-start.7 = (bf16[1024,1,2,64]{0,3,2,1:T(8,128)(2,1)S(1)}, bf16[1024,1,2,64]{0,3,2,1:T(8,128)(2,1)}, u32[]{:S(2)}) copy-start(bf16[1024,1,2,64]{0,3,2,1:T(8,128)(2,1)} %param.7) | copy-start | bytes 786436
  18.9 2.0 %copy-start = (bf16[4096,512]{1,0:T(8,128)(2,1)}, bf16[4096,512]{1,0:T(8,128)(2,1)S(1)}, u32[]{:S(2)}) copy-start(bf16[4096,512]{1,0:T(8,128)(2,1)S(1)} %shard_map.94.w_own) | copy-start | bytes 12582916
  21.0 2.2 %copy-start.1 = (bf16[4096,512]{1,0:T(8,128)(2,1)S(1)}, bf16[4096,512]{1,0:T(8,128)(2,1)}, u32[]{:S(2)}) copy-start(bf16[4096,512]{1,0:T(8,128)(2,1)} %copy-done) | copy-start | bytes 12582916
  26.4 11.8 %copy-start.22 = (bf16[128,1024]{1,0:T(8,128)(2,1)}, bf16[128,1024]{1,0:T(8,128)(2,1)S(1)}, u32[]{:S(2)}) copy-start(bf16[128,1024]{1,0:T(8,128)(2,1)S(1)} %collective-permute-done.5) | copy-start | bytes 786436
  26.4 11.5 %collective-permute-start.7 = (bf16[128,1024]{1,0:T(8,128)(2,1)S(1)}, bf16[128,1024]{1,0:T(8,128)(2,1)}, u32[]{:S(2)}, u32[]{:S(2)}) collective-permute-start(bf16[128,1024]{1,0:T(8,128)(2,1)S(1)} %collective-permute-done.5), channel_id=1, source_target_pairs={{4,0},{8,12},{5,1},{9,13},{6,2},{10,14},{7,3},{11,15},{20,16},{24,... | collective-permute-start | bytes 786440 | tf_op jit(solution)/shard_map/ppermute | solution.py:310
  27.9 12.1 %collective-permute-start.8 = (bf16[128,1024]{1,0:T(8,128)(2,1)S(1)}, bf16[128,1024]{1,0:T(8,128)(2,1)S(1)}, u32[]{:S(2)}, u32[]{:S(2)}) collective-permute-start(bf16[128,1024]{1,0:T(8,128)(2,1)S(1)} %add.150.refs_0_.refs_2_), channel_id=1, source_target_pairs={{0,2},{2,0},{1,3},{3,1},{4,6},{6,4},{5,7},{7,5},{8,10},{10,8},{9,1... | collective-permute-start | bytes 786440 | tf_op jit(solution)/shard_map/ppermute | solution.py:338
  28.5 2.2 %copy-start.2 = (bf16[4096,512]{1,0:T(8,128)(2,1)S(1)}, bf16[4096,512]{1,0:T(8,128)(2,1)}, u32[]{:S(2)}) copy-start(bf16[4096,512]{1,0:T(8,128)(2,1)} %copy-done) | copy-start | bytes 12582916
  30.6 7.3 %copy-start.23 = (s32[2,2,128]{2,1,0:T(2,128)S(1)}, s32[2,2,128]{2,1,0:T(2,128)}, u32[]{:S(2)}) copy-start(s32[2,2,128]{2,1,0:T(2,128)} %param.9) | copy-start | bytes 6148
  33.6 0.8 copy-start.14
  39.4 12.5 %collective-permute-start.9 = (bf16[128,1024]{1,0:T(8,128)(2,1)S(1)}, bf16[128,1024]{1,0:T(8,128)(2,1)}, u32[]{:S(2)}, u32[]{:S(2)}) collective-permute-start(bf16[128,1024]{1,0:T(8,128)(2,1)S(1)} %add.151.refs_0_.refs_4_), channel_id=1, source_target_pairs={{0,2},{2,0},{1,3},{3,1},{4,6},{6,4},{5,7},{7,5},{8,10},{10,8},{9,1... | collective-permute-start | bytes 786440 | tf_op jit(solution)/shard_map/ppermute | solution.py:338
  40.0 2.2 %copy-start.3 = (bf16[4096,512]{1,0:T(8,128)(2,1)S(1)}, bf16[4096,512]{1,0:T(8,128)(2,1)}, u32[]{:S(2)}) copy-start(bf16[4096,512]{1,0:T(8,128)(2,1)} %copy-done) | copy-start | bytes 12582916
  42.2 1.0 copy-start.15
  43.2 7.0 %copy-start.8 = (bf16[128,1024]{1,0:T(8,128)(2,1)}, bf16[128,1024]{1,0:T(8,128)(2,1)S(1)}, u32[]{:S(2)}) copy-start(bf16[128,1024]{1,0:T(8,128)(2,1)S(1)} %collective-permute-done.8.refs_1_.refs_3_) | copy-start | bytes 786436
  46.5 5.2 %copy-start.10 = (f32[128,1024]{1,0:T(8,128)}, f32[128,1024]{1,0:T(8,128)S(1)}, u32[]{:S(2)}) copy-start(f32[128,1024]{1,0:T(8,128)S(1)} %get-tuple-element.67.refs_0_) | copy-start | bytes 1572868
  46.5 5.2 %copy-start.16 = (f32[128,1024]{1,0:T(8,128)}, f32[128,1024]{1,0:T(8,128)S(1)}, u32[]{:S(2)}) copy-start(f32[128,1024]{1,0:T(8,128)S(1)} %get-tuple-element.68.refs_1_) | copy-start | bytes 1572868
  51.7 49.9 %collective-permute-start.15 = (bf16[7,128,1024]{2,1,0:T(8,128)(2,1)}, bf16[7,128,1024]{2,1,0:T(8,128)(2,1)S(1)}, u32[]{:S(2)}, u32[]{:S(2)}) collective-permute-start(bf16[7,128,1024]{2,1,0:T(8,128)(2,1)} %bitcast_dynamic-update-slice_fusion), channel_id=1, source_target_pairs={{0,1},{1,0},{2,3},{3,2},{4,5},{5,4},{6,7},{7,6},{8,9},{9,8},{10,11... | collective-permute-start | bytes 5505032 | tf_op jit(solution)/shard_map/ppermute | solution.py:309
  51.9 2.2 %copy-start.4 = (bf16[4096,512]{1,0:T(8,128)(2,1)S(1)}, bf16[4096,512]{1,0:T(8,128)(2,1)}, u32[]{:S(2)}) copy-start(bf16[4096,512]{1,0:T(8,128)(2,1)} %copy-done) | copy-start | bytes 12582916
  54.1 1.0 copy-start.17
  58.0 0.8 copy-start.12
  58.8 4.5 %collective-permute-start.12 = (f32[2,8,128]{2,1,0:T(8,128)S(1)}, f32[2,8,128]{2,1,0:T(8,128)S(1)}, u32[]{:S(2)}, u32[]{:S(2)}) collective-permute-start(f32[2,8,128]{2,1,0:T(8,128)S(1)} %pad_maximum_fusion), channel_id=1, source_target_pairs={{0,6},{2,4},{4,2},{6,0},{8,14},{10,12},{12,10},{14,8},{1,7},{3,5},... | collective-permute-start | bytes 24584 | tf_op jit(solution)/shard_map/ppermute | solution.py:406
  61.4 3.7 %collective-permute-start.11 = (f32[2,8,128]{2,1,0:T(8,128)S(1)}, f32[2,8,128]{2,1,0:T(8,128)S(1)}, u32[]{:S(2)}, u32[]{:S(2)}) collective-permute-start(f32[2,8,128]{2,1,0:T(8,128)S(1)} %pad_maximum_fusion), channel_id=1, source_target_pairs={{0,4},{4,0},{8,12},{12,8},{1,5},{5,1},{9,13},{13,9},{2,6},{6,2},{1... | collective-permute-start | bytes 24584 | tf_op jit(solution)/shard_map/ppermute | solution.py:310
  61.8 3.7 %collective-permute-start.10 = (f32[2,8,128]{2,1,0:T(8,128)S(1)}, f32[2,8,128]{2,1,0:T(8,128)S(1)}, u32[]{:S(2)}, u32[]{:S(2)}) collective-permute-start(f32[2,8,128]{2,1,0:T(8,128)S(1)} %pad_maximum_fusion), channel_id=1, source_target_pairs={{0,2},{2,0},{1,3},{3,1},{4,6},{6,4},{5,7},{7,5},{8,10},{10,8},{9,1... | collective-permute-start | bytes 24584 | tf_op jit(solution)/shard_map/ppermute | solution.py:338
  65.5 4.7 %collective-permute-start.13 = (f32[8,256]{1,0:T(8,128)S(1)}, f32[8,256]{1,0:T(8,128)}, u32[]{:S(2)}, u32[]{:S(2)}) collective-permute-start(f32[8,256]{1,0:T(8,128)S(1)} %pad_maximum_fusion.1.refs_3_), channel_id=1, source_target_pairs={{0,8},{8,0},{4,12},{12,4},{1,9},{9,1},{5,13},{13,5},{2,10},{10,2},... | collective-permute-start | bytes 24584 | tf_op jit(solution)/shard_map/ppermute | solution.py:310
  70.2 2.2 %copy-start.5 = (bf16[4096,512]{1,0:T(8,128)(2,1)S(1)}, bf16[4096,512]{1,0:T(8,128)(2,1)}, u32[]{:S(2)}) copy-start(bf16[4096,512]{1,0:T(8,128)(2,1)} %copy-done) | copy-start | bytes 12582916
  72.4 1.0 copy-start.11
  73.5 1.0 copy-start.13
  74.5 0.7 copy-start.18
  75.2 0.7 copy-start.19
  75.9 0.7 copy-start.20
  76.5 0.7 copy-start.21
  80.7 7.2 %collective-permute-start.17 = (bf16[1024,128]{1,0:T(8,128)(2,1)S(1)}, bf16[1024,128]{1,0:T(8,128)(2,1)S(1)}, u32[]{:S(2)}, u32[]{:S(2)}) collective-permute-start(bf16[1024,128]{1,0:T(8,128)(2,1)S(1)} %get-tuple-element.86), channel_id=1, source_target_pairs={{0,2},{2,0},{1,3},{3,1},{4,6},{6,4},{5,7},{7,5},{8,10},{10,8},{9,1... | collective-permute-start | bytes 786440 | tf_op jit(solution)/shard_map/ppermute | solution.py:420
  85.9 6.8 %collective-permute-start.20 = (bf16[1024,128]{1,0:T(8,128)(2,1)S(1)}, bf16[1024,128]{1,0:T(8,128)(2,1)S(1)}, u32[]{:S(2)}, u32[]{:S(2)}) collective-permute-start(bf16[1024,128]{1,0:T(8,128)(2,1)S(1)} %get-tuple-element.91), channel_id=1, source_target_pairs={{0,2},{2,0},{1,3},{3,1},{4,6},{6,4},{5,7},{7,5},{8,10},{10,8},{9,1... | collective-permute-start | bytes 786440 | tf_op jit(solution)/shard_map/ppermute | solution.py:420
  88.0 8.9 %collective-permute-start.18 = (bf16[1024,128]{1,0:T(8,128)(2,1)S(1)}, bf16[1024,128]{1,0:T(8,128)(2,1)S(1)}, u32[]{:S(2)}, u32[]{:S(2)}) collective-permute-start(bf16[1024,128]{1,0:T(8,128)(2,1)S(1)} %shard_map.101), channel_id=1, source_target_pairs={{0,4},{12,8},{1,5},{13,9},{2,6},{14,10},{3,7},{15,11},{16,20},{28,... | collective-permute-start | bytes 786440 | tf_op jit(solution)/shard_map/ppermute | solution.py:310
  92.8 8.1 %collective-permute-start.24 = (bf16[1024,128]{1,0:T(8,128)(2,1)S(1)}, bf16[1024,128]{1,0:T(8,128)(2,1)S(1)}, u32[]{:S(2)}, u32[]{:S(2)}) collective-permute-start(bf16[1024,128]{1,0:T(8,128)(2,1)S(1)} %shard_map.106), channel_id=1, source_target_pairs={{0,4},{12,8},{1,5},{13,9},{2,6},{14,10},{3,7},{15,11},{16,20},{28,... | collective-permute-start | bytes 786440 | tf_op jit(solution)/shard_map/ppermute | solution.py:310
  96.4 4.6 %collective-permute-start.14 = (bf16[2,128,512]{2,1,0:T(8,128)(2,1)S(1)}, bf16[2,128,512]{2,1,0:T(8,128)(2,1)S(1)}, u32[]{:S(2)}, u32[]{:S(2)}) collective-permute-start(bf16[2,128,512]{2,1,0:T(8,128)(2,1)S(1)} %get-tuple-element.76), channel_id=1, source_target_pairs={{0,1},{1,0},{2,3},{3,2},{4,5},{5,4},{6,7},{7,6},{8,9},{9,8},{10,11... | collective-permute-start | bytes 786440 | tf_op jit(solution)/shard_map/ppermute | solution.py:309
  97.0 9.7 %collective-permute-start.19 = (bf16[1024,128]{1,0:T(8,128)(2,1)S(1)}, bf16[1024,128]{1,0:T(8,128)(2,1)S(1)}, u32[]{:S(2)}, u32[]{:S(2)}) collective-permute-start(bf16[1024,128]{1,0:T(8,128)(2,1)S(1)} %shard_map.102), channel_id=1, source_target_pairs={{4,8},{8,4},{5,9},{9,5},{6,10},{10,6},{7,11},{11,7},{20,24},{24,20... | collective-permute-start | bytes 786440 | tf_op jit(solution)/shard_map/ppermute | solution.py:310
  97.7 9.7 %collective-permute-start.22 = (bf16[1024,128]{1,0:T(8,128)(2,1)S(1)}, bf16[1024,128]{1,0:T(8,128)(2,1)S(1)}, u32[]{:S(2)}, u32[]{:S(2)}) collective-permute-start(bf16[1024,128]{1,0:T(8,128)(2,1)S(1)} %get-tuple-element.95), channel_id=1, source_target_pairs={{0,2},{2,0},{1,3},{3,1},{4,6},{6,4},{5,7},{7,5},{8,10},{10,8},{9,1... | collective-permute-start | bytes 786440 | tf_op jit(solution)/shard_map/ppermute | solution.py:420
  100.9 10.9 %collective-permute-start.26 = (f32[1,128]{1,0:T(1,128)S(1)}, f32[1,128]{1,0:T(1,128)S(1)}, u32[]{:S(2)}, u32[]{:S(2)}) collective-permute-start(f32[1,128]{1,0:T(1,128)S(1)} %get-tuple-element.100), channel_id=1, source_target_pairs={{0,1},{1,0},{2,3},{3,2},{4,5},{5,4},{6,7},{7,6},{8,9},{9,8},{10,11... | collective-permute-start | bytes 1544 | tf_op jit(solution)/shard_map/ppermute | solution.py:309
  101.0 11.3 %collective-permute-start.16 = (bf16[1,128,1024]{2,1,0:T(8,128)(2,1)}, bf16[1,128,1024]{2,1,0:T(8,128)(2,1)S(1)}, u32[]{:S(2)}, u32[]{:S(2)}) collective-permute-start(bf16[1,128,1024]{2,1,0:T(8,128)(2,1)} %bitcast.38), channel_id=1, source_target_pairs={{0,1},{1,0},{2,3},{3,2},{4,5},{5,4},{6,7},{7,6},{8,9},{9,8},{10,11... | collective-permute-start | bytes 786440 | tf_op jit(solution)/shard_map/ppermute | solution.py:309
  101.6 14.0 %collective-permute-start.21 = (bf16[1024,128]{1,0:T(8,128)(2,1)S(1)}, bf16[1024,128]{1,0:T(8,128)(2,1)S(1)}, u32[]{:S(2)}, u32[]{:S(2)}) collective-permute-start(bf16[1024,128]{1,0:T(8,128)(2,1)S(1)} %get-tuple-element.93), channel_id=1, source_target_pairs={{0,2},{2,0},{1,3},{3,1},{4,6},{6,4},{5,7},{7,5},{8,10},{10,8},{9,1... | collective-permute-start | bytes 786440 | tf_op jit(solution)/shard_map/ppermute | solution.py:420
  103.9 8.4 %copy-start.9 = (bf16[128,1024]{1,0:T(8,128)(2,1)S(1)}, bf16[128,1024]{1,0:T(8,128)(2,1)}, u32[]{:S(2)}) copy-start(bf16[128,1024]{1,0:T(8,128)(2,1)} %copy-done.8) | copy-start | bytes 786436
  106.7 8.9 %collective-permute-start.25 = (bf16[1024,128]{1,0:T(8,128)(2,1)S(1)}, bf16[1024,128]{1,0:T(8,128)(2,1)S(1)}, u32[]{:S(2)}, u32[]{:S(2)}) collective-permute-start(bf16[1024,128]{1,0:T(8,128)(2,1)S(1)} %shard_map.107), channel_id=1, source_target_pairs={{4,8},{8,4},{5,9},{9,5},{6,10},{10,6},{7,11},{11,7},{20,24},{24,20... | collective-permute-start | bytes 786440 | tf_op jit(solution)/shard_map/ppermute | solution.py:310
  107.5 10.3 %collective-permute-start.23 = (bf16[1024,128]{1,0:T(8,128)(2,1)S(1)}, bf16[1024,128]{1,0:T(8,128)(2,1)S(1)}, u32[]{:S(2)}, u32[]{:S(2)}) collective-permute-start(bf16[1024,128]{1,0:T(8,128)(2,1)S(1)} %shard_map.105), channel_id=1, source_target_pairs={{0,4},{4,0},{8,12},{12,8},{1,5},{5,1},{9,13},{13,9},{2,6},{6,2},{1... | collective-permute-start | bytes 786440 | tf_op jit(solution)/shard_map/ppermute | solution.py:310

commit v6 on v5

--- a/solution.py
+++ b/solution.py
@@ -9,7 +9,8 @@
 
 BETA = 0.1
 F32, BF16 = jnp.float32, jnp.bfloat16
-VMEM_BYTES = 16 * 1024 * 1024
+VMEM_BYTES = 40 * 1024 * 1024
+WORK_BYTES = 32 * 1024 * 1024
 IN_VMEM = pl.BlockSpec(memory_space=pltpu.VMEM)
 IN_SMEM = pl.BlockSpec(memory_space=pltpu.SMEM)
 IN_PLACE = pl.BlockSpec(memory_space=pl.ANY)
@@ -36,8 +37,13 @@
     return jax.ShapeDtypeStruct(shape, kind)
 
 
+def work_shape(w):
+    times = max(2, -(-WORK_BYTES // (w.size * w.dtype.itemsize)))
+    return shape_of((times * w.shape[0], w.shape[1]), w.dtype)
+
+
 def hold_kernel(w, out, sem):
-    copy = pltpu.make_async_copy(w, out, sem)
+    copy = pltpu.make_async_copy(w, out.at[pl.ds(0, w.shape[0]), :], sem)
     copy.start()
     copy.wait()
 
@@ -45,13 +51,23 @@
 def hold(w):
     return pl.pallas_call(
         hold_kernel,
-        out_shape=shape_of(w.shape, w.dtype),
+        out_shape=work_shape(w),
         in_specs=[IN_PLACE],
-        out_specs=IN_VMEM,
+        out_specs=IN_PLACE,
         scratch_shapes=[pltpu.SemaphoreType.DMA],
         compiler_params=params(),
         cost_estimate=cost(1, 4 * w.size),
     )(w)
+
+
+def fetch(work, width, start, part, slots, i, sems, far=None):
+    own = work.at[pl.ds(start, part), :]
+    far = work.at[pl.ds(width + start, part), :] if far is None else far.at[pl.ds(start, part), :]
+    copies = []
+    for j, w in enumerate((own, far)):
+        copies.append(pltpu.make_async_copy(w, slots.at[i, j], sems.at[i, j]))
+        copies[-1].start()
+    return copies
 
 
 def row_stats(own, far, wanted, first_own, first_far):
@@ -68,59 +84,79 @@
     return jnp.where(lane == 0, top, jnp.where(lane == 1, total, picked)).T[:8, :]
 
 
-def logits_kernel(plan, columns, part, n_voc, meta, w_own, w_far, *refs):
+def logits_kernel(plan, columns, part, n_voc, fresh, meta, work, *refs):
     refs = list(refs)
+    width = part * n_voc
+    far = refs.pop(0) if fresh else None
     chunks = {(t, i): refs.pop(0) for t, parts, _, _ in plan for i in parts}
     accs = {t: refs.pop(0) for t, _, has_acc, _ in plan if has_acc}
     wanted = {t: refs.pop(0) for t, _, _, done in plan if done}
     used = sorted({i for _, parts, _, _ in plan for i in parts})
+    slots, sems = refs[-2:]
+    coming = [
+        fetch(work, width, pl.multiple_of(meta[i] * part, part), part, slots, n, sems, far) for n, i in enumerate(used)
+    ]
+    if fresh:
+        kept = pltpu.make_async_copy(far, refs[-3].at[pl.ds(width, width), :], sems.at[len(used), 0])
+        kept.start()
     outs = {}
     stats = {}
     for t, _, _, done in plan:
         outs[t] = refs.pop(0)
         if done:
             stats[t] = refs.pop(0)
-    for i in used:
-        at_part = pl.ds(pl.multiple_of(meta[i] * part, part), part)
+    for n, i in enumerate(used):
+        for copy in coming[n]:
+            copy.wait()
         for t, parts, has_acc, _ in plan:
             if i not in parts:
                 continue
             x = chunks[t, i][...]
-            for j, w in enumerate((w_own, w_far)):
+            for j in range(2):
                 at = slice(j * columns, (j + 1) * columns)
-                product = jnp.dot(x, w[at_part, :], preferred_element_type=F32)
+                product = jnp.dot(x, slots[n, j], preferred_element_type=F32)
                 if i != parts[0]:
                     product += outs[t][:, at]
                 elif has_acc:
                     product += accs[t][:, at]
                 outs[t][:, at] = product
     for t in stats:
-        own, far = outs[t][:, :columns], outs[t][:, columns:]
-        stats[t][...] = row_stats(own, far, wanted[t][...], meta[n_voc], meta[n_voc + 1])
-
-
-def logits_call(plan, meta, weights, part, n_voc):
-    columns = weights[0].shape[1]
-    chunks = [c for _, parts, _, _ in plan for c in parts.values()]
+        own, beside = outs[t][:, :columns], outs[t][:, columns:]
+        stats[t][...] = row_stats(own, beside, wanted[t][...], meta[n_voc], meta[n_voc + 1])
+    if fresh:
+        kept.wait()
+
+
+def logits_call(plan, work, meta, part, n_voc, far=None):
+    columns = work.shape[1]
     accs = [acc for _, _, acc, _ in plan if acc is not None]
     wanted = [w for _, _, _, w in plan if w is not None]
+    chunks = [parts[i] for _, parts, _, _ in plan for i in sorted(parts)]
     rows = chunks[0].shape[0]
     out_shape = []
     for _, _, _, w in plan:
         out_shape.append(shape_of((rows, 2 * columns), F32))
         if w is not None:
             out_shape.append(shape_of((8, rows), F32))
+    out_specs = [IN_VMEM] * len(out_shape)
     kernel_plan = [(t, sorted(parts), acc is not None, w is not None) for t, parts, acc, w in plan]
-    chunks = [parts[i] for _, parts, _, _ in plan for i in sorted(parts)]
-    operands = list(weights) + chunks + accs + wanted
+    n_used = len({i for _, parts, _, _ in plan for i in parts})
+    fresh = far is not None
+    in_place = [work] + ([far] if fresh else [])
+    if fresh:
+        out_shape.append(shape_of(work.shape, work.dtype))
+        out_specs.append(IN_PLACE)
+    operands = chunks + accs + wanted
     return pl.pallas_call(
-        functools.partial(logits_kernel, kernel_plan, columns, part, n_voc),
+        functools.partial(logits_kernel, kernel_plan, columns, part, n_voc, fresh),
         out_shape=out_shape,
-        in_specs=[IN_SMEM] + [IN_VMEM] * len(operands),
-        out_specs=[IN_VMEM] * len(out_shape),
+        in_specs=[IN_SMEM] + [IN_PLACE] * len(in_place) + [IN_VMEM] * len(operands),
+        out_specs=out_specs,
+        scratch_shapes=[pltpu.VMEM((n_used, 2, part, columns), BF16), pltpu.SemaphoreType.DMA((n_used + fresh, 2))],
+        input_output_aliases={1: len(out_shape) - 1} if fresh else {},
         compiler_params=params(),
-        cost_estimate=cost(4 * len(chunks) * rows * part * columns, len(chunks) * 4 * part * columns),
-    )(meta, *operands)
+        cost_estimate=cost(4 * len(chunks) * rows * part * columns, n_used * 4 * part * columns),
+    )(meta, *in_place, *operands)
 
 
 def spread(flipped_own, flipped_far, w_own, w_far, kept, send):
@@ -132,13 +168,15 @@
         out[...] = here[:, t * rows:(t + 1) * rows].astype(BF16)
 
 
-def grads_kernel(n_blocks, n_stats, columns, part, window, meta, start, sums, refer, cotangent, w_own, w_far, *refs):
+def grads_kernel(n_blocks, n_stats, columns, part, width, window, meta, start, sums, refer, cotangent, work, *refs):
     refs = list(refs)
     logits = [refs.pop(0) for _ in range(n_blocks)]
     target = refs.pop(0)
     stats = [refs.pop(0) for _ in range(n_stats)]
+    slots, sems = refs[-2:]
     grads_own, grads_far, flipped_own, flipped_far, loss, kept = refs[:6]
-    send = refs[6:]
+    send = refs[6:-2]
+    coming = fetch(work, width, pl.multiple_of(meta[0] * part, part), part, slots, 0, sems)
     rows = logits[0].shape[0]
     pair, me_ctx = meta[3], meta[4]
     top = stats[0][0:1, :]
@@ -176,50 +214,62 @@
             g = weight_t * (hit - jnp.exp(l - top_t) * inverse_t)
             grads[t] = g.astype(BF16)
             flipped[:, at] = g.T.astype(BF16)
-    at_part = pl.ds(pl.multiple_of(meta[0] * part, part), part)
-    spread(flipped_own[...], flipped_far[...], w_own[at_part, :], w_far[at_part, :], kept, send)
-
-
-def spread_kernel(part, n_parts, meta, w_own, w_far, flipped_own, flipped_far, *outs):
+    for copy in coming:
+        copy.wait()
+    spread(flipped_own[...], flipped_far[...], slots[0, 0], slots[0, 1], kept, send)
+
+
+def spread_kernel(part, width, n_parts, meta, work, flipped_own, flipped_far, *refs):
+    outs, slots, sems = refs[:-2], refs[-2], refs[-1]
     each = len(outs) // n_parts
+    coming = [
+        fetch(work, width, pl.multiple_of(meta[i] * part, part), part, slots, i, sems) for i in range(n_parts)
+    ]
     for i in range(n_parts):
+        for copy in coming[i]:
+            copy.wait()
         kept, *send = outs[i * each:(i + 1) * each]
-        at_part = pl.ds(pl.multiple_of(meta[i] * part, part), part)
-        spread(flipped_own[...], flipped_far[...], w_own[at_part, :], w_far[at_part, :], kept, send)
+        spread(flipped_own[...], flipped_far[...], slots[i, 0], slots[i, 1], kept, send)
 
 
 def spread_shapes(n_blocks, rows, part):
     return [shape_of((part, rows), F32)] + [shape_of((part, rows), BF16)] * (n_blocks - 1)
 
 
-def grads_call(logits, target, stats, small, weights, meta, part, window):
-    n_blocks, rows, columns = len(logits), logits[0].shape[0], weights[0].shape[1]
+def weight_slots(n_parts, part, columns):
+    return [pltpu.VMEM((n_parts, 2, part, columns), BF16), pltpu.SemaphoreType.DMA((n_parts, 2))]
+
+
+def grads_call(logits, target, stats, small, work, meta, part, width, window):
+    n_blocks, rows, columns = len(logits), logits[0].shape[0], work.shape[1]
     grads = shape_of((n_blocks, rows, columns), BF16)
     flipped = shape_of((columns, n_blocks * rows), BF16)
     out_shape = [grads, grads, flipped, flipped, shape_of((1, 128), F32)] + spread_shapes(n_blocks, rows, part)
     operands = list(logits) + [target] + list(stats)
     return pl.pallas_call(
-        functools.partial(grads_kernel, n_blocks, len(stats), columns, part, window),
+        functools.partial(grads_kernel, n_blocks, len(stats), columns, part, width, window),
         out_shape=out_shape,
-        in_specs=[IN_SMEM] * 5 + [IN_VMEM] * (2 + len(operands)),
+        in_specs=[IN_SMEM] * 5 + [IN_PLACE] + [IN_VMEM] * len(operands),
         out_specs=[IN_VMEM] * len(out_shape),
+        scratch_shapes=weight_slots(1, part, columns),
         compiler_params=params(),
         cost_estimate=cost(4 * n_blocks * rows * part * columns, 8 * part * columns),
-    )(meta, *small, *weights, *operands)
-
-
-def spread_call(flipped_own, flipped_far, weights, k_ids, part, rows):
+    )(meta, *small, work, *operands)
+
+
+def spread_call(flipped_own, flipped_far, work, k_ids, part, width, rows):
     columns, n_rows = flipped_own.shape
     n_parts = len(k_ids)
     out_shape = spread_shapes(n_rows // rows, rows, part) * n_parts
     outs = pl.pallas_call(
-        functools.partial(spread_kernel, part, n_parts),
+        functools.partial(spread_kernel, part, width, n_parts),
         out_shape=out_shape,
-        in_specs=[IN_SMEM] + [IN_VMEM] * 4,
+        in_specs=[IN_SMEM] + [IN_PLACE] + [IN_VMEM] * 2,
         out_specs=[IN_VMEM] * len(out_shape),
+        scratch_shapes=weight_slots(n_parts, part, columns),
         compiler_params=params(),
         cost_estimate=cost(4 * n_parts * n_rows * part * columns, 4 * n_parts * part * columns),
-    )(jnp.stack(k_ids).astype(jnp.int32), *weights, flipped_own, flipped_far)
+    )(jnp.stack(k_ids).astype(jnp.int32), work, flipped_own, flipped_far)
     each = len(outs) // n_parts
     return [(outs[i * each], list(outs[i * each + 1:(i + 1) * each])) for i in range(n_parts)]
 
@@ -281,7 +331,7 @@
         out_specs=IN_PLACE,
         scratch_shapes=[pltpu.VMEM((2, part, columns), BF16), pltpu.SemaphoreType.DMA((2,))],
         input_output_aliases={1 + len(operands): 0} if here else {},
-        compiler_params=params(),
+        compiler_params=pltpu.CompilerParams(vmem_limit_bytes=16 * 1024 * 1024),
         cost_estimate=cost(
             4 * n_blocks * rows * len(slots_here) * part * columns,
             4 * n_blocks * len(slots_here) * rows * part + 2 * len(slots_here) * part * columns,
@@ -319,7 +369,9 @@
     ]
     meta = jnp.stack(part_of + firsts).astype(jnp.int32)
 
-    weights = (hold(head_weight), dp_swap(head_weight))
+    far_weights = dp_swap(head_weight)
+    work = hold(head_weight)
+    width = head_weight.shape[0]
 
     pair = lax.broadcasted_iota(jnp.int32, targets.shape, 0)
 
@@ -334,7 +386,7 @@
 
     own = hidden.transpose(1, 2, 3, 0).reshape(rows, part)
     final = n_voc - 1
-    call = functools.partial(logits_call, meta=meta, weights=weights, part=part, n_voc=n_voc)
+    call = functools.partial(logits_call, meta=meta, part=part, n_voc=n_voc)
     cross = lambda a: [lax.ppermute(a, "ctx", ring(n_ctx, t)) for t in beyond]
     chunk = {}
 
@@ -343,21 +395,27 @@
         for t, a in zip(beyond, over):
             chunk[t, i] = a
 
+    def first_logits(work):
+        plan = [(0, {j: chunk[0, j] for j in (0, 1)}, None, None)]
+        plan += [(t, {0: chunk[t, 0]}, None, None) for t in beyond]
+        *logits, work = call(plan, work, far=far_weights)
+        return logits, work
+
     def more_logits(i, logits):
-        if logits is None:
-            return call([(0, {j: chunk[0, j] for j in (0, 1)}, None, None)] + [(t, {0: chunk[t, 0]}, None, None) for t in beyond])
-        return call(
-            [(0, {i: chunk[0, i]}, logits[0], None)] + [(t, {i - 1: chunk[t, i - 1]}, logits[t], None) for t in beyond]
-        )
+        plan = [(0, {i: chunk[0, i]}, logits[0], None)]
+        plan += [(t, {i - 1: chunk[t, i - 1]}, logits[t], None) for t in beyond]
+        return call(plan, work)
 
     arrive(0, own, cross(own))
     if line:
         first = along(own, PAIRS_OUT)
         inner = along(own, PAIR_IN)
+        (first, inner), (work,) = together([first, inner], [work])
         over = cross(first)
         outer, inner_last = along(inner, TO_ENDS), along(first, PAIR_IN)
         arrive(1, first, over)
-        over, (inner, outer, inner_last), logits = together(over, [inner, outer, inner_last], more_logits(1, None))
+        logits, work = first_logits(work)
+        over, (inner, outer, inner_last), logits = together(over, [inner, outer, inner_last], logits)
         arrive(1, first, over)
         arrive(2, inner + outer, cross(inner + outer))
         outer = along(inner_last, TO_ENDS)
@@ -368,7 +426,11 @@
         logits = None
         for i in range(1, final):
             arrive(i, near[i], cross(near[i]))
-            (near[i + 1],), logits = together([near[i + 1]], more_logits(i, logits))
+            if logits is None:
+                logits, work = first_logits(work)
+            else:
+                logits = more_logits(i, logits)
+            (near[i + 1],), logits = together([near[i + 1]], logits)
         last = near[final]
     arrive(final, last, cross(last))
     (raw_targets,), _ = together([targets], logits)
@@ -377,10 +439,11 @@
 
     done = call(
         [(0, {final: chunk[0, final]}, logits[0], wanted[0])]
-        + [(t, {final - 1: chunk[t, final - 1]}, logits[t], None) for t in beyond]
+        + [(t, {final - 1: chunk[t, final - 1]}, logits[t], None) for t in beyond],
+        work,
     )
     logits, stats = [done[0]] + list(done[2:]), [done[1]]
-    done = call([(t, {final: chunk[t, final]}, logits[t], wanted[t]) for t in beyond])
+    done = call([(t, {final: chunk[t, final]}, logits[t], wanted[t]) for t in beyond], work)
     logits = [logits[0]] + list(done[0::2])
     stats = stats + list(done[1::2])
 
@@ -413,36 +476,52 @@
     meta_grads = jnp.stack([part_of[final]] + firsts + [me_dp, me_ctx]).astype(jnp.int32)
     small = (response_start, other_sums, ref_logp, loss_cotangent)
     grads_own, grads_far, flipped_own, flipped_far, loss, kept, *send = grads_call(
-        logits, target, all_stats, small, weights, meta_grads, part, window
+        logits, target, all_stats, small, work, meta_grads, part, width, window
     )
     theirs = dp_swap(grads_far)
     far_late = dp_swap(jnp.stack(together([chunk[k] for k in late], [kept])[0]))
     back = lambda cs: [lax.ppermute(c, "ctx", ring(n_ctx, -t)) for t, c in zip(beyond, cs)]
     shares = {final: (kept, list(send))}
     leave = list(range(final))[::-1]
-    for i, share in zip(leave, spread_call(flipped_own, flipped_far, weights, [part_of[i] for i in leave], part, rows)):
+    for i, share in zip(leave, spread_call(flipped_own, flipped_far, work, [part_of[i] for i in leave], part, width, rows)):
         shares[i] = share
 
     over = {}
+    near_over = lambda i, *more: add_call(shares[i][0], over[i] + list(more))
+    head = functools.partial(head_call, near=chunk, far=[(soon, far_soon), (late, far_late)], meta=meta)
+    early, rest = list(range(n_voc // 2)), list(range(n_voc // 2, n_voc))
+    landed, grad_head = [], None
     for i in range(n_voc)[::-1]:
-        send = shares[i][1]
-        if i + 2 in over:
-            over[i + 2], send = together(over[i + 2], send)
-        over[i] = back(send)
-    near_over = lambda i, *more: add_call(shares[i][0], over[i] + list(more))
-    head = functools.partial(head_call, near=chunk, far=[(soon, far_soon), (late, far_late)], grads=[grads_own, theirs], meta=meta)
-    early, rest = list(range(n_voc // 2)), list(range(n_voc // 2, n_voc))
-    grad_head = head(early)
-    if line:
-        up_3 = along(near_over(3), FROM_ENDS)
-        up_2 = along(near_over(2), FROM_ENDS)
-        up_3 = along(near_over(3, up_3), PAIR_IN)
-        (up_3,), (grad_head,) = together([up_3], [grad_head])
-        landed = [along(near_over(1, up_3), PAIRS_OUT), along(near_over(2, up_2), PAIR_IN)]
-    else:
-        landed = [along(near_over(i), ring(n_voc, -i)) for i in range(1, n_voc)]
-    grad_head = head(rest, out=grad_head)
-    (kept,), (grad_head,) = together([shares[0][0]], [grad_head])
+        over[i] = back(shares[i][1])
+        came, beside = [], []
+        if not line:
+            came = [along(near_over(i + 1), ring(n_voc, -(i + 1)))] if i < final else []
+        elif i == 2:
+            came = [along(near_over(3), FROM_ENDS)]
+        elif i == 1:
+            came = [along(near_over(3, landed[0]), PAIR_IN), along(near_over(2), FROM_ENDS)]
+        elif i == 0:
+            came = [along(near_over(1, landed[0]), PAIRS_OUT), along(near_over(2, landed[1]), PAIR_IN)]
+        if i == 0:
+            beside = [head(rest, grads=[grads_own, theirs], out=grad_head)]
+        elif i == 1:
+            beside = [head(early, grads=[grads_own, theirs])]
+        elif i == final:
+            beside = [a for j in leave for a in [shares[j][0]] + shares[j][1]]
+        elif i == final - 1:
+            beside = [theirs, far_late]
+        over[i], came, beside = together(over[i], came, beside)
+        landed = came if line else landed + came
+        if i <= 1:
+            grad_head, = beside
+        elif i == final:
+            for j in leave:
+                shares[j] = (beside[0], beside[1:n_ctx])
+                beside = beside[n_ctx:]
+        elif i == final - 1:
+            theirs, far_late = beside
+            head = functools.partial(head_call, near=chunk, far=[(soon, far_soon), (late, far_late)], meta=meta)
+    kept = shares[0][0]
     summed = add_call(kept, over[0] + landed, turned=True)
     grad_hidden = summed.reshape(1, sides, window, part).transpose(3, 0, 1, 2)
 

time: 120 us -> 232 us (1.93)
  Pallas kernels: 27.4 us -> 156 us
  local copies, waits for them, and re-layouts: 30 us -> 17.1 us
  starting transfers between devices: 39.7 us -> 32.5 us
  waiting for transfers between devices: 18 us -> 20.7 us
    pallas_call x4, Pallas kernels: 12.3 us -> 139 us  [logits_call(): pl.pallas_call(functools.partial(logits_kernel, kernel_plan, columns, par...]
    unnamed x54 -> x42, local copies, waits for them, and re-layouts: 28 us -> 15 us
    ppermute x12, starting transfers between devices: 24.1 us -> 20.6 us  [shards(): along = lambda a, by: lax.ppermute(a, 'vocab', by)]
    pallas_call x2, Pallas kernels: 4.27 us -> 7.28 us  [the longest x1 5.31 us: spread_call(): pl.pallas_call(functools.partial(spread_kernel, part, width, n_parts), ou...]
  transfers between devices with their start and end apart: 27 -> 27, of which waited for: 11 -> 9; matrix products, arithmetic and copies ran while one was open for 8% -> 4% of each run, Pallas kernels for 22% -> 68%
where the time goes in v6:
time: 232 us; the launch traced here: 230 us
  Pallas kernels  156 us (67%)
  starting transfers between devices  32.5 us (14%)
  waiting for transfers between devices  20.7 us (9%)
  local copies, waits for them, and re-layouts  17.1 us (7%)
  other arithmetic  2.54 us (1%)
    pallas_call x4, Pallas kernels, logits_call(): pl.pallas_call(functools.partial(logits_kernel, kernel_plan, columns, par...  139 us
    ppermute x12, starting transfers between devices, shards(): along = lambda a, by: lax.ppermute(a, 'vocab', by)  20.6 us
    unnamed x42, local copies, waits for them, and re-layouts  15 us
    ppermute x12, waiting for transfers between devices, shards(): along = lambda a, by: lax.ppermute(a, 'vocab', by)  13.7 us
    pallas_call x2, Pallas kernels, head_call(): pl.pallas_call(functools.partial(head_kernel, slots_here, list(near), [ke...  6.09 us
    pallas_call x1, Pallas kernels, spread_call(): pl.pallas_call(functools.partial(spread_kernel, part, width, n_parts), ou...  5.31 us
    ppermute x4, starting transfers between devices, shards(): lax.ppermute(c, 'ctx', ring(n_ctx, -t))  5.02 us
    ppermute x5, starting transfers between devices, shards(): cross = lambda a: [lax.ppermute(a, 'ctx', ring(n_ctx, t)) for t in beyond]  4.78 us
  transfers between devices with their start and end apart: 27, of which 9 were waited for; matrix products, arithmetic and copies ran while one was open for 4% of the time, Pallas kernels for 68%

profile of v6, /device:TPU:0, one launch (start us, length us, event | category | flops | bytes accessed | tf_op | source)
XLA Modules:
  0.0 230.2 jit_solution(7373696534779791310)
XLA Ops:
  0.6 0.5 collective-permute-start.2
  1.1 2.7 %collective-permute-start = (bf16[128,1024]{1,0:T(8,128)(2,1)}, bf16[128,1024]{1,0:T(8,128)(2,1)S(1)}, u32[]{:S(2)}, u32[]{:S(2)}) collective-permute-start(bf16[128,1024]{1,0:T(8,128)(2,1)} %bitcast.153), channel_id=1, source_target_pairs={{0,4},{4,0},{8,12},{12,8},{1,5},{5,1},{9,13},{13,9},{2,6},{6,2},{1... | collective-permute-start | bytes 786440 | tf_op jit(solution)/shard_map/ppermute | solution.py:360
  3.8 0.7 collective-permute-start.1
  4.5 1.6 collective-permute-start.3
  6.0 2.2 copy-done
  8.2 2.0 shard_map.94.work
  10.2 0.7 collective-permute-done.refs_2_.refs_4_
  10.9 1.7 collective-permute-start.4
  12.6 1.3 collective-permute-start.5
  13.9 0.7 collective-permute-start.6
  14.7 128.8 %shard_map.95 = (f32[128,1024]{1,0:T(8,128)S(1)}, f32[128,1024]{1,0:T(8,128)S(1)}, bf16[32768,512]{1,0:T(8,128)(2,1)}) custom-call(s32[6]{0:T(128)S(1)} %stack.96.meta, bf16[32768,512]{1,0:T(8,128)(2,1)} %shard_map.94.work, bf16[4096,512]{1,0:T(8,128)(2,1)} %collective-permute-done.2.refs_0_, ...), custom_call_target="tpu_custom_call", output_to_operand_aliasing={{2}: (1, {})} | custom-call | flops 805306368 | bytes 4194304 | tf_op jit(solution)/shard_map/pallas_call | solution.py:150
  143.5 1.3 collective-permute-start.7
  145.0 0.4 collective-permute-start.8
  145.4 3.2 %shard_map.96 = (f32[128,1024]{1,0:T(8,128)S(1)}, f32[128,1024]{1,0:T(8,128)S(1)}) custom-call(s32[6]{0:T(128)S(1)} %stack.96.meta, bf16[32768,512]{1,0:T(8,128)(2,1)} %get-tuple-element.69.work, bf16[128,1024]{1,0:T(8,128)(2,1)S(1)} %add.150.refs_0_.refs_2_, bf16[128,1024]{1,0:T(8,128)(2,1)S(1)} %collective-permute-done.4.refs_1_.refs_5_, ...), custom_call_target="tpu_custom_call" | custom-call | flops 536870912 | bytes 4194304 | tf_op jit(solution)/shard_map/pallas_call | solution.py:150
  148.6 0.8 copy-done.4
  149.4 8.3 %collective-permute-done.7 = bf16[128,1024]{1,0:T(8,128)(2,1)} collective-permute-done((bf16[128,1024]{1,0:T(8,128)(2,1)S(1)}, bf16[128,1024]{1,0:T(8,128)(2,1)}, u32[]{:S(2)}, u32[]{:S(2)}) %collective-permute-start.7) | collective-permute-done | bytes 262176 | tf_op jit(solution)/shard_map/ppermute | solution.py:360
  158.1 1.1 add.151.refs_0_.refs_4_
  159.2 0.6 collective-permute-start.9
  159.8 1.0 copy-done.5
  160.8 3.4 %shard_map.97 = (f32[128,1024]{1,0:T(8,128)S(1)}, f32[8,128]{1,0:T(8,128)S(1)}, f32[128,1024]{1,0:T(8,128)S(1)}) custom-call(s32[6]{0:T(128)S(1)} %stack.96.meta, bf16[32768,512]{1,0:T(8,128)(2,1)} %get-tuple-element.69.work, bf16[128,1024]{1,0:T(8,128)(2,1)S(1)} %add.151.refs_0_.refs_4_, bf16[128,1024]{1,0:T(8,128)(2,1)S(1)} %collective-permute-done.8.refs_1_.refs_3_, ...), custom_call_target="tpu_custom_call" | custom-call | flops 536870912 | bytes 4194304 | tf_op jit(solution)/shard_map/pallas_call | solution.py:150
  164.3 0.8 bitcast_dynamic-update-slice_fusion.6
  165.1 0.7 bitcast_dynamic-update-slice_fusion.5
  165.8 0.7 bitcast_dynamic-update-slice_fusion.4
  166.5 0.7 bitcast_dynamic-update-slice_fusion.3
  167.3 0.7 bitcast_dynamic-update-slice_fusion.2
  168.0 0.7 bitcast_dynamic-update-slice_fusion.1
  168.7 0.7 bitcast_dynamic-update-slice_fusion
  169.6 1.0 copy-done.7
  170.7 3.2 %shard_map.98 = (f32[128,1024]{1,0:T(8,128)S(1)}, f32[8,128]{1,0:T(8,128)S(1)}) custom-call(s32[6]{0:T(128)S(1)} %stack.96.meta, bf16[32768,512]{1,0:T(8,128)(2,1)} %get-tuple-element.69.work, bf16[128,1024]{1,0:T(8,128)(2,1)} %collective-permute-done.9.refs_0_.refs_5_, f32[128,1024]{1,0:T(8,128)S(1)} %copy-done.7, s32[128,1]{1,0:T(8,128)S(1)} %copy.17.refs_2_), custom_call_target="tpu_custom_call" | custom-call | flops 268435456 | bytes 2097152 | tf_op jit(solution)/shard_map/pallas_call | solution.py:150
  173.9 0.8 copy-done.10
  174.7 1.0 collective-permute-start.12
  175.7 2.0 collective-permute-start.11
  177.7 0.5 collective-permute-start.10
  178.3 1.0 collective-permute-done.12
  179.3 0.1 collective-permute-done.11
  179.4 1.9 collective-permute-done.10
  181.4 0.1 collective-permute-start.13
  181.5 0.6 pad_add_fusion
  182.1 0.8 copy.18.refs_2_
  182.9 3.2 %collective-permute-done.13.refs_4_ = f32[8,256]{1,0:T(8,128)} collective-permute-done((f32[8,256]{1,0:T(8,128)S(1)}, f32[8,256]{1,0:T(8,128)}, u32[]{:S(2)}, u32[]{:S(2)}) %collective-permute-start.13) | collective-permute-done | bytes 8224 | tf_op jit(solution)/shard_map/ppermute | solution.py:360
  186.1 1.0 copy-done.9
  187.1 1.0 copy-done.11
  188.2 0.7 copy-done.12
  188.9 0.7 copy-done.13
  189.5 0.7 copy-done.14
  190.2 0.7 copy-done.15
  190.9 3.0 %shard_map.99 = (bf16[2,128,512]{2,1,0:T(8,128)(2,1)S(1)}, bf16[2,128,512]{2,1,0:T(8,128)(2,1)S(1)}, bf16[512,256]{1,0:T(8,128)(2,1)S(1)}, bf16[512,256]{1,0:T(8...) custom-call(s32[5]{0:T(128)S(1)} %stack.92.meta, s32[2]{0:T(128)S(1)} %copy-done.14, ...), custom_call_target="tpu_custom_call" | custom-call | flops 536870912 | bytes 4194304 | tf_op jit(solution)/shard_map/pallas_call | solution.py:249
  193.9 0.6 collective-permute-start.14
  194.6 0.5 collective-permute-start.20
  195.1 5.3 %shard_map.100 = (f32[1024,128]{1,0:T(8,128)S(1)}, bf16[1024,128]{1,0:T(8,128)(2,1)S(1)}, f32[1024,128]{1,0:T(8,128)S(1)}, bf16[1024,128]{1,0:T(8,128)(2,1)S(1)}...) custom-call(s32[3]{0:T(128)S(1)} %pad_add_fusion.1.meta, bf16[32768,512]{1,0:T(8,128)(2,1)} %get-tuple-element.69.work, ...), custom_call_target="tpu_custom_call" | custom-call | flops 1610612736 | bytes 6291456 | tf_op jit(solution)/shard_map/pallas_call | solution.py:264
  200.4 1.6 collective-permute-start.17
  202.0 2.0 collective-permute-start.18
  204.0 1.6 collective-permute-start.16
  205.6 4.0 %collective-permute-done.17.refs_0_ = bf16[1024,128]{1,0:T(8,128)(2,1)S(1)} collective-permute-done((bf16[1024,128]{1,0:T(8,128)(2,1)S(1)}, bf16[1024,128]{1,0:T(8,128)(2,1)S(1)}, u32[]{:S(2)}, u32[]{:S(2)}) %collective-permute-start.17) | collective-permute-done | bytes 262176 | tf_op jit(solution)/shard_map/ppermute | solution.py:483
  209.7 0.7 collective-permute-start.21
  210.5 6.0 %collective-permute-start.22 = (bf16[1024,128]{1,0:T(8,128)(2,1)S(1)}, bf16[1024,128]{1,0:T(8,128)(2,1)S(1)}, u32[]{:S(2)}, u32[]{:S(2)}) collective-permute-start(bf16[1024,128]{1,0:T(8,128)(2,1)S(1)} %shard_map.103), channel_id=1, source_target_pairs={{0,4},{12,8},{1,5},{13,9},{2,6},{14,10},{3,7},{15,11},{16,20},{28,... | collective-permute-start | bytes 786440 | tf_op jit(solution)/shard_map/ppermute | solution.py:360
  216.6 1.3 collective-permute-start.15
  217.9 2.8 %shard_map.104.refs_8_ = bf16[4096,512]{1,0:T(8,128)(2,1)} custom-call(s32[6]{0:T(128)S(1)} %stack.96.meta, bf16[2,128,512]{2,1,0:T(8,128)(2,1)S(1)} %get-tuple-element.112.refs_0_, bf16[2,128,512]{2,1,0:T(8,128)(2,1)S(1)} %collective-permute-done.19.refs_1_, bf16[128,1024]{1,0:T(8,128)(2,1)S(1)} %bitcast.158, ...), custom_call_target="tpu_custom_call" | custom-call | flops 1073741824 | bytes 4194304 | tf_op jit(solution)/shard_map/pallas_call | solution.py:327
  221.0 2.5 %collective-permute-start.24 = (bf16[1024,128]{1,0:T(8,128)(2,1)S(1)}, bf16[1024,128]{1,0:T(8,128)(2,1)S(1)}, u32[]{:S(2)}, u32[]{:S(2)}) collective-permute-start(bf16[1024,128]{1,0:T(8,128)(2,1)S(1)} %shard_map.105), channel_id=1, source_target_pairs={{0,4},{4,0},{8,12},{12,8},{1,5},{5,1},{9,13},{13,9},{2,6},{6,2},{1... | collective-permute-start | bytes 786440 | tf_op jit(solution)/shard_map/ppermute | solution.py:360
  223.6 0.7 collective-permute-start.25
  224.3 0.5 bitcast_select_fusion
  224.8 3.3 %shard_map.107 = bf16[4096,512]{1,0:T(8,128)(2,1)} custom-call(s32[6]{0:T(128)S(1)} %stack.96.meta, bf16[2,128,512]{2,1,0:T(8,128)(2,1)S(1)} %get-tuple-element.112.refs_0_, bf16[2,128,512]{2,1,0:T(8,128)(2,1)S(1)} %collective-permute-done.19.refs_1_, bf16[128,1024]{1,0:T(8,128)(2,1)S(1)} %add.150.refs_0_.refs_2_, ...), custom_call_target="tpu_custom_call", output_to_operand_aliasing={{}: (9, {})} | custom-call | flops 1073741824 | bytes 4194304 | tf_op jit(solution)/shard_map/pallas_call | solution.py:327
  228.1 1.3 collective-permute-done.24.refs_1_
  229.4 0.9 shard_map.108
  (68 shorter events, 1.6 us)
Async XLA Ops:
  0.6 14.1 %collective-permute-start.2 = (bf16[4096,512]{1,0:T(8,128)(2,1)}, bf16[4096,512]{1,0:T(8,128)(2,1)}, u32[]{:S(2)}, u32[]{:S(2)}) collective-permute-start(bf16[4096,512]{1,0:T(8,128)(2,1)} %w.1), channel_id=1, source_target_pairs={{0,1},{1,0},{2,3},{3,2},{4,5},{5,4},{6,7},{7,6},{8,9},{9,8},{10,11... | collective-permute-start | bytes 12582920 | tf_op jit(solution)/shard_map/ppermute | solution.py:359
  1.1 9.8 %collective-permute-start = (bf16[128,1024]{1,0:T(8,128)(2,1)}, bf16[128,1024]{1,0:T(8,128)(2,1)S(1)}, u32[]{:S(2)}, u32[]{:S(2)}) collective-permute-start(bf16[128,1024]{1,0:T(8,128)(2,1)} %bitcast.153), channel_id=1, source_target_pairs={{0,4},{4,0},{8,12},{12,8},{1,5},{5,1},{9,13},{13,9},{2,6},{6,2},{1... | collective-permute-start | bytes 786440 | tf_op jit(solution)/shard_map/ppermute | solution.py:360
  3.8 7.1 %collective-permute-start.1 = (bf16[128,1024]{1,0:T(8,128)(2,1)}, bf16[128,1024]{1,0:T(8,128)(2,1)S(1)}, u32[]{:S(2)}, u32[]{:S(2)}) collective-permute-start(bf16[128,1024]{1,0:T(8,128)(2,1)} %bitcast.154), channel_id=1, source_target_pairs={{4,8},{8,4},{5,9},{9,5},{6,10},{10,6},{7,11},{11,7},{20,24},{24,20... | collective-permute-start | bytes 786440 | tf_op jit(solution)/shard_map/ppermute | solution.py:360
  4.5 10.2 %collective-permute-start.3 = (bf16[128,1024]{1,0:T(8,128)(2,1)}, bf16[128,1024]{1,0:T(8,128)(2,1)S(1)}, u32[]{:S(2)}, u32[]{:S(2)}) collective-permute-start(bf16[128,1024]{1,0:T(8,128)(2,1)} %bitcast.155), channel_id=1, source_target_pairs={{0,2},{2,0},{1,3},{3,1},{4,6},{6,4},{5,7},{7,5},{8,10},{10,8},{9,1... | collective-permute-start | bytes 786440 | tf_op jit(solution)/shard_map/ppermute | solution.py:390
  6.0 2.2 copy-start
  8.2 6.5 %copy-start.1 = (bf16[1024,1,2,64]{0,3,2,1:T(8,128)(2,1)S(1)}, bf16[1024,1,2,64]{0,3,2,1:T(8,128)(2,1)}, u32[]{:S(2)}) copy-start(bf16[1024,1,2,64]{0,3,2,1:T(8,128)(2,1)} %param.7) | copy-start | bytes 786436
  10.9 132.6 %collective-permute-start.4 = (bf16[128,1024]{1,0:T(8,128)(2,1)S(1)}, bf16[128,1024]{1,0:T(8,128)(2,1)S(1)}, u32[]{:S(2)}, u32[]{:S(2)}) collective-permute-start(bf16[128,1024]{1,0:T(8,128)(2,1)S(1)} %collective-permute-done.refs_2_.refs_4_), channel_id=1, source_target_pairs={{0,2},{2,0},{1,3},{3,1},{4,6},{6,4},{5,7},{7,5},{8,10},{10,8},{9,1... | collective-permute-start | bytes 786440 | tf_op jit(solution)/shard_map/ppermute | solution.py:390
  12.6 130.9 %collective-permute-start.5 = (bf16[128,1024]{1,0:T(8,128)(2,1)S(1)}, bf16[128,1024]{1,0:T(8,128)(2,1)S(1)}, u32[]{:S(2)}, u32[]{:S(2)}) collective-permute-start(bf16[128,1024]{1,0:T(8,128)(2,1)S(1)} %collective-permute-done.1), channel_id=1, source_target_pairs={{4,0},{8,12},{5,1},{9,13},{6,2},{10,14},{7,3},{11,15},{20,16},{24,... | collective-permute-start | bytes 786440 | tf_op jit(solution)/shard_map/ppermute | solution.py:360
  13.9 129.6 %collective-permute-start.6 = (bf16[128,1024]{1,0:T(8,128)(2,1)S(1)}, bf16[128,1024]{1,0:T(8,128)(2,1)S(1)}, u32[]{:S(2)}, u32[]{:S(2)}) collective-permute-start(bf16[128,1024]{1,0:T(8,128)(2,1)S(1)} %collective-permute-done.refs_2_.refs_4_), channel_id=1, source_target_pairs={{4,8},{8,4},{5,9},{9,5},{6,10},{10,6},{7,11},{11,7},{20,24},{24,20... | collective-permute-start | bytes 786440 | tf_op jit(solution)/shard_map/ppermute | solution.py:360
  143.5 5.1 %copy-start.16 = (bf16[128,1024]{1,0:T(8,128)(2,1)}, bf16[128,1024]{1,0:T(8,128)(2,1)S(1)}, u32[]{:S(2)}) copy-start(bf16[128,1024]{1,0:T(8,128)(2,1)S(1)} %collective-permute-done.6) | copy-start | bytes 786436
  143.5 14.2 %collective-permute-start.7 = (bf16[128,1024]{1,0:T(8,128)(2,1)S(1)}, bf16[128,1024]{1,0:T(8,128)(2,1)}, u32[]{:S(2)}, u32[]{:S(2)}) collective-permute-start(bf16[128,1024]{1,0:T(8,128)(2,1)S(1)} %collective-permute-done.6), channel_id=1, source_target_pairs={{4,0},{8,12},{5,1},{9,13},{6,2},{10,14},{7,3},{11,15},{20,16},{24,... | collective-permute-start | bytes 786440 | tf_op jit(solution)/shard_map/ppermute | solution.py:360
  145.0 14.8 %collective-permute-start.8 = (bf16[128,1024]{1,0:T(8,128)(2,1)S(1)}, bf16[128,1024]{1,0:T(8,128)(2,1)S(1)}, u32[]{:S(2)}, u32[]{:S(2)}) collective-permute-start(bf16[128,1024]{1,0:T(8,128)(2,1)S(1)} %add.150.refs_0_.refs_2_), channel_id=1, source_target_pairs={{0,2},{2,0},{1,3},{3,1},{4,6},{6,4},{5,7},{7,5},{8,10},{10,8},{9,1... | collective-permute-start | bytes 786440 | tf_op jit(solution)/shard_map/ppermute | solution.py:390
  145.4 12.4 %copy-start.17 = (s32[2,2,128]{2,1,0:T(2,128)S(1)}, s32[2,2,128]{2,1,0:T(2,128)}, u32[]{:S(2)}) copy-start(s32[2,2,128]{2,1,0:T(2,128)} %param.9) | copy-start | bytes 6148
  148.6 0.8 copy-start.4
  159.2 10.4 %collective-permute-start.9 = (bf16[128,1024]{1,0:T(8,128)(2,1)S(1)}, bf16[128,1024]{1,0:T(8,128)(2,1)}, u32[]{:S(2)}, u32[]{:S(2)}) collective-permute-start(bf16[128,1024]{1,0:T(8,128)(2,1)S(1)} %add.151.refs_0_.refs_4_), channel_id=1, source_target_pairs={{0,2},{2,0},{1,3},{3,1},{4,6},{6,4},{5,7},{7,5},{8,10},{10,8},{9,1... | collective-permute-start | bytes 786440 | tf_op jit(solution)/shard_map/ppermute | solution.py:390
  159.8 1.0 copy-start.5
  160.8 7.1 %copy-start.2 = (bf16[128,1024]{1,0:T(8,128)(2,1)}, bf16[128,1024]{1,0:T(8,128)(2,1)S(1)}, u32[]{:S(2)}) copy-start(bf16[128,1024]{1,0:T(8,128)(2,1)S(1)} %collective-permute-done.8.refs_1_.refs_3_) | copy-start | bytes 786436
  164.3 4.4 %copy-start.6 = (f32[128,1024]{1,0:T(8,128)}, f32[128,1024]{1,0:T(8,128)S(1)}, u32[]{:S(2)}) copy-start(f32[128,1024]{1,0:T(8,128)S(1)} %get-tuple-element.87.refs_1_) | copy-start | bytes 1572868
  164.3 5.1 %copy-start.8 = (f32[128,1024]{1,0:T(8,128)}, f32[128,1024]{1,0:T(8,128)S(1)}, u32[]{:S(2)}) copy-start(f32[128,1024]{1,0:T(8,128)S(1)} %get-tuple-element.86.refs_0_) | copy-start | bytes 1572868
  169.4 47.2 %collective-permute-start.23 = (bf16[7,128,1024]{2,1,0:T(8,128)(2,1)}, bf16[7,128,1024]{2,1,0:T(8,128)(2,1)S(1)}, u32[]{:S(2)}, u32[]{:S(2)}) collective-permute-start(bf16[7,128,1024]{2,1,0:T(8,128)(2,1)} %bitcast_dynamic-update-slice_fusion), channel_id=1, source_target_pairs={{0,1},{1,0},{2,3},{3,2},{4,5},{5,4},{6,7},{7,6},{8,9},{9,8},{10,11... | collective-permute-start | bytes 5505032 | tf_op jit(solution)/shard_map/ppermute | solution.py:359
  169.6 1.0 copy-start.7
  173.9 0.8 copy-start.10
  174.7 4.5 %collective-permute-start.12 = (f32[2,8,128]{2,1,0:T(8,128)S(1)}, f32[2,8,128]{2,1,0:T(8,128)S(1)}, u32[]{:S(2)}, u32[]{:S(2)}) collective-permute-start(f32[2,8,128]{2,1,0:T(8,128)S(1)} %pad_maximum_fusion), channel_id=1, source_target_pairs={{0,6},{2,4},{4,2},{6,0},{8,14},{10,12},{12,10},{14,8},{1,7},{3,5},... | collective-permute-start | bytes 24584 | tf_op jit(solution)/shard_map/ppermute | solution.py:469
  175.7 3.7 %collective-permute-start.11 = (f32[2,8,128]{2,1,0:T(8,128)S(1)}, f32[2,8,128]{2,1,0:T(8,128)S(1)}, u32[]{:S(2)}, u32[]{:S(2)}) collective-permute-start(f32[2,8,128]{2,1,0:T(8,128)S(1)} %pad_maximum_fusion), channel_id=1, source_target_pairs={{0,4},{4,0},{8,12},{12,8},{1,5},{5,1},{9,13},{13,9},{2,6},{6,2},{1... | collective-permute-start | bytes 24584 | tf_op jit(solution)/shard_map/ppermute | solution.py:360
  177.7 3.7 %collective-permute-start.10 = (f32[2,8,128]{2,1,0:T(8,128)S(1)}, f32[2,8,128]{2,1,0:T(8,128)S(1)}, u32[]{:S(2)}, u32[]{:S(2)}) collective-permute-start(f32[2,8,128]{2,1,0:T(8,128)S(1)} %pad_maximum_fusion), channel_id=1, source_target_pairs={{0,2},{2,0},{1,3},{3,1},{4,6},{6,4},{5,7},{7,5},{8,10},{10,8},{9,1... | collective-permute-start | bytes 24584 | tf_op jit(solution)/shard_map/ppermute | solution.py:390
  181.4 4.7 %collective-permute-start.13 = (f32[8,256]{1,0:T(8,128)S(1)}, f32[8,256]{1,0:T(8,128)}, u32[]{:S(2)}, u32[]{:S(2)}) collective-permute-start(f32[8,256]{1,0:T(8,128)S(1)} %pad_maximum_fusion.1.refs_3_), channel_id=1, source_target_pairs={{0,8},{8,0},{4,12},{12,4},{1,9},{9,1},{5,13},{13,5},{2,10},{10,2},... | collective-permute-start | bytes 24584 | tf_op jit(solution)/shard_map/ppermute | solution.py:360
  186.1 1.0 copy-start.9
  187.1 1.0 copy-start.11
  188.2 0.7 copy-start.12
  188.9 0.7 copy-start.13
  189.5 0.7 copy-start.14
  190.2 0.7 copy-start.15
  193.9 6.5 %collective-permute-start.14 = (bf16[1024,128]{1,0:T(8,128)(2,1)S(1)}, bf16[1024,128]{1,0:T(8,128)(2,1)S(1)}, u32[]{:S(2)}, u32[]{:S(2)}) collective-permute-start(bf16[1024,128]{1,0:T(8,128)(2,1)S(1)} %get-tuple-element.91), channel_id=1, source_target_pairs={{0,2},{2,0},{1,3},{3,1},{4,6},{6,4},{5,7},{7,5},{8,10},{10,8},{9,1... | collective-permute-start | bytes 786440 | tf_op jit(solution)/shard_map/ppermute | solution.py:483
  194.6 9.4 %collective-permute-start.19 = (bf16[2,128,512]{2,1,0:T(8,128)(2,1)S(1)}, bf16[2,128,512]{2,1,0:T(8,128)(2,1)S(1)}, u32[]{:S(2)}, u32[]{:S(2)}) collective-permute-start(bf16[2,128,512]{2,1,0:T(8,128)(2,1)S(1)} %get-tuple-element.107), channel_id=1, source_target_pairs={{0,1},{1,0},{2,3},{3,2},{4,5},{5,4},{6,7},{7,6},{8,9},{9,8},{10,11... | collective-permute-start | bytes 786440 | tf_op jit(solution)/shard_map/ppermute | solution.py:359
  194.6 11.0 %collective-permute-start.20 = (bf16[1,128,1024]{2,1,0:T(8,128)(2,1)}, bf16[1,128,1024]{2,1,0:T(8,128)(2,1)S(1)}, u32[]{:S(2)}, u32[]{:S(2)}) collective-permute-start(bf16[1,128,1024]{2,1,0:T(8,128)(2,1)} %bitcast.31), channel_id=1, source_target_pairs={{0,1},{1,0},{2,3},{3,2},{4,5},{5,4},{6,7},{7,6},{8,9},{9,8},{10,11... | collective-permute-start | bytes 786440 | tf_op jit(solution)/shard_map/ppermute | solution.py:359
  200.4 9.2 %collective-permute-start.17 = (bf16[1024,128]{1,0:T(8,128)(2,1)S(1)}, bf16[1024,128]{1,0:T(8,128)(2,1)S(1)}, u32[]{:S(2)}, u32[]{:S(2)}) collective-permute-start(bf16[1024,128]{1,0:T(8,128)(2,1)S(1)} %get-tuple-element.106), channel_id=1, source_target_pairs={{0,2},{2,0},{1,3},{3,1},{4,6},{6,4},{5,7},{7,5},{8,10},{10,8},{9,1... | collective-permute-start | bytes 786440 | tf_op jit(solution)/shard_map/ppermute | solution.py:483
  202.0 7.6 %collective-permute-start.18 = (bf16[1024,128]{1,0:T(8,128)(2,1)S(1)}, bf16[1024,128]{1,0:T(8,128)(2,1)S(1)}, u32[]{:S(2)}, u32[]{:S(2)}) collective-permute-start(bf16[1024,128]{1,0:T(8,128)(2,1)S(1)} %shard_map.101), channel_id=1, source_target_pairs={{0,4},{12,8},{1,5},{13,9},{2,6},{14,10},{3,7},{15,11},{16,20},{28,... | collective-permute-start | bytes 786440 | tf_op jit(solution)/shard_map/ppermute | solution.py:360
  204.0 16.8 %collective-permute-start.16 = (bf16[1024,128]{1,0:T(8,128)(2,1)S(1)}, bf16[1024,128]{1,0:T(8,128)(2,1)S(1)}, u32[]{:S(2)}, u32[]{:S(2)}) collective-permute-start(bf16[1024,128]{1,0:T(8,128)(2,1)S(1)} %get-tuple-element.103), channel_id=1, source_target_pairs={{0,2},{2,0},{1,3},{3,1},{4,6},{6,4},{5,7},{7,5},{8,10},{10,8},{9,1... | collective-permute-start | bytes 786440 | tf_op jit(solution)/shard_map/ppermute | solution.py:483
  209.7 11.1 %collective-permute-start.21 = (bf16[1024,128]{1,0:T(8,128)(2,1)S(1)}, bf16[1024,128]{1,0:T(8,128)(2,1)S(1)}, u32[]{:S(2)}, u32[]{:S(2)}) collective-permute-start(bf16[1024,128]{1,0:T(8,128)(2,1)S(1)} %shard_map.102), channel_id=1, source_target_pairs={{4,8},{8,4},{5,9},{9,5},{6,10},{10,6},{7,11},{11,7},{20,24},{24,20... | collective-permute-start | bytes 786440 | tf_op jit(solution)/shard_map/ppermute | solution.py:360
  210.5 10.4 %collective-permute-start.22 = (bf16[1024,128]{1,0:T(8,128)(2,1)S(1)}, bf16[1024,128]{1,0:T(8,128)(2,1)S(1)}, u32[]{:S(2)}, u32[]{:S(2)}) collective-permute-start(bf16[1024,128]{1,0:T(8,128)(2,1)S(1)} %shard_map.103), channel_id=1, source_target_pairs={{0,4},{12,8},{1,5},{13,9},{2,6},{14,10},{3,7},{15,11},{16,20},{28,... | collective-permute-start | bytes 786440 | tf_op jit(solution)/shard_map/ppermute | solution.py:360
  216.5 7.8 %collective-permute-start.26 = (f32[1,128]{1,0:T(1,128)S(1)}, f32[1,128]{1,0:T(1,128)S(1)}, u32[]{:S(2)}, u32[]{:S(2)}) collective-permute-start(f32[1,128]{1,0:T(1,128)S(1)} %get-tuple-element.130), channel_id=1, source_target_pairs={{0,1},{1,0},{2,3},{3,2},{4,5},{5,4},{6,7},{7,6},{8,9},{9,8},{10,11... | collective-permute-start | bytes 1544 | tf_op jit(solution)/shard_map/ppermute | solution.py:359
  216.6 11.5 %collective-permute-start.15 = (bf16[1024,128]{1,0:T(8,128)(2,1)S(1)}, bf16[1024,128]{1,0:T(8,128)(2,1)S(1)}, u32[]{:S(2)}, u32[]{:S(2)}) collective-permute-start(bf16[1024,128]{1,0:T(8,128)(2,1)S(1)} %get-tuple-element.101), channel_id=1, source_target_pairs={{0,2},{2,0},{1,3},{3,1},{4,6},{6,4},{5,7},{7,5},{8,10},{10,8},{9,1... | collective-permute-start | bytes 786440 | tf_op jit(solution)/shard_map/ppermute | solution.py:483
  220.8 4.1 %copy-start.3 = (bf16[128,1024]{1,0:T(8,128)(2,1)S(1)}, bf16[128,1024]{1,0:T(8,128)(2,1)}, u32[]{:S(2)}) copy-start(bf16[128,1024]{1,0:T(8,128)(2,1)} %copy-done.2) | copy-start | bytes 786436
  221.0 8.4 %collective-permute-start.24 = (bf16[1024,128]{1,0:T(8,128)(2,1)S(1)}, bf16[1024,128]{1,0:T(8,128)(2,1)S(1)}, u32[]{:S(2)}, u32[]{:S(2)}) collective-permute-start(bf16[1024,128]{1,0:T(8,128)(2,1)S(1)} %shard_map.105), channel_id=1, source_target_pairs={{0,4},{4,0},{8,12},{12,8},{1,5},{5,1},{9,13},{13,9},{2,6},{6,2},{1... | collective-permute-start | bytes 786440 | tf_op jit(solution)/shard_map/ppermute | solution.py:360
  223.6 5.7 %collective-permute-start.25 = (bf16[1024,128]{1,0:T(8,128)(2,1)S(1)}, bf16[1024,128]{1,0:T(8,128)(2,1)S(1)}, u32[]{:S(2)}, u32[]{:S(2)}) collective-permute-start(bf16[1024,128]{1,0:T(8,128)(2,1)S(1)} %shard_map.106), channel_id=1, source_target_pairs={{4,8},{8,4},{5,9},{9,5},{6,10},{10,6},{7,11},{11,7},{20,24},{24,20... | collective-permute-start | bytes 786440 | tf_op jit(solution)/shard_map/ppermute | solution.py:360

commit v7 on v6

--- a/solution.py
+++ b/solution.py
@@ -9,8 +9,8 @@
 
 BETA = 0.1
 F32, BF16 = jnp.float32, jnp.bfloat16
-VMEM_BYTES = 40 * 1024 * 1024
-WORK_BYTES = 32 * 1024 * 1024
+VMEM_BYTES = 16 * 1024 * 1024
+WORK_BYTES = 52 * 1024 * 1024
 IN_VMEM = pl.BlockSpec(memory_space=pltpu.VMEM)
 IN_SMEM = pl.BlockSpec(memory_space=pltpu.SMEM)
 IN_PLACE = pl.BlockSpec(memory_space=pl.ANY)
@@ -60,12 +60,11 @@
     )(w)
 
 
-def fetch(work, width, start, part, slots, i, sems, far=None):
-    own = work.at[pl.ds(start, part), :]
-    far = work.at[pl.ds(width + start, part), :] if far is None else far.at[pl.ds(start, part), :]
+def fetch(work, width, start, part, slots, i, sems, own_only=False):
     copies = []
-    for j, w in enumerate((own, far)):
-        copies.append(pltpu.make_async_copy(w, slots.at[i, j], sems.at[i, j]))
+    for j in range(1 if own_only else 2):
+        source = work.at[pl.ds(j * width + start, part), :]
+        copies.append(pltpu.make_async_copy(source, slots.at[i, j], sems.at[i, j]))
         copies[-1].start()
     return copies
 
@@ -92,12 +91,17 @@
     accs = {t: refs.pop(0) for t, _, has_acc, _ in plan if has_acc}
     wanted = {t: refs.pop(0) for t, _, _, done in plan if done}
     used = sorted({i for _, parts, _, _ in plan for i in parts})
+    starts = [pl.multiple_of(meta[i] * part, part) for i in used]
+    if fresh:
+        held, far_sems = refs[-2:]
+        refs = refs[:-2]
+        into = pltpu.make_async_copy(far, held, far_sems.at[0])
+        into.start()
     slots, sems = refs[-2:]
-    coming = [
-        fetch(work, width, pl.multiple_of(meta[i] * part, part), part, slots, n, sems, far) for n, i in enumerate(used)
-    ]
+    coming = [fetch(work, width, start, part, slots, n, sems, fresh) for n, start in enumerate(starts)]
     if fresh:
-        kept = pltpu.make_async_copy(far, refs[-3].at[pl.ds(width, width), :], sems.at[len(used), 0])
+        into.wait()
+        kept = pltpu.make_async_copy(held, refs[-3].at[pl.ds(width, width), :], far_sems.at[1])
         kept.start()
     outs = {}
     stats = {}
@@ -114,7 +118,8 @@
             x = chunks[t, i][...]
             for j in range(2):
                 at = slice(j * columns, (j + 1) * columns)
-                product = jnp.dot(x, slots[n, j], preferred_element_type=F32)
+                w = held[pl.ds(starts[n], part), :] if fresh and j else slots[n, j]
+                product = jnp.dot(x, w, preferred_element_type=F32)
                 if i != parts[0]:
                     product += outs[t][:, at]
                 elif has_acc:
@@ -152,7 +157,8 @@
         out_shape=out_shape,
         in_specs=[IN_SMEM] + [IN_PLACE] * len(in_place) + [IN_VMEM] * len(operands),
         out_specs=out_specs,
-        scratch_shapes=[pltpu.VMEM((n_used, 2, part, columns), BF16), pltpu.SemaphoreType.DMA((n_used + fresh, 2))],
+        scratch_shapes=[pltpu.VMEM((n_used, 2 - fresh, part, columns), BF16), pltpu.SemaphoreType.DMA((n_used, 2))]
+        + ([pltpu.VMEM((part * n_voc, columns), BF16), pltpu.SemaphoreType.DMA((2,))] if fresh else []),
         input_output_aliases={1: len(out_shape) - 1} if fresh else {},
         compiler_params=params(),
         cost_estimate=cost(4 * len(chunks) * rows * part * columns, n_used * 4 * part * columns),
@@ -483,8 +489,16 @@
     back = lambda cs: [lax.ppermute(c, "ctx", ring(n_ctx, -t)) for t, c in zip(beyond, cs)]
     shares = {final: (kept, list(send))}
     leave = list(range(final))[::-1]
-    for i, share in zip(leave, spread_call(flipped_own, flipped_far, work, [part_of[i] for i in leave], part, width, rows)):
-        shares[i] = share
+
+    def more_shares(slots):
+        done = spread_call(flipped_own, flipped_far, work, [part_of[i] for i in slots], part, width, rows)
+        shares.update(zip(slots, done))
+        return [a for i in slots for a in [shares[i][0]] + shares[i][1]]
+
+    def set_shares(slots, flat):
+        for i in slots:
+            shares[i] = (flat[0], list(flat[1:n_ctx]))
+            flat = flat[n_ctx:]
 
     over = {}
     near_over = lambda i, *more: add_call(shares[i][0], over[i] + list(more))
@@ -507,20 +521,22 @@
         elif i == 1:
             beside = [head(early, grads=[grads_own, theirs])]
         elif i == final:
-            beside = [a for j in leave for a in [shares[j][0]] + shares[j][1]]
+            beside = more_shares(leave[:2])
         elif i == final - 1:
-            beside = [theirs, far_late]
-        over[i], came, beside = together(over[i], came, beside)
+            beside = [theirs, far_late] + more_shares(leave[2:])
+        sends = shares[i - 1][1] if i and i - 1 in shares else []
+        over[i], came, beside, sends = together(over[i], came, beside, sends)
         landed = came if line else landed + came
         if i <= 1:
             grad_head, = beside
         elif i == final:
-            for j in leave:
-                shares[j] = (beside[0], beside[1:n_ctx])
-                beside = beside[n_ctx:]
+            set_shares(leave[:2], beside)
         elif i == final - 1:
-            theirs, far_late = beside
+            theirs, far_late = beside[:2]
+            set_shares(leave[2:], beside[2:])
             head = functools.partial(head_call, near=chunk, far=[(soon, far_soon), (late, far_late)], meta=meta)
+        if sends:
+            shares[i - 1] = (shares[i - 1][0], list(sends))
     kept = shares[0][0]
     summed = add_call(kept, over[0] + landed, turned=True)
     grad_hidden = summed.reshape(1, sides, window, part).transpose(3, 0, 1, 2)

time: 232 us -> 110 us (0.47)
  Pallas kernels: 156 us -> 33.9 us
    pallas_call x4, Pallas kernels: 139 us -> 14.7 us  [logits_call(): pl.pallas_call(functools.partial(logits_kernel, kernel_plan, columns, par...]
    ppermute x12, starting transfers between devices: 20.6 us -> 23.3 us  [shards(): along = lambda a, by: lax.ppermute(a, 'vocab', by)]
    pallas_call x1 -> x2, Pallas kernels: 5.31 us -> 6.85 us  [spread_call(): pl.pallas_call(functools.partial(spread_kernel, part, width, n_parts), ou...]
  transfers between devices with their start and end apart: 27 -> 27, of which waited for: 9 -> 13; matrix products, arithmetic and copies ran while one was open for 4% -> 8% of each run, Pallas kernels for 68% -> 31%
where the time goes in v7:
time: 110 us; the launch traced here: 108 us
  starting transfers between devices  34 us (31%)
  Pallas kernels  33.9 us (31%)
  waiting for transfers between devices  19.5 us (18%)
  local copies, waits for them, and re-layouts  17 us (15%)
  other arithmetic  2.5 us (2%)
  between operations  1.11 us (1%)
    ppermute x12, starting transfers between devices, shards(): along = lambda a, by: lax.ppermute(a, 'vocab', by)  23.3 us
    unnamed x42, local copies, waits for them, and re-layouts  15 us
    pallas_call x4, Pallas kernels, logits_call(): pl.pallas_call(functools.partial(logits_kernel, kernel_plan, columns, par...  14.7 us
    ppermute x12, waiting for transfers between devices, shards(): along = lambda a, by: lax.ppermute(a, 'vocab', by)  14.6 us
    pallas_call x2, Pallas kernels, spread_call(): pl.pallas_call(functools.partial(spread_kernel, part, width, n_parts), ou...  6.85 us
    pallas_call x2, Pallas kernels, head_call(): pl.pallas_call(functools.partial(head_kernel, slots_here, list(near), [ke...  6.08 us
    ppermute x5, starting transfers between devices, shards(): cross = lambda a: [lax.ppermute(a, 'ctx', ring(n_ctx, t)) for t in beyond]  4.97 us
    ppermute x4, starting transfers between devices, shards(): lax.ppermute(c, 'ctx', ring(n_ctx, -t))  3.33 us
  transfers between devices with their start and end apart: 27, of which 13 were waited for; matrix products, arithmetic and copies ran while one was open for 8% of the time, Pallas kernels for 31%

profile of v7, /device:TPU:0, one launch (start us, length us, event | category | flops | bytes accessed | tf_op | source)
XLA Modules:
  0.0 108.1 jit_solution(4137510803038953899)
XLA Ops:
  0.6 0.5 collective-permute-start.2
  1.1 2.7 %collective-permute-start = (bf16[128,1024]{1,0:T(8,128)(2,1)}, bf16[128,1024]{1,0:T(8,128)(2,1)S(1)}, u32[]{:S(2)}, u32[]{:S(2)}) collective-permute-start(bf16[128,1024]{1,0:T(8,128)(2,1)} %bitcast.153), channel_id=1, source_target_pairs={{0,4},{4,0},{8,12},{12,8},{1,5},{5,1},{9,13},{13,9},{2,6},{6,2},{1... | collective-permute-start | bytes 786440 | tf_op jit(solution)/shard_map/ppermute | solution.py:366
  3.8 0.7 collective-permute-start.1
  4.5 1.6 %collective-permute-start.3 = (bf16[128,1024]{1,0:T(8,128)(2,1)}, bf16[128,1024]{1,0:T(8,128)(2,1)S(1)}, u32[]{:S(2)}, u32[]{:S(2)}) collective-permute-start(bf16[128,1024]{1,0:T(8,128)(2,1)} %bitcast.155), channel_id=1, source_target_pairs={{0,2},{2,0},{1,3},{3,1},{4,6},{6,4},{5,7},{7,5},{8,10},{10,8},{9,1... | collective-permute-start | bytes 786440 | tf_op jit(solution)/shard_map/ppermute | solution.py:396
  6.0 2.2 %copy-done = bf16[4096,512]{1,0:T(8,128)(2,1)S(1)} copy-done((bf16[4096,512]{1,0:T(8,128)(2,1)S(1)}, bf16[4096,512]{1,0:T(8,128)(2,1)}, u32[]{:S(2)}) %copy-start) | copy-done | bytes 4194328
  8.2 2.0 %shard_map.94.work = bf16[53248,512]{1,0:T(8,128)(2,1)} custom-call(bf16[4096,512]{1,0:T(8,128)(2,1)S(1)} %copy-done), custom_call_target="tpu_custom_call" | custom-call | flops 1 | bytes 8388608 | tf_op jit(solution)/shard_map/pallas_call | solution.py:52
  10.2 0.7 collective-permute-done.refs_2_.refs_4_
  10.9 1.7 %collective-permute-start.4 = (bf16[128,1024]{1,0:T(8,128)(2,1)S(1)}, bf16[128,1024]{1,0:T(8,128)(2,1)S(1)}, u32[]{:S(2)}, u32[]{:S(2)}) collective-permute-start(bf16[128,1024]{1,0:T(8,128)(2,1)S(1)} %collective-permute-done.refs_2_.refs_4_), channel_id=1, source_target_pairs={{0,2},{2,0},{1,3},{3,1},{4,6},{6,4},{5,7},{7,5},{8,10},{10,8},{9,1... | collective-permute-start | bytes 786440 | tf_op jit(solution)/shard_map/ppermute | solution.py:396
  12.6 1.3 %collective-permute-start.5 = (bf16[128,1024]{1,0:T(8,128)(2,1)S(1)}, bf16[128,1024]{1,0:T(8,128)(2,1)S(1)}, u32[]{:S(2)}, u32[]{:S(2)}) collective-permute-start(bf16[128,1024]{1,0:T(8,128)(2,1)S(1)} %collective-permute-done.1), channel_id=1, source_target_pairs={{4,0},{8,12},{5,1},{9,13},{6,2},{10,14},{7,3},{11,15},{20,16},{24,... | collective-permute-start | bytes 786440 | tf_op jit(solution)/shard_map/ppermute | solution.py:366
  13.9 0.7 collective-permute-start.6
  14.7 4.8 %shard_map.95 = (f32[128,1024]{1,0:T(8,128)S(1)}, f32[128,1024]{1,0:T(8,128)S(1)}, bf16[53248,512]{1,0:T(8,128)(2,1)}) custom-call(s32[6]{0:T(128)S(1)} %stack.96.meta, bf16[53248,512]{1,0:T(8,128)(2,1)} %shard_map.94.work, bf16[4096,512]{1,0:T(8,128)(2,1)} %collective-permute-done.2.refs_0_, ...), custom_call_target="tpu_custom_call", output_to_operand_aliasing={{2}: (1, {})} | custom-call | flops 805306368 | bytes 4194304 | tf_op jit(solution)/shard_map/pallas_call | solution.py:155
  19.5 4.8 %collective-permute-done.5 = bf16[128,1024]{1,0:T(8,128)(2,1)S(1)} collective-permute-done((bf16[128,1024]{1,0:T(8,128)(2,1)S(1)}, bf16[128,1024]{1,0:T(8,128)(2,1)S(1)}, u32[]{:S(2)}, u32[]{:S(2)}) %collective-permute-start.5) | collective-permute-done | bytes 262176 | tf_op jit(solution)/shard_map/ppermute | solution.py:366
  24.3 1.3 %collective-permute-start.7 = (bf16[128,1024]{1,0:T(8,128)(2,1)S(1)}, bf16[128,1024]{1,0:T(8,128)(2,1)}, u32[]{:S(2)}, u32[]{:S(2)}) collective-permute-start(bf16[128,1024]{1,0:T(8,128)(2,1)S(1)} %collective-permute-done.6), channel_id=1, source_target_pairs={{4,0},{8,12},{5,1},{9,13},{6,2},{10,14},{7,3},{11,15},{20,16},{24,... | collective-permute-start | bytes 786440 | tf_op jit(solution)/shard_map/ppermute | solution.py:366
  25.7 0.6 collective-permute-start.8
  26.3 3.2 %shard_map.96 = (f32[128,1024]{1,0:T(8,128)S(1)}, f32[128,1024]{1,0:T(8,128)S(1)}) custom-call(s32[6]{0:T(128)S(1)} %stack.96.meta, bf16[53248,512]{1,0:T(8,128)(2,1)} %get-tuple-element.71.work, bf16[128,1024]{1,0:T(8,128)(2,1)S(1)} %add.150.refs_0_.refs_2_, bf16[128,1024]{1,0:T(8,128)(2,1)S(1)} %collective-permute-done.4.refs_1_.refs_5_, ...), custom_call_target="tpu_custom_call" | custom-call | flops 536870912 | bytes 4194304 | tf_op jit(solution)/shard_map/pallas_call | solution.py:155
  29.5 0.8 copy-done.8
  30.3 3.9 %collective-permute-done.7 = bf16[128,1024]{1,0:T(8,128)(2,1)} collective-permute-done((bf16[128,1024]{1,0:T(8,128)(2,1)S(1)}, bf16[128,1024]{1,0:T(8,128)(2,1)}, u32[]{:S(2)}, u32[]{:S(2)}) %collective-permute-start.7) | collective-permute-done | bytes 262176 | tf_op jit(solution)/shard_map/ppermute | solution.py:366
  34.6 1.1 %add.151.refs_0_.refs_4_ = bf16[128,1024]{1,0:T(8,128)(2,1)S(1)} add(bf16[128,1024]{1,0:T(8,128)(2,1)} %copy-done.16, bf16[128,1024]{1,0:T(8,128)(2,1)} %collective-permute-done.7) | non-fusion elementwise | flops 131072 | bytes 786432 | tf_op jit(solution)/shard_map/add | solution.py:429
  35.7 0.6 collective-permute-start.9
  36.3 1.0 copy-done.9
  37.4 3.4 %shard_map.97 = (f32[128,1024]{1,0:T(8,128)S(1)}, f32[8,128]{1,0:T(8,128)S(1)}, f32[128,1024]{1,0:T(8,128)S(1)}) custom-call(s32[6]{0:T(128)S(1)} %stack.96.meta, bf16[53248,512]{1,0:T(8,128)(2,1)} %get-tuple-element.71.work, bf16[128,1024]{1,0:T(8,128)(2,1)S(1)} %add.151.refs_0_.refs_4_, bf16[128,1024]{1,0:T(8,128)(2,1)S(1)} %collective-permute-done.8.refs_1_.refs_3_, ...), custom_call_target="tpu_custom_call" | custom-call | flops 536870912 | bytes 4194304 | tf_op jit(solution)/shard_map/pallas_call | solution.py:155
  40.8 0.8 bitcast_dynamic-update-slice_fusion.6
  41.6 0.7 bitcast_dynamic-update-slice_fusion.5
  42.4 0.7 bitcast_dynamic-update-slice_fusion.4
  43.1 0.7 bitcast_dynamic-update-slice_fusion.3
  43.8 0.7 bitcast_dynamic-update-slice_fusion.2
  44.5 0.7 bitcast_dynamic-update-slice_fusion.1
  45.2 0.7 bitcast_dynamic-update-slice_fusion
  46.2 1.0 copy-done.11
  47.2 3.2 %shard_map.98 = (f32[128,1024]{1,0:T(8,128)S(1)}, f32[8,128]{1,0:T(8,128)S(1)}) custom-call(s32[6]{0:T(128)S(1)} %stack.96.meta, bf16[53248,512]{1,0:T(8,128)(2,1)} %get-tuple-element.71.work, bf16[128,1024]{1,0:T(8,128)(2,1)} %collective-permute-done.9.refs_0_.refs_5_, f32[128,1024]{1,0:T(8,128)S(1)} %copy-done.11, s32[128,1]{1,0:T(8,128)S(1)} %copy.17.refs_2_), custom_call_target="tpu_custom_call" | custom-call | flops 268435456 | bytes 2097152 | tf_op jit(solution)/shard_map/pallas_call | solution.py:155
  50.5 0.8 copy-done.6
  51.2 1.3 %collective-permute-start.12 = (f32[2,8,128]{2,1,0:T(8,128)S(1)}, f32[2,8,128]{2,1,0:T(8,128)S(1)}, u32[]{:S(2)}, u32[]{:S(2)}) collective-permute-start(f32[2,8,128]{2,1,0:T(8,128)S(1)} %pad_maximum_fusion), channel_id=1, source_target_pairs={{0,6},{2,4},{4,2},{6,0},{8,14},{10,12},{12,10},{14,8},{1,7},{3,5},... | collective-permute-start | bytes 24584 | tf_op jit(solution)/shard_map/ppermute | solution.py:475
  52.5 1.6 %collective-permute-start.11 = (f32[2,8,128]{2,1,0:T(8,128)S(1)}, f32[2,8,128]{2,1,0:T(8,128)S(1)}, u32[]{:S(2)}, u32[]{:S(2)}) collective-permute-start(f32[2,8,128]{2,1,0:T(8,128)S(1)} %pad_maximum_fusion), channel_id=1, source_target_pairs={{0,4},{4,0},{8,12},{12,8},{1,5},{5,1},{9,13},{13,9},{2,6},{6,2},{1... | collective-permute-start | bytes 24584 | tf_op jit(solution)/shard_map/ppermute | solution.py:366
  54.2 0.5 collective-permute-start.10
  54.8 1.0 collective-permute-done.12
  56.2 1.6 %collective-permute-done.10 = f32[2,8,128]{2,1,0:T(8,128)S(1)} collective-permute-done((f32[2,8,128]{2,1,0:T(8,128)S(1)}, f32[2,8,128]{2,1,0:T(8,128)S(1)}, u32[]{:S(2)}, u32[]{:S(2)}) %collective-permute-start.10) | collective-permute-done | bytes 8224 | tf_op jit(solution)/shard_map/ppermute | solution.py:396
  57.9 1.3 %collective-permute-start.13 = (f32[8,256]{1,0:T(8,128)S(1)}, f32[8,256]{1,0:T(8,128)}, u32[]{:S(2)}, u32[]{:S(2)}) collective-permute-start(f32[8,256]{1,0:T(8,128)S(1)} %pad_maximum_fusion.1.refs_3_), channel_id=1, source_target_pairs={{0,8},{8,0},{4,12},{12,4},{1,9},{9,1},{5,13},{13,5},{2,10},{10,2},... | collective-permute-start | bytes 24584 | tf_op jit(solution)/shard_map/ppermute | solution.py:366
  59.2 0.5 pad_add_fusion
  59.7 0.7 copy.18.refs_2_
  60.5 2.1 %collective-permute-done.13.refs_4_ = f32[8,256]{1,0:T(8,128)} collective-permute-done((f32[8,256]{1,0:T(8,128)S(1)}, f32[8,256]{1,0:T(8,128)}, u32[]{:S(2)}, u32[]{:S(2)}) %collective-permute-start.13) | collective-permute-done | bytes 8224 | tf_op jit(solution)/shard_map/ppermute | solution.py:366
  62.6 1.0 copy-done.5
  63.7 1.0 copy-done.7
  64.7 0.7 copy-done.12
  65.4 0.7 copy-done.13
  66.1 0.7 copy-done.14
  66.7 0.7 copy-done.15
  67.4 3.0 %shard_map.99 = (bf16[2,128,512]{2,1,0:T(8,128)(2,1)S(1)}, bf16[2,128,512]{2,1,0:T(8,128)(2,1)S(1)}, bf16[512,256]{1,0:T(8,128)(2,1)S(1)}, bf16[512,256]{1,0:T(8...) custom-call(s32[5]{0:T(128)S(1)} %stack.92.meta, s32[2]{0:T(128)S(1)} %copy-done.14, ...), custom_call_target="tpu_custom_call" | custom-call | flops 536870912 | bytes 4194304 | tf_op jit(solution)/shard_map/pallas_call | solution.py:255
  70.4 0.6 collective-permute-start.14
  71.6 4.6 %shard_map.100 = (f32[1024,128]{1,0:T(8,128)S(1)}, bf16[1024,128]{1,0:T(8,128)(2,1)S(1)}, f32[1024,128]{1,0:T(8,128)S(1)}, bf16[1024,128]{1,0:T(8,128)(2,1)S(1)}) custom-call(s32[2]{0:T(128)S(1)} %pad_add_fusion.1.meta, bf16[53248,512]{1,0:T(8,128)(2,1)} %get-tuple-element.71.work, bf16[512,256]{1,0:T(8,128)(2,1)S(1)} %get-tuple-element.94.flipped_own, ...), custom_call_target="tpu_custom_call" | custom-call | flops 1073741824 | bytes 4194304 | tf_op jit(solution)/shard_map/pallas_call | solution.py:270
  76.2 0.7 collective-permute-done.14.refs_0_
  76.8 0.9 collective-permute-start.15
  77.8 2.9 %collective-permute-start.16 = (bf16[1024,128]{1,0:T(8,128)(2,1)S(1)}, bf16[1024,128]{1,0:T(8,128)(2,1)S(1)}, u32[]{:S(2)}, u32[]{:S(2)}) collective-permute-start(bf16[1024,128]{1,0:T(8,128)(2,1)S(1)} %shard_map.101), channel_id=1, source_target_pairs={{0,4},{12,8},{1,5},{13,9},{2,6},{14,10},{3,7},{15,11},{16,20},{28,... | collective-permute-start | bytes 786440 | tf_op jit(solution)/shard_map/ppermute | solution.py:366
  80.7 2.3 %shard_map.102 = (f32[1024,128]{1,0:T(8,128)S(1)}, bf16[1024,128]{1,0:T(8,128)(2,1)S(1)}) custom-call(s32[1]{0:T(128)} %bitcast.5.meta, bf16[53248,512]{1,0:T(8,128)(2,1)} %get-tuple-element.71.work, bf16[512,256]{1,0:T(8,128)(2,1)S(1)} %get-tuple-element.94.flipped_own, bf16[512,256]{1,0:T(8,128)(2,1)S(1)} %get-tuple-element.95.flipped_far), custom_call_target="tpu_custom_call" | custom-call | flops 536870912 | bytes 2097152 | tf_op jit(solution)/shard_map/pallas_call | solution.py:270
  83.0 1.5 %collective-permute-done.15.refs_0_ = bf16[1024,128]{1,0:T(8,128)(2,1)S(1)} collective-permute-done((bf16[1024,128]{1,0:T(8,128)(2,1)S(1)}, bf16[1024,128]{1,0:T(8,128)(2,1)S(1)}, u32[]{:S(2)}, u32[]{:S(2)}) %collective-permute-start.15) | collective-permute-done | bytes 262176 | tf_op jit(solution)/shard_map/ppermute | solution.py:489
  84.5 1.1 %collective-permute-done.16.refs_1_ = bf16[1024,128]{1,0:T(8,128)(2,1)S(1)} collective-permute-done((bf16[1024,128]{1,0:T(8,128)(2,1)S(1)}, bf16[1024,128]{1,0:T(8,128)(2,1)S(1)}, u32[]{:S(2)}, u32[]{:S(2)}) %collective-permute-start.16) | collective-permute-done | bytes 262176 | tf_op jit(solution)/shard_map/ppermute | solution.py:366
  85.6 1.5 %collective-permute-start.19 = (bf16[1024,128]{1,0:T(8,128)(2,1)S(1)}, bf16[1024,128]{1,0:T(8,128)(2,1)S(1)}, u32[]{:S(2)}, u32[]{:S(2)}) collective-permute-start(bf16[1024,128]{1,0:T(8,128)(2,1)S(1)} %get-tuple-element.109), channel_id=1, source_target_pairs={{0,2},{2,0},{1,3},{3,1},{4,6},{6,4},{5,7},{7,5},{8,10},{10,8},{9,1... | collective-permute-start | bytes 786440 | tf_op jit(solution)/shard_map/ppermute | solution.py:489
  87.2 0.7 collective-permute-start.20
  88.0 7.0 %collective-permute-start.21 = (bf16[1024,128]{1,0:T(8,128)(2,1)S(1)}, bf16[1024,128]{1,0:T(8,128)(2,1)S(1)}, u32[]{:S(2)}, u32[]{:S(2)}) collective-permute-start(bf16[1024,128]{1,0:T(8,128)(2,1)S(1)} %shard_map.104), channel_id=1, source_target_pairs={{0,4},{12,8},{1,5},{13,9},{2,6},{14,10},{3,7},{15,11},{16,20},{28,... | collective-permute-start | bytes 786440 | tf_op jit(solution)/shard_map/ppermute | solution.py:366
  95.1 2.8 %shard_map.105.refs_8_ = bf16[4096,512]{1,0:T(8,128)(2,1)} custom-call(s32[6]{0:T(128)S(1)} %stack.96.meta, bf16[2,128,512]{2,1,0:T(8,128)(2,1)S(1)} %get-tuple-element.113.refs_0_, bf16[2,128,512]{2,1,0:T(8,128)(2,1)S(1)} %collective-permute-done.17.refs_1_, bf16[128,1024]{1,0:T(8,128)(2,1)S(1)} %bitcast.158, ...), custom_call_target="tpu_custom_call" | custom-call | flops 1073741824 | bytes 4194304 | tf_op jit(solution)/shard_map/pallas_call | solution.py:333
  98.0 1.1 %collective-permute-done.21.refs_1_ = bf16[1024,128]{1,0:T(8,128)(2,1)S(1)} collective-permute-done((bf16[1024,128]{1,0:T(8,128)(2,1)S(1)}, bf16[1024,128]{1,0:T(8,128)(2,1)S(1)}, u32[]{:S(2)}, u32[]{:S(2)}) %collective-permute-start.21) | collective-permute-done | bytes 262176 | tf_op jit(solution)/shard_map/ppermute | solution.py:366
  99.5 2.5 %collective-permute-start.24 = (bf16[1024,128]{1,0:T(8,128)(2,1)S(1)}, bf16[1024,128]{1,0:T(8,128)(2,1)S(1)}, u32[]{:S(2)}, u32[]{:S(2)}) collective-permute-start(bf16[1024,128]{1,0:T(8,128)(2,1)S(1)} %shard_map.106), channel_id=1, source_target_pairs={{0,4},{4,0},{8,12},{12,8},{1,5},{5,1},{9,13},{13,9},{2,6},{6,2},{1... | collective-permute-start | bytes 786440 | tf_op jit(solution)/shard_map/ppermute | solution.py:366
  102.1 0.7 collective-permute-start.25
  103.4 3.3 %shard_map.108 = bf16[4096,512]{1,0:T(8,128)(2,1)} custom-call(s32[6]{0:T(128)S(1)} %stack.96.meta, bf16[2,128,512]{2,1,0:T(8,128)(2,1)S(1)} %get-tuple-element.113.refs_0_, bf16[2,128,512]{2,1,0:T(8,128)(2,1)S(1)} %collective-permute-done.17.refs_1_, bf16[128,1024]{1,0:T(8,128)(2,1)S(1)} %add.150.refs_0_.refs_2_, ...), custom_call_target="tpu_custom_call", output_to_operand_aliasing={{}: (9, {})} | custom-call | flops 1073741824 | bytes 4194304 | tf_op jit(solution)/shard_map/pallas_call | solution.py:333
  107.2 0.9 shard_map.109
  (69 shorter events, 3.8 us)
Async XLA Ops:
  0.6 14.1 %collective-permute-start.2 = (bf16[4096,512]{1,0:T(8,128)(2,1)}, bf16[4096,512]{1,0:T(8,128)(2,1)}, u32[]{:S(2)}, u32[]{:S(2)}) collective-permute-start(bf16[4096,512]{1,0:T(8,128)(2,1)} %w.1), channel_id=1, source_target_pairs={{0,1},{1,0},{2,3},{3,2},{4,5},{5,4},{6,7},{7,6},{8,9},{9,8},{10,11... | collective-permute-start | bytes 12582920 | tf_op jit(solution)/shard_map/ppermute | solution.py:365
  1.1 9.8 %collective-permute-start = (bf16[128,1024]{1,0:T(8,128)(2,1)}, bf16[128,1024]{1,0:T(8,128)(2,1)S(1)}, u32[]{:S(2)}, u32[]{:S(2)}) collective-permute-start(bf16[128,1024]{1,0:T(8,128)(2,1)} %bitcast.153), channel_id=1, source_target_pairs={{0,4},{4,0},{8,12},{12,8},{1,5},{5,1},{9,13},{13,9},{2,6},{6,2},{1... | collective-permute-start | bytes 786440 | tf_op jit(solution)/shard_map/ppermute | solution.py:366
  3.8 7.1 %collective-permute-start.1 = (bf16[128,1024]{1,0:T(8,128)(2,1)}, bf16[128,1024]{1,0:T(8,128)(2,1)S(1)}, u32[]{:S(2)}, u32[]{:S(2)}) collective-permute-start(bf16[128,1024]{1,0:T(8,128)(2,1)} %bitcast.154), channel_id=1, source_target_pairs={{4,8},{8,4},{5,9},{9,5},{6,10},{10,6},{7,11},{11,7},{20,24},{24,20... | collective-permute-start | bytes 786440 | tf_op jit(solution)/shard_map/ppermute | solution.py:366
  4.5 10.2 %collective-permute-start.3 = (bf16[128,1024]{1,0:T(8,128)(2,1)}, bf16[128,1024]{1,0:T(8,128)(2,1)S(1)}, u32[]{:S(2)}, u32[]{:S(2)}) collective-permute-start(bf16[128,1024]{1,0:T(8,128)(2,1)} %bitcast.155), channel_id=1, source_target_pairs={{0,2},{2,0},{1,3},{3,1},{4,6},{6,4},{5,7},{7,5},{8,10},{10,8},{9,1... | collective-permute-start | bytes 786440 | tf_op jit(solution)/shard_map/ppermute | solution.py:396
  6.0 2.2 %copy-start = (bf16[4096,512]{1,0:T(8,128)(2,1)S(1)}, bf16[4096,512]{1,0:T(8,128)(2,1)}, u32[]{:S(2)}) copy-start(bf16[4096,512]{1,0:T(8,128)(2,1)} %w.1) | copy-start | bytes 12582916
  8.2 6.5 %copy-start.1 = (bf16[1024,1,2,64]{0,3,2,1:T(8,128)(2,1)S(1)}, bf16[1024,1,2,64]{0,3,2,1:T(8,128)(2,1)}, u32[]{:S(2)}) copy-start(bf16[1024,1,2,64]{0,3,2,1:T(8,128)(2,1)} %param.7) | copy-start | bytes 786436
  10.9 8.6 %collective-permute-start.4 = (bf16[128,1024]{1,0:T(8,128)(2,1)S(1)}, bf16[128,1024]{1,0:T(8,128)(2,1)S(1)}, u32[]{:S(2)}, u32[]{:S(2)}) collective-permute-start(bf16[128,1024]{1,0:T(8,128)(2,1)S(1)} %collective-permute-done.refs_2_.refs_4_), channel_id=1, source_target_pairs={{0,2},{2,0},{1,3},{3,1},{4,6},{6,4},{5,7},{7,5},{8,10},{10,8},{9,1... | collective-permute-start | bytes 786440 | tf_op jit(solution)/shard_map/ppermute | solution.py:396
  12.6 11.7 %collective-permute-start.5 = (bf16[128,1024]{1,0:T(8,128)(2,1)S(1)}, bf16[128,1024]{1,0:T(8,128)(2,1)S(1)}, u32[]{:S(2)}, u32[]{:S(2)}) collective-permute-start(bf16[128,1024]{1,0:T(8,128)(2,1)S(1)} %collective-permute-done.1), channel_id=1, source_target_pairs={{4,0},{8,12},{5,1},{9,13},{6,2},{10,14},{7,3},{11,15},{20,16},{24,... | collective-permute-start | bytes 786440 | tf_op jit(solution)/shard_map/ppermute | solution.py:366
  13.9 10.4 %collective-permute-start.6 = (bf16[128,1024]{1,0:T(8,128)(2,1)S(1)}, bf16[128,1024]{1,0:T(8,128)(2,1)S(1)}, u32[]{:S(2)}, u32[]{:S(2)}) collective-permute-start(bf16[128,1024]{1,0:T(8,128)(2,1)S(1)} %collective-permute-done.refs_2_.refs_4_), channel_id=1, source_target_pairs={{4,8},{8,4},{5,9},{9,5},{6,10},{10,6},{7,11},{11,7},{20,24},{24,20... | collective-permute-start | bytes 786440 | tf_op jit(solution)/shard_map/ppermute | solution.py:366
  24.3 5.2 %copy-start.16 = (bf16[128,1024]{1,0:T(8,128)(2,1)}, bf16[128,1024]{1,0:T(8,128)(2,1)S(1)}, u32[]{:S(2)}) copy-start(bf16[128,1024]{1,0:T(8,128)(2,1)S(1)} %collective-permute-done.6) | copy-start | bytes 786436
  24.3 10.0 %collective-permute-start.7 = (bf16[128,1024]{1,0:T(8,128)(2,1)S(1)}, bf16[128,1024]{1,0:T(8,128)(2,1)}, u32[]{:S(2)}, u32[]{:S(2)}) collective-permute-start(bf16[128,1024]{1,0:T(8,128)(2,1)S(1)} %collective-permute-done.6), channel_id=1, source_target_pairs={{4,0},{8,12},{5,1},{9,13},{6,2},{10,14},{7,3},{11,15},{20,16},{24,... | collective-permute-start | bytes 786440 | tf_op jit(solution)/shard_map/ppermute | solution.py:366
  25.7 10.6 %collective-permute-start.8 = (bf16[128,1024]{1,0:T(8,128)(2,1)S(1)}, bf16[128,1024]{1,0:T(8,128)(2,1)S(1)}, u32[]{:S(2)}, u32[]{:S(2)}) collective-permute-start(bf16[128,1024]{1,0:T(8,128)(2,1)S(1)} %add.150.refs_0_.refs_2_), channel_id=1, source_target_pairs={{0,2},{2,0},{1,3},{3,1},{4,6},{6,4},{5,7},{7,5},{8,10},{10,8},{9,1... | collective-permute-start | bytes 786440 | tf_op jit(solution)/shard_map/ppermute | solution.py:396
  26.3 8.0 %copy-start.17 = (s32[2,2,128]{2,1,0:T(2,128)S(1)}, s32[2,2,128]{2,1,0:T(2,128)}, u32[]{:S(2)}) copy-start(s32[2,2,128]{2,1,0:T(2,128)} %param.9) | copy-start | bytes 6148
  29.5 0.8 copy-start.8
  35.7 10.4 %collective-permute-start.9 = (bf16[128,1024]{1,0:T(8,128)(2,1)S(1)}, bf16[128,1024]{1,0:T(8,128)(2,1)}, u32[]{:S(2)}, u32[]{:S(2)}) collective-permute-start(bf16[128,1024]{1,0:T(8,128)(2,1)S(1)} %add.151.refs_0_.refs_4_), channel_id=1, source_target_pairs={{0,2},{2,0},{1,3},{3,1},{4,6},{6,4},{5,7},{7,5},{8,10},{10,8},{9,1... | collective-permute-start | bytes 786440 | tf_op jit(solution)/shard_map/ppermute | solution.py:396
  36.3 1.0 copy-start.9
  37.4 7.1 %copy-start.2 = (bf16[128,1024]{1,0:T(8,128)(2,1)}, bf16[128,1024]{1,0:T(8,128)(2,1)S(1)}, u32[]{:S(2)}) copy-start(bf16[128,1024]{1,0:T(8,128)(2,1)S(1)} %collective-permute-done.8.refs_1_.refs_3_) | copy-start | bytes 786436
  40.8 5.1 %copy-start.4 = (f32[128,1024]{1,0:T(8,128)}, f32[128,1024]{1,0:T(8,128)S(1)}, u32[]{:S(2)}) copy-start(f32[128,1024]{1,0:T(8,128)S(1)} %get-tuple-element.88.refs_0_) | copy-start | bytes 1572868
  40.8 5.1 %copy-start.10 = (f32[128,1024]{1,0:T(8,128)}, f32[128,1024]{1,0:T(8,128)S(1)}, u32[]{:S(2)}) copy-start(f32[128,1024]{1,0:T(8,128)S(1)} %get-tuple-element.89.refs_1_) | copy-start | bytes 1572868
  46.0 49.1 %collective-permute-start.22 = (bf16[7,128,1024]{2,1,0:T(8,128)(2,1)}, bf16[7,128,1024]{2,1,0:T(8,128)(2,1)S(1)}, u32[]{:S(2)}, u32[]{:S(2)}) collective-permute-start(bf16[7,128,1024]{2,1,0:T(8,128)(2,1)} %bitcast_dynamic-update-slice_fusion), channel_id=1, source_target_pairs={{0,1},{1,0},{2,3},{3,2},{4,5},{5,4},{6,7},{7,6},{8,9},{9,8},{10,11... | collective-permute-start | bytes 5505032 | tf_op jit(solution)/shard_map/ppermute | solution.py:365
  46.2 1.0 copy-start.11
  50.4 0.8 copy-start.6
  51.2 4.5 %collective-permute-start.12 = (f32[2,8,128]{2,1,0:T(8,128)S(1)}, f32[2,8,128]{2,1,0:T(8,128)S(1)}, u32[]{:S(2)}, u32[]{:S(2)}) collective-permute-start(f32[2,8,128]{2,1,0:T(8,128)S(1)} %pad_maximum_fusion), channel_id=1, source_target_pairs={{0,6},{2,4},{4,2},{6,0},{8,14},{10,12},{12,10},{14,8},{1,7},{3,5},... | collective-permute-start | bytes 24584 | tf_op jit(solution)/shard_map/ppermute | solution.py:475
  52.5 3.7 %collective-permute-start.11 = (f32[2,8,128]{2,1,0:T(8,128)S(1)}, f32[2,8,128]{2,1,0:T(8,128)S(1)}, u32[]{:S(2)}, u32[]{:S(2)}) collective-permute-start(f32[2,8,128]{2,1,0:T(8,128)S(1)} %pad_maximum_fusion), channel_id=1, source_target_pairs={{0,4},{4,0},{8,12},{12,8},{1,5},{5,1},{9,13},{13,9},{2,6},{6,2},{1... | collective-permute-start | bytes 24584 | tf_op jit(solution)/shard_map/ppermute | solution.py:366
  54.2 3.7 %collective-permute-start.10 = (f32[2,8,128]{2,1,0:T(8,128)S(1)}, f32[2,8,128]{2,1,0:T(8,128)S(1)}, u32[]{:S(2)}, u32[]{:S(2)}) collective-permute-start(f32[2,8,128]{2,1,0:T(8,128)S(1)} %pad_maximum_fusion), channel_id=1, source_target_pairs={{0,2},{2,0},{1,3},{3,1},{4,6},{6,4},{5,7},{7,5},{8,10},{10,8},{9,1... | collective-permute-start | bytes 24584 | tf_op jit(solution)/shard_map/ppermute | solution.py:396
  57.9 4.7 %collective-permute-start.13 = (f32[8,256]{1,0:T(8,128)S(1)}, f32[8,256]{1,0:T(8,128)}, u32[]{:S(2)}, u32[]{:S(2)}) collective-permute-start(f32[8,256]{1,0:T(8,128)S(1)} %pad_maximum_fusion.1.refs_3_), channel_id=1, source_target_pairs={{0,8},{8,0},{4,12},{12,4},{1,9},{9,1},{5,13},{13,5},{2,10},{10,2},... | collective-permute-start | bytes 24584 | tf_op jit(solution)/shard_map/ppermute | solution.py:366
  62.6 1.0 copy-start.5
  63.7 1.0 copy-start.7
  64.7 0.7 copy-start.12
  65.4 0.7 copy-start.13
  66.1 0.7 copy-start.14
  66.7 0.7 copy-start.15
  70.4 6.4 %collective-permute-start.14 = (bf16[1024,128]{1,0:T(8,128)(2,1)S(1)}, bf16[1024,128]{1,0:T(8,128)(2,1)S(1)}, u32[]{:S(2)}, u32[]{:S(2)}) collective-permute-start(bf16[1024,128]{1,0:T(8,128)(2,1)S(1)} %get-tuple-element.93), channel_id=1, source_target_pairs={{0,2},{2,0},{1,3},{3,1},{4,6},{6,4},{5,7},{7,5},{8,10},{10,8},{9,1... | collective-permute-start | bytes 786440 | tf_op jit(solution)/shard_map/ppermute | solution.py:489
  71.1 11.9 %collective-permute-start.17 = (bf16[2,128,512]{2,1,0:T(8,128)(2,1)S(1)}, bf16[2,128,512]{2,1,0:T(8,128)(2,1)S(1)}, u32[]{:S(2)}, u32[]{:S(2)}) collective-permute-start(bf16[2,128,512]{2,1,0:T(8,128)(2,1)S(1)} %get-tuple-element.103), channel_id=1, source_target_pairs={{0,1},{1,0},{2,3},{3,2},{4,5},{5,4},{6,7},{7,6},{8,9},{9,8},{10,11... | collective-permute-start | bytes 786440 | tf_op jit(solution)/shard_map/ppermute | solution.py:365
  71.1 11.9 %collective-permute-start.18 = (bf16[1,128,1024]{2,1,0:T(8,128)(2,1)}, bf16[1,128,1024]{2,1,0:T(8,128)(2,1)S(1)}, u32[]{:S(2)}, u32[]{:S(2)}) collective-permute-start(bf16[1,128,1024]{2,1,0:T(8,128)(2,1)} %bitcast.31), channel_id=1, source_target_pairs={{0,1},{1,0},{2,3},{3,2},{4,5},{5,4},{6,7},{7,6},{8,9},{9,8},{10,11... | collective-permute-start | bytes 786440 | tf_op jit(solution)/shard_map/ppermute | solution.py:365
  76.8 7.7 %collective-permute-start.15 = (bf16[1024,128]{1,0:T(8,128)(2,1)S(1)}, bf16[1024,128]{1,0:T(8,128)(2,1)S(1)}, u32[]{:S(2)}, u32[]{:S(2)}) collective-permute-start(bf16[1024,128]{1,0:T(8,128)(2,1)S(1)} %get-tuple-element.100), channel_id=1, source_target_pairs={{0,2},{2,0},{1,3},{3,1},{4,6},{6,4},{5,7},{7,5},{8,10},{10,8},{9,1... | collective-permute-start | bytes 786440 | tf_op jit(solution)/shard_map/ppermute | solution.py:489
  77.8 7.8 %collective-permute-start.16 = (bf16[1024,128]{1,0:T(8,128)(2,1)S(1)}, bf16[1024,128]{1,0:T(8,128)(2,1)S(1)}, u32[]{:S(2)}, u32[]{:S(2)}) collective-permute-start(bf16[1024,128]{1,0:T(8,128)(2,1)S(1)} %shard_map.101), channel_id=1, source_target_pairs={{0,4},{12,8},{1,5},{13,9},{2,6},{14,10},{3,7},{15,11},{16,20},{28,... | collective-permute-start | bytes 786440 | tf_op jit(solution)/shard_map/ppermute | solution.py:366
  85.6 12.3 %collective-permute-start.19 = (bf16[1024,128]{1,0:T(8,128)(2,1)S(1)}, bf16[1024,128]{1,0:T(8,128)(2,1)S(1)}, u32[]{:S(2)}, u32[]{:S(2)}) collective-permute-start(bf16[1024,128]{1,0:T(8,128)(2,1)S(1)} %get-tuple-element.109), channel_id=1, source_target_pairs={{0,2},{2,0},{1,3},{3,1},{4,6},{6,4},{5,7},{7,5},{8,10},{10,8},{9,1... | collective-permute-start | bytes 786440 | tf_op jit(solution)/shard_map/ppermute | solution.py:489
  87.2 10.7 %collective-permute-start.20 = (bf16[1024,128]{1,0:T(8,128)(2,1)S(1)}, bf16[1024,128]{1,0:T(8,128)(2,1)S(1)}, u32[]{:S(2)}, u32[]{:S(2)}) collective-permute-start(bf16[1024,128]{1,0:T(8,128)(2,1)S(1)} %shard_map.103), channel_id=1, source_target_pairs={{4,8},{8,4},{5,9},{9,5},{6,10},{10,6},{7,11},{11,7},{20,24},{24,20... | collective-permute-start | bytes 786440 | tf_op jit(solution)/shard_map/ppermute | solution.py:366
  88.0 11.1 %collective-permute-start.21 = (bf16[1024,128]{1,0:T(8,128)(2,1)S(1)}, bf16[1024,128]{1,0:T(8,128)(2,1)S(1)}, u32[]{:S(2)}, u32[]{:S(2)}) collective-permute-start(bf16[1024,128]{1,0:T(8,128)(2,1)S(1)} %shard_map.104), channel_id=1, source_target_pairs={{0,4},{12,8},{1,5},{13,9},{2,6},{14,10},{3,7},{15,11},{16,20},{28,... | collective-permute-start | bytes 786440 | tf_op jit(solution)/shard_map/ppermute | solution.py:366
  95.0 7.8 %collective-permute-start.26 = (f32[1,128]{1,0:T(1,128)S(1)}, f32[1,128]{1,0:T(1,128)S(1)}, u32[]{:S(2)}, u32[]{:S(2)}) collective-permute-start(f32[1,128]{1,0:T(1,128)S(1)} %get-tuple-element.134), channel_id=1, source_target_pairs={{0,1},{1,0},{2,3},{3,2},{4,5},{5,4},{6,7},{7,6},{8,9},{9,8},{10,11... | collective-permute-start | bytes 1544 | tf_op jit(solution)/shard_map/ppermute | solution.py:365
  97.9 5.4 %copy-start.3 = (bf16[128,1024]{1,0:T(8,128)(2,1)S(1)}, bf16[128,1024]{1,0:T(8,128)(2,1)}, u32[]{:S(2)}) copy-start(bf16[128,1024]{1,0:T(8,128)(2,1)} %copy-done.2) | copy-start | bytes 786436
  99.1 7.7 %collective-permute-start.23 = (bf16[1024,128]{1,0:T(8,128)(2,1)S(1)}, bf16[1024,128]{1,0:T(8,128)(2,1)S(1)}, u32[]{:S(2)}, u32[]{:S(2)}) collective-permute-start(bf16[1024,128]{1,0:T(8,128)(2,1)S(1)} %get-tuple-element.123), channel_id=1, source_target_pairs={{0,2},{2,0},{1,3},{3,1},{4,6},{6,4},{5,7},{7,5},{8,10},{10,8},{9,1... | collective-permute-start | bytes 786440 | tf_op jit(solution)/shard_map/ppermute | solution.py:489
  99.5 7.7 %collective-permute-start.24 = (bf16[1024,128]{1,0:T(8,128)(2,1)S(1)}, bf16[1024,128]{1,0:T(8,128)(2,1)S(1)}, u32[]{:S(2)}, u32[]{:S(2)}) collective-permute-start(bf16[1024,128]{1,0:T(8,128)(2,1)S(1)} %shard_map.106), channel_id=1, source_target_pairs={{0,4},{4,0},{8,12},{12,8},{1,5},{5,1},{9,13},{13,9},{2,6},{6,2},{1... | collective-permute-start | bytes 786440 | tf_op jit(solution)/shard_map/ppermute | solution.py:366
  102.1 5.0 %collective-permute-start.25 = (bf16[1024,128]{1,0:T(8,128)(2,1)S(1)}, bf16[1024,128]{1,0:T(8,128)(2,1)S(1)}, u32[]{:S(2)}, u32[]{:S(2)}) collective-permute-start(bf16[1024,128]{1,0:T(8,128)(2,1)S(1)} %shard_map.107), channel_id=1, source_target_pairs={{4,8},{8,4},{5,9},{9,5},{6,10},{10,6},{7,11},{11,7},{20,24},{24,20... | collective-permute-start | bytes 786440 | tf_op jit(solution)/shard_map/ppermute | solution.py:366

commit v8 on v7

--- a/solution.py
+++ b/solution.py
@@ -83,13 +83,14 @@
     return jnp.where(lane == 0, top, jnp.where(lane == 1, total, picked)).T[:8, :]
 
 
-def logits_kernel(plan, columns, part, n_voc, fresh, meta, work, *refs):
+def logits_kernel(plan, columns, part, n_voc, fresh, n_earlier, meta, work, *refs):
     refs = list(refs)
     width = part * n_voc
     far = refs.pop(0) if fresh else None
     chunks = {(t, i): refs.pop(0) for t, parts, _, _ in plan for i in parts}
     accs = {t: refs.pop(0) for t, _, has_acc, _ in plan if has_acc}
     wanted = {t: refs.pop(0) for t, _, _, done in plan if done}
+    earlier = [refs.pop(0) for _ in range(n_earlier)]
     used = sorted({i for _, parts, _, _ in plan for i in parts})
     starts = [pl.multiple_of(meta[i] * part, part) for i in used]
     if fresh:
@@ -103,12 +104,7 @@
         into.wait()
         kept = pltpu.make_async_copy(held, refs[-3].at[pl.ds(width, width), :], far_sems.at[1])
         kept.start()
-    outs = {}
-    stats = {}
-    for t, _, _, done in plan:
-        outs[t] = refs.pop(0)
-        if done:
-            stats[t] = refs.pop(0)
+    outs = {t: refs.pop(0) for t, _, _, _ in plan}
     for n, i in enumerate(used):
         for copy in coming[n]:
             copy.wait()
@@ -125,24 +121,26 @@
                 elif has_acc:
                     product += accs[t][:, at]
                 outs[t][:, at] = product
-    for t in stats:
-        own, beside = outs[t][:, :columns], outs[t][:, columns:]
-        stats[t][...] = row_stats(own, beside, wanted[t][...], meta[n_voc], meta[n_voc + 1])
+    if wanted:
+        stats = refs[0]
+        for n, a in enumerate(earlier):
+            stats[n] = a[0]
+        for n, t in enumerate(wanted, n_earlier):
+            own, beside = outs[t][:, :columns], outs[t][:, columns:]
+            stats[n] = row_stats(own, beside, wanted[t][...], meta[n_voc], meta[n_voc + 1])
     if fresh:
         kept.wait()
 
 
-def logits_call(plan, work, meta, part, n_voc, far=None):
+def logits_call(plan, work, meta, part, n_voc, far=None, earlier=()):
     columns = work.shape[1]
     accs = [acc for _, _, acc, _ in plan if acc is not None]
     wanted = [w for _, _, _, w in plan if w is not None]
     chunks = [parts[i] for _, parts, _, _ in plan for i in sorted(parts)]
     rows = chunks[0].shape[0]
-    out_shape = []
-    for _, _, _, w in plan:
-        out_shape.append(shape_of((rows, 2 * columns), F32))
-        if w is not None:
-            out_shape.append(shape_of((8, rows), F32))
+    out_shape = [shape_of((rows, 2 * columns), F32)] * len(plan)
+    if wanted:
+        out_shape.append(shape_of((len(earlier) + len(wanted), 8, rows), F32))
     out_specs = [IN_VMEM] * len(out_shape)
     kernel_plan = [(t, sorted(parts), acc is not None, w is not None) for t, parts, acc, w in plan]
     n_used = len({i for _, parts, _, _ in plan for i in parts})
@@ -151,9 +149,9 @@
     if fresh:
         out_shape.append(shape_of(work.shape, work.dtype))
         out_specs.append(IN_PLACE)
-    operands = chunks + accs + wanted
-    return pl.pallas_call(
-        functools.partial(logits_kernel, kernel_plan, columns, part, n_voc, fresh),
+    operands = chunks + accs + wanted + list(earlier)
+    return pl.pallas_call(
+        functools.partial(logits_kernel, kernel_plan, columns, part, n_voc, fresh, len(earlier)),
         out_shape=out_shape,
         in_specs=[IN_SMEM] + [IN_PLACE] * len(in_place) + [IN_VMEM] * len(operands),
         out_specs=out_specs,
@@ -174,7 +172,7 @@
         out[...] = here[:, t * rows:(t + 1) * rows].astype(BF16)
 
 
-def grads_kernel(n_blocks, n_stats, columns, part, width, window, meta, start, sums, refer, cotangent, work, *refs):
+def grads_kernel(n_blocks, n_stats, columns, part, width, window, meta, small, work, *refs):
     refs = list(refs)
     logits = [refs.pop(0) for _ in range(n_blocks)]
     target = refs.pop(0)
@@ -184,7 +182,7 @@
     send = refs[6:-2]
     coming = fetch(work, width, pl.multiple_of(meta[0] * part, part), part, slots, 0, sems)
     rows = logits[0].shape[0]
-    pair, me_ctx = meta[3], meta[4]
+    me_ctx, start = meta[3], meta[4]
     top = stats[0][0:1, :]
     for s in stats[1:]:
         top = jnp.maximum(top, s[0:1, :])
@@ -197,15 +195,14 @@
     masks = []
     for t in range(n_blocks):
         block = lax.rem(me_ctx + (n_blocks - t), n_blocks)
-        seen = lax.rem(row, window) + block * window >= start[pair]
+        seen = lax.rem(row, window) + block * window >= start
         masks.append(jnp.where(seen, jnp.where(row < window, 1.0, -1.0), 0.0))
     signed_mask = jnp.concatenate(masks, axis=1)
     token_logp = picked - top - jnp.log(total)
-    offset = (sums[pair, 0] - refer[pair, 0]) - (sums[pair, 1] - refer[pair, 1])
     zeros = jnp.zeros((1, 128), F32)
-    margin = BETA * (jnp.sum(signed_mask * token_logp, axis=1, keepdims=True) + (zeros + offset))
+    margin = BETA * (jnp.sum(signed_mask * token_logp, axis=1, keepdims=True) + (zeros + small[0]))
     loss[...] = jnp.maximum(-margin, 0.0) + jnp.log1p(jnp.exp(-jnp.abs(margin)))
-    factor = -BETA * (1.0 / (1.0 + jnp.exp(margin))) * cotangent[pair]
+    factor = -BETA * (1.0 / (1.0 + jnp.exp(margin))) * small[1]
     weight = factor[:, 0:1] * signed_mask
     lines = lax.broadcasted_iota(jnp.int32, (128, top.shape[1]), 0)
     packed = jnp.where(lines == 0, top, jnp.where(lines == 1, weight, 1.0 / total)).T
@@ -255,12 +252,12 @@
     return pl.pallas_call(
         functools.partial(grads_kernel, n_blocks, len(stats), columns, part, width, window),
         out_shape=out_shape,
-        in_specs=[IN_SMEM] * 5 + [IN_PLACE] + [IN_VMEM] * len(operands),
+        in_specs=[IN_SMEM] * 2 + [IN_PLACE] + [IN_VMEM] * len(operands),
         out_specs=[IN_VMEM] * len(out_shape),
         scratch_shapes=weight_slots(1, part, columns),
         compiler_params=params(),
         cost_estimate=cost(4 * n_blocks * rows * part * columns, 8 * part * columns),
-    )(meta, *small, work, *operands)
+    )(meta, small, work, *operands)
 
 
 def spread_call(flipped_own, flipped_far, work, k_ids, part, width, rows):
@@ -278,6 +275,69 @@
     )(jnp.stack(k_ids).astype(jnp.int32), work, flipped_own, flipped_far)
     each = len(outs) // n_parts
     return [(outs[i * each], list(outs[i * each + 1:(i + 1) * each])) for i in range(n_parts)]
+
+
+def either_kernel(a, b, out):
+    out[...] = a[...] + b[...]
+
+
+def either(a, b):
+    return pl.pallas_call(
+        either_kernel,
+        out_shape=shape_of(a.shape, a.dtype),
+        in_specs=[IN_VMEM] * 2,
+        out_specs=IN_VMEM,
+        compiler_params=params(),
+        cost_estimate=cost(a.size, 6 * a.size),
+    )(a, b)
+
+
+def stack_kernel(*refs):
+    *arrays, out, sems = refs
+    copies = [pltpu.make_async_copy(a, out.at[i], sems.at[i]) for i, a in enumerate(arrays)]
+    for copy in copies:
+        copy.start()
+    for copy in copies:
+        copy.wait()
+
+
+def stack_call(arrays):
+    return pl.pallas_call(
+        stack_kernel,
+        out_shape=shape_of((len(arrays),) + arrays[0].shape, arrays[0].dtype),
+        in_specs=[IN_PLACE] * len(arrays),
+        out_specs=IN_PLACE,
+        scratch_shapes=[pltpu.SemaphoreType.DMA((len(arrays),))],
+        compiler_params=params(),
+        cost_estimate=cost(1, 4 * len(arrays) * arrays[0].size),
+    )(*arrays)
+
+
+def merge_kernel(turns, *refs):
+    *seen, out = refs
+    n_blocks, _, rows = seen[0].shape
+    out[...] = jnp.zeros_like(out)
+    for b in range(n_blocks):
+        these = [s[(b - t) % n_blocks] for t, s in zip(turns, seen)]
+        top = these[0][0:1, :]
+        for s in these[1:]:
+            top = jnp.maximum(top, s[0:1, :])
+        at = slice(b * rows, (b + 1) * rows)
+        out[0:1, at] = top
+        out[1:2, at] = sum(s[1:2, :] * jnp.exp(s[0:1, :] - top) for s in these)
+        out[2:3, at] = sum(s[2:3, :] for s in these)
+
+
+def merge_call(turns, seen):
+    n_blocks, lines, rows = seen[0].shape
+    return pl.pallas_call(
+        functools.partial(merge_kernel, turns),
+        out_shape=shape_of((lines, n_blocks * rows), F32),
+        in_specs=[IN_VMEM] * len(seen),
+        out_specs=IN_VMEM,
+        compiler_params=params(),
+        cost_estimate=cost(1, 4 * len(seen) * n_blocks * lines * rows),
+    )(*seen)
 
 
 def add_kernel(turned, kept, *refs):
@@ -379,20 +439,23 @@
     work = hold(head_weight)
     width = head_weight.shape[0]
 
-    pair = lax.broadcasted_iota(jnp.int32, targets.shape, 0)
-
-    def by_block(all_targets):
-        mine = jnp.sum(jnp.where(pair == me_dp, all_targets, 0), axis=0)
-        blocks = [mine[:, b * window:(b + 1) * window].reshape(rows) for b in range(n_ctx)]
-        wanted = []
-        for t in range(n_ctx):
-            at = (me_ctx - t) % n_ctx
-            wanted.append(sum(jnp.where(at == b, blocks[b], 0) for b in range(n_ctx))[:, None])
-        return wanted
+    def mine(a):
+        pair = lax.broadcasted_iota(jnp.int32, a.shape, 0)
+        return jnp.sum(jnp.where(pair == me_dp, a, jnp.zeros_like(a)), axis=0)
+
+    blocks = [mine(targets)[:, b * window:(b + 1) * window].reshape(rows) for b in range(n_ctx)]
+    wanted = []
+    for t in range(n_ctx):
+        at = (me_ctx - t) % n_ctx
+        wanted.append(sum(jnp.where(at == b, blocks[b], 0) for b in range(n_ctx))[:, None])
+    target = jnp.concatenate(wanted)
+    ratio = mine(other_sums) - mine(ref_logp)
+    small = jnp.stack([ratio[0] - ratio[1], mine(loss_cotangent)])
+    meta_grads = jnp.stack([part_of[n_voc - 1]] + firsts + [me_ctx, mine(response_start)]).astype(jnp.int32)
 
     own = hidden.transpose(1, 2, 3, 0).reshape(rows, part)
     final = n_voc - 1
-    call = functools.partial(logits_call, meta=meta, part=part, n_voc=n_voc)
+    call = lambda *args, **more: logits_call(*args, meta=meta, part=part, n_voc=n_voc, **more)
     cross = lambda a: [lax.ppermute(a, "ctx", ring(n_ctx, t)) for t in beyond]
     chunk = {}
 
@@ -416,17 +479,20 @@
     if line:
         first = along(own, PAIRS_OUT)
         inner = along(own, PAIR_IN)
-        (first, inner), (work,) = together([first, inner], [work])
+        (first, inner), (work, target, small, meta_grads, meta), wanted = together(
+            [first, inner], [work, target, small, meta_grads, meta], wanted
+        )
         over = cross(first)
         outer, inner_last = along(inner, TO_ENDS), along(first, PAIR_IN)
         arrive(1, first, over)
         logits, work = first_logits(work)
         over, (inner, outer, inner_last), logits = together(over, [inner, outer, inner_last], logits)
         arrive(1, first, over)
-        arrive(2, inner + outer, cross(inner + outer))
+        inner = either(inner, outer)
+        arrive(2, inner, cross(inner))
         outer = along(inner_last, TO_ENDS)
         (inner_last, outer), logits = together([inner_last, outer], more_logits(2, logits))
-        last = inner_last + outer
+        last = either(inner_last, outer)
     else:
         near = [own] + [along(own, ring(n_voc, i)) for i in range(1, n_voc)]
         logits = None
@@ -439,56 +505,38 @@
             (near[i + 1],), logits = together([near[i + 1]], logits)
         last = near[final]
     arrive(final, last, cross(last))
-    (raw_targets,), _ = together([targets], logits)
-    wanted = by_block(raw_targets)
-    target = jnp.concatenate(wanted)
-
     done = call(
         [(0, {final: chunk[0, final]}, logits[0], wanted[0])]
         + [(t, {final - 1: chunk[t, final - 1]}, logits[t], None) for t in beyond],
         work,
     )
-    logits, stats = [done[0]] + list(done[2:]), [done[1]]
-    done = call([(t, {final: chunk[t, final]}, logits[t], wanted[t]) for t in beyond], work)
-    logits = [logits[0]] + list(done[0::2])
-    stats = stats + list(done[1::2])
-
-    late = [(t, final) for t in beyond]
-    soon = [k for k in chunk if k not in late]
-    far_soon = dp_swap(jnp.stack(together([chunk[k] for k in soon], [stats[0]])[0]))
-
-    def merge(seen):
-        merged = []
-        for b in range(n_ctx):
-            these = [s[(b - t) % n_ctx] for t, s in seen]
-            top = these[0][0]
-            for s in these[1:]:
-                top = jnp.maximum(top, s[0])
-            total = sum(s[1] * jnp.exp(s[0] - top) for s in these)
-            picked = sum(s[2] for s in these)
-            merged.append(jnp.pad(jnp.stack([top, total, picked]), ((0, 5), (0, 0))))
-        return jnp.concatenate(merged, axis=1)
-
-    stats = jnp.stack(stats)
+    last, done = together([chunk[t, final] for t in beyond], list(done))
+    arrive(final, chunk[0, final], last)
+    *logits, stats = done
+
+    far_chunks = dp_swap(stack_call(list(chunk.values())))
+
+    *others, stats = call(
+        [(t, {final: chunk[t, final]}, logits[t], wanted[t]) for t in beyond], work, earlier=[stats]
+    )
+    logits = [logits[0]] + others
+
     if line and n_ctx == 2:
         corner = [(2 * a + c, 2 * b + (1 - c)) for a, b in PAIRS_OUT for c in range(2)]
         diagonal = lax.ppermute(stats, ("vocab", "ctx"), corner)
-        merged = merge([(0, stats), (1, cross(stats)[0]), (0, along(stats, PAIRS_OUT)), (1, diagonal)])
+        merged = merge_call([0, 1, 0, 1], [stats, cross(stats)[0], along(stats, PAIRS_OUT), diagonal])
         all_stats = [merged, along(merged, SWAP_HALVES)]
     else:
-        merged = merge([(0, stats)] + list(zip(beyond, cross(stats))))
+        merged = merge_call([0] + beyond, [stats] + cross(stats))
         all_stats = [merged] + [along(merged, ring(n_voc, s)) for s in range(1, n_voc)]
 
-    meta_grads = jnp.stack([part_of[final]] + firsts + [me_dp, me_ctx]).astype(jnp.int32)
-    small = (response_start, other_sums, ref_logp, loss_cotangent)
     grads_own, grads_far, flipped_own, flipped_far, loss, kept, *send = grads_call(
         logits, target, all_stats, small, work, meta_grads, part, width, window
     )
     theirs = dp_swap(grads_far)
-    far_late = dp_swap(jnp.stack(together([chunk[k] for k in late], [kept])[0]))
+
     back = lambda cs: [lax.ppermute(c, "ctx", ring(n_ctx, -t)) for t, c in zip(beyond, cs)]
     shares = {final: (kept, list(send))}
-    leave = list(range(final))[::-1]
 
     def more_shares(slots):
         done = spread_call(flipped_own, flipped_far, work, [part_of[i] for i in slots], part, width, rows)
@@ -502,8 +550,6 @@
 
     over = {}
     near_over = lambda i, *more: add_call(shares[i][0], over[i] + list(more))
-    head = functools.partial(head_call, near=chunk, far=[(soon, far_soon), (late, far_late)], meta=meta)
-    early, rest = list(range(n_voc // 2)), list(range(n_voc // 2, n_voc))
     landed, grad_head = [], None
     for i in range(n_voc)[::-1]:
         over[i] = back(shares[i][1])
@@ -516,27 +562,20 @@
             came = [along(near_over(3, landed[0]), PAIR_IN), along(near_over(2), FROM_ENDS)]
         elif i == 0:
             came = [along(near_over(1, landed[0]), PAIRS_OUT), along(near_over(2, landed[1]), PAIR_IN)]
-        if i == 0:
-            beside = [head(rest, grads=[grads_own, theirs], out=grad_head)]
-        elif i == 1:
-            beside = [head(early, grads=[grads_own, theirs])]
-        elif i == final:
-            beside = more_shares(leave[:2])
-        elif i == final - 1:
-            beside = [theirs, far_late] + more_shares(leave[2:])
-        sends = shares[i - 1][1] if i and i - 1 in shares else []
-        over[i], came, beside, sends = together(over[i], came, beside, sends)
+        if i:
+            beside = more_shares([i - 1])
+        else:
+            grad_head = head_call(list(range(n_voc)), chunk, [(list(chunk), far_chunks)], [grads_own, theirs], meta)
+            beside = [grad_head]
+        swapped = [theirs] if i == final - 1 else []
+        over[i], came, beside, swapped = together(over[i], came, beside, swapped)
         landed = came if line else landed + came
-        if i <= 1:
+        if i:
+            set_shares([i - 1], beside)
+        else:
             grad_head, = beside
-        elif i == final:
-            set_shares(leave[:2], beside)
-        elif i == final - 1:
-            theirs, far_late = beside[:2]
-            set_shares(leave[2:], beside[2:])
-            head = functools.partial(head_call, near=chunk, far=[(soon, far_soon), (late, far_late)], meta=meta)
-        if sends:
-            shares[i - 1] = (shares[i - 1][0], list(sends))
+        if swapped:
+            theirs, = swapped
     kept = shares[0][0]
     summed = add_call(kept, over[0] + landed, turned=True)
     grad_hidden = summed.reshape(1, sides, window, part).transpose(3, 0, 1, 2)

time: 110 us -> 104 us (0.945); the launches traced: 108 us -> 104 us
  local copies, waits for them, and re-layouts: 17 us -> 7.82 us
  waiting for transfers between devices: 19.5 us -> 25.7 us
  starting transfers between devices: 34 us -> 28.8 us
  other arithmetic: 2.5 us -> 4.82 us
    unnamed x42 -> x14, local copies, waits for them, and re-layouts: 15 us -> 5.86 us
    ppermute x4, waiting for transfers between devices: 2.31 us -> 9.58 us  [shards(): lax.ppermute(c, 'ctx', ring(n_ctx, -t))]
    ppermute x12, starting transfers between devices: 23.3 us -> 17.8 us  [shards(): along = lambda a, by: lax.ppermute(a, 'vocab', by)]
    reduce_sum x1 -> x4, other arithmetic: 0.08 us -> 3.5 us  [mine(): return jnp.sum(jnp.where(pair == me_dp, a, jnp.zeros_like(a)), axis=0)]
    ppermute x12, waiting for transfers between devices: 14.6 us -> 12.4 us  [shards(): along = lambda a, by: lax.ppermute(a, 'vocab', by)]
    ppermute x1, waiting for transfers between devices: 0.98 us -> 2.8 us  [shards(): diagonal = lax.ppermute(stats, ('vocab', 'ctx'), corner)]
    pallas_call x0 -> x4, Pallas kernels: none -> 1.45 us  [the longest x1 1.37 us: stack_call(): pl.pallas_call(stack_kernel, out_shape=shape_of((len(arrays),) + arrays[0...]
    ppermute x5, starting transfers between devices: 4.97 us -> 6.25 us  [shards(): cross = lambda a: [lax.ppermute(a, 'ctx', ring(n_ctx, t)) for t in beyond]]
  transfers between devices with their start and end apart: 27 -> 26, of which waited for: 13 -> 11; matrix products, arithmetic and copies ran while one was open for 8% -> 7% of each run, Pallas kernels for 31% -> 31%
where the time goes in v8:
time: 104 us
  Pallas kernels  34.3 us (33%)
  starting transfers between devices  28.8 us (28%)
  waiting for transfers between devices  25.7 us (25%)
  local copies, waits for them, and re-layouts  7.82 us (8%)
  other arithmetic  4.82 us (5%)
  between operations  2.21 us (2%)
    ppermute x12, starting transfers between devices, shards(): along = lambda a, by: lax.ppermute(a, 'vocab', by)  17.8 us
    pallas_call x4, Pallas kernels, logits_call(): pl.pallas_call(functools.partial(logits_kernel, kernel_plan, columns, par...  14.3 us
    ppermute x12, waiting for transfers between devices, shards(): along = lambda a, by: lax.ppermute(a, 'vocab', by)  12.4 us
    ppermute x4, waiting for transfers between devices, shards(): lax.ppermute(c, 'ctx', ring(n_ctx, -t))  9.58 us
    pallas_call x3, Pallas kernels, spread_call(): pl.pallas_call(functools.partial(spread_kernel, part, width, n_parts), ou...  6.8 us
    ppermute x5, starting transfers between devices, shards(): cross = lambda a: [lax.ppermute(a, 'ctx', ring(n_ctx, t)) for t in beyond]  6.25 us
    unnamed x14, local copies, waits for them, and re-layouts  5.86 us
    pallas_call x1, Pallas kernels, head_call(): pl.pallas_call(functools.partial(head_kernel, slots_here, list(near), [ke...  5.63 us
  transfers between devices with their start and end apart: 26, of which 11 were waited for; matrix products, arithmetic and copies ran while one was open for 7% of the time, Pallas kernels for 31%

profile of v8, /device:TPU:0, one launch (start us, length us, event | category | flops | bytes accessed | tf_op | source)
XLA Modules:
  0.0 103.7 jit_solution(12503707023967389004)
XLA Ops:
  0.6 0.5 collective-permute-start.2
  1.1 2.7 %collective-permute-start = (bf16[128,1024]{1,0:T(8,128)(2,1)}, bf16[128,1024]{1,0:T(8,128)(2,1)S(1)}, u32[]{:S(2)}, u32[]{:S(2)}) collective-permute-start(bf16[128,1024]{1,0:T(8,128)(2,1)} %bitcast.19), channel_id=1, source_target_pairs={{0,4},{4,0},{8,12},{12,8},{1,5},{5,1},{9,13},{13,9},{2,6},{6,2},{1... | collective-permute-start | bytes 786440 | tf_op jit(solution)/shard_map/ppermute | solution.py:426
  3.8 0.7 collective-permute-start.1
  4.5 1.6 %collective-permute-start.3 = (bf16[128,1024]{1,0:T(8,128)(2,1)}, bf16[128,1024]{1,0:T(8,128)(2,1)S(1)}, u32[]{:S(2)}, u32[]{:S(2)}) collective-permute-start(bf16[128,1024]{1,0:T(8,128)(2,1)} %bitcast.21), channel_id=1, source_target_pairs={{0,2},{2,0},{1,3},{3,1},{4,6},{6,4},{5,7},{7,5},{8,10},{10,8},{9,1... | collective-permute-start | bytes 786440 | tf_op jit(solution)/shard_map/ppermute | solution.py:459
  6.0 0.8 select_reduce_fusion
  7.0 0.8 select_reduce_fusion.1
  7.8 1.4 %select_reduce_fusion.3 = s32[]{:T(128)} fusion(s32[2]{0:T(128)} %param.10, s32[]{:T(128)S(6)} %axis_index.35), kind=kLoop, calls=%fused_computation.8 | loop fusion | flops 5 | bytes 16 | tf_op jit(solution)/shard_map/reduce_sum | solution.py:444
  9.2 0.6 fusion
  9.8 2.2 %copy-done = bf16[4096,512]{1,0:T(8,128)(2,1)S(1)} copy-done((bf16[4096,512]{1,0:T(8,128)(2,1)S(1)}, bf16[4096,512]{1,0:T(8,128)(2,1)}, u32[]{:S(2)}) %copy-start) | copy-done | bytes 4194328
  12.0 2.0 %shard_map.94.work = bf16[53248,512]{1,0:T(8,128)(2,1)} custom-call(bf16[4096,512]{1,0:T(8,128)(2,1)S(1)} %copy-done), custom_call_target="tpu_custom_call" | custom-call | flops 1 | bytes 8388608 | tf_op jit(solution)/shard_map/pallas_call | solution.py:52
  15.2 0.8 stack.50.meta
  16.0 0.6 select_reduce_fusion.4
  16.6 0.7 pad_maximum_fusion.small
  17.4 0.6 collective-permute-start.4
  17.9 1.3 %collective-permute-start.5 = (bf16[128,1024]{1,0:T(8,128)(2,1)S(1)}, bf16[128,1024]{1,0:T(8,128)(2,1)S(1)}, u32[]{:S(2)}, u32[]{:S(2)}) collective-permute-start(bf16[128,1024]{1,0:T(8,128)(2,1)S(1)} %collective-permute-done.1.a), channel_id=1, source_target_pairs={{4,0},{8,12},{5,1},{9,13},{6,2},{10,14},{7,3},{11,15},{20,16},{24,... | collective-permute-start | bytes 786440 | tf_op jit(solution)/shard_map/ppermute | solution.py:426
  19.2 0.7 collective-permute-start.6
  19.9 4.8 %shard_map.95 = (f32[128,1024]{1,0:T(8,128)S(1)}, f32[128,1024]{1,0:T(8,128)S(1)}, bf16[53248,512]{1,0:T(8,128)(2,1)}) custom-call(s32[6]{0:T(128)S(1)} %stack.54.meta, bf16[53248,512]{1,0:T(8,128)(2,1)} %shard_map.94.work, bf16[4096,512]{1,0:T(8,128)(2,1)} %collective-permute-done.2.refs_0_, ...), custom_call_target="tpu_custom_call", output_to_operand_aliasing={{2}: (1, {})} | custom-call | flops 805306368 | bytes 4194304 | tf_op jit(solution)/shard_map/pallas_call | solution.py:153
  24.8 0.7 collective-permute-done.4.refs_1_.refs_3_.refs_5_
  25.5 3.9 %collective-permute-done.5.b = bf16[128,1024]{1,0:T(8,128)(2,1)S(1)} collective-permute-done((bf16[128,1024]{1,0:T(8,128)(2,1)S(1)}, bf16[128,1024]{1,0:T(8,128)(2,1)S(1)}, u32[]{:S(2)}, u32[]{:S(2)}) %collective-permute-start.5) | collective-permute-done | bytes 262176 | tf_op jit(solution)/shard_map/ppermute | solution.py:426
  29.4 1.3 %collective-permute-start.7 = (bf16[128,1024]{1,0:T(8,128)(2,1)S(1)}, bf16[128,1024]{1,0:T(8,128)(2,1)S(1)}, u32[]{:S(2)}, u32[]{:S(2)}) collective-permute-start(bf16[128,1024]{1,0:T(8,128)(2,1)S(1)} %collective-permute-done.6.a), channel_id=1, source_target_pairs={{4,0},{8,12},{5,1},{9,13},{6,2},{10,14},{7,3},{11,15},{20,16},{24,... | collective-permute-start | bytes 786440 | tf_op jit(solution)/shard_map/ppermute | solution.py:426
  30.7 1.6 %collective-permute-start.9 = (bf16[128,1024]{1,0:T(8,128)(2,1)S(1)}, bf16[128,1024]{1,0:T(8,128)(2,1)S(1)}, u32[]{:S(2)}, u32[]{:S(2)}) collective-permute-start(bf16[128,1024]{1,0:T(8,128)(2,1)S(1)} %shard_map.96.refs_0_.refs_4_.refs_6_), channel_id=1, source_target_pairs={{0,2},{2,0},{1,3},{3,1},{4,6},{6,4},{5,7},{7,5},{8,10},{10,8},{9,1... | collective-permute-start | bytes 786440 | tf_op jit(solution)/shard_map/ppermute | solution.py:459
  32.3 3.2 %shard_map.97 = (f32[128,1024]{1,0:T(8,128)S(1)}, f32[128,1024]{1,0:T(8,128)S(1)}) custom-call(s32[6]{0:T(128)S(1)} %stack.54.meta, bf16[53248,512]{1,0:T(8,128)(2,1)} %get-tuple-element.71.work, bf16[128,1024]{1,0:T(8,128)(2,1)S(1)} %shard_map.96.refs_0_.refs_4_.refs_6_, bf16[128,1024]{1,0:T(8,128)(2,1)S(1)} %collective-permute-done.4.refs_1_.refs_3_.refs_5_, ...), custom_call_target="tpu_custom_call" | custom-call | flops 536870912 | bytes 4194304 | tf_op jit(solution)/shard_map/pallas_call | solution.py:153
  35.5 0.8 copy-done.2
  36.3 2.9 %collective-permute-done.7.b = bf16[128,1024]{1,0:T(8,128)(2,1)S(1)} collective-permute-done((bf16[128,1024]{1,0:T(8,128)(2,1)S(1)}, bf16[128,1024]{1,0:T(8,128)(2,1)S(1)}, u32[]{:S(2)}, u32[]{:S(2)}) %collective-permute-start.7) | collective-permute-done | bytes 262176 | tf_op jit(solution)/shard_map/ppermute | solution.py:426
  39.2 1.6 %collective-permute-start.8 = (bf16[128,1024]{1,0:T(8,128)(2,1)S(1)}, bf16[128,1024]{1,0:T(8,128)(2,1)S(1)}, u32[]{:S(2)}, u32[]{:S(2)}) collective-permute-start(bf16[128,1024]{1,0:T(8,128)(2,1)S(1)} %shard_map.98.refs_0_.refs_6_.refs_8_), channel_id=1, source_target_pairs={{0,2},{2,0},{1,3},{3,1},{4,6},{6,4},{5,7},{7,5},{8,10},{10,8},{9,1... | collective-permute-start | bytes 786440 | tf_op jit(solution)/shard_map/ppermute | solution.py:459
  40.8 0.1 copy.15.refs_4_
  40.9 1.0 copy-done.3
  41.9 3.4 %shard_map.99 = (f32[128,1024]{1,0:T(8,128)S(1)}, f32[128,1024]{1,0:T(8,128)S(1)}, f32[1,8,128]{2,1,0:T(8,128)S(1)}) custom-call(s32[6]{0:T(128)S(1)} %stack.54.meta, bf16[53248,512]{1,0:T(8,128)(2,1)} %get-tuple-element.71.work, bf16[128,1024]{1,0:T(8,128)(2,1)S(1)} %shard_map.98.refs_0_.refs_6_.refs_8_, ...), custom_call_target="tpu_custom_call" | custom-call | flops 536870912 | bytes 4194304 | tf_op jit(solution)/shard_map/pallas_call | solution.py:153
  45.4 0.8 copy-done.4
  46.2 1.4 %shard_map.111 = bf16[8,128,1024]{2,1,0:T(8,128)(2,1)} custom-call(bf16[128,1024]{1,0:T(8,128)(2,1)S(1)} %bitcast.23, bf16[128,1024]{1,0:T(8,128)(2,1)S(1)} %collective-permute-done.3.refs_3_.refs_1_, bf16[128,1024]{1,0:T(8,128)(2,1)S(1)} %collective-permute-done.refs_2_.refs_4_, bf16[128,1024]{1,0:T(8,128)(2,1)S(1)} %collective-permute-done.4.refs_1_.refs_3_.refs_5_, ...), custom_call_target="tpu_custom_call" | custom-call | flops 1 | bytes 4194304 | tf_op jit(solution)/shard_map/pallas_call | solution.py:305
  47.7 0.1 copy.16.refs_2_
  47.8 1.0 %copy-done.5 = f32[128,1024]{1,0:T(8,128)S(1)} copy-done((f32[128,1024]{1,0:T(8,128)S(1)}, f32[128,1024]{1,0:T(8,128)}, u32[]{:S(2)}) %copy-start.5) | copy-done | bytes 524312
  48.8 2.8 %shard_map.100 = (f32[128,1024]{1,0:T(8,128)S(1)}, f32[2,8,128]{2,1,0:T(8,128)S(1)}) custom-call(s32[6]{0:T(128)S(1)} %stack.54.meta, bf16[53248,512]{1,0:T(8,128)(2,1)} %get-tuple-element.71.work, bf16[128,1024]{1,0:T(8,128)(2,1)S(1)} %collective-permute-done.8.refs_0_.refs_7_.refs_9_, f32[128,1024]{1,0:T(8,128)S(1)} %copy-done.5, ...), custom_call_target="tpu_custom_call" | custom-call | flops 268435456 | bytes 2097152 | tf_op jit(solution)/shard_map/pallas_call | solution.py:153
  51.6 1.0 collective-permute-start.10
  52.6 1.9 %collective-permute-start.11 = (f32[2,8,128]{2,1,0:T(8,128)S(1)}, f32[2,8,128]{2,1,0:T(8,128)S(1)}, u32[]{:S(2)}, u32[]{:S(2)}) collective-permute-start(f32[2,8,128]{2,1,0:T(8,128)S(1)} %get-tuple-element.98.refs_0_), channel_id=1, source_target_pairs={{0,4},{4,0},{8,12},{12,8},{1,5},{5,1},{9,13},{13,9},{2,6},{6,2},{1... | collective-permute-start | bytes 24584 | tf_op jit(solution)/shard_map/ppermute | solution.py:426
  54.5 0.6 collective-permute-start.12
  55.2 0.2 collective-permute-done.10.refs_1_
  55.3 0.9 collective-permute-done.11.refs_2_
  56.3 2.8 %collective-permute-done.12.refs_3_ = f32[2,8,128]{2,1,0:T(8,128)S(1)} collective-permute-done((f32[2,8,128]{2,1,0:T(8,128)S(1)}, f32[2,8,128]{2,1,0:T(8,128)S(1)}, u32[]{:S(2)}, u32[]{:S(2)}) %collective-permute-start.12) | collective-permute-done | bytes 8224 | tf_op jit(solution)/shard_map/ppermute | solution.py:526
  59.1 0.2 collective-permute-start.13
  59.3 0.1 copy.17.refs_2_
  59.5 4.3 %collective-permute-done.13.refs_4_ = f32[8,256]{1,0:T(8,128)S(1)} collective-permute-done((f32[8,256]{1,0:T(8,128)S(1)}, f32[8,256]{1,0:T(8,128)S(1)}, u32[]{:S(2)}, u32[]{:S(2)}) %collective-permute-start.13) | collective-permute-done | bytes 8224 | tf_op jit(solution)/shard_map/ppermute | solution.py:426
  63.7 2.8 %shard_map.102 = (bf16[2,128,512]{2,1,0:T(8,128)(2,1)S(1)}, bf16[2,128,512]{2,1,0:T(8,128)(2,1)S(1)}, bf16[512,256]{1,0:T(8,128)(2,1)S(1)}, bf16[512,256]{1,0:T(...) custom-call(s32[5]{0:T(128)S(1)} %stack.50.meta, ...), custom_call_target="tpu_custom_call" | custom-call | flops 536870912 | bytes 4194304 | tf_op jit(solution)/shard_map/pallas_call | solution.py:252
  66.6 0.1 collective-permute-start.14
  66.7 2.3 %shard_map.103 = (f32[1024,128]{1,0:T(8,128)S(1)}, bf16[1024,128]{1,0:T(8,128)(2,1)S(1)}) custom-call(s32[1]{0:T(128)} %bitcast.11.meta, bf16[53248,512]{1,0:T(8,128)(2,1)} %get-tuple-element.71.work, bf16[512,256]{1,0:T(8,128)(2,1)S(1)} %get-tuple-element.100.flipped_own, bf16[512,256]{1,0:T(8,128)(2,1)S(1)} %get-tuple-element.101.flipped_far), custom_call_target="tpu_custom_call" | custom-call | flops 536870912 | bytes 2097152 | tf_op jit(solution)/shard_map/pallas_call | solution.py:267
  69.0 4.0 %collective-permute-done.14.refs_0_ = bf16[1024,128]{1,0:T(8,128)(2,1)S(1)} collective-permute-done((bf16[1024,128]{1,0:T(8,128)(2,1)S(1)}, bf16[1024,128]{1,0:T(8,128)(2,1)S(1)}, u32[]{:S(2)}, u32[]{:S(2)}) %collective-permute-start.14) | collective-permute-done | bytes 262176 | tf_op jit(solution)/shard_map/ppermute | solution.py:538
  73.1 2.0 %collective-permute-start.16 = (bf16[1024,128]{1,0:T(8,128)(2,1)S(1)}, bf16[1024,128]{1,0:T(8,128)(2,1)S(1)}, u32[]{:S(2)}, u32[]{:S(2)}) collective-permute-start(bf16[1024,128]{1,0:T(8,128)(2,1)S(1)} %shard_map.104), channel_id=1, source_target_pairs={{0,4},{12,8},{1,5},{13,9},{2,6},{14,10},{3,7},{15,11},{16,20},{28,... | collective-permute-start | bytes 786440 | tf_op jit(solution)/shard_map/ppermute | solution.py:426
  75.1 1.1 %collective-permute-start.15 = (bf16[1024,128]{1,0:T(8,128)(2,1)S(1)}, bf16[1024,128]{1,0:T(8,128)(2,1)S(1)}, u32[]{:S(2)}, u32[]{:S(2)}) collective-permute-start(bf16[1024,128]{1,0:T(8,128)(2,1)S(1)} %get-tuple-element.104), channel_id=1, source_target_pairs={{0,2},{2,0},{1,3},{3,1},{4,6},{6,4},{5,7},{7,5},{8,10},{10,8},{9,1... | collective-permute-start | bytes 786440 | tf_op jit(solution)/shard_map/ppermute | solution.py:538
  76.3 2.3 %shard_map.105 = (f32[1024,128]{1,0:T(8,128)S(1)}, bf16[1024,128]{1,0:T(8,128)(2,1)S(1)}) custom-call(s32[1]{0:T(128)} %bitcast.10.meta, bf16[53248,512]{1,0:T(8,128)(2,1)} %get-tuple-element.71.work, bf16[512,256]{1,0:T(8,128)(2,1)S(1)} %get-tuple-element.100.flipped_own, bf16[512,256]{1,0:T(8,128)(2,1)S(1)} %get-tuple-element.101.flipped_far), custom_call_target="tpu_custom_call" | custom-call | flops 536870912 | bytes 2097152 | tf_op jit(solution)/shard_map/pallas_call | solution.py:267
  78.6 0.4 collective-permute-done.16.refs_1_
  79.0 2.6 %collective-permute-done.15.refs_0_ = bf16[1024,128]{1,0:T(8,128)(2,1)S(1)} collective-permute-done((bf16[1024,128]{1,0:T(8,128)(2,1)S(1)}, bf16[1024,128]{1,0:T(8,128)(2,1)S(1)}, u32[]{:S(2)}, u32[]{:S(2)}) %collective-permute-start.15) | collective-permute-done | bytes 262176 | tf_op jit(solution)/shard_map/ppermute | solution.py:538
  81.6 1.8 %collective-permute-start.20 = (bf16[1024,128]{1,0:T(8,128)(2,1)S(1)}, bf16[1024,128]{1,0:T(8,128)(2,1)S(1)}, u32[]{:S(2)}, u32[]{:S(2)}) collective-permute-start(bf16[1024,128]{1,0:T(8,128)(2,1)S(1)} %shard_map.107), channel_id=1, source_target_pairs={{0,4},{12,8},{1,5},{13,9},{2,6},{14,10},{3,7},{15,11},{16,20},{28,... | collective-permute-start | bytes 786440 | tf_op jit(solution)/shard_map/ppermute | solution.py:426
  83.5 0.1 shard_map.106
  83.6 0.7 collective-permute-start.19
  84.2 1.1 %collective-permute-start.18 = (bf16[1024,128]{1,0:T(8,128)(2,1)S(1)}, bf16[1024,128]{1,0:T(8,128)(2,1)S(1)}, u32[]{:S(2)}, u32[]{:S(2)}) collective-permute-start(bf16[1024,128]{1,0:T(8,128)(2,1)S(1)} %get-tuple-element.110), channel_id=1, source_target_pairs={{0,2},{2,0},{1,3},{3,1},{4,6},{6,4},{5,7},{7,5},{8,10},{10,8},{9,1... | collective-permute-start | bytes 786440 | tf_op jit(solution)/shard_map/ppermute | solution.py:538
  85.4 2.3 %shard_map.108 = (f32[1024,128]{1,0:T(8,128)S(1)}, bf16[1024,128]{1,0:T(8,128)(2,1)S(1)}) custom-call(s32[1]{0:T(128)} %bitcast.9.meta, bf16[53248,512]{1,0:T(8,128)(2,1)} %get-tuple-element.71.work, bf16[512,256]{1,0:T(8,128)(2,1)S(1)} %get-tuple-element.100.flipped_own, bf16[512,256]{1,0:T(8,128)(2,1)S(1)} %get-tuple-element.101.flipped_far), custom_call_target="tpu_custom_call" | custom-call | flops 536870912 | bytes 2097152 | tf_op jit(solution)/shard_map/pallas_call | solution.py:267
  87.7 3.0 %collective-permute-done.18.refs_0_ = bf16[1024,128]{1,0:T(8,128)(2,1)S(1)} collective-permute-done((bf16[1024,128]{1,0:T(8,128)(2,1)S(1)}, bf16[1024,128]{1,0:T(8,128)(2,1)S(1)}, u32[]{:S(2)}, u32[]{:S(2)}) %collective-permute-start.18) | collective-permute-done | bytes 262176 | tf_op jit(solution)/shard_map/ppermute | solution.py:538
  90.7 0.1 shard_map.110
  90.8 0.7 collective-permute-start.23
  91.6 3.9 %collective-permute-start.22 = (bf16[1024,128]{1,0:T(8,128)(2,1)S(1)}, bf16[1024,128]{1,0:T(8,128)(2,1)S(1)}, u32[]{:S(2)}, u32[]{:S(2)}) collective-permute-start(bf16[1024,128]{1,0:T(8,128)(2,1)S(1)} %shard_map.109), channel_id=1, source_target_pairs={{0,4},{4,0},{8,12},{12,8},{1,5},{5,1},{9,13},{13,9},{2,6},{6,2},{1... | collective-permute-start | bytes 786440 | tf_op jit(solution)/shard_map/ppermute | solution.py:426
  95.5 1.1 %collective-permute-start.21 = (bf16[1024,128]{1,0:T(8,128)(2,1)S(1)}, bf16[1024,128]{1,0:T(8,128)(2,1)S(1)}, u32[]{:S(2)}, u32[]{:S(2)}) collective-permute-start(bf16[1024,128]{1,0:T(8,128)(2,1)S(1)} %get-tuple-element.117), channel_id=1, source_target_pairs={{0,2},{2,0},{1,3},{3,1},{4,6},{6,4},{5,7},{7,5},{8,10},{10,8},{9,1... | collective-permute-start | bytes 786440 | tf_op jit(solution)/shard_map/ppermute | solution.py:538
  96.6 0.5 bitcast_select_fusion
  97.1 5.6 %shard_map.112 = bf16[4096,512]{1,0:T(8,128)(2,1)} custom-call(s32[6]{0:T(128)S(1)} %stack.54.meta, bf16[2,128,512]{2,1,0:T(8,128)(2,1)S(1)} %get-tuple-element.122.refs_0_, bf16[2,128,512]{2,1,0:T(8,128)(2,1)S(1)} %collective-permute-done.17.refs_1_, bf16[128,1024]{1,0:T(8,128)(2,1)S(1)} %bitcast.24, ...), custom_call_target="tpu_custom_call" | custom-call | flops 2147483648 | bytes 8388608 | tf_op jit(solution)/shard_map/pallas_call | solution.py:393
  102.8 0.9 shard_map.113
  (40 shorter events, 0.8 us)
Async XLA Ops:
  0.6 19.3 %collective-permute-start.2 = (bf16[4096,512]{1,0:T(8,128)(2,1)}, bf16[4096,512]{1,0:T(8,128)(2,1)}, u32[]{:S(2)}, u32[]{:S(2)}) collective-permute-start(bf16[4096,512]{1,0:T(8,128)(2,1)} %w.1), channel_id=1, source_target_pairs={{0,1},{1,0},{2,3},{3,2},{4,5},{5,4},{6,7},{7,6},{8,9},{9,8},{10,11... | collective-permute-start | bytes 12582920 | tf_op jit(solution)/shard_map/ppermute | solution.py:425
  1.1 16.2 %collective-permute-start = (bf16[128,1024]{1,0:T(8,128)(2,1)}, bf16[128,1024]{1,0:T(8,128)(2,1)S(1)}, u32[]{:S(2)}, u32[]{:S(2)}) collective-permute-start(bf16[128,1024]{1,0:T(8,128)(2,1)} %bitcast.19), channel_id=1, source_target_pairs={{0,4},{4,0},{8,12},{12,8},{1,5},{5,1},{9,13},{13,9},{2,6},{6,2},{1... | collective-permute-start | bytes 786440 | tf_op jit(solution)/shard_map/ppermute | solution.py:426
  3.8 13.6 %collective-permute-start.1 = (bf16[128,1024]{1,0:T(8,128)(2,1)}, bf16[128,1024]{1,0:T(8,128)(2,1)S(1)}, u32[]{:S(2)}, u32[]{:S(2)}) collective-permute-start(bf16[128,1024]{1,0:T(8,128)(2,1)} %bitcast.20), channel_id=1, source_target_pairs={{4,8},{8,4},{5,9},{9,5},{6,10},{10,6},{7,11},{11,7},{20,24},{24,20... | collective-permute-start | bytes 786440 | tf_op jit(solution)/shard_map/ppermute | solution.py:426
  4.5 15.4 %collective-permute-start.3 = (bf16[128,1024]{1,0:T(8,128)(2,1)}, bf16[128,1024]{1,0:T(8,128)(2,1)S(1)}, u32[]{:S(2)}, u32[]{:S(2)}) collective-permute-start(bf16[128,1024]{1,0:T(8,128)(2,1)} %bitcast.21), channel_id=1, source_target_pairs={{0,2},{2,0},{1,3},{3,1},{4,6},{6,4},{5,7},{7,5},{8,10},{10,8},{9,1... | collective-permute-start | bytes 786440 | tf_op jit(solution)/shard_map/ppermute | solution.py:459
  9.8 2.2 %copy-start = (bf16[4096,512]{1,0:T(8,128)(2,1)S(1)}, bf16[4096,512]{1,0:T(8,128)(2,1)}, u32[]{:S(2)}) copy-start(bf16[4096,512]{1,0:T(8,128)(2,1)} %w.1) | copy-start | bytes 12582916
  12.0 4.1 %copy-start.6 = (f32[2]{0:T(128)S(1)}, f32[2]{0:T(128)}, u32[]{:S(2)}) copy-start(f32[2]{0:T(128)} %param.13) | copy-start | bytes 28
  12.0 8.0 %copy-start.1 = (bf16[1024,1,2,64]{0,3,2,1:T(8,128)(2,1)S(1)}, bf16[1024,1,2,64]{0,3,2,1:T(8,128)(2,1)}, u32[]{:S(2)}) copy-start(bf16[1024,1,2,64]{0,3,2,1:T(8,128)(2,1)} %param.7) | copy-start | bytes 786436
  17.4 8.1 %collective-permute-start.4 = (bf16[128,1024]{1,0:T(8,128)(2,1)S(1)}, bf16[128,1024]{1,0:T(8,128)(2,1)S(1)}, u32[]{:S(2)}, u32[]{:S(2)}) collective-permute-start(bf16[128,1024]{1,0:T(8,128)(2,1)S(1)} %collective-permute-done.refs_2_.refs_4_), channel_id=1, source_target_pairs={{0,2},{2,0},{1,3},{3,1},{4,6},{6,4},{5,7},{7,5},{8,10},{10,8},{9,1... | collective-permute-start | bytes 786440 | tf_op jit(solution)/shard_map/ppermute | solution.py:459
  17.9 11.4 %collective-permute-start.5 = (bf16[128,1024]{1,0:T(8,128)(2,1)S(1)}, bf16[128,1024]{1,0:T(8,128)(2,1)S(1)}, u32[]{:S(2)}, u32[]{:S(2)}) collective-permute-start(bf16[128,1024]{1,0:T(8,128)(2,1)S(1)} %collective-permute-done.1.a), channel_id=1, source_target_pairs={{4,0},{8,12},{5,1},{9,13},{6,2},{10,14},{7,3},{11,15},{20,16},{24,... | collective-permute-start | bytes 786440 | tf_op jit(solution)/shard_map/ppermute | solution.py:426
  19.2 10.2 %collective-permute-start.6 = (bf16[128,1024]{1,0:T(8,128)(2,1)S(1)}, bf16[128,1024]{1,0:T(8,128)(2,1)S(1)}, u32[]{:S(2)}, u32[]{:S(2)}) collective-permute-start(bf16[128,1024]{1,0:T(8,128)(2,1)S(1)} %collective-permute-done.refs_2_.refs_4_), channel_id=1, source_target_pairs={{4,8},{8,4},{5,9},{9,5},{6,10},{10,6},{7,11},{11,7},{20,24},{24,20... | collective-permute-start | bytes 786440 | tf_op jit(solution)/shard_map/ppermute | solution.py:426
  29.4 9.8 %collective-permute-start.7 = (bf16[128,1024]{1,0:T(8,128)(2,1)S(1)}, bf16[128,1024]{1,0:T(8,128)(2,1)S(1)}, u32[]{:S(2)}, u32[]{:S(2)}) collective-permute-start(bf16[128,1024]{1,0:T(8,128)(2,1)S(1)} %collective-permute-done.6.a), channel_id=1, source_target_pairs={{4,0},{8,12},{5,1},{9,13},{6,2},{10,14},{7,3},{11,15},{20,16},{24,... | collective-permute-start | bytes 786440 | tf_op jit(solution)/shard_map/ppermute | solution.py:426
  30.7 10.2 %collective-permute-start.9 = (bf16[128,1024]{1,0:T(8,128)(2,1)S(1)}, bf16[128,1024]{1,0:T(8,128)(2,1)S(1)}, u32[]{:S(2)}, u32[]{:S(2)}) collective-permute-start(bf16[128,1024]{1,0:T(8,128)(2,1)S(1)} %shard_map.96.refs_0_.refs_4_.refs_6_), channel_id=1, source_target_pairs={{0,2},{2,0},{1,3},{3,1},{4,6},{6,4},{5,7},{7,5},{8,10},{10,8},{9,1... | collective-permute-start | bytes 786440 | tf_op jit(solution)/shard_map/ppermute | solution.py:459
  35.5 0.8 copy-start.2
  39.2 7.0 %collective-permute-start.8 = (bf16[128,1024]{1,0:T(8,128)(2,1)S(1)}, bf16[128,1024]{1,0:T(8,128)(2,1)S(1)}, u32[]{:S(2)}, u32[]{:S(2)}) collective-permute-start(bf16[128,1024]{1,0:T(8,128)(2,1)S(1)} %shard_map.98.refs_0_.refs_6_.refs_8_), channel_id=1, source_target_pairs={{0,2},{2,0},{1,3},{3,1},{4,6},{6,4},{5,7},{7,5},{8,10},{10,8},{9,1... | collective-permute-start | bytes 786440 | tf_op jit(solution)/shard_map/ppermute | solution.py:459
  40.9 1.0 %copy-start.3 = (f32[128,1024]{1,0:T(8,128)S(1)}, f32[128,1024]{1,0:T(8,128)}, u32[]{:S(2)}) copy-start(f32[128,1024]{1,0:T(8,128)} %copy-done.2) | copy-start | bytes 1572868
  45.4 0.8 copy-start.4
  47.6 49.5 %collective-permute-start.24 = (bf16[8,128,1024]{2,1,0:T(8,128)(2,1)}, bf16[8,128,1024]{2,1,0:T(8,128)(2,1)}, u32[]{:S(2)}, u32[]{:S(2)}) collective-permute-start(bf16[8,128,1024]{2,1,0:T(8,128)(2,1)} %shard_map.111), channel_id=1, source_target_pairs={{0,1},{1,0},{2,3},{3,2},{4,5},{5,4},{6,7},{7,6},{8,9},{9,8},{10,11... | collective-permute-start | bytes 6291464 | tf_op jit(solution)/shard_map/ppermute | solution.py:425
  47.8 1.0 %copy-start.5 = (f32[128,1024]{1,0:T(8,128)S(1)}, f32[128,1024]{1,0:T(8,128)}, u32[]{:S(2)}) copy-start(f32[128,1024]{1,0:T(8,128)} %copy-done.4) | copy-start | bytes 1572868
  51.6 3.7 %collective-permute-start.10 = (f32[2,8,128]{2,1,0:T(8,128)S(1)}, f32[2,8,128]{2,1,0:T(8,128)S(1)}, u32[]{:S(2)}, u32[]{:S(2)}) collective-permute-start(f32[2,8,128]{2,1,0:T(8,128)S(1)} %get-tuple-element.98.refs_0_), channel_id=1, source_target_pairs={{0,2},{2,0},{1,3},{3,1},{4,6},{6,4},{5,7},{7,5},{8,10},{10,8},{9,1... | collective-permute-start | bytes 24584 | tf_op jit(solution)/shard_map/ppermute | solution.py:459
  52.6 3.7 %collective-permute-start.11 = (f32[2,8,128]{2,1,0:T(8,128)S(1)}, f32[2,8,128]{2,1,0:T(8,128)S(1)}, u32[]{:S(2)}, u32[]{:S(2)}) collective-permute-start(f32[2,8,128]{2,1,0:T(8,128)S(1)} %get-tuple-element.98.refs_0_), channel_id=1, source_target_pairs={{0,4},{4,0},{8,12},{12,8},{1,5},{5,1},{9,13},{13,9},{2,6},{6,2},{1... | collective-permute-start | bytes 24584 | tf_op jit(solution)/shard_map/ppermute | solution.py:426
  54.5 4.5 %collective-permute-start.12 = (f32[2,8,128]{2,1,0:T(8,128)S(1)}, f32[2,8,128]{2,1,0:T(8,128)S(1)}, u32[]{:S(2)}, u32[]{:S(2)}) collective-permute-start(f32[2,8,128]{2,1,0:T(8,128)S(1)} %get-tuple-element.98.refs_0_), channel_id=1, source_target_pairs={{0,6},{2,4},{4,2},{6,0},{8,14},{10,12},{12,10},{14,8},{1,7},{3,5},... | collective-permute-start | bytes 24584 | tf_op jit(solution)/shard_map/ppermute | solution.py:526
  59.1 4.6 %collective-permute-start.13 = (f32[8,256]{1,0:T(8,128)S(1)}, f32[8,256]{1,0:T(8,128)S(1)}, u32[]{:S(2)}, u32[]{:S(2)}) collective-permute-start(f32[8,256]{1,0:T(8,128)S(1)} %shard_map.101.refs_3_), channel_id=1, source_target_pairs={{0,8},{8,0},{4,12},{12,4},{1,9},{9,1},{5,13},{13,5},{2,10},{10,2},... | collective-permute-start | bytes 24584 | tf_op jit(solution)/shard_map/ppermute | solution.py:426
  66.6 6.4 %collective-permute-start.14 = (bf16[1024,128]{1,0:T(8,128)(2,1)S(1)}, bf16[1024,128]{1,0:T(8,128)(2,1)S(1)}, u32[]{:S(2)}, u32[]{:S(2)}) collective-permute-start(bf16[1024,128]{1,0:T(8,128)(2,1)S(1)} %get-tuple-element.99), channel_id=1, source_target_pairs={{0,2},{2,0},{1,3},{3,1},{4,6},{6,4},{5,7},{7,5},{8,10},{10,8},{9,1... | collective-permute-start | bytes 786440 | tf_op jit(solution)/shard_map/ppermute | solution.py:538
  66.7 11.8 %collective-permute-start.17 = (bf16[2,128,512]{2,1,0:T(8,128)(2,1)S(1)}, bf16[2,128,512]{2,1,0:T(8,128)(2,1)S(1)}, u32[]{:S(2)}, u32[]{:S(2)}) collective-permute-start(bf16[2,128,512]{2,1,0:T(8,128)(2,1)S(1)} %get-tuple-element.109), channel_id=1, source_target_pairs={{0,1},{1,0},{2,3},{3,2},{4,5},{5,4},{6,7},{7,6},{8,9},{9,8},{10,11... | collective-permute-start | bytes 786440 | tf_op jit(solution)/shard_map/ppermute | solution.py:425
  73.1 5.9 %collective-permute-start.16 = (bf16[1024,128]{1,0:T(8,128)(2,1)S(1)}, bf16[1024,128]{1,0:T(8,128)(2,1)S(1)}, u32[]{:S(2)}, u32[]{:S(2)}) collective-permute-start(bf16[1024,128]{1,0:T(8,128)(2,1)S(1)} %shard_map.104), channel_id=1, source_target_pairs={{0,4},{12,8},{1,5},{13,9},{2,6},{14,10},{3,7},{15,11},{16,20},{28,... | collective-permute-start | bytes 786440 | tf_op jit(solution)/shard_map/ppermute | solution.py:426
  75.1 6.4 %collective-permute-start.15 = (bf16[1024,128]{1,0:T(8,128)(2,1)S(1)}, bf16[1024,128]{1,0:T(8,128)(2,1)S(1)}, u32[]{:S(2)}, u32[]{:S(2)}) collective-permute-start(bf16[1024,128]{1,0:T(8,128)(2,1)S(1)} %get-tuple-element.104), channel_id=1, source_target_pairs={{0,2},{2,0},{1,3},{3,1},{4,6},{6,4},{5,7},{7,5},{8,10},{10,8},{9,1... | collective-permute-start | bytes 786440 | tf_op jit(solution)/shard_map/ppermute | solution.py:538
  81.6 6.0 %collective-permute-start.20 = (bf16[1024,128]{1,0:T(8,128)(2,1)S(1)}, bf16[1024,128]{1,0:T(8,128)(2,1)S(1)}, u32[]{:S(2)}, u32[]{:S(2)}) collective-permute-start(bf16[1024,128]{1,0:T(8,128)(2,1)S(1)} %shard_map.107), channel_id=1, source_target_pairs={{0,4},{12,8},{1,5},{13,9},{2,6},{14,10},{3,7},{15,11},{16,20},{28,... | collective-permute-start | bytes 786440 | tf_op jit(solution)/shard_map/ppermute | solution.py:426
  83.6 4.1 %collective-permute-start.19 = (bf16[1024,128]{1,0:T(8,128)(2,1)S(1)}, bf16[1024,128]{1,0:T(8,128)(2,1)S(1)}, u32[]{:S(2)}, u32[]{:S(2)}) collective-permute-start(bf16[1024,128]{1,0:T(8,128)(2,1)S(1)} %shard_map.106), channel_id=1, source_target_pairs={{4,8},{8,4},{5,9},{9,5},{6,10},{10,6},{7,11},{11,7},{20,24},{24,20... | collective-permute-start | bytes 786440 | tf_op jit(solution)/shard_map/ppermute | solution.py:426
  84.2 6.4 %collective-permute-start.18 = (bf16[1024,128]{1,0:T(8,128)(2,1)S(1)}, bf16[1024,128]{1,0:T(8,128)(2,1)S(1)}, u32[]{:S(2)}, u32[]{:S(2)}) collective-permute-start(bf16[1024,128]{1,0:T(8,128)(2,1)S(1)} %get-tuple-element.110), channel_id=1, source_target_pairs={{0,2},{2,0},{1,3},{3,1},{4,6},{6,4},{5,7},{7,5},{8,10},{10,8},{9,1... | collective-permute-start | bytes 786440 | tf_op jit(solution)/shard_map/ppermute | solution.py:538
  85.4 11.2 %collective-permute-start.25 = (f32[1,128]{1,0:T(1,128)S(1)}, f32[1,128]{1,0:T(1,128)S(1)}, u32[]{:S(2)}, u32[]{:S(2)}) collective-permute-start(f32[1,128]{1,0:T(1,128)S(1)} %get-tuple-element.128), channel_id=1, source_target_pairs={{0,1},{1,0},{2,3},{3,2},{4,5},{5,4},{6,7},{7,6},{8,9},{9,8},{10,11... | collective-permute-start | bytes 1544 | tf_op jit(solution)/shard_map/ppermute | solution.py:425
  90.8 11.9 %collective-permute-start.23 = (bf16[1024,128]{1,0:T(8,128)(2,1)S(1)}, bf16[1024,128]{1,0:T(8,128)(2,1)S(1)}, u32[]{:S(2)}, u32[]{:S(2)}) collective-permute-start(bf16[1024,128]{1,0:T(8,128)(2,1)S(1)} %shard_map.110), channel_id=1, source_target_pairs={{4,8},{8,4},{5,9},{9,5},{6,10},{10,6},{7,11},{11,7},{20,24},{24,20... | collective-permute-start | bytes 786440 | tf_op jit(solution)/shard_map/ppermute | solution.py:426
  91.6 11.2 %collective-permute-start.22 = (bf16[1024,128]{1,0:T(8,128)(2,1)S(1)}, bf16[1024,128]{1,0:T(8,128)(2,1)S(1)}, u32[]{:S(2)}, u32[]{:S(2)}) collective-permute-start(bf16[1024,128]{1,0:T(8,128)(2,1)S(1)} %shard_map.109), channel_id=1, source_target_pairs={{0,4},{4,0},{8,12},{12,8},{1,5},{5,1},{9,13},{13,9},{2,6},{6,2},{1... | collective-permute-start | bytes 786440 | tf_op jit(solution)/shard_map/ppermute | solution.py:426
  95.5 7.3 %collective-permute-start.21 = (bf16[1024,128]{1,0:T(8,128)(2,1)S(1)}, bf16[1024,128]{1,0:T(8,128)(2,1)S(1)}, u32[]{:S(2)}, u32[]{:S(2)}) collective-permute-start(bf16[1024,128]{1,0:T(8,128)(2,1)S(1)} %get-tuple-element.117), channel_id=1, source_target_pairs={{0,2},{2,0},{1,3},{3,1},{4,6},{6,4},{5,7},{7,5},{8,10},{10,8},{9,1... | collective-permute-start | bytes 786440 | tf_op jit(solution)/shard_map/ppermute | solution.py:538

commit v9 on v8

--- a/solution.py
+++ b/solution.py
@@ -175,7 +175,7 @@
 def grads_kernel(n_blocks, n_stats, columns, part, width, window, meta, small, work, *refs):
     refs = list(refs)
     logits = [refs.pop(0) for _ in range(n_blocks)]
-    target = refs.pop(0)
+    target = [refs.pop(0) for _ in range(n_blocks)]
     stats = [refs.pop(0) for _ in range(n_stats)]
     slots, sems = refs[-2:]
     grads_own, grads_far, flipped_own, flipped_far, loss, kept = refs[:6]
@@ -209,7 +209,7 @@
     for t in range(n_blocks):
         at = slice(t * rows, (t + 1) * rows)
         top_t, weight_t, inverse_t = packed[at, 0:1], packed[at, 1:2], packed[at, 2:3]
-        wanted = target[at, :]
+        wanted = target[t][...]
         for j, (grads, flipped) in enumerate(((grads_own, flipped_own), (grads_far, flipped_far))):
             l = logits[t][:, j * columns:(j + 1) * columns]
             column = lax.broadcasted_iota(jnp.int32, l.shape, 1) + meta[1 + j]
@@ -248,7 +248,7 @@
     grads = shape_of((n_blocks, rows, columns), BF16)
     flipped = shape_of((columns, n_blocks * rows), BF16)
     out_shape = [grads, grads, flipped, flipped, shape_of((1, 128), F32)] + spread_shapes(n_blocks, rows, part)
-    operands = list(logits) + [target] + list(stats)
+    operands = list(logits) + list(target) + list(stats)
     return pl.pallas_call(
         functools.partial(grads_kernel, n_blocks, len(stats), columns, part, width, window),
         out_shape=out_shape,
@@ -448,10 +448,6 @@
     for t in range(n_ctx):
         at = (me_ctx - t) % n_ctx
         wanted.append(sum(jnp.where(at == b, blocks[b], 0) for b in range(n_ctx))[:, None])
-    target = jnp.concatenate(wanted)
-    ratio = mine(other_sums) - mine(ref_logp)
-    small = jnp.stack([ratio[0] - ratio[1], mine(loss_cotangent)])
-    meta_grads = jnp.stack([part_of[n_voc - 1]] + firsts + [me_ctx, mine(response_start)]).astype(jnp.int32)
 
     own = hidden.transpose(1, 2, 3, 0).reshape(rows, part)
     final = n_voc - 1
@@ -465,28 +461,33 @@
             chunk[t, i] = a
 
     def first_logits(work):
-        plan = [(0, {j: chunk[0, j] for j in (0, 1)}, None, None)]
-        plan += [(t, {0: chunk[t, 0]}, None, None) for t in beyond]
-        *logits, work = call(plan, work, far=far_weights)
+        *logits, work = call([(0, {j: chunk[0, j] for j in (0, 1)}, None, None)], work, far=far_weights)
         return logits, work
 
     def more_logits(i, logits):
-        plan = [(0, {i: chunk[0, i]}, logits[0], None)]
-        plan += [(t, {i - 1: chunk[t, i - 1]}, logits[t], None) for t in beyond]
-        return call(plan, work)
+        return call([(0, {i: chunk[0, i]}, logits[0], None)], work)
+
+    scalars = [response_start, other_sums, ref_logp, loss_cotangent]
+
+    def prepare(begin, others, refer, cotangent):
+        ratio = mine(others) - mine(refer)
+        small = jnp.stack([ratio[0] - ratio[1], mine(cotangent)])
+        return [small, jnp.stack([part_of[final]] + firsts + [me_ctx, mine(begin)]).astype(jnp.int32)]
 
     arrive(0, own, cross(own))
     if line:
         first = along(own, PAIRS_OUT)
         inner = along(own, PAIR_IN)
-        (first, inner), (work, target, small, meta_grads, meta), wanted = together(
-            [first, inner], [work, target, small, meta_grads, meta], wanted
-        )
+        (first, inner), (work, meta), over = together([first, inner], [work, meta], [chunk[t, 0] for t in beyond])
+        arrive(0, own, over)
         over = cross(first)
         outer, inner_last = along(inner, TO_ENDS), along(first, PAIR_IN)
         arrive(1, first, over)
         logits, work = first_logits(work)
-        over, (inner, outer, inner_last), logits = together(over, [inner, outer, inner_last], logits)
+        logits, raw = together(logits, scalars)
+        over, (inner, outer, inner_last), logits, wanted, (small, meta_grads) = together(
+            over, [inner, outer, inner_last], logits, wanted, prepare(*raw)
+        )
         arrive(1, first, over)
         inner = either(inner, outer)
         arrive(2, inner, cross(inner))
@@ -504,22 +505,20 @@
                 logits = more_logits(i, logits)
             (near[i + 1],), logits = together([near[i + 1]], logits)
         last = near[final]
+        small, meta_grads = prepare(*scalars)
     arrive(final, last, cross(last))
-    done = call(
-        [(0, {final: chunk[0, final]}, logits[0], wanted[0])]
-        + [(t, {final - 1: chunk[t, final - 1]}, logits[t], None) for t in beyond],
-        work,
+    late = [(t, final) for t in beyond]
+    soon = [k for k in chunk if k not in late]
+    done = call([(0, {final: chunk[0, final]}, logits[0], wanted[0])], work)
+    last, (near_logits, stats), (stacked,) = together(
+        [chunk[k] for k in late], list(done), [stack_call([chunk[k] for k in soon])]
     )
-    last, done = together([chunk[t, final] for t in beyond], list(done))
     arrive(final, chunk[0, final], last)
-    *logits, stats = done
-
-    far_chunks = dp_swap(stack_call(list(chunk.values())))
-
-    *others, stats = call(
-        [(t, {final: chunk[t, final]}, logits[t], wanted[t]) for t in beyond], work, earlier=[stats]
+    *logits, stats = call(
+        [(t, {i: chunk[t, i] for i in range(n_voc)}, None, wanted[t]) for t in beyond], work, earlier=[stats]
     )
-    logits = [logits[0]] + others
+    logits = [near_logits] + logits
+    far_soon = dp_swap(stacked)
 
     if line and n_ctx == 2:
         corner = [(2 * a + c, 2 * b + (1 - c)) for a, b in PAIRS_OUT for c in range(2)]
@@ -531,9 +530,10 @@
         all_stats = [merged] + [along(merged, ring(n_voc, s)) for s in range(1, n_voc)]
 
     grads_own, grads_far, flipped_own, flipped_far, loss, kept, *send = grads_call(
-        logits, target, all_stats, small, work, meta_grads, part, width, window
+        logits, wanted, all_stats, small, work, meta_grads, part, width, window
     )
-    theirs = dp_swap(grads_far)
+    theirs, far_loss = dp_swap(grads_far), dp_swap(loss)
+    far_late = dp_swap(jnp.stack(together([chunk[k] for k in late], [kept])[0]))
 
     back = lambda cs: [lax.ppermute(c, "ctx", ring(n_ctx, -t)) for t, c in zip(beyond, cs)]
     shares = {final: (kept, list(send))}
@@ -561,13 +561,15 @@
         elif i == 1:
             came = [along(near_over(3, landed[0]), PAIR_IN), along(near_over(2), FROM_ENDS)]
         elif i == 0:
-            came = [along(near_over(1, landed[0]), PAIRS_OUT), along(near_over(2, landed[1]), PAIR_IN)]
+            outer = near_over(1, landed[0])
+            (outer,), landed = together([outer], landed)
+            came = [along(outer, PAIRS_OUT), along(near_over(2, landed[1]), PAIR_IN)]
         if i:
             beside = more_shares([i - 1])
         else:
-            grad_head = head_call(list(range(n_voc)), chunk, [(list(chunk), far_chunks)], [grads_own, theirs], meta)
+            grad_head = head_call(list(range(n_voc)), chunk, [(soon, far_soon), (late, far_late)], [grads_own, theirs], meta)
             beside = [grad_head]
-        swapped = [theirs] if i == final - 1 else []
+        swapped = [theirs, far_loss, far_late] if i == final - 1 else []
         over[i], came, beside, swapped = together(over[i], came, beside, swapped)
         landed = came if line else landed + came
         if i:
@@ -575,12 +577,11 @@
         else:
             grad_head, = beside
         if swapped:
-            theirs, = swapped
+            theirs, far_loss, far_late = swapped
     kept = shares[0][0]
     summed = add_call(kept, over[0] + landed, turned=True)
     grad_hidden = summed.reshape(1, sides, window, part).transpose(3, 0, 1, 2)
 
-    far_loss = dp_swap(loss)
     owner = lax.broadcasted_iota(jnp.int32, (n_dp,), 0)
     pair_loss = jnp.where(owner == me_dp, loss[0, :n_dp], far_loss[0, :n_dp])
     return (grad_hidden, grad_head, pair_loss)

time: 104 us -> 102 us (0.981)
  starting transfers between devices: 28.8 us -> 33.2 us
  local copies, waits for them, and re-layouts: 7.82 us -> 3.98 us
  waiting for transfers between devices: 25.7 us -> 23.9 us
  other arithmetic: 4.82 us -> 3.4 us
    unnamed x14 -> x12, local copies, waits for them, and re-layouts: 5.86 us -> 2.21 us
    ppermute x5, waiting for transfers between devices: 0.91 us -> 3.51 us  [shards(): cross = lambda a: [lax.ppermute(a, 'ctx', ring(n_ctx, t)) for t in beyond]]
    ppermute x4, waiting for transfers between devices: 9.58 us -> 7.27 us  [shards(): lax.ppermute(c, 'ctx', ring(n_ctx, -t))]
    ppermute x4, starting transfers between devices: 3.52 us -> 5.63 us  [shards(): lax.ppermute(c, 'ctx', ring(n_ctx, -t))]
    ppermute x12, starting transfers between devices: 17.8 us -> 19.8 us  [shards(): along = lambda a, by: lax.ppermute(a, 'vocab', by)]
    reduce_sum x4, other arithmetic: 3.5 us -> 2.09 us  [mine(): return jnp.sum(jnp.where(pair == me_dp, a, jnp.zeros_like(a)), axis=0)]
    ppermute x5, starting transfers between devices: 6.25 us -> 4.85 us  [shards(): cross = lambda a: [lax.ppermute(a, 'ctx', ring(n_ctx, t)) for t in beyond]]
    ppermute x1, starting transfers between devices: 0.64 us -> 1.92 us  [shards(): diagonal = lax.ppermute(stats, ('vocab', 'ctx'), corner)]
  transfers between devices with their start and end apart: 26 -> 27, of which waited for: 11 -> 12; matrix products, arithmetic and copies ran while one was open for 7% -> 5% of each run, Pallas kernels for 31% -> 33%
where the time goes in v9:
time: 102 us
  Pallas kernels  34.6 us (34%)
  starting transfers between devices  33.2 us (33%)
  waiting for transfers between devices  23.9 us (23%)
  local copies, waits for them, and re-layouts  3.98 us (4%)
  other arithmetic  3.4 us (3%)
  between operations  2.35 us (2%)
    ppermute x12, starting transfers between devices, shards(): along = lambda a, by: lax.ppermute(a, 'vocab', by)  19.8 us
    pallas_call x4, Pallas kernels, logits_call(): pl.pallas_call(functools.partial(logits_kernel, kernel_plan, columns, par...  14.9 us
    ppermute x12, waiting for transfers between devices, shards(): along = lambda a, by: lax.ppermute(a, 'vocab', by)  11.2 us
    ppermute x4, waiting for transfers between devices, shards(): lax.ppermute(c, 'ctx', ring(n_ctx, -t))  7.27 us
    pallas_call x3, Pallas kernels, spread_call(): pl.pallas_call(functools.partial(spread_kernel, part, width, n_parts), ou...  6.8 us
    ppermute x4, starting transfers between devices, shards(): lax.ppermute(c, 'ctx', ring(n_ctx, -t))  5.63 us
    pallas_call x1, Pallas kernels, head_call(): pl.pallas_call(functools.partial(head_kernel, slots_here, list(near), [ke...  5.53 us
    ppermute x5, starting transfers between devices, shards(): cross = lambda a: [lax.ppermute(a, 'ctx', ring(n_ctx, t)) for t in beyond]  4.85 us
  transfers between devices with their start and end apart: 27, of which 12 were waited for; matrix products, arithmetic and copies ran while one was open for 5% of the time, Pallas kernels for 33%

profile of v9, /device:TPU:0, one launch (start us, length us, event | category | flops | bytes accessed | tf_op | source)
XLA Modules:
  0.0 101.5 jit_solution(4832876278575859728)
XLA Ops:
  0.6 0.5 collective-permute-start.6
  1.1 2.7 %collective-permute-start = (bf16[128,1024]{1,0:T(8,128)(2,1)}, bf16[128,1024]{1,0:T(8,128)(2,1)S(1)}, u32[]{:S(2)}, u32[]{:S(2)}) collective-permute-start(bf16[128,1024]{1,0:T(8,128)(2,1)} %bitcast.20), channel_id=1, source_target_pairs={{0,4},{4,0},{8,12},{12,8},{1,5},{5,1},{9,13},{13,9},{2,6},{6,2},{1... | collective-permute-start | bytes 786440 | tf_op jit(solution)/shard_map/ppermute | solution.py:426
  3.8 0.7 collective-permute-start.1
  4.5 1.6 %collective-permute-start.2 = (bf16[128,1024]{1,0:T(8,128)(2,1)}, bf16[128,1024]{1,0:T(8,128)(2,1)S(1)}, u32[]{:S(2)}, u32[]{:S(2)}) collective-permute-start(bf16[128,1024]{1,0:T(8,128)(2,1)} %bitcast.22), channel_id=1, source_target_pairs={{0,2},{2,0},{1,3},{3,1},{4,6},{6,4},{5,7},{7,5},{8,10},{10,8},{9,1... | collective-permute-start | bytes 786440 | tf_op jit(solution)/shard_map/ppermute | solution.py:455
  6.0 0.8 select_reduce_fusion
  6.8 2.2 %copy-done = bf16[4096,512]{1,0:T(8,128)(2,1)S(1)} copy-done((bf16[4096,512]{1,0:T(8,128)(2,1)S(1)}, bf16[4096,512]{1,0:T(8,128)(2,1)}, u32[]{:S(2)}) %copy-start) | copy-done | bytes 4194328
  9.0 2.0 %shard_map.94.work = bf16[53248,512]{1,0:T(8,128)(2,1)} custom-call(bf16[4096,512]{1,0:T(8,128)(2,1)S(1)} %copy-done), custom_call_target="tpu_custom_call" | custom-call | flops 1 | bytes 8388608 | tf_op jit(solution)/shard_map/pallas_call | solution.py:52
  11.1 0.1 add.93
  11.3 0.1 stack.52.meta
  11.4 1.7 %collective-permute-done.2.refs_1_.refs_0_.refs_3_ = bf16[128,1024]{1,0:T(8,128)(2,1)S(1)} collective-permute-done((bf16[128,1024]{1,0:T(8,128)(2,1)}, bf16[128,1024]{1,0:T(8,128)(2,1)S(1)}, u32[]{:S(2)}, u32[]{:S(2)}) %collective-permute-start.2) | collective-permute-done | bytes 262176 | tf_op jit(solution)/shard_map/ppermute | solution.py:455
  13.1 1.5 %collective-permute-start.3 = (bf16[128,1024]{1,0:T(8,128)(2,1)S(1)}, bf16[128,1024]{1,0:T(8,128)(2,1)S(1)}, u32[]{:S(2)}, u32[]{:S(2)}) collective-permute-start(bf16[128,1024]{1,0:T(8,128)(2,1)S(1)} %collective-permute-done.refs_2_.refs_4_), channel_id=1, source_target_pairs={{0,2},{2,0},{1,3},{3,1},{4,6},{6,4},{5,7},{7,5},{8,10},{10,8},{9,1... | collective-permute-start | bytes 786440 | tf_op jit(solution)/shard_map/ppermute | solution.py:455
  14.6 0.7 collective-permute-start.5
  15.3 1.3 %collective-permute-start.4 = (bf16[128,1024]{1,0:T(8,128)(2,1)S(1)}, bf16[128,1024]{1,0:T(8,128)(2,1)S(1)}, u32[]{:S(2)}, u32[]{:S(2)}) collective-permute-start(bf16[128,1024]{1,0:T(8,128)(2,1)S(1)} %collective-permute-done.1.a), channel_id=1, source_target_pairs={{4,0},{8,12},{5,1},{9,13},{6,2},{10,14},{7,3},{11,15},{20,16},{24,... | collective-permute-start | bytes 786440 | tf_op jit(solution)/shard_map/ppermute | solution.py:426
  16.6 4.8 %shard_map.95 = (f32[128,1024]{1,0:T(8,128)S(1)}, bf16[53248,512]{1,0:T(8,128)(2,1)}) custom-call(s32[6]{0:T(128)S(1)} %stack.52.meta, bf16[53248,512]{1,0:T(8,128)(2,1)} %shard_map.94.work, bf16[4096,512]{1,0:T(8,128)(2,1)} %collective-permute-done.6.refs_0_, bf16[128,1024]{1,0:T(8,128)(2,1)S(1)} %bitcast.23, ...), custom_call_target="tpu_custom_call", output_to_operand_aliasing={{1}: (1, {})} | custom-call | flops 536870912 | bytes 4194304 | tf_op jit(solution)/shard_map/pallas_call | solution.py:153
  21.4 0.6 select_reduce_fusion.3
  22.1 0.1 select_reduce_fusion.1
  22.2 0.6 fusion
  22.8 0.7 stack.57.meta
  24.8 0.6 select_reduce_fusion.4
  25.4 0.7 pad_maximum_fusion.small
  26.1 1.3 %collective-permute-done.4.b = bf16[128,1024]{1,0:T(8,128)(2,1)S(1)} collective-permute-done((bf16[128,1024]{1,0:T(8,128)(2,1)S(1)}, bf16[128,1024]{1,0:T(8,128)(2,1)S(1)}, u32[]{:S(2)}, u32[]{:S(2)}) %collective-permute-start.4) | collective-permute-done | bytes 262176 | tf_op jit(solution)/shard_map/ppermute | solution.py:426
  27.4 1.3 %collective-permute-start.7 = (bf16[128,1024]{1,0:T(8,128)(2,1)S(1)}, bf16[128,1024]{1,0:T(8,128)(2,1)S(1)}, u32[]{:S(2)}, u32[]{:S(2)}) collective-permute-start(bf16[128,1024]{1,0:T(8,128)(2,1)S(1)} %collective-permute-done.5.a), channel_id=1, source_target_pairs={{4,0},{8,12},{5,1},{9,13},{6,2},{10,14},{7,3},{11,15},{20,16},{24,... | collective-permute-start | bytes 786440 | tf_op jit(solution)/shard_map/ppermute | solution.py:426
  28.8 0.6 collective-permute-start.9
  29.4 2.5 %shard_map.97.refs_1_ = f32[128,1024]{1,0:T(8,128)S(1)} custom-call(s32[6]{0:T(128)S(1)} %stack.52.meta, bf16[53248,512]{1,0:T(8,128)(2,1)} %get-tuple-element.82.work, bf16[128,1024]{1,0:T(8,128)(2,1)S(1)} %shard_map.96.refs_0_.refs_4_.refs_6_, f32[128,1024]{1,0:T(8,128)S(1)} %get-tuple-element.86.refs_1_), custom_call_target="tpu_custom_call" | custom-call | flops 268435456 | bytes 2097152 | tf_op jit(solution)/shard_map/pallas_call | solution.py:153
  31.9 6.4 %collective-permute-done.7.b = bf16[128,1024]{1,0:T(8,128)(2,1)S(1)} collective-permute-done((bf16[128,1024]{1,0:T(8,128)(2,1)S(1)}, bf16[128,1024]{1,0:T(8,128)(2,1)S(1)}, u32[]{:S(2)}, u32[]{:S(2)}) %collective-permute-start.7) | collective-permute-done | bytes 262176 | tf_op jit(solution)/shard_map/ppermute | solution.py:426
  38.3 0.6 collective-permute-start.8
  38.9 0.1 copy.11.refs_2_
  39.0 1.3 %shard_map.100 = bf16[7,128,1024]{2,1,0:T(8,128)(2,1)} custom-call(bf16[128,1024]{1,0:T(8,128)(2,1)S(1)} %bitcast.24, bf16[128,1024]{1,0:T(8,128)(2,1)S(1)} %collective-permute-done.2.refs_1_.refs_0_.refs_3_, bf16[128,1024]{1,0:T(8,128)(2,1)S(1)} %collective-permute-done.refs_2_.refs_4_, ...), custom_call_target="tpu_custom_call" | custom-call | flops 1 | bytes 3670016 | tf_op jit(solution)/shard_map/pallas_call | solution.py:305
  40.3 2.8 %shard_map.99 = (f32[128,1024]{1,0:T(8,128)S(1)}, f32[1,8,128]{2,1,0:T(8,128)S(1)}) custom-call(s32[6]{0:T(128)S(1)} %stack.52.meta, bf16[53248,512]{1,0:T(8,128)(2,1)} %get-tuple-element.82.work, bf16[128,1024]{1,0:T(8,128)(2,1)S(1)} %shard_map.98.refs_0_.refs_6_.refs_8_, f32[128,1024]{1,0:T(8,128)S(1)} %shard_map.97.refs_1_, s32[128,1]{1,0:T(8,128)S(1)} %copy.11.refs_2_), custom_call_target="tpu_custom_call" | custom-call | flops 268435456 | bytes 2097152 | tf_op jit(solution)/shard_map/pallas_call | solution.py:153
  43.1 1.6 %collective-permute-done.8.refs_3_.refs_9_ = bf16[128,1024]{1,0:T(8,128)(2,1)S(1)} collective-permute-done((bf16[128,1024]{1,0:T(8,128)(2,1)S(1)}, bf16[128,1024]{1,0:T(8,128)(2,1)S(1)}, u32[]{:S(2)}, u32[]{:S(2)}) %collective-permute-start.8) | collective-permute-done | bytes 262176 | tf_op jit(solution)/shard_map/ppermute | solution.py:455
  44.8 0.1 copy.12.refs_4_.refs_3_
  44.9 4.7 %shard_map.101 = (f32[128,1024]{1,0:T(8,128)S(1)}, f32[2,8,128]{2,1,0:T(8,128)S(1)}) custom-call(s32[6]{0:T(128)S(1)} %stack.52.meta, bf16[53248,512]{1,0:T(8,128)(2,1)} %get-tuple-element.82.work, bf16[128,1024]{1,0:T(8,128)(2,1)S(1)} %collective-permute-done.2.refs_1_.refs_0_.refs_3_, bf16[128,1024]{1,0:T(8,128)(2,1)S(1)} %collective-permute-done.3.refs_3_.refs_1_.refs_5_, ...), custom_call_target="tpu_custom_call" | custom-call | flops 1073741824 | bytes 8388608 | tf_op jit(solution)/shard_map/pallas_call | solution.py:153
  49.6 0.6 collective-permute-start.10
  50.2 1.0 %collective-permute-start.11 = (f32[2,8,128]{2,1,0:T(8,128)S(1)}, f32[2,8,128]{2,1,0:T(8,128)S(1)}, u32[]{:S(2)}, u32[]{:S(2)}) collective-permute-start(f32[2,8,128]{2,1,0:T(8,128)S(1)} %get-tuple-element.100.refs_0_), channel_id=1, source_target_pairs={{0,4},{4,0},{8,12},{12,8},{1,5},{5,1},{9,13},{13,9},{2,6},{6,2},{1... | collective-permute-start | bytes 24584 | tf_op jit(solution)/shard_map/ppermute | solution.py:426
  51.2 1.9 %collective-permute-start.12 = (f32[2,8,128]{2,1,0:T(8,128)S(1)}, f32[2,8,128]{2,1,0:T(8,128)S(1)}, u32[]{:S(2)}, u32[]{:S(2)}) collective-permute-start(f32[2,8,128]{2,1,0:T(8,128)S(1)} %get-tuple-element.100.refs_0_), channel_id=1, source_target_pairs={{0,6},{2,4},{4,2},{6,0},{8,14},{10,12},{12,10},{14,8},{1,7},{3,5},... | collective-permute-start | bytes 24584 | tf_op jit(solution)/shard_map/ppermute | solution.py:525
  53.1 0.2 collective-permute-done.10.refs_1_
  53.3 0.5 collective-permute-done.11.refs_2_
  53.8 1.9 %collective-permute-done.12.refs_3_ = f32[2,8,128]{2,1,0:T(8,128)S(1)} collective-permute-done((f32[2,8,128]{2,1,0:T(8,128)S(1)}, f32[2,8,128]{2,1,0:T(8,128)S(1)}, u32[]{:S(2)}, u32[]{:S(2)}) %collective-permute-start.12) | collective-permute-done | bytes 8224 | tf_op jit(solution)/shard_map/ppermute | solution.py:525
  55.8 1.9 %collective-permute-start.13 = (f32[8,256]{1,0:T(8,128)S(1)}, f32[8,256]{1,0:T(8,128)S(1)}, u32[]{:S(2)}, u32[]{:S(2)}) collective-permute-start(f32[8,256]{1,0:T(8,128)S(1)} %shard_map.102.refs_4_), channel_id=1, source_target_pairs={{0,8},{8,0},{4,12},{12,4},{1,9},{9,1},{5,13},{13,5},{2,10},{10,2},... | collective-permute-start | bytes 24584 | tf_op jit(solution)/shard_map/ppermute | solution.py:426
  57.7 2.7 %collective-permute-done.13.refs_5_ = f32[8,256]{1,0:T(8,128)S(1)} collective-permute-done((f32[8,256]{1,0:T(8,128)S(1)}, f32[8,256]{1,0:T(8,128)S(1)}, u32[]{:S(2)}, u32[]{:S(2)}) %collective-permute-start.13) | collective-permute-done | bytes 8224 | tf_op jit(solution)/shard_map/ppermute | solution.py:426
  60.4 2.8 %shard_map.103 = (bf16[2,128,512]{2,1,0:T(8,128)(2,1)S(1)}, bf16[2,128,512]{2,1,0:T(8,128)(2,1)S(1)}, bf16[512,256]{1,0:T(8,128)(2,1)S(1)}, bf16[512,256]{1,0:T(...) custom-call(s32[5]{0:T(128)S(1)} %stack.57.meta, ...), custom_call_target="tpu_custom_call" | custom-call | flops 536870912 | bytes 4194304 | tf_op jit(solution)/shard_map/pallas_call | solution.py:252
  63.3 1.6 %collective-permute-start.14 = (bf16[1024,128]{1,0:T(8,128)(2,1)S(1)}, bf16[1024,128]{1,0:T(8,128)(2,1)S(1)}, u32[]{:S(2)}, u32[]{:S(2)}) collective-permute-start(bf16[1024,128]{1,0:T(8,128)(2,1)S(1)} %get-tuple-element.101), channel_id=1, source_target_pairs={{0,2},{2,0},{1,3},{3,1},{4,6},{6,4},{5,7},{7,5},{8,10},{10,8},{9,1... | collective-permute-start | bytes 786440 | tf_op jit(solution)/shard_map/ppermute | solution.py:538
  64.8 0.5 collective-permute-start.17
  65.3 2.3 %shard_map.104 = (f32[1024,128]{1,0:T(8,128)S(1)}, bf16[1024,128]{1,0:T(8,128)(2,1)S(1)}) custom-call(s32[1]{0:T(128)} %bitcast.5.meta, bf16[53248,512]{1,0:T(8,128)(2,1)} %get-tuple-element.82.work, bf16[512,256]{1,0:T(8,128)(2,1)S(1)} %get-tuple-element.102.flipped_own, bf16[512,256]{1,0:T(8,128)(2,1)S(1)} %get-tuple-element.103.flipped_far), custom_call_target="tpu_custom_call" | custom-call | flops 536870912 | bytes 2097152 | tf_op jit(solution)/shard_map/pallas_call | solution.py:267
  67.6 2.1 %collective-permute-done.14.refs_0_ = bf16[1024,128]{1,0:T(8,128)(2,1)S(1)} collective-permute-done((bf16[1024,128]{1,0:T(8,128)(2,1)S(1)}, bf16[1024,128]{1,0:T(8,128)(2,1)S(1)}, u32[]{:S(2)}, u32[]{:S(2)}) %collective-permute-start.14) | collective-permute-done | bytes 262176 | tf_op jit(solution)/shard_map/ppermute | solution.py:538
  69.8 2.9 %collective-permute-start.16 = (bf16[1024,128]{1,0:T(8,128)(2,1)S(1)}, bf16[1024,128]{1,0:T(8,128)(2,1)S(1)}, u32[]{:S(2)}, u32[]{:S(2)}) collective-permute-start(bf16[1024,128]{1,0:T(8,128)(2,1)S(1)} %shard_map.105), channel_id=1, source_target_pairs={{0,4},{12,8},{1,5},{13,9},{2,6},{14,10},{3,7},{15,11},{16,20},{28,... | collective-permute-start | bytes 786440 | tf_op jit(solution)/shard_map/ppermute | solution.py:426
  72.7 1.6 %collective-permute-start.15 = (bf16[1024,128]{1,0:T(8,128)(2,1)S(1)}, bf16[1024,128]{1,0:T(8,128)(2,1)S(1)}, u32[]{:S(2)}, u32[]{:S(2)}) collective-permute-start(bf16[1024,128]{1,0:T(8,128)(2,1)S(1)} %get-tuple-element.106), channel_id=1, source_target_pairs={{0,2},{2,0},{1,3},{3,1},{4,6},{6,4},{5,7},{7,5},{8,10},{10,8},{9,1... | collective-permute-start | bytes 786440 | tf_op jit(solution)/shard_map/ppermute | solution.py:538
  74.3 2.3 %shard_map.106 = (f32[1024,128]{1,0:T(8,128)S(1)}, bf16[1024,128]{1,0:T(8,128)(2,1)S(1)}) custom-call(s32[1]{0:T(128)} %bitcast.4.meta, bf16[53248,512]{1,0:T(8,128)(2,1)} %get-tuple-element.82.work, bf16[512,256]{1,0:T(8,128)(2,1)S(1)} %get-tuple-element.102.flipped_own, bf16[512,256]{1,0:T(8,128)(2,1)S(1)} %get-tuple-element.103.flipped_far), custom_call_target="tpu_custom_call" | custom-call | flops 536870912 | bytes 2097152 | tf_op jit(solution)/shard_map/pallas_call | solution.py:267
  76.5 0.3 collective-permute-done.16.refs_1_
  76.8 2.3 %collective-permute-done.15.refs_0_ = bf16[1024,128]{1,0:T(8,128)(2,1)S(1)} collective-permute-done((bf16[1024,128]{1,0:T(8,128)(2,1)S(1)}, bf16[1024,128]{1,0:T(8,128)(2,1)S(1)}, u32[]{:S(2)}, u32[]{:S(2)}) %collective-permute-start.15) | collective-permute-done | bytes 262176 | tf_op jit(solution)/shard_map/ppermute | solution.py:538
  79.2 2.1 %collective-permute-start.22 = (bf16[1024,128]{1,0:T(8,128)(2,1)S(1)}, bf16[1024,128]{1,0:T(8,128)(2,1)S(1)}, u32[]{:S(2)}, u32[]{:S(2)}) collective-permute-start(bf16[1024,128]{1,0:T(8,128)(2,1)S(1)} %shard_map.108), channel_id=1, source_target_pairs={{0,4},{12,8},{1,5},{13,9},{2,6},{14,10},{3,7},{15,11},{16,20},{28,... | collective-permute-start | bytes 786440 | tf_op jit(solution)/shard_map/ppermute | solution.py:426
  81.3 0.1 shard_map.107
  81.4 0.7 collective-permute-start.21
  82.1 1.3 %collective-permute-start.20 = (bf16[1024,128]{1,0:T(8,128)(2,1)S(1)}, bf16[1024,128]{1,0:T(8,128)(2,1)S(1)}, u32[]{:S(2)}, u32[]{:S(2)}) collective-permute-start(bf16[1024,128]{1,0:T(8,128)(2,1)S(1)} %get-tuple-element.114), channel_id=1, source_target_pairs={{0,2},{2,0},{1,3},{3,1},{4,6},{6,4},{5,7},{7,5},{8,10},{10,8},{9,1... | collective-permute-start | bytes 786440 | tf_op jit(solution)/shard_map/ppermute | solution.py:538
  83.3 2.3 %shard_map.109 = (f32[1024,128]{1,0:T(8,128)S(1)}, bf16[1024,128]{1,0:T(8,128)(2,1)S(1)}) custom-call(s32[1]{0:T(128)} %bitcast.3.meta, bf16[53248,512]{1,0:T(8,128)(2,1)} %get-tuple-element.82.work, bf16[512,256]{1,0:T(8,128)(2,1)S(1)} %get-tuple-element.102.flipped_own, bf16[512,256]{1,0:T(8,128)(2,1)S(1)} %get-tuple-element.103.flipped_far), custom_call_target="tpu_custom_call" | custom-call | flops 536870912 | bytes 2097152 | tf_op jit(solution)/shard_map/pallas_call | solution.py:267
  85.6 2.9 %collective-permute-done.20.refs_0_ = bf16[1024,128]{1,0:T(8,128)(2,1)S(1)} collective-permute-done((bf16[1024,128]{1,0:T(8,128)(2,1)S(1)}, bf16[1024,128]{1,0:T(8,128)(2,1)S(1)}, u32[]{:S(2)}, u32[]{:S(2)}) %collective-permute-start.20) | collective-permute-done | bytes 262176 | tf_op jit(solution)/shard_map/ppermute | solution.py:538
  88.5 0.1 shard_map.110
  88.6 0.1 shard_map.111
  88.7 0.7 collective-permute-start.25
  89.4 3.9 %collective-permute-start.24 = (bf16[1024,128]{1,0:T(8,128)(2,1)S(1)}, bf16[1024,128]{1,0:T(8,128)(2,1)S(1)}, u32[]{:S(2)}, u32[]{:S(2)}) collective-permute-start(bf16[1024,128]{1,0:T(8,128)(2,1)S(1)} %shard_map.110), channel_id=1, source_target_pairs={{0,4},{4,0},{8,12},{12,8},{1,5},{5,1},{9,13},{13,9},{2,6},{6,2},{1... | collective-permute-start | bytes 786440 | tf_op jit(solution)/shard_map/ppermute | solution.py:426
  93.3 1.2 %collective-permute-start.23 = (bf16[1024,128]{1,0:T(8,128)(2,1)S(1)}, bf16[1024,128]{1,0:T(8,128)(2,1)S(1)}, u32[]{:S(2)}, u32[]{:S(2)}) collective-permute-start(bf16[1024,128]{1,0:T(8,128)(2,1)S(1)} %get-tuple-element.121), channel_id=1, source_target_pairs={{0,2},{2,0},{1,3},{3,1},{4,6},{6,4},{5,7},{7,5},{8,10},{10,8},{9,1... | collective-permute-start | bytes 786440 | tf_op jit(solution)/shard_map/ppermute | solution.py:538
  94.5 0.5 bitcast_select_fusion
  95.0 5.5 %shard_map.112 = bf16[4096,512]{1,0:T(8,128)(2,1)} custom-call(s32[6]{0:T(128)S(1)} %stack.52.meta, bf16[2,128,512]{2,1,0:T(8,128)(2,1)S(1)} %get-tuple-element.128.refs_0_, bf16[2,128,512]{2,1,0:T(8,128)(2,1)S(1)} %collective-permute-done.17.refs_1_, bf16[128,1024]{1,0:T(8,128)(2,1)S(1)} %bitcast.25, ...), custom_call_target="tpu_custom_call" | custom-call | flops 2147483648 | bytes 8388608 | tf_op jit(solution)/shard_map/pallas_call | solution.py:393
  100.6 0.9 shard_map.113
  (38 shorter events, 0.4 us)
Async XLA Ops:
  0.6 16.0 %collective-permute-start.6 = (bf16[4096,512]{1,0:T(8,128)(2,1)}, bf16[4096,512]{1,0:T(8,128)(2,1)}, u32[]{:S(2)}, u32[]{:S(2)}) collective-permute-start(bf16[4096,512]{1,0:T(8,128)(2,1)} %w.1), channel_id=1, source_target_pairs={{0,1},{1,0},{2,3},{3,2},{4,5},{5,4},{6,7},{7,6},{8,9},{9,8},{10,11... | collective-permute-start | bytes 12582920 | tf_op jit(solution)/shard_map/ppermute | solution.py:425
  1.1 10.2 %collective-permute-start = (bf16[128,1024]{1,0:T(8,128)(2,1)}, bf16[128,1024]{1,0:T(8,128)(2,1)S(1)}, u32[]{:S(2)}, u32[]{:S(2)}) collective-permute-start(bf16[128,1024]{1,0:T(8,128)(2,1)} %bitcast.20), channel_id=1, source_target_pairs={{0,4},{4,0},{8,12},{12,8},{1,5},{5,1},{9,13},{13,9},{2,6},{6,2},{1... | collective-permute-start | bytes 786440 | tf_op jit(solution)/shard_map/ppermute | solution.py:426
  3.8 7.6 %collective-permute-start.1 = (bf16[128,1024]{1,0:T(8,128)(2,1)}, bf16[128,1024]{1,0:T(8,128)(2,1)S(1)}, u32[]{:S(2)}, u32[]{:S(2)}) collective-permute-start(bf16[128,1024]{1,0:T(8,128)(2,1)} %bitcast.21), channel_id=1, source_target_pairs={{4,8},{8,4},{5,9},{9,5},{6,10},{10,6},{7,11},{11,7},{20,24},{24,20... | collective-permute-start | bytes 786440 | tf_op jit(solution)/shard_map/ppermute | solution.py:426
  4.5 8.6 %collective-permute-start.2 = (bf16[128,1024]{1,0:T(8,128)(2,1)}, bf16[128,1024]{1,0:T(8,128)(2,1)S(1)}, u32[]{:S(2)}, u32[]{:S(2)}) collective-permute-start(bf16[128,1024]{1,0:T(8,128)(2,1)} %bitcast.22), channel_id=1, source_target_pairs={{0,2},{2,0},{1,3},{3,1},{4,6},{6,4},{5,7},{7,5},{8,10},{10,8},{9,1... | collective-permute-start | bytes 786440 | tf_op jit(solution)/shard_map/ppermute | solution.py:455
  6.8 2.2 %copy-start = (bf16[4096,512]{1,0:T(8,128)(2,1)S(1)}, bf16[4096,512]{1,0:T(8,128)(2,1)}, u32[]{:S(2)}) copy-start(bf16[4096,512]{1,0:T(8,128)(2,1)} %w.1) | copy-start | bytes 12582916
  9.0 7.6 %copy-start.1 = (bf16[1024,1,2,64]{0,3,2,1:T(8,128)(2,1)S(1)}, bf16[1024,1,2,64]{0,3,2,1:T(8,128)(2,1)}, u32[]{:S(2)}) copy-start(bf16[1024,1,2,64]{0,3,2,1:T(8,128)(2,1)} %param.7) | copy-start | bytes 786436
  11.4 10.1 %copy-start.4 = (s32[2]{0:T(128)S(1)}, s32[2]{0:T(128)}, u32[]{:S(2)}) copy-start(s32[2]{0:T(128)} %param.10) | copy-start | bytes 28
  11.4 10.7 %copy-start.2 = (f32[2,2]{1,0:T(2,128)S(1)}, f32[2,2]{1,0:T(2,128)}, u32[]{:S(2)}) copy-start(f32[2,2]{1,0:T(2,128)} %param.12) | copy-start | bytes 52
  11.4 10.7 %copy-start.3 = (f32[2,2]{1,0:T(2,128)S(1)}, f32[2,2]{1,0:T(2,128)}, u32[]{:S(2)}) copy-start(f32[2,2]{1,0:T(2,128)} %param.11) | copy-start | bytes 52
  11.4 13.4 %copy-start.5 = (f32[2]{0:T(128)S(1)}, f32[2]{0:T(128)}, u32[]{:S(2)}) copy-start(f32[2]{0:T(128)} %param.13) | copy-start | bytes 28
  13.1 13.0 %collective-permute-start.3 = (bf16[128,1024]{1,0:T(8,128)(2,1)S(1)}, bf16[128,1024]{1,0:T(8,128)(2,1)S(1)}, u32[]{:S(2)}, u32[]{:S(2)}) collective-permute-start(bf16[128,1024]{1,0:T(8,128)(2,1)S(1)} %collective-permute-done.refs_2_.refs_4_), channel_id=1, source_target_pairs={{0,2},{2,0},{1,3},{3,1},{4,6},{6,4},{5,7},{7,5},{8,10},{10,8},{9,1... | collective-permute-start | bytes 786440 | tf_op jit(solution)/shard_map/ppermute | solution.py:455
  14.6 12.8 %collective-permute-start.5 = (bf16[128,1024]{1,0:T(8,128)(2,1)S(1)}, bf16[128,1024]{1,0:T(8,128)(2,1)S(1)}, u32[]{:S(2)}, u32[]{:S(2)}) collective-permute-start(bf16[128,1024]{1,0:T(8,128)(2,1)S(1)} %collective-permute-done.refs_2_.refs_4_), channel_id=1, source_target_pairs={{4,8},{8,4},{5,9},{9,5},{6,10},{10,6},{7,11},{11,7},{20,24},{24,20... | collective-permute-start | bytes 786440 | tf_op jit(solution)/shard_map/ppermute | solution.py:426
  15.3 12.1 %collective-permute-start.4 = (bf16[128,1024]{1,0:T(8,128)(2,1)S(1)}, bf16[128,1024]{1,0:T(8,128)(2,1)S(1)}, u32[]{:S(2)}, u32[]{:S(2)}) collective-permute-start(bf16[128,1024]{1,0:T(8,128)(2,1)S(1)} %collective-permute-done.1.a), channel_id=1, source_target_pairs={{4,0},{8,12},{5,1},{9,13},{6,2},{10,14},{7,3},{11,15},{20,16},{24,... | collective-permute-start | bytes 786440 | tf_op jit(solution)/shard_map/ppermute | solution.py:426
  27.4 10.8 %collective-permute-start.7 = (bf16[128,1024]{1,0:T(8,128)(2,1)S(1)}, bf16[128,1024]{1,0:T(8,128)(2,1)S(1)}, u32[]{:S(2)}, u32[]{:S(2)}) collective-permute-start(bf16[128,1024]{1,0:T(8,128)(2,1)S(1)} %collective-permute-done.5.a), channel_id=1, source_target_pairs={{4,0},{8,12},{5,1},{9,13},{6,2},{10,14},{7,3},{11,15},{20,16},{24,... | collective-permute-start | bytes 786440 | tf_op jit(solution)/shard_map/ppermute | solution.py:426
  28.8 10.3 %collective-permute-start.9 = (bf16[128,1024]{1,0:T(8,128)(2,1)S(1)}, bf16[128,1024]{1,0:T(8,128)(2,1)S(1)}, u32[]{:S(2)}, u32[]{:S(2)}) collective-permute-start(bf16[128,1024]{1,0:T(8,128)(2,1)S(1)} %shard_map.96.refs_0_.refs_4_.refs_6_), channel_id=1, source_target_pairs={{0,2},{2,0},{1,3},{3,1},{4,6},{6,4},{5,7},{7,5},{8,10},{10,8},{9,1... | collective-permute-start | bytes 786440 | tf_op jit(solution)/shard_map/ppermute | solution.py:455
  38.3 6.4 %collective-permute-start.8 = (bf16[128,1024]{1,0:T(8,128)(2,1)S(1)}, bf16[128,1024]{1,0:T(8,128)(2,1)S(1)}, u32[]{:S(2)}, u32[]{:S(2)}) collective-permute-start(bf16[128,1024]{1,0:T(8,128)(2,1)S(1)} %shard_map.98.refs_0_.refs_6_.refs_8_), channel_id=1, source_target_pairs={{0,2},{2,0},{1,3},{3,1},{4,6},{6,4},{5,7},{7,5},{8,10},{10,8},{9,1... | collective-permute-start | bytes 786440 | tf_op jit(solution)/shard_map/ppermute | solution.py:455
  44.7 50.3 %collective-permute-start.26 = (bf16[7,128,1024]{2,1,0:T(8,128)(2,1)}, bf16[7,128,1024]{2,1,0:T(8,128)(2,1)}, u32[]{:S(2)}, u32[]{:S(2)}) collective-permute-start(bf16[7,128,1024]{2,1,0:T(8,128)(2,1)} %shard_map.100), channel_id=1, source_target_pairs={{0,1},{1,0},{2,3},{3,2},{4,5},{5,4},{6,7},{7,6},{8,9},{9,8},{10,11... | collective-permute-start | bytes 5505032 | tf_op jit(solution)/shard_map/ppermute | solution.py:425
  49.6 3.7 %collective-permute-start.10 = (f32[2,8,128]{2,1,0:T(8,128)S(1)}, f32[2,8,128]{2,1,0:T(8,128)S(1)}, u32[]{:S(2)}, u32[]{:S(2)}) collective-permute-start(f32[2,8,128]{2,1,0:T(8,128)S(1)} %get-tuple-element.100.refs_0_), channel_id=1, source_target_pairs={{0,2},{2,0},{1,3},{3,1},{4,6},{6,4},{5,7},{7,5},{8,10},{10,8},{9,1... | collective-permute-start | bytes 24584 | tf_op jit(solution)/shard_map/ppermute | solution.py:455
  50.2 3.7 %collective-permute-start.11 = (f32[2,8,128]{2,1,0:T(8,128)S(1)}, f32[2,8,128]{2,1,0:T(8,128)S(1)}, u32[]{:S(2)}, u32[]{:S(2)}) collective-permute-start(f32[2,8,128]{2,1,0:T(8,128)S(1)} %get-tuple-element.100.refs_0_), channel_id=1, source_target_pairs={{0,4},{4,0},{8,12},{12,8},{1,5},{5,1},{9,13},{13,9},{2,6},{6,2},{1... | collective-permute-start | bytes 24584 | tf_op jit(solution)/shard_map/ppermute | solution.py:426
  51.2 4.5 %collective-permute-start.12 = (f32[2,8,128]{2,1,0:T(8,128)S(1)}, f32[2,8,128]{2,1,0:T(8,128)S(1)}, u32[]{:S(2)}, u32[]{:S(2)}) collective-permute-start(f32[2,8,128]{2,1,0:T(8,128)S(1)} %get-tuple-element.100.refs_0_), channel_id=1, source_target_pairs={{0,6},{2,4},{4,2},{6,0},{8,14},{10,12},{12,10},{14,8},{1,7},{3,5},... | collective-permute-start | bytes 24584 | tf_op jit(solution)/shard_map/ppermute | solution.py:525
  55.8 4.6 %collective-permute-start.13 = (f32[8,256]{1,0:T(8,128)S(1)}, f32[8,256]{1,0:T(8,128)S(1)}, u32[]{:S(2)}, u32[]{:S(2)}) collective-permute-start(f32[8,256]{1,0:T(8,128)S(1)} %shard_map.102.refs_4_), channel_id=1, source_target_pairs={{0,8},{8,0},{4,12},{12,4},{1,9},{9,1},{5,13},{13,5},{2,10},{10,2},... | collective-permute-start | bytes 24584 | tf_op jit(solution)/shard_map/ppermute | solution.py:426
  63.3 6.4 %collective-permute-start.14 = (bf16[1024,128]{1,0:T(8,128)(2,1)S(1)}, bf16[1024,128]{1,0:T(8,128)(2,1)S(1)}, u32[]{:S(2)}, u32[]{:S(2)}) collective-permute-start(bf16[1024,128]{1,0:T(8,128)(2,1)S(1)} %get-tuple-element.101), channel_id=1, source_target_pairs={{0,2},{2,0},{1,3},{3,1},{4,6},{6,4},{5,7},{7,5},{8,10},{10,8},{9,1... | collective-permute-start | bytes 786440 | tf_op jit(solution)/shard_map/ppermute | solution.py:538
  64.8 11.7 %collective-permute-start.19 = (bf16[1,128,1024]{2,1,0:T(8,128)(2,1)S(1)}, bf16[1,128,1024]{2,1,0:T(8,128)(2,1)S(1)}, u32[]{:S(2)}, u32[]{:S(2)}) collective-permute-start(bf16[1,128,1024]{2,1,0:T(8,128)(2,1)S(1)} %bitcast.26), channel_id=1, source_target_pairs={{0,1},{1,0},{2,3},{3,2},{4,5},{5,4},{6,7},{7,6},{8,9},{9,8},{10,11... | collective-permute-start | bytes 786440 | tf_op jit(solution)/shard_map/ppermute | solution.py:425
  64.8 11.7 %collective-permute-start.17 = (bf16[2,128,512]{2,1,0:T(8,128)(2,1)S(1)}, bf16[2,128,512]{2,1,0:T(8,128)(2,1)S(1)}, u32[]{:S(2)}, u32[]{:S(2)}) collective-permute-start(bf16[2,128,512]{2,1,0:T(8,128)(2,1)S(1)} %get-tuple-element.111), channel_id=1, source_target_pairs={{0,1},{1,0},{2,3},{3,2},{4,5},{5,4},{6,7},{7,6},{8,9},{9,8},{10,11... | collective-permute-start | bytes 786440 | tf_op jit(solution)/shard_map/ppermute | solution.py:425
  65.3 7.4 %collective-permute-start.18 = (f32[1,128]{1,0:T(1,128)S(1)}, f32[1,128]{1,0:T(1,128)S(1)}, u32[]{:S(2)}, u32[]{:S(2)}) collective-permute-start(f32[1,128]{1,0:T(1,128)S(1)} %get-tuple-element.112), channel_id=1, source_target_pairs={{0,1},{1,0},{2,3},{3,2},{4,5},{5,4},{6,7},{7,6},{8,9},{9,8},{10,11... | collective-permute-start | bytes 1544 | tf_op jit(solution)/shard_map/ppermute | solution.py:425
  69.8 7.0 %collective-permute-start.16 = (bf16[1024,128]{1,0:T(8,128)(2,1)S(1)}, bf16[1024,128]{1,0:T(8,128)(2,1)S(1)}, u32[]{:S(2)}, u32[]{:S(2)}) collective-permute-start(bf16[1024,128]{1,0:T(8,128)(2,1)S(1)} %shard_map.105), channel_id=1, source_target_pairs={{0,4},{12,8},{1,5},{13,9},{2,6},{14,10},{3,7},{15,11},{16,20},{28,... | collective-permute-start | bytes 786440 | tf_op jit(solution)/shard_map/ppermute | solution.py:426
  72.7 6.4 %collective-permute-start.15 = (bf16[1024,128]{1,0:T(8,128)(2,1)S(1)}, bf16[1024,128]{1,0:T(8,128)(2,1)S(1)}, u32[]{:S(2)}, u32[]{:S(2)}) collective-permute-start(bf16[1024,128]{1,0:T(8,128)(2,1)S(1)} %get-tuple-element.106), channel_id=1, source_target_pairs={{0,2},{2,0},{1,3},{3,1},{4,6},{6,4},{5,7},{7,5},{8,10},{10,8},{9,1... | collective-permute-start | bytes 786440 | tf_op jit(solution)/shard_map/ppermute | solution.py:538
  79.2 6.4 %collective-permute-start.22 = (bf16[1024,128]{1,0:T(8,128)(2,1)S(1)}, bf16[1024,128]{1,0:T(8,128)(2,1)S(1)}, u32[]{:S(2)}, u32[]{:S(2)}) collective-permute-start(bf16[1024,128]{1,0:T(8,128)(2,1)S(1)} %shard_map.108), channel_id=1, source_target_pairs={{0,4},{12,8},{1,5},{13,9},{2,6},{14,10},{3,7},{15,11},{16,20},{28,... | collective-permute-start | bytes 786440 | tf_op jit(solution)/shard_map/ppermute | solution.py:426
  81.4 4.3 %collective-permute-start.21 = (bf16[1024,128]{1,0:T(8,128)(2,1)S(1)}, bf16[1024,128]{1,0:T(8,128)(2,1)S(1)}, u32[]{:S(2)}, u32[]{:S(2)}) collective-permute-start(bf16[1024,128]{1,0:T(8,128)(2,1)S(1)} %shard_map.107), channel_id=1, source_target_pairs={{4,8},{8,4},{5,9},{9,5},{6,10},{10,6},{7,11},{11,7},{20,24},{24,20... | collective-permute-start | bytes 786440 | tf_op jit(solution)/shard_map/ppermute | solution.py:426
  82.1 6.4 %collective-permute-start.20 = (bf16[1024,128]{1,0:T(8,128)(2,1)S(1)}, bf16[1024,128]{1,0:T(8,128)(2,1)S(1)}, u32[]{:S(2)}, u32[]{:S(2)}) collective-permute-start(bf16[1024,128]{1,0:T(8,128)(2,1)S(1)} %get-tuple-element.114), channel_id=1, source_target_pairs={{0,2},{2,0},{1,3},{3,1},{4,6},{6,4},{5,7},{7,5},{8,10},{10,8},{9,1... | collective-permute-start | bytes 786440 | tf_op jit(solution)/shard_map/ppermute | solution.py:538
  88.7 11.9 %collective-permute-start.25 = (bf16[1024,128]{1,0:T(8,128)(2,1)S(1)}, bf16[1024,128]{1,0:T(8,128)(2,1)S(1)}, u32[]{:S(2)}, u32[]{:S(2)}) collective-permute-start(bf16[1024,128]{1,0:T(8,128)(2,1)S(1)} %shard_map.111), channel_id=1, source_target_pairs={{4,8},{8,4},{5,9},{9,5},{6,10},{10,6},{7,11},{11,7},{20,24},{24,20... | collective-permute-start | bytes 786440 | tf_op jit(solution)/shard_map/ppermute | solution.py:426
  89.4 11.2 %collective-permute-start.24 = (bf16[1024,128]{1,0:T(8,128)(2,1)S(1)}, bf16[1024,128]{1,0:T(8,128)(2,1)S(1)}, u32[]{:S(2)}, u32[]{:S(2)}) collective-permute-start(bf16[1024,128]{1,0:T(8,128)(2,1)S(1)} %shard_map.110), channel_id=1, source_target_pairs={{0,4},{4,0},{8,12},{12,8},{1,5},{5,1},{9,13},{13,9},{2,6},{6,2},{1... | collective-permute-start | bytes 786440 | tf_op jit(solution)/shard_map/ppermute | solution.py:426
  93.3 7.3 %collective-permute-start.23 = (bf16[1024,128]{1,0:T(8,128)(2,1)S(1)}, bf16[1024,128]{1,0:T(8,128)(2,1)S(1)}, u32[]{:S(2)}, u32[]{:S(2)}) collective-permute-start(bf16[1024,128]{1,0:T(8,128)(2,1)S(1)} %get-tuple-element.121), channel_id=1, source_target_pairs={{0,2},{2,0},{1,3},{3,1},{4,6},{6,4},{5,7},{7,5},{8,10},{10,8},{9,1... | collective-permute-start | bytes 786440 | tf_op jit(solution)/shard_map/ppermute | solution.py:538

commit v10 on v9

--- a/solution.py
+++ b/solution.py
@@ -433,7 +433,8 @@
     firsts = [
         ((me_voc * n_ctx + me_ctx) * n_dp + owner) * columns for owner in (me_dp, (me_dp + 1) % n_dp)
     ]
-    meta = jnp.stack(part_of + firsts).astype(jnp.int32)
+    came_from = [(me_voc - i) % n_voc for i in range(n_voc)]
+    meta = jnp.stack(came_from + firsts).astype(jnp.int32)
 
     far_weights = dp_swap(head_weight)
     work = hold(head_weight)
@@ -460,13 +461,6 @@
         for t, a in zip(beyond, over):
             chunk[t, i] = a
 
-    def first_logits(work):
-        *logits, work = call([(0, {j: chunk[0, j] for j in (0, 1)}, None, None)], work, far=far_weights)
-        return logits, work
-
-    def more_logits(i, logits):
-        return call([(0, {i: chunk[0, i]}, logits[0], None)], work)
-
     scalars = [response_start, other_sums, ref_logp, loss_cotangent]
 
     def prepare(begin, others, refer, cotangent):
@@ -474,46 +468,30 @@
         small = jnp.stack([ratio[0] - ratio[1], mine(cotangent)])
         return [small, jnp.stack([part_of[final]] + firsts + [me_ctx, mine(begin)]).astype(jnp.int32)]
 
-    arrive(0, own, cross(own))
-    if line:
-        first = along(own, PAIRS_OUT)
-        inner = along(own, PAIR_IN)
-        (first, inner), (work, meta), over = together([first, inner], [work, meta], [chunk[t, 0] for t in beyond])
-        arrive(0, own, over)
-        over = cross(first)
-        outer, inner_last = along(inner, TO_ENDS), along(first, PAIR_IN)
-        arrive(1, first, over)
-        logits, work = first_logits(work)
-        logits, raw = together(logits, scalars)
-        over, (inner, outer, inner_last), logits, wanted, (small, meta_grads) = together(
-            over, [inner, outer, inner_last], logits, wanted, prepare(*raw)
-        )
-        arrive(1, first, over)
-        inner = either(inner, outer)
-        arrive(2, inner, cross(inner))
-        outer = along(inner_last, TO_ENDS)
-        (inner_last, outer), logits = together([inner_last, outer], more_logits(2, logits))
-        last = either(inner_last, outer)
-    else:
-        near = [own] + [along(own, ring(n_voc, i)) for i in range(1, n_voc)]
-        logits = None
-        for i in range(1, final):
-            arrive(i, near[i], cross(near[i]))
-            if logits is None:
-                logits, work = first_logits(work)
-            else:
-                logits = more_logits(i, logits)
-            (near[i + 1],), logits = together([near[i + 1]], logits)
-        last = near[final]
-        small, meta_grads = prepare(*scalars)
-    arrive(final, last, cross(last))
-    late = [(t, final) for t in beyond]
+    near = sorted({1, n_voc - 1})
+    rest = [i for i in range(1, n_voc) if i not in near]
+    came = [along(own, ring(n_voc, i)) for i in near]
+    came, over, (work, meta, again) = together(came, cross(own), [work, meta, own])
+    arrive(0, own, over)
+    over = [cross(c) for c in came]
+    for i, c, o in zip(near, came, over):
+        arrive(i, c, o)
+    came = [along(again, ring(n_voc, i)) for i in rest]
+    logits, work = call([(0, {i: chunk[0, i] for i in [0] + near}, None, None)], work, far=far_weights)
+    (logits,), raw = together([logits], scalars)
+    came, wanted, (logits, small, meta_grads), *over = together(came, wanted, [logits] + prepare(*raw), *over)
+    for i, o in zip(near, over):
+        arrive(i, chunk[0, i], o)
+    for i, c in zip(rest, came):
+        arrive(i, c, cross(c))
+
+    late = [(t, i) for i in rest for t in beyond]
     soon = [k for k in chunk if k not in late]
-    done = call([(0, {final: chunk[0, final]}, logits[0], wanted[0])], work)
+    done = call([(0, {i: chunk[0, i] for i in rest}, logits, wanted[0])], work)
     last, (near_logits, stats), (stacked,) = together(
         [chunk[k] for k in late], list(done), [stack_call([chunk[k] for k in soon])]
     )
-    arrive(final, chunk[0, final], last)
+    chunk.update(zip(late, last))
     *logits, stats = call(
         [(t, {i: chunk[t, i] for i in range(n_voc)}, None, wanted[t]) for t in beyond], work, earlier=[stats]
     )

time: 102 us -> 106 us (1.039)
  Pallas kernels: 34.6 us -> 41.2 us
  waiting for transfers between devices: 23.9 us -> 19.1 us
  local copies, waits for them, and re-layouts: 3.98 us -> 5.55 us
  starting transfers between devices: 33.2 us -> 34.3 us
    pallas_call x6, Pallas kernels: 1.29 us -> 7.29 us  [add_call(): pl.pallas_call(functools.partial(add_kernel, turned), out_shape=shape_of(...]
    ppermute x12 -> x10, waiting for transfers between devices: 11.2 us -> 8.69 us  [shards(): along = lambda a, by: lax.ppermute(a, 'vocab', by)]
    pallas_call x4 -> x3, Pallas kernels: 14.9 us -> 12.8 us  [logits_call(): pl.pallas_call(functools.partial(logits_kernel, kernel_plan, columns, par...]
    ppermute x5, waiting for transfers between devices: 3.51 us -> 1.81 us  [shards(): cross = lambda a: [lax.ppermute(a, 'ctx', ring(n_ctx, t)) for t in beyond]]
    unnamed x12 -> x24, local copies, waits for them, and re-layouts: 2.21 us -> 3.76 us
    pallas_call x3, Pallas kernels: 6.8 us -> 8.29 us  [spread_call(): pl.pallas_call(functools.partial(spread_kernel, part, width, n_parts), ou...]
    ppermute x12 -> x10, starting transfers between devices: 19.8 us -> 20.8 us  [shards(): along = lambda a, by: lax.ppermute(a, 'vocab', by)]
  transfers between devices with their start and end apart: 27 -> 25, of which waited for: 12 -> 12; matrix products, arithmetic and copies ran while one was open for 5% -> 5% of each run, Pallas kernels for 33% -> 38%
where the time goes in v10:
time: 106 us
  Pallas kernels  41.2 us (39%)
  starting transfers between devices  34.3 us (32%)
  waiting for transfers between devices  19.1 us (18%)
  local copies, waits for them, and re-layouts  5.55 us (5%)
  other arithmetic  3.4 us (3%)
  between operations  2.3 us (2%)
    ppermute x10, starting transfers between devices, shards(): along = lambda a, by: lax.ppermute(a, 'vocab', by)  20.8 us
    pallas_call x3, Pallas kernels, logits_call(): pl.pallas_call(functools.partial(logits_kernel, kernel_plan, columns, par...  12.8 us
    ppermute x10, waiting for transfers between devices, shards(): along = lambda a, by: lax.ppermute(a, 'vocab', by)  8.69 us
    pallas_call x3, Pallas kernels, spread_call(): pl.pallas_call(functools.partial(spread_kernel, part, width, n_parts), ou...  8.29 us
    ppermute x4, waiting for transfers between devices, shards(): lax.ppermute(c, 'ctx', ring(n_ctx, -t))  7.5 us
    pallas_call x6, Pallas kernels, add_call(): pl.pallas_call(functools.partial(add_kernel, turned), out_shape=shape_of(...  7.29 us
    pallas_call x1, Pallas kernels, head_call(): pl.pallas_call(functools.partial(head_kernel, slots_here, list(near), [ke...  5.71 us
    ppermute x5, starting transfers between devices, shards(): cross = lambda a: [lax.ppermute(a, 'ctx', ring(n_ctx, t)) for t in beyond]  5.58 us
  transfers between devices with their start and end apart: 25, of which 12 were waited for; matrix products, arithmetic and copies ran while one was open for 5% of the time, Pallas kernels for 38%

profile of v10, /device:TPU:0, one launch (start us, length us, event | category | flops | bytes accessed | tf_op | source)
XLA Modules:
  0.0 105.8 jit_solution(5084830250173615785)
XLA Ops:
  0.6 0.5 collective-permute-start.4
  1.1 2.6 %collective-permute-start = (bf16[128,1024]{1,0:T(8,128)(2,1)}, bf16[128,1024]{1,0:T(8,128)(2,1)S(1)}, u32[]{:S(2)}, u32[]{:S(2)}) collective-permute-start(bf16[128,1024]{1,0:T(8,128)(2,1)} %bitcast.24), channel_id=1, source_target_pairs={{0,4},{4,8},{8,12},{12,0},{1,5},{5,9},{9,13},{13,1},{2,6},{6,10},{... | collective-permute-start | bytes 786440 | tf_op jit(solution)/shard_map/ppermute | solution.py:426
  3.8 2.1 %collective-permute-start.1 = (bf16[128,1024]{1,0:T(8,128)(2,1)}, bf16[128,1024]{1,0:T(8,128)(2,1)S(1)}, u32[]{:S(2)}, u32[]{:S(2)}) collective-permute-start(bf16[128,1024]{1,0:T(8,128)(2,1)} %bitcast.25), channel_id=1, source_target_pairs={{0,12},{4,0},{8,4},{12,8},{1,13},{5,1},{9,5},{13,9},{2,14},{6,2},{... | collective-permute-start | bytes 786440 | tf_op jit(solution)/shard_map/ppermute | solution.py:426
  5.9 1.6 %collective-permute-start.2 = (bf16[128,1024]{1,0:T(8,128)(2,1)}, bf16[128,1024]{1,0:T(8,128)(2,1)S(1)}, u32[]{:S(2)}, u32[]{:S(2)}) collective-permute-start(bf16[128,1024]{1,0:T(8,128)(2,1)} %bitcast.26), channel_id=1, source_target_pairs={{0,2},{2,0},{1,3},{3,1},{4,6},{6,4},{5,7},{7,5},{8,10},{10,8},{9,1... | collective-permute-start | bytes 786440 | tf_op jit(solution)/shard_map/ppermute | solution.py:456
  7.5 0.8 select_reduce_fusion
  8.3 2.2 %copy-done = bf16[4096,512]{1,0:T(8,128)(2,1)S(1)} copy-done((bf16[4096,512]{1,0:T(8,128)(2,1)S(1)}, bf16[4096,512]{1,0:T(8,128)(2,1)}, u32[]{:S(2)}) %copy-start) | copy-done | bytes 4194328
  10.5 2.0 %shard_map.94.work = bf16[53248,512]{1,0:T(8,128)(2,1)} custom-call(bf16[4096,512]{1,0:T(8,128)(2,1)S(1)} %copy-done), custom_call_target="tpu_custom_call" | custom-call | flops 1 | bytes 8388608 | tf_op jit(solution)/shard_map/pallas_call | solution.py:52
  12.7 0.1 add.104
  12.8 0.1 stack.60.meta
  12.9 0.3 collective-permute-done.refs_2_.refs_4_
  13.2 4.8 %collective-permute-done.1.refs_3_.refs_4_.refs_6_ = bf16[128,1024]{1,0:T(8,128)(2,1)S(1)} collective-permute-done((bf16[128,1024]{1,0:T(8,128)(2,1)}, bf16[128,1024]{1,0:T(8,128)(2,1)S(1)}, u32[]{:S(2)}, u32[]{:S(2)}) %collective-permute-start.1) | collective-permute-done | bytes 262176 | tf_op jit(solution)/shard_map/ppermute | solution.py:426
  18.0 1.4 %collective-permute-start.3 = (bf16[128,1024]{1,0:T(8,128)(2,1)S(1)}, bf16[128,1024]{1,0:T(8,128)(2,1)S(1)}, u32[]{:S(2)}, u32[]{:S(2)}) collective-permute-start(bf16[128,1024]{1,0:T(8,128)(2,1)S(1)} %bitcast.27), channel_id=1, source_target_pairs={{0,8},{4,12},{8,0},{12,4},{1,9},{5,13},{9,1},{13,5},{2,10},{6,14},... | collective-permute-start | bytes 786440 | tf_op jit(solution)/shard_map/ppermute | solution.py:426
  19.4 1.5 %collective-permute-start.5 = (bf16[128,1024]{1,0:T(8,128)(2,1)S(1)}, bf16[128,1024]{1,0:T(8,128)(2,1)S(1)}, u32[]{:S(2)}, u32[]{:S(2)}) collective-permute-start(bf16[128,1024]{1,0:T(8,128)(2,1)S(1)} %collective-permute-done.refs_2_.refs_4_), channel_id=1, source_target_pairs={{0,2},{2,0},{1,3},{3,1},{4,6},{6,4},{5,7},{7,5},{8,10},{10,8},{9,1... | collective-permute-start | bytes 786440 | tf_op jit(solution)/shard_map/ppermute | solution.py:456
  20.9 0.5 collective-permute-start.6
  21.4 4.8 %shard_map.95 = (f32[128,1024]{1,0:T(8,128)S(1)}, bf16[53248,512]{1,0:T(8,128)(2,1)}) custom-call(s32[6]{0:T(128)S(1)} %stack.60.meta, bf16[53248,512]{1,0:T(8,128)(2,1)} %shard_map.94.work, bf16[4096,512]{1,0:T(8,128)(2,1)} %collective-permute-done.4.refs_0_, bf16[128,1024]{1,0:T(8,128)(2,1)S(1)} %bitcast.28, ...), custom_call_target="tpu_custom_call", output_to_operand_aliasing={{1}: (1, {})} | custom-call | flops 805306368 | bytes 6291456 | tf_op jit(solution)/shard_map/pallas_call | solution.py:153
  26.2 0.6 select_reduce_fusion.3
  26.9 0.1 select_reduce_fusion.1
  26.9 0.6 fusion
  28.8 0.7 stack.66.meta
  29.6 0.6 select_reduce_fusion.4
  30.2 0.7 pad_maximum_fusion.small
  30.9 1.3 %collective-permute-done.3.refs_0_.refs_6_.refs_8_ = bf16[128,1024]{1,0:T(8,128)(2,1)S(1)} collective-permute-done((bf16[128,1024]{1,0:T(8,128)(2,1)S(1)}, bf16[128,1024]{1,0:T(8,128)(2,1)S(1)}, u32[]{:S(2)}, u32[]{:S(2)}) %collective-permute-start.3) | collective-permute-done | bytes 262176 | tf_op jit(solution)/shard_map/ppermute | solution.py:426
  32.2 0.4 collective-permute-done.6.refs_5_.refs_3_.refs_7_
  32.6 1.4 %collective-permute-start.7 = (bf16[128,1024]{1,0:T(8,128)(2,1)S(1)}, bf16[128,1024]{1,0:T(8,128)(2,1)}, u32[]{:S(2)}, u32[]{:S(2)}) collective-permute-start(bf16[128,1024]{1,0:T(8,128)(2,1)S(1)} %collective-permute-done.3.refs_0_.refs_6_.refs_8_), channel_id=1, source_target_pairs={{0,2},{2,0},{1,3},{3,1},{4,6},{6,4},{5,7},{7,5},{8,10},{10,8},{9,1... | collective-permute-start | bytes 786440 | tf_op jit(solution)/shard_map/ppermute | solution.py:456
  33.9 1.3 %shard_map.97 = bf16[7,128,1024]{2,1,0:T(8,128)(2,1)} custom-call(bf16[128,1024]{1,0:T(8,128)(2,1)S(1)} %bitcast.29, bf16[128,1024]{1,0:T(8,128)(2,1)S(1)} %collective-permute-done.2.refs_1_.refs_0_.refs_3_, bf16[128,1024]{1,0:T(8,128)(2,1)S(1)} %collective-permute-done.refs_2_.refs_4_, bf16[128,1024]{1,0:T(8,128)(2,1)S(1)} %collective-permute-done.5.refs_3_.refs_1_.refs_5_, ...), custom_call_target="tpu_custom_call" | custom-call | flops 1 | bytes 3670016 | tf_op jit(solution)/shard_map/pallas_call | solution.py:305
  35.2 0.1 copy.11.refs_2_
  35.3 2.8 %shard_map.96 = (f32[128,1024]{1,0:T(8,128)S(1)}, f32[1,8,128]{2,1,0:T(8,128)S(1)}) custom-call(s32[6]{0:T(128)S(1)} %stack.60.meta, bf16[53248,512]{1,0:T(8,128)(2,1)} %get-tuple-element.80.work, bf16[128,1024]{1,0:T(8,128)(2,1)S(1)} %collective-permute-done.3.refs_0_.refs_6_.refs_8_, f32[128,1024]{1,0:T(8,128)S(1)} %get-tuple-element.82.refs_1_, ...), custom_call_target="tpu_custom_call" | custom-call | flops 268435456 | bytes 2097152 | tf_op jit(solution)/shard_map/pallas_call | solution.py:153
  38.1 0.8 copy-done.2
  39.0 0.4 collective-permute-done.7.refs_2_.refs_9_
  39.4 0.1 copy.12.refs_4_.refs_3_
  39.5 5.2 %shard_map.98 = (f32[128,1024]{1,0:T(8,128)S(1)}, f32[2,8,128]{2,1,0:T(8,128)S(1)}) custom-call(s32[6]{0:T(128)S(1)} %stack.60.meta, bf16[53248,512]{1,0:T(8,128)(2,1)} %get-tuple-element.80.work, bf16[128,1024]{1,0:T(8,128)(2,1)S(1)} %collective-permute-done.2.refs_1_.refs_0_.refs_3_, bf16[128,1024]{1,0:T(8,128)(2,1)S(1)} %collective-permute-done.5.refs_3_.refs_1_.refs_5_, ...), custom_call_target="tpu_custom_call" | custom-call | flops 1073741824 | bytes 8388608 | tf_op jit(solution)/shard_map/pallas_call | solution.py:153
  44.7 2.0 %collective-permute-start.10 = (f32[2,8,128]{2,1,0:T(8,128)S(1)}, f32[2,8,128]{2,1,0:T(8,128)S(1)}, u32[]{:S(2)}, u32[]{:S(2)}) collective-permute-start(f32[2,8,128]{2,1,0:T(8,128)S(1)} %get-tuple-element.94.refs_0_), channel_id=1, source_target_pairs={{0,6},{2,4},{4,2},{6,0},{8,14},{10,12},{12,10},{14,8},{1,7},{3,5},... | collective-permute-start | bytes 24584 | tf_op jit(solution)/shard_map/ppermute | solution.py:503
  46.7 0.6 collective-permute-start.8
  47.3 1.0 collective-permute-start.9
  48.2 1.1 %collective-permute-done.10.refs_3_ = f32[2,8,128]{2,1,0:T(8,128)S(1)} collective-permute-done((f32[2,8,128]{2,1,0:T(8,128)S(1)}, f32[2,8,128]{2,1,0:T(8,128)S(1)}, u32[]{:S(2)}, u32[]{:S(2)}) %collective-permute-start.10) | collective-permute-done | bytes 8224 | tf_op jit(solution)/shard_map/ppermute | solution.py:503
  49.3 1.1 %collective-permute-done.8.refs_1_ = f32[2,8,128]{2,1,0:T(8,128)S(1)} collective-permute-done((f32[2,8,128]{2,1,0:T(8,128)S(1)}, f32[2,8,128]{2,1,0:T(8,128)S(1)}, u32[]{:S(2)}, u32[]{:S(2)}) %collective-permute-start.8) | collective-permute-done | bytes 8224 | tf_op jit(solution)/shard_map/ppermute | solution.py:456
  50.4 0.6 collective-permute-done.9.refs_2_
  50.9 2.9 %collective-permute-start.11 = (f32[8,256]{1,0:T(8,128)S(1)}, f32[8,256]{1,0:T(8,128)S(1)}, u32[]{:S(2)}, u32[]{:S(2)}) collective-permute-start(f32[8,256]{1,0:T(8,128)S(1)} %shard_map.99.refs_4_), channel_id=1, source_target_pairs={{0,8},{8,0},{4,12},{12,4},{1,9},{9,1},{5,13},{13,5},{2,10},{10,2},... | collective-permute-start | bytes 24584 | tf_op jit(solution)/shard_map/ppermute | solution.py:426
  53.8 1.7 %collective-permute-done.11.refs_5_ = f32[8,256]{1,0:T(8,128)S(1)} collective-permute-done((f32[8,256]{1,0:T(8,128)S(1)}, f32[8,256]{1,0:T(8,128)S(1)}, u32[]{:S(2)}, u32[]{:S(2)}) %collective-permute-start.11) | collective-permute-done | bytes 8224 | tf_op jit(solution)/shard_map/ppermute | solution.py:426
  55.6 3.8 %shard_map.100 = (bf16[2,128,512]{2,1,0:T(8,128)(2,1)S(1)}, bf16[2,128,512]{2,1,0:T(8,128)(2,1)}, bf16[512,256]{1,0:T(8,128)(2,1)S(1)}, bf16[512,256]{1,0:T(8,12...) custom-call(s32[5]{0:T(128)S(1)} %stack.66.meta, ...), custom_call_target="tpu_custom_call" | custom-call | flops 536870912 | bytes 4194304 | tf_op jit(solution)/shard_map/pallas_call | solution.py:252
  59.4 0.7 copy-done.6
  60.1 1.5 %collective-permute-start.12 = (bf16[1024,128]{1,0:T(8,128)(2,1)}, bf16[1024,128]{1,0:T(8,128)(2,1)}, u32[]{:S(2)}, u32[]{:S(2)}) collective-permute-start(bf16[1024,128]{1,0:T(8,128)(2,1)} %get-tuple-element.95), channel_id=1, source_target_pairs={{0,2},{2,0},{1,3},{3,1},{4,6},{6,4},{5,7},{7,5},{8,10},{10,8},{9,1... | collective-permute-start | bytes 786440 | tf_op jit(solution)/shard_map/ppermute | solution.py:516
  61.6 0.5 collective-permute-start.15
  62.1 3.0 %shard_map.101 = (f32[1024,128]{1,0:T(8,128)S(1)}, bf16[1024,128]{1,0:T(8,128)(2,1)}) custom-call(s32[1]{0:T(128)} %bitcast.13.meta, bf16[53248,512]{1,0:T(8,128)(2,1)} %get-tuple-element.80.work, bf16[512,256]{1,0:T(8,128)(2,1)S(1)} %get-tuple-element.96.flipped_own, bf16[512,256]{1,0:T(8,128)(2,1)S(1)} %get-tuple-element.97.flipped_far), custom_call_target="tpu_custom_call" | custom-call | flops 536870912 | bytes 2097152 | tf_op jit(solution)/shard_map/pallas_call | solution.py:267
  65.1 1.7 %collective-permute-done.12.refs_0_ = bf16[1024,128]{1,0:T(8,128)(2,1)} collective-permute-done((bf16[1024,128]{1,0:T(8,128)(2,1)}, bf16[1024,128]{1,0:T(8,128)(2,1)}, u32[]{:S(2)}, u32[]{:S(2)}) %collective-permute-start.12) | collective-permute-done | bytes 262176 | tf_op jit(solution)/shard_map/ppermute | solution.py:516
  66.8 1.7 %shard_map.102 = bf16[1024,128]{1,0:T(8,128)(2,1)} custom-call(f32[1024,128]{1,0:T(8,128)S(1)} %get-tuple-element.101.kept, bf16[1024,128]{1,0:T(8,128)(2,1)} %collective-permute-done.12.refs_0_), custom_call_target="tpu_custom_call" | custom-call | flops 131072 | bytes 524288 | tf_op jit(solution)/shard_map/pallas_call | solution.py:352
  68.5 3.6 %collective-permute-start.14 = (bf16[1024,128]{1,0:T(8,128)(2,1)}, bf16[1024,128]{1,0:T(8,128)(2,1)}, u32[]{:S(2)}, u32[]{:S(2)}) collective-permute-start(bf16[1024,128]{1,0:T(8,128)(2,1)} %shard_map.102), channel_id=1, source_target_pairs={{0,4},{12,8},{1,5},{13,9},{2,6},{14,10},{3,7},{15,11},{16,20},{28,... | collective-permute-start | bytes 786440 | tf_op jit(solution)/shard_map/ppermute | solution.py:426
  72.0 1.5 %collective-permute-start.13 = (bf16[1024,128]{1,0:T(8,128)(2,1)}, bf16[1024,128]{1,0:T(8,128)(2,1)}, u32[]{:S(2)}, u32[]{:S(2)}) collective-permute-start(bf16[1024,128]{1,0:T(8,128)(2,1)} %get-tuple-element.100), channel_id=1, source_target_pairs={{0,2},{2,0},{1,3},{3,1},{4,6},{6,4},{5,7},{7,5},{8,10},{10,8},{9,1... | collective-permute-start | bytes 786440 | tf_op jit(solution)/shard_map/ppermute | solution.py:516
  73.5 3.0 %shard_map.103 = (f32[1024,128]{1,0:T(8,128)S(1)}, bf16[1024,128]{1,0:T(8,128)(2,1)}) custom-call(s32[1]{0:T(128)} %bitcast.14.meta, bf16[53248,512]{1,0:T(8,128)(2,1)} %get-tuple-element.80.work, bf16[512,256]{1,0:T(8,128)(2,1)S(1)} %get-tuple-element.96.flipped_own, bf16[512,256]{1,0:T(8,128)(2,1)S(1)} %get-tuple-element.97.flipped_far), custom_call_target="tpu_custom_call" | custom-call | flops 536870912 | bytes 2097152 | tf_op jit(solution)/shard_map/pallas_call | solution.py:267
  76.5 2.6 %collective-permute-done.13.refs_0_ = bf16[1024,128]{1,0:T(8,128)(2,1)} collective-permute-done((bf16[1024,128]{1,0:T(8,128)(2,1)}, bf16[1024,128]{1,0:T(8,128)(2,1)}, u32[]{:S(2)}, u32[]{:S(2)}) %collective-permute-start.13) | collective-permute-done | bytes 262176 | tf_op jit(solution)/shard_map/ppermute | solution.py:516
  79.1 1.7 %shard_map.105 = bf16[1024,128]{1,0:T(8,128)(2,1)} custom-call(f32[1024,128]{1,0:T(8,128)S(1)} %get-tuple-element.110.kept, bf16[1024,128]{1,0:T(8,128)(2,1)} %collective-permute-done.13.refs_0_), custom_call_target="tpu_custom_call" | custom-call | flops 131072 | bytes 524288 | tf_op jit(solution)/shard_map/pallas_call | solution.py:352
  80.8 2.2 %collective-permute-start.20 = (bf16[1024,128]{1,0:T(8,128)(2,1)}, bf16[1024,128]{1,0:T(8,128)(2,1)}, u32[]{:S(2)}, u32[]{:S(2)}) collective-permute-start(bf16[1024,128]{1,0:T(8,128)(2,1)} %shard_map.105), channel_id=1, source_target_pairs={{0,4},{12,8},{1,5},{13,9},{2,6},{14,10},{3,7},{15,11},{16,20},{28,... | collective-permute-start | bytes 786440 | tf_op jit(solution)/shard_map/ppermute | solution.py:426
  83.0 1.8 %shard_map.104 = bf16[1024,128]{1,0:T(8,128)(2,1)} custom-call(f32[1024,128]{1,0:T(8,128)S(1)} %get-tuple-element.101.kept, bf16[1024,128]{1,0:T(8,128)(2,1)} %collective-permute-done.12.refs_0_, bf16[1024,128]{1,0:T(8,128)(2,1)} %collective-permute-done.14.refs_1_), custom_call_target="tpu_custom_call" | custom-call | flops 131072 | bytes 524288 | tf_op jit(solution)/shard_map/pallas_call | solution.py:352
  84.8 0.7 collective-permute-start.19
  85.5 1.0 collective-permute-start.18
  86.5 2.3 %shard_map.106 = (f32[1024,128]{1,0:T(8,128)S(1)}, bf16[1024,128]{1,0:T(8,128)(2,1)S(1)}) custom-call(s32[1]{0:T(128)} %bitcast.16.meta, bf16[53248,512]{1,0:T(8,128)(2,1)} %get-tuple-element.80.work, bf16[512,256]{1,0:T(8,128)(2,1)S(1)} %get-tuple-element.96.flipped_own, bf16[512,256]{1,0:T(8,128)(2,1)S(1)} %get-tuple-element.97.flipped_far), custom_call_target="tpu_custom_call" | custom-call | flops 536870912 | bytes 2097152 | tf_op jit(solution)/shard_map/pallas_call | solution.py:267
  88.8 3.3 %collective-permute-done.18.refs_0_ = bf16[1024,128]{1,0:T(8,128)(2,1)S(1)} collective-permute-done((bf16[1024,128]{1,0:T(8,128)(2,1)}, bf16[1024,128]{1,0:T(8,128)(2,1)S(1)}, u32[]{:S(2)}, u32[]{:S(2)}) %collective-permute-start.18) | collective-permute-done | bytes 262176 | tf_op jit(solution)/shard_map/ppermute | solution.py:516
  92.2 1.1 %shard_map.108 = bf16[1024,128]{1,0:T(8,128)(2,1)S(1)} custom-call(f32[1024,128]{1,0:T(8,128)S(1)} %get-tuple-element.110.kept, bf16[1024,128]{1,0:T(8,128)(2,1)} %collective-permute-done.13.refs_0_, bf16[1024,128]{1,0:T(8,128)(2,1)} %collective-permute-done.20.refs_1_), custom_call_target="tpu_custom_call" | custom-call | flops 131072 | bytes 524288 | tf_op jit(solution)/shard_map/pallas_call | solution.py:352
  93.3 0.7 collective-permute-start.23
  94.0 3.8 %collective-permute-start.22 = (bf16[1024,128]{1,0:T(8,128)(2,1)S(1)}, bf16[1024,128]{1,0:T(8,128)(2,1)S(1)}, u32[]{:S(2)}, u32[]{:S(2)}) collective-permute-start(bf16[1024,128]{1,0:T(8,128)(2,1)S(1)} %shard_map.107), channel_id=1, source_target_pairs={{0,4},{4,0},{8,12},{12,8},{1,5},{5,1},{9,13},{13,9},{2,6},{6,2},{1... | collective-permute-start | bytes 786440 | tf_op jit(solution)/shard_map/ppermute | solution.py:426
  97.8 0.8 collective-permute-start.21
  98.6 0.5 bitcast_select_fusion
  99.1 5.7 %shard_map.109 = bf16[4096,512]{1,0:T(8,128)(2,1)} custom-call(s32[6]{0:T(128)S(1)} %stack.60.meta, bf16[2,128,512]{2,1,0:T(8,128)(2,1)S(1)} %copy-done.7, bf16[2,128,512]{2,1,0:T(8,128)(2,1)} %collective-permute-done.15.refs_1_, bf16[128,1024]{1,0:T(8,128)(2,1)S(1)} %bitcast.30, bf16[128,1024]{1,0:T(8,128)(2,1)S(1)} %collective-permute-done.2.refs_1_.refs_0_.refs_3_, ...), custom_call_target="tpu_custom_call" | custom-call | flops 2147483648 | bytes 8388608 | tf_op jit(solution)/shard_map/pallas_call | solution.py:393
  104.9 0.9 shard_map.110
  (43 shorter events, 0.4 us)
Async XLA Ops:
  0.6 20.8 %collective-permute-start.4 = (bf16[4096,512]{1,0:T(8,128)(2,1)}, bf16[4096,512]{1,0:T(8,128)(2,1)}, u32[]{:S(2)}, u32[]{:S(2)}) collective-permute-start(bf16[4096,512]{1,0:T(8,128)(2,1)} %w.1), channel_id=1, source_target_pairs={{0,1},{1,0},{2,3},{3,2},{4,5},{5,4},{6,7},{7,6},{8,9},{9,8},{10,11... | collective-permute-start | bytes 12582920 | tf_op jit(solution)/shard_map/ppermute | solution.py:425
  1.1 12.1 %collective-permute-start = (bf16[128,1024]{1,0:T(8,128)(2,1)}, bf16[128,1024]{1,0:T(8,128)(2,1)S(1)}, u32[]{:S(2)}, u32[]{:S(2)}) collective-permute-start(bf16[128,1024]{1,0:T(8,128)(2,1)} %bitcast.24), channel_id=1, source_target_pairs={{0,4},{4,8},{8,12},{12,0},{1,5},{5,9},{9,13},{13,1},{2,6},{6,10},{... | collective-permute-start | bytes 786440 | tf_op jit(solution)/shard_map/ppermute | solution.py:426
  3.8 14.2 %collective-permute-start.1 = (bf16[128,1024]{1,0:T(8,128)(2,1)}, bf16[128,1024]{1,0:T(8,128)(2,1)S(1)}, u32[]{:S(2)}, u32[]{:S(2)}) collective-permute-start(bf16[128,1024]{1,0:T(8,128)(2,1)} %bitcast.25), channel_id=1, source_target_pairs={{0,12},{4,0},{8,4},{12,8},{1,13},{5,1},{9,5},{13,9},{2,14},{6,2},{... | collective-permute-start | bytes 786440 | tf_op jit(solution)/shard_map/ppermute | solution.py:426
  5.9 12.1 %collective-permute-start.2 = (bf16[128,1024]{1,0:T(8,128)(2,1)}, bf16[128,1024]{1,0:T(8,128)(2,1)S(1)}, u32[]{:S(2)}, u32[]{:S(2)}) collective-permute-start(bf16[128,1024]{1,0:T(8,128)(2,1)} %bitcast.26), channel_id=1, source_target_pairs={{0,2},{2,0},{1,3},{3,1},{4,6},{6,4},{5,7},{7,5},{8,10},{10,8},{9,1... | collective-permute-start | bytes 786440 | tf_op jit(solution)/shard_map/ppermute | solution.py:456
  8.3 2.2 %copy-start = (bf16[4096,512]{1,0:T(8,128)(2,1)S(1)}, bf16[4096,512]{1,0:T(8,128)(2,1)}, u32[]{:S(2)}) copy-start(bf16[4096,512]{1,0:T(8,128)(2,1)} %w.1) | copy-start | bytes 12582916
  10.5 7.5 %copy-start.1 = (bf16[1024,1,2,64]{0,3,2,1:T(8,128)(2,1)S(1)}, bf16[1024,1,2,64]{0,3,2,1:T(8,128)(2,1)}, u32[]{:S(2)}) copy-start(bf16[1024,1,2,64]{0,3,2,1:T(8,128)(2,1)} %param.7) | copy-start | bytes 786436
  12.9 13.3 %copy-start.10 = (s32[2]{0:T(128)S(1)}, s32[2]{0:T(128)}, u32[]{:S(2)}) copy-start(s32[2]{0:T(128)} %param.10) | copy-start | bytes 28
  12.9 13.9 %copy-start.8 = (f32[2,2]{1,0:T(2,128)S(1)}, f32[2,2]{1,0:T(2,128)}, u32[]{:S(2)}) copy-start(f32[2,2]{1,0:T(2,128)} %param.12) | copy-start | bytes 52
  12.9 13.9 %copy-start.9 = (f32[2,2]{1,0:T(2,128)S(1)}, f32[2,2]{1,0:T(2,128)}, u32[]{:S(2)}) copy-start(f32[2,2]{1,0:T(2,128)} %param.11) | copy-start | bytes 52
  12.9 16.7 %copy-start.11 = (f32[2]{0:T(128)S(1)}, f32[2]{0:T(128)}, u32[]{:S(2)}) copy-start(f32[2]{0:T(128)} %param.13) | copy-start | bytes 28
  18.0 14.2 %collective-permute-start.3 = (bf16[128,1024]{1,0:T(8,128)(2,1)S(1)}, bf16[128,1024]{1,0:T(8,128)(2,1)S(1)}, u32[]{:S(2)}, u32[]{:S(2)}) collective-permute-start(bf16[128,1024]{1,0:T(8,128)(2,1)S(1)} %bitcast.27), channel_id=1, source_target_pairs={{0,8},{4,12},{8,0},{12,4},{1,9},{5,13},{9,1},{13,5},{2,10},{6,14},... | collective-permute-start | bytes 786440 | tf_op jit(solution)/shard_map/ppermute | solution.py:426
  19.4 12.8 %collective-permute-start.5 = (bf16[128,1024]{1,0:T(8,128)(2,1)S(1)}, bf16[128,1024]{1,0:T(8,128)(2,1)S(1)}, u32[]{:S(2)}, u32[]{:S(2)}) collective-permute-start(bf16[128,1024]{1,0:T(8,128)(2,1)S(1)} %collective-permute-done.refs_2_.refs_4_), channel_id=1, source_target_pairs={{0,2},{2,0},{1,3},{3,1},{4,6},{6,4},{5,7},{7,5},{8,10},{10,8},{9,1... | collective-permute-start | bytes 786440 | tf_op jit(solution)/shard_map/ppermute | solution.py:456
  20.9 11.7 %collective-permute-start.6 = (bf16[128,1024]{1,0:T(8,128)(2,1)S(1)}, bf16[128,1024]{1,0:T(8,128)(2,1)S(1)}, u32[]{:S(2)}, u32[]{:S(2)}) collective-permute-start(bf16[128,1024]{1,0:T(8,128)(2,1)S(1)} %collective-permute-done.1.refs_3_.refs_4_.refs_6_), channel_id=1, source_target_pairs={{0,2},{2,0},{1,3},{3,1},{4,6},{6,4},{5,7},{7,5},{8,10},{10,8},{9,1... | collective-permute-start | bytes 786440 | tf_op jit(solution)/shard_map/ppermute | solution.py:456
  32.6 6.8 %collective-permute-start.7 = (bf16[128,1024]{1,0:T(8,128)(2,1)S(1)}, bf16[128,1024]{1,0:T(8,128)(2,1)}, u32[]{:S(2)}, u32[]{:S(2)}) collective-permute-start(bf16[128,1024]{1,0:T(8,128)(2,1)S(1)} %collective-permute-done.3.refs_0_.refs_6_.refs_8_), channel_id=1, source_target_pairs={{0,2},{2,0},{1,3},{3,1},{4,6},{6,4},{5,7},{7,5},{8,10},{10,8},{9,1... | collective-permute-start | bytes 786440 | tf_op jit(solution)/shard_map/ppermute | solution.py:456
  38.1 0.9 copy-start.2
  39.4 59.8 %collective-permute-start.24 = (bf16[7,128,1024]{2,1,0:T(8,128)(2,1)}, bf16[7,128,1024]{2,1,0:T(8,128)(2,1)}, u32[]{:S(2)}, u32[]{:S(2)}) collective-permute-start(bf16[7,128,1024]{2,1,0:T(8,128)(2,1)} %shard_map.97), channel_id=1, source_target_pairs={{0,1},{1,0},{2,3},{3,2},{4,5},{5,4},{6,7},{7,6},{8,9},{9,8},{10,11... | collective-permute-start | bytes 5505032 | tf_op jit(solution)/shard_map/ppermute | solution.py:425
  39.5 16.1 %copy-start.3 = (f32[128,1024]{1,0:T(8,128)S(1)}, f32[128,1024]{1,0:T(8,128)}, u32[]{:S(2)}) copy-start(f32[128,1024]{1,0:T(8,128)} %copy-done.2) | copy-start | bytes 1572868
  44.7 4.6 %collective-permute-start.10 = (f32[2,8,128]{2,1,0:T(8,128)S(1)}, f32[2,8,128]{2,1,0:T(8,128)S(1)}, u32[]{:S(2)}, u32[]{:S(2)}) collective-permute-start(f32[2,8,128]{2,1,0:T(8,128)S(1)} %get-tuple-element.94.refs_0_), channel_id=1, source_target_pairs={{0,6},{2,4},{4,2},{6,0},{8,14},{10,12},{12,10},{14,8},{1,7},{3,5},... | collective-permute-start | bytes 24584 | tf_op jit(solution)/shard_map/ppermute | solution.py:503
  46.7 3.7 %collective-permute-start.8 = (f32[2,8,128]{2,1,0:T(8,128)S(1)}, f32[2,8,128]{2,1,0:T(8,128)S(1)}, u32[]{:S(2)}, u32[]{:S(2)}) collective-permute-start(f32[2,8,128]{2,1,0:T(8,128)S(1)} %get-tuple-element.94.refs_0_), channel_id=1, source_target_pairs={{0,2},{2,0},{1,3},{3,1},{4,6},{6,4},{5,7},{7,5},{8,10},{10,8},{9,1... | collective-permute-start | bytes 24584 | tf_op jit(solution)/shard_map/ppermute | solution.py:456
  47.3 3.7 %collective-permute-start.9 = (f32[2,8,128]{2,1,0:T(8,128)S(1)}, f32[2,8,128]{2,1,0:T(8,128)S(1)}, u32[]{:S(2)}, u32[]{:S(2)}) collective-permute-start(f32[2,8,128]{2,1,0:T(8,128)S(1)} %get-tuple-element.94.refs_0_), channel_id=1, source_target_pairs={{0,4},{4,0},{8,12},{12,8},{1,5},{5,1},{9,13},{13,9},{2,6},{6,2},{1... | collective-permute-start | bytes 24584 | tf_op jit(solution)/shard_map/ppermute | solution.py:426
  50.9 4.6 %collective-permute-start.11 = (f32[8,256]{1,0:T(8,128)S(1)}, f32[8,256]{1,0:T(8,128)S(1)}, u32[]{:S(2)}, u32[]{:S(2)}) collective-permute-start(f32[8,256]{1,0:T(8,128)S(1)} %shard_map.99.refs_4_), channel_id=1, source_target_pairs={{0,8},{8,0},{4,12},{12,4},{1,9},{9,1},{5,13},{13,5},{2,10},{10,2},... | collective-permute-start | bytes 24584 | tf_op jit(solution)/shard_map/ppermute | solution.py:426
  59.4 0.7 copy-start.6
  60.1 6.7 %collective-permute-start.12 = (bf16[1024,128]{1,0:T(8,128)(2,1)}, bf16[1024,128]{1,0:T(8,128)(2,1)}, u32[]{:S(2)}, u32[]{:S(2)}) collective-permute-start(bf16[1024,128]{1,0:T(8,128)(2,1)} %get-tuple-element.95), channel_id=1, source_target_pairs={{0,2},{2,0},{1,3},{3,1},{4,6},{6,4},{5,7},{7,5},{8,10},{10,8},{9,1... | collective-permute-start | bytes 786440 | tf_op jit(solution)/shard_map/ppermute | solution.py:516
  61.6 14.9 %collective-permute-start.17 = (bf16[1,128,1024]{2,1,0:T(8,128)(2,1)}, bf16[1,128,1024]{2,1,0:T(8,128)(2,1)}, u32[]{:S(2)}, u32[]{:S(2)}) collective-permute-start(bf16[1,128,1024]{2,1,0:T(8,128)(2,1)} %bitcast.15), channel_id=1, source_target_pairs={{0,1},{1,0},{2,3},{3,2},{4,5},{5,4},{6,7},{7,6},{8,9},{9,8},{10,11... | collective-permute-start | bytes 786440 | tf_op jit(solution)/shard_map/ppermute | solution.py:425
  61.6 14.9 %collective-permute-start.15 = (bf16[2,128,512]{2,1,0:T(8,128)(2,1)}, bf16[2,128,512]{2,1,0:T(8,128)(2,1)}, u32[]{:S(2)}, u32[]{:S(2)}) collective-permute-start(bf16[2,128,512]{2,1,0:T(8,128)(2,1)} %get-tuple-element.105), channel_id=1, source_target_pairs={{0,1},{1,0},{2,3},{3,2},{4,5},{5,4},{6,7},{7,6},{8,9},{9,8},{10,11... | collective-permute-start | bytes 786440 | tf_op jit(solution)/shard_map/ppermute | solution.py:425
  62.1 9.9 %collective-permute-start.16 = (f32[1,128]{1,0:T(1,128)S(1)}, f32[1,128]{1,0:T(1,128)S(1)}, u32[]{:S(2)}, u32[]{:S(2)}) collective-permute-start(f32[1,128]{1,0:T(1,128)S(1)} %get-tuple-element.106), channel_id=1, source_target_pairs={{0,1},{1,0},{2,3},{3,2},{4,5},{5,4},{6,7},{7,6},{8,9},{9,8},{10,11... | collective-permute-start | bytes 1544 | tf_op jit(solution)/shard_map/ppermute | solution.py:425
  68.5 8.1 %collective-permute-start.14 = (bf16[1024,128]{1,0:T(8,128)(2,1)}, bf16[1024,128]{1,0:T(8,128)(2,1)}, u32[]{:S(2)}, u32[]{:S(2)}) collective-permute-start(bf16[1024,128]{1,0:T(8,128)(2,1)} %shard_map.102), channel_id=1, source_target_pairs={{0,4},{12,8},{1,5},{13,9},{2,6},{14,10},{3,7},{15,11},{16,20},{28,... | collective-permute-start | bytes 786440 | tf_op jit(solution)/shard_map/ppermute | solution.py:426
  72.0 7.1 %collective-permute-start.13 = (bf16[1024,128]{1,0:T(8,128)(2,1)}, bf16[1024,128]{1,0:T(8,128)(2,1)}, u32[]{:S(2)}, u32[]{:S(2)}) collective-permute-start(bf16[1024,128]{1,0:T(8,128)(2,1)} %get-tuple-element.100), channel_id=1, source_target_pairs={{0,2},{2,0},{1,3},{3,1},{4,6},{6,4},{5,7},{7,5},{8,10},{10,8},{9,1... | collective-permute-start | bytes 786440 | tf_op jit(solution)/shard_map/ppermute | solution.py:516
  76.5 8.3 %copy-start.4 = (f32[1024,128]{1,0:T(8,128)}, f32[1024,128]{1,0:T(8,128)S(1)}, u32[]{:S(2)}) copy-start(f32[1024,128]{1,0:T(8,128)S(1)} %get-tuple-element.116.kept) | copy-start | bytes 1572868
  80.8 8.0 %collective-permute-start.20 = (bf16[1024,128]{1,0:T(8,128)(2,1)}, bf16[1024,128]{1,0:T(8,128)(2,1)}, u32[]{:S(2)}, u32[]{:S(2)}) collective-permute-start(bf16[1024,128]{1,0:T(8,128)(2,1)} %shard_map.105), channel_id=1, source_target_pairs={{0,4},{12,8},{1,5},{13,9},{2,6},{14,10},{3,7},{15,11},{16,20},{28,... | collective-permute-start | bytes 786440 | tf_op jit(solution)/shard_map/ppermute | solution.py:426
  84.8 4.0 %collective-permute-start.19 = (bf16[1024,128]{1,0:T(8,128)(2,1)}, bf16[1024,128]{1,0:T(8,128)(2,1)S(1)}, u32[]{:S(2)}, u32[]{:S(2)}) collective-permute-start(bf16[1024,128]{1,0:T(8,128)(2,1)} %shard_map.104), channel_id=1, source_target_pairs={{4,8},{8,4},{5,9},{9,5},{6,10},{10,6},{7,11},{11,7},{20,24},{24,20... | collective-permute-start | bytes 786440 | tf_op jit(solution)/shard_map/ppermute | solution.py:426
  85.5 6.6 %collective-permute-start.18 = (bf16[1024,128]{1,0:T(8,128)(2,1)}, bf16[1024,128]{1,0:T(8,128)(2,1)S(1)}, u32[]{:S(2)}, u32[]{:S(2)}) collective-permute-start(bf16[1024,128]{1,0:T(8,128)(2,1)} %get-tuple-element.108), channel_id=1, source_target_pairs={{0,2},{2,0},{1,3},{3,1},{4,6},{6,4},{5,7},{7,5},{8,10},{10,8},{9,1... | collective-permute-start | bytes 786440 | tf_op jit(solution)/shard_map/ppermute | solution.py:516
  86.5 5.7 %copy-start.5 = (f32[1024,128]{1,0:T(8,128)S(1)}, f32[1024,128]{1,0:T(8,128)}, u32[]{:S(2)}) copy-start(f32[1024,128]{1,0:T(8,128)} %copy-done.4) | copy-start | bytes 1572868
  86.5 12.7 %copy-start.7 = (bf16[2,128,512]{2,1,0:T(8,128)(2,1)S(1)}, bf16[2,128,512]{2,1,0:T(8,128)(2,1)}, u32[]{:S(2)}) copy-start(bf16[2,128,512]{2,1,0:T(8,128)(2,1)} %copy-done.6) | copy-start | bytes 786436
  93.3 11.5 %collective-permute-start.23 = (bf16[1024,128]{1,0:T(8,128)(2,1)S(1)}, bf16[1024,128]{1,0:T(8,128)(2,1)S(1)}, u32[]{:S(2)}, u32[]{:S(2)}) collective-permute-start(bf16[1024,128]{1,0:T(8,128)(2,1)S(1)} %shard_map.108), channel_id=1, source_target_pairs={{4,8},{8,4},{5,9},{9,5},{6,10},{10,6},{7,11},{11,7},{20,24},{24,20... | collective-permute-start | bytes 786440 | tf_op jit(solution)/shard_map/ppermute | solution.py:426
  94.0 10.9 %collective-permute-start.22 = (bf16[1024,128]{1,0:T(8,128)(2,1)S(1)}, bf16[1024,128]{1,0:T(8,128)(2,1)S(1)}, u32[]{:S(2)}, u32[]{:S(2)}) collective-permute-start(bf16[1024,128]{1,0:T(8,128)(2,1)S(1)} %shard_map.107), channel_id=1, source_target_pairs={{0,4},{4,0},{8,12},{12,8},{1,5},{5,1},{9,13},{13,9},{2,6},{6,2},{1... | collective-permute-start | bytes 786440 | tf_op jit(solution)/shard_map/ppermute | solution.py:426
  97.8 7.1 %collective-permute-start.21 = (bf16[1024,128]{1,0:T(8,128)(2,1)S(1)}, bf16[1024,128]{1,0:T(8,128)(2,1)S(1)}, u32[]{:S(2)}, u32[]{:S(2)}) collective-permute-start(bf16[1024,128]{1,0:T(8,128)(2,1)S(1)} %get-tuple-element.115), channel_id=1, source_target_pairs={{0,2},{2,0},{1,3},{3,1},{4,6},{6,4},{5,7},{7,5},{8,10},{10,8},{9,1... | collective-permute-start | bytes 786440 | tf_op jit(solution)/shard_map/ppermute | solution.py:516

commit v11 on v10

--- a/solution.py
+++ b/solution.py
@@ -359,13 +359,15 @@
     )(kept, *arrived)
 
 
-def head_kernel(slots_here, near_keys, far_keys, part, has_out, meta, *refs):
+def head_kernel(slots_here, keys_of, part, meta, *refs):
     refs = list(refs)
     grads = [refs.pop(0), refs.pop(0)]
-    near = {k: refs.pop(0) for k in near_keys}
-    stacks = [refs.pop(0) for _ in far_keys]
-    far = {k: stack.at[i] for stack, keys in zip(stacks, far_keys) for i, k in enumerate(keys)}
-    out, ready, sems = refs[has_out:]
+    near, far = {}, {}
+    for chunks in (near, far):
+        for keys in keys_of:
+            stack = refs.pop(0)
+            chunks.update((k, stack.at[i]) for i, k in enumerate(keys))
+    out, ready, sems = refs
     n_blocks, rows, columns = grads[0].shape
     right = jnp.concatenate([g[...].reshape(n_blocks * rows, columns) for g in grads])
     copies = []
@@ -382,27 +384,24 @@
         copy.wait()
 
 
-def head_call(slots_here, near, far, grads, meta, out=None):
+def head_call(keys_of, near, far, grads, meta):
     n_blocks, rows, columns = grads[0].shape
-    n_parts = len(near) // n_blocks
-    part = near[0, 0].shape[1]
-    near = {k: c for k, c in near.items() if k[1] in slots_here}
-    far = [(keys, stack) for keys, stack in far if any(k[1] in slots_here for k in keys)]
-    operands = list(grads) + list(near.values()) + [stack for _, stack in far]
-    here = [] if out is None else [out]
-    return pl.pallas_call(
-        functools.partial(head_kernel, slots_here, list(near), [keys for keys, _ in far], part, len(here)),
+    n_parts = sum(len(keys) for keys in keys_of) // n_blocks
+    part = near[0].shape[2]
+    slots_here = list(range(n_parts))
+    operands = list(grads) + list(near) + list(far)
+    return pl.pallas_call(
+        functools.partial(head_kernel, slots_here, keys_of, part),
         out_shape=shape_of((n_parts * part, columns), BF16),
-        in_specs=[IN_SMEM] + [IN_VMEM] * len(operands) + [IN_PLACE] * len(here),
+        in_specs=[IN_SMEM] + [IN_VMEM] * len(operands),
         out_specs=IN_PLACE,
         scratch_shapes=[pltpu.VMEM((2, part, columns), BF16), pltpu.SemaphoreType.DMA((2,))],
-        input_output_aliases={1 + len(operands): 0} if here else {},
-        compiler_params=pltpu.CompilerParams(vmem_limit_bytes=16 * 1024 * 1024),
+        compiler_params=params(),
         cost_estimate=cost(
-            4 * n_blocks * rows * len(slots_here) * part * columns,
-            4 * n_blocks * len(slots_here) * rows * part + 2 * len(slots_here) * part * columns,
+            4 * n_blocks * rows * n_parts * part * columns,
+            4 * n_blocks * n_parts * rows * part + 2 * n_parts * part * columns,
         ),
-    )(meta, *operands, *here)
+    )(meta, *operands)
 
 
 def together(*groups):
@@ -511,7 +510,8 @@
         logits, wanted, all_stats, small, work, meta_grads, part, width, window
     )
     theirs, far_loss = dp_swap(grads_far), dp_swap(loss)
-    far_late = dp_swap(jnp.stack(together([chunk[k] for k in late], [kept])[0]))
+    near_late = jnp.stack(together([chunk[k] for k in late], [kept])[0])
+    far_late = dp_swap(near_late)
 
     back = lambda cs: [lax.ppermute(c, "ctx", ring(n_ctx, -t)) for t, c in zip(beyond, cs)]
     shares = {final: (kept, list(send))}
@@ -545,7 +545,7 @@
         if i:
             beside = more_shares([i - 1])
         else:
-            grad_head = head_call(list(range(n_voc)), chunk, [(soon, far_soon), (late, far_late)], [grads_own, theirs], meta)
+            grad_head = head_call([soon, late], [stacked, near_late], [far_soon, far_late], [grads_own, theirs], meta)
             beside = [grad_head]
         swapped = [theirs, far_loss, far_late] if i == final - 1 else []
         over[i], came, beside, swapped = together(over[i], came, beside, swapped)

time: 106 us -> 107 us (level)
  starting transfers between devices: 34.3 us -> 31.3 us
  local copies, waits for them, and re-layouts: 5.55 us -> 7.33 us
  waiting for transfers between devices: 19.1 us -> 20.3 us
    ppermute x10, starting transfers between devices: 20.8 us -> 18.9 us  [shards(): along = lambda a, by: lax.ppermute(a, 'vocab', by)]
    unnamed x24 -> x28, local copies, waits for them, and re-layouts: 3.76 us -> 5.54 us
    ppermute x4, starting transfers between devices: 4.84 us -> 3.41 us  [shards(): lax.ppermute(c, 'ctx', ring(n_ctx, -t))]
    ppermute x10, waiting for transfers between devices: 8.69 us -> 9.88 us  [shards(): along = lambda a, by: lax.ppermute(a, 'vocab', by)]
  transfers between devices with their start and end apart: 25 -> 25, of which waited for: 12 -> 11; matrix products, arithmetic and copies ran while one was open for 5% -> 5% of each run, Pallas kernels for 38% -> 38%
where the time goes in v11:
time: 107 us; the launch traced here: 106 us
  Pallas kernels  41.4 us (39%)
  starting transfers between devices  31.3 us (29%)
  waiting for transfers between devices  20.3 us (19%)
  local copies, waits for them, and re-layouts  7.33 us (7%)
  other arithmetic  3.4 us (3%)
  between operations  2.29 us (2%)
    ppermute x10, starting transfers between devices, shards(): along = lambda a, by: lax.ppermute(a, 'vocab', by)  18.9 us
    pallas_call x3, Pallas kernels, logits_call(): pl.pallas_call(functools.partial(logits_kernel, kernel_plan, columns, par...  13.2 us
    ppermute x10, waiting for transfers between devices, shards(): along = lambda a, by: lax.ppermute(a, 'vocab', by)  9.88 us
    ppermute x4, waiting for transfers between devices, shards(): lax.ppermute(c, 'ctx', ring(n_ctx, -t))  8.56 us
    pallas_call x3, Pallas kernels, spread_call(): pl.pallas_call(functools.partial(spread_kernel, part, width, n_parts), ou...  8.29 us
    pallas_call x6, Pallas kernels, add_call(): pl.pallas_call(functools.partial(add_kernel, turned), out_shape=shape_of(...  7.3 us
    ppermute x5, starting transfers between devices, shards(): cross = lambda a: [lax.ppermute(a, 'ctx', ring(n_ctx, t)) for t in beyond]  6.5 us
    pallas_call x1, Pallas kernels, head_call(): pl.pallas_call(functools.partial(head_kernel, slots_here, keys_of, part),...  5.72 us
  transfers between devices with their start and end apart: 25, of which 11 were waited for; matrix products, arithmetic and copies ran while one was open for 5% of the time, Pallas kernels for 38%

profile of v11, /device:TPU:0, one launch (start us, length us, event | category | flops | bytes accessed | tf_op | source)
XLA Modules:
  0.0 106.1 jit_solution(7726663929562483185)
XLA Ops:
  0.6 0.5 collective-permute-start.4
  1.1 2.6 %collective-permute-start = (bf16[128,1024]{1,0:T(8,128)(2,1)}, bf16[128,1024]{1,0:T(8,128)(2,1)S(1)}, u32[]{:S(2)}, u32[]{:S(2)}) collective-permute-start(bf16[128,1024]{1,0:T(8,128)(2,1)} %bitcast.24), channel_id=1, source_target_pairs={{0,4},{4,8},{8,12},{12,0},{1,5},{5,9},{9,13},{13,1},{2,6},{6,10},{... | collective-permute-start | bytes 786440 | tf_op jit(solution)/shard_map/ppermute | solution.py:425
  3.8 2.1 %collective-permute-start.1 = (bf16[128,1024]{1,0:T(8,128)(2,1)}, bf16[128,1024]{1,0:T(8,128)(2,1)S(1)}, u32[]{:S(2)}, u32[]{:S(2)}) collective-permute-start(bf16[128,1024]{1,0:T(8,128)(2,1)} %bitcast.25), channel_id=1, source_target_pairs={{0,12},{4,0},{8,4},{12,8},{1,13},{5,1},{9,5},{13,9},{2,14},{6,2},{... | collective-permute-start | bytes 786440 | tf_op jit(solution)/shard_map/ppermute | solution.py:425
  5.9 1.6 %collective-permute-start.2 = (bf16[128,1024]{1,0:T(8,128)(2,1)}, bf16[128,1024]{1,0:T(8,128)(2,1)S(1)}, u32[]{:S(2)}, u32[]{:S(2)}) collective-permute-start(bf16[128,1024]{1,0:T(8,128)(2,1)} %bitcast.26), channel_id=1, source_target_pairs={{0,2},{2,0},{1,3},{3,1},{4,6},{6,4},{5,7},{7,5},{8,10},{10,8},{9,1... | collective-permute-start | bytes 786440 | tf_op jit(solution)/shard_map/ppermute | solution.py:455
  7.5 0.8 select_reduce_fusion
  8.3 2.2 %copy-done = bf16[4096,512]{1,0:T(8,128)(2,1)S(1)} copy-done((bf16[4096,512]{1,0:T(8,128)(2,1)S(1)}, bf16[4096,512]{1,0:T(8,128)(2,1)}, u32[]{:S(2)}) %copy-start) | copy-done | bytes 4194328
  10.5 2.0 %shard_map.94.work = bf16[53248,512]{1,0:T(8,128)(2,1)} custom-call(bf16[4096,512]{1,0:T(8,128)(2,1)S(1)} %copy-done), custom_call_target="tpu_custom_call" | custom-call | flops 1 | bytes 8388608 | tf_op jit(solution)/shard_map/pallas_call | solution.py:52
  12.7 0.1 add.104
  12.9 0.3 collective-permute-done.refs_2_
  13.2 4.8 %collective-permute-done.1.refs_3_.refs_4_ = bf16[128,1024]{1,0:T(8,128)(2,1)S(1)} collective-permute-done((bf16[128,1024]{1,0:T(8,128)(2,1)}, bf16[128,1024]{1,0:T(8,128)(2,1)S(1)}, u32[]{:S(2)}, u32[]{:S(2)}) %collective-permute-start.1) | collective-permute-done | bytes 262176 | tf_op jit(solution)/shard_map/ppermute | solution.py:425
  18.0 1.4 %collective-permute-start.3 = (bf16[128,1024]{1,0:T(8,128)(2,1)S(1)}, bf16[128,1024]{1,0:T(8,128)(2,1)}, u32[]{:S(2)}, u32[]{:S(2)}) collective-permute-start(bf16[128,1024]{1,0:T(8,128)(2,1)S(1)} %bitcast.27), channel_id=1, source_target_pairs={{0,8},{4,12},{8,0},{12,4},{1,9},{5,13},{9,1},{13,5},{2,10},{6,14},... | collective-permute-start | bytes 786440 | tf_op jit(solution)/shard_map/ppermute | solution.py:425
  19.4 1.5 %collective-permute-start.5 = (bf16[128,1024]{1,0:T(8,128)(2,1)S(1)}, bf16[128,1024]{1,0:T(8,128)(2,1)S(1)}, u32[]{:S(2)}, u32[]{:S(2)}) collective-permute-start(bf16[128,1024]{1,0:T(8,128)(2,1)S(1)} %collective-permute-done.refs_2_), channel_id=1, source_target_pairs={{0,2},{2,0},{1,3},{3,1},{4,6},{6,4},{5,7},{7,5},{8,10},{10,8},{9,1... | collective-permute-start | bytes 786440 | tf_op jit(solution)/shard_map/ppermute | solution.py:455
  20.9 0.5 collective-permute-start.6
  21.4 4.8 %shard_map.95 = (f32[128,1024]{1,0:T(8,128)S(1)}, bf16[53248,512]{1,0:T(8,128)(2,1)}) custom-call(s32[6]{0:T(128)S(1)} %stack.60.meta, bf16[53248,512]{1,0:T(8,128)(2,1)} %shard_map.94.work, bf16[4096,512]{1,0:T(8,128)(2,1)} %collective-permute-done.4.refs_0_, bf16[128,1024]{1,0:T(8,128)(2,1)S(1)} %bitcast.28, ...), custom_call_target="tpu_custom_call", output_to_operand_aliasing={{1}: (1, {})} | custom-call | flops 805306368 | bytes 6291456 | tf_op jit(solution)/shard_map/pallas_call | solution.py:153
  26.2 0.8 copy-done.4
  27.0 0.6 select_reduce_fusion.3
  27.7 0.1 select_reduce_fusion.1
  27.7 0.6 fusion
  29.6 0.7 stack.66.meta
  30.4 0.6 select_reduce_fusion.4
  31.0 0.7 pad_maximum_fusion.small
  31.7 0.6 collective-permute-done.3.refs_0_.refs_6_
  32.3 0.3 collective-permute-done.6.refs_5_.refs_3_
  32.6 1.4 %collective-permute-start.7 = (bf16[128,1024]{1,0:T(8,128)(2,1)}, bf16[128,1024]{1,0:T(8,128)(2,1)}, u32[]{:S(2)}, u32[]{:S(2)}) collective-permute-start(bf16[128,1024]{1,0:T(8,128)(2,1)} %collective-permute-done.3.refs_0_.refs_6_), channel_id=1, source_target_pairs={{0,2},{2,0},{1,3},{3,1},{4,6},{6,4},{5,7},{7,5},{8,10},{10,8},{9,1... | collective-permute-start | bytes 786440 | tf_op jit(solution)/shard_map/ppermute | solution.py:455
  33.9 1.1 %shard_map.97.refs_2_ = bf16[7,128,1024]{2,1,0:T(8,128)(2,1)S(1)} custom-call(bf16[128,1024]{1,0:T(8,128)(2,1)S(1)} %bitcast.29, bf16[128,1024]{1,0:T(8,128)(2,1)S(1)} %collective-permute-done.2.refs_1_.refs_0_, bf16[128,1024]{1,0:T(8,128)(2,1)S(1)} %collective-permute-done.refs_2_, bf16[128,1024]{1,0:T(8,128)(2,1)S(1)} %collective-permute-done.5.refs_3_.refs_1_, ...), custom_call_target="tpu_custom_call" | custom-call | flops 1 | bytes 3670016 | tf_op jit(solution)/shard_map/pallas_call | solution.py:305
  35.1 0.1 copy.11.refs_2_
  35.2 1.0 copy-done.5
  36.2 3.2 %shard_map.96 = (f32[128,1024]{1,0:T(8,128)S(1)}, f32[1,8,128]{2,1,0:T(8,128)S(1)}) custom-call(s32[6]{0:T(128)S(1)} %stack.60.meta, bf16[53248,512]{1,0:T(8,128)(2,1)} %get-tuple-element.80.work, bf16[128,1024]{1,0:T(8,128)(2,1)} %collective-permute-done.3.refs_0_.refs_6_, f32[128,1024]{1,0:T(8,128)S(1)} %copy-done.5, s32[128,1]{1,0:T(8,128)S(1)} %copy.11.refs_2_), custom_call_target="tpu_custom_call" | custom-call | flops 268435456 | bytes 2097152 | tf_op jit(solution)/shard_map/pallas_call | solution.py:153
  39.5 0.8 copy-done.2
  40.2 0.1 copy.12.refs_4_.refs_3_
  40.4 5.2 %shard_map.98 = (f32[128,1024]{1,0:T(8,128)S(1)}, f32[2,8,128]{2,1,0:T(8,128)S(1)}) custom-call(s32[6]{0:T(128)S(1)} %stack.60.meta, bf16[53248,512]{1,0:T(8,128)(2,1)} %get-tuple-element.80.work, bf16[128,1024]{1,0:T(8,128)(2,1)S(1)} %collective-permute-done.2.refs_1_.refs_0_, bf16[128,1024]{1,0:T(8,128)(2,1)S(1)} %collective-permute-done.5.refs_3_.refs_1_, ...), custom_call_target="tpu_custom_call" | custom-call | flops 1073741824 | bytes 8388608 | tf_op jit(solution)/shard_map/pallas_call | solution.py:153
  45.6 1.5 %collective-permute-start.10 = (f32[2,8,128]{2,1,0:T(8,128)S(1)}, f32[2,8,128]{2,1,0:T(8,128)S(1)}, u32[]{:S(2)}, u32[]{:S(2)}) collective-permute-start(f32[2,8,128]{2,1,0:T(8,128)S(1)} %get-tuple-element.94.refs_0_), channel_id=1, source_target_pairs={{0,6},{2,4},{4,2},{6,0},{8,14},{10,12},{12,10},{14,8},{1,7},{3,5},... | collective-permute-start | bytes 24584 | tf_op jit(solution)/shard_map/ppermute | solution.py:502
  47.0 1.5 %collective-permute-start.8 = (f32[2,8,128]{2,1,0:T(8,128)S(1)}, f32[2,8,128]{2,1,0:T(8,128)S(1)}, u32[]{:S(2)}, u32[]{:S(2)}) collective-permute-start(f32[2,8,128]{2,1,0:T(8,128)S(1)} %get-tuple-element.94.refs_0_), channel_id=1, source_target_pairs={{0,2},{2,0},{1,3},{3,1},{4,6},{6,4},{5,7},{7,5},{8,10},{10,8},{9,1... | collective-permute-start | bytes 24584 | tf_op jit(solution)/shard_map/ppermute | solution.py:455
  48.5 0.6 collective-permute-start.9
  49.1 1.1 collective-permute-done.10.refs_3_
  50.2 0.5 collective-permute-done.8.refs_1_
  50.7 1.5 %collective-permute-done.9.refs_2_ = f32[2,8,128]{2,1,0:T(8,128)S(1)} collective-permute-done((f32[2,8,128]{2,1,0:T(8,128)S(1)}, f32[2,8,128]{2,1,0:T(8,128)S(1)}, u32[]{:S(2)}, u32[]{:S(2)}) %collective-permute-start.9) | collective-permute-done | bytes 8224 | tf_op jit(solution)/shard_map/ppermute | solution.py:425
  52.2 1.9 %collective-permute-start.11 = (f32[8,256]{1,0:T(8,128)S(1)}, f32[8,256]{1,0:T(8,128)S(1)}, u32[]{:S(2)}, u32[]{:S(2)}) collective-permute-start(f32[8,256]{1,0:T(8,128)S(1)} %shard_map.99.refs_4_), channel_id=1, source_target_pairs={{0,8},{8,0},{4,12},{12,4},{1,9},{9,1},{5,13},{13,5},{2,10},{10,2},... | collective-permute-start | bytes 24584 | tf_op jit(solution)/shard_map/ppermute | solution.py:425
  54.2 2.7 %collective-permute-done.11.refs_5_ = f32[8,256]{1,0:T(8,128)S(1)} collective-permute-done((f32[8,256]{1,0:T(8,128)S(1)}, f32[8,256]{1,0:T(8,128)S(1)}, u32[]{:S(2)}, u32[]{:S(2)}) %collective-permute-start.11) | collective-permute-done | bytes 8224 | tf_op jit(solution)/shard_map/ppermute | solution.py:425
  56.8 3.8 %shard_map.100 = (bf16[2,128,512]{2,1,0:T(8,128)(2,1)S(1)}, bf16[2,128,512]{2,1,0:T(8,128)(2,1)}, bf16[512,256]{1,0:T(8,128)(2,1)S(1)}, bf16[512,256]{1,0:T(8,12...) custom-call(s32[5]{0:T(128)S(1)} %stack.66.meta, ...), custom_call_target="tpu_custom_call" | custom-call | flops 536870912 | bytes 4194304 | tf_op jit(solution)/shard_map/pallas_call | solution.py:252
  60.6 0.7 copy-done.8
  61.3 0.6 collective-permute-start.12
  61.9 0.5 collective-permute-start.15
  62.4 3.0 %shard_map.101 = (f32[1024,128]{1,0:T(8,128)S(1)}, bf16[1024,128]{1,0:T(8,128)(2,1)}) custom-call(s32[1]{0:T(128)} %bitcast.13.meta, bf16[53248,512]{1,0:T(8,128)(2,1)} %get-tuple-element.80.work, bf16[512,256]{1,0:T(8,128)(2,1)S(1)} %get-tuple-element.96.flipped_own, bf16[512,256]{1,0:T(8,128)(2,1)S(1)} %get-tuple-element.97.flipped_far), custom_call_target="tpu_custom_call" | custom-call | flops 536870912 | bytes 2097152 | tf_op jit(solution)/shard_map/pallas_call | solution.py:267
  65.4 2.6 %collective-permute-done.12.refs_0_ = bf16[1024,128]{1,0:T(8,128)(2,1)} collective-permute-done((bf16[1024,128]{1,0:T(8,128)(2,1)}, bf16[1024,128]{1,0:T(8,128)(2,1)}, u32[]{:S(2)}, u32[]{:S(2)}) %collective-permute-start.12) | collective-permute-done | bytes 262176 | tf_op jit(solution)/shard_map/ppermute | solution.py:516
  68.0 1.7 %shard_map.102 = bf16[1024,128]{1,0:T(8,128)(2,1)} custom-call(f32[1024,128]{1,0:T(8,128)S(1)} %get-tuple-element.101.kept, bf16[1024,128]{1,0:T(8,128)(2,1)} %collective-permute-done.12.refs_0_), custom_call_target="tpu_custom_call" | custom-call | flops 131072 | bytes 524288 | tf_op jit(solution)/shard_map/pallas_call | solution.py:352
  69.7 3.3 %collective-permute-start.14 = (bf16[1024,128]{1,0:T(8,128)(2,1)}, bf16[1024,128]{1,0:T(8,128)(2,1)}, u32[]{:S(2)}, u32[]{:S(2)}) collective-permute-start(bf16[1024,128]{1,0:T(8,128)(2,1)} %shard_map.102), channel_id=1, source_target_pairs={{0,4},{12,8},{1,5},{13,9},{2,6},{14,10},{3,7},{15,11},{16,20},{28,... | collective-permute-start | bytes 786440 | tf_op jit(solution)/shard_map/ppermute | solution.py:425
  73.0 0.9 collective-permute-start.13
  73.8 3.0 %shard_map.103 = (f32[1024,128]{1,0:T(8,128)S(1)}, bf16[1024,128]{1,0:T(8,128)(2,1)}) custom-call(s32[1]{0:T(128)} %bitcast.14.meta, bf16[53248,512]{1,0:T(8,128)(2,1)} %get-tuple-element.80.work, bf16[512,256]{1,0:T(8,128)(2,1)S(1)} %get-tuple-element.96.flipped_own, bf16[512,256]{1,0:T(8,128)(2,1)S(1)} %get-tuple-element.97.flipped_far), custom_call_target="tpu_custom_call" | custom-call | flops 536870912 | bytes 2097152 | tf_op jit(solution)/shard_map/pallas_call | solution.py:267
  76.8 2.8 %collective-permute-done.13.refs_0_ = bf16[1024,128]{1,0:T(8,128)(2,1)} collective-permute-done((bf16[1024,128]{1,0:T(8,128)(2,1)}, bf16[1024,128]{1,0:T(8,128)(2,1)}, u32[]{:S(2)}, u32[]{:S(2)}) %collective-permute-start.13) | collective-permute-done | bytes 262176 | tf_op jit(solution)/shard_map/ppermute | solution.py:516
  79.7 1.7 %shard_map.105 = bf16[1024,128]{1,0:T(8,128)(2,1)} custom-call(f32[1024,128]{1,0:T(8,128)S(1)} %get-tuple-element.110.kept, bf16[1024,128]{1,0:T(8,128)(2,1)} %collective-permute-done.13.refs_0_), custom_call_target="tpu_custom_call" | custom-call | flops 131072 | bytes 524288 | tf_op jit(solution)/shard_map/pallas_call | solution.py:352
  81.4 2.0 %collective-permute-start.20 = (bf16[1024,128]{1,0:T(8,128)(2,1)}, bf16[1024,128]{1,0:T(8,128)(2,1)}, u32[]{:S(2)}, u32[]{:S(2)}) collective-permute-start(bf16[1024,128]{1,0:T(8,128)(2,1)} %shard_map.105), channel_id=1, source_target_pairs={{0,4},{12,8},{1,5},{13,9},{2,6},{14,10},{3,7},{15,11},{16,20},{28,... | collective-permute-start | bytes 786440 | tf_op jit(solution)/shard_map/ppermute | solution.py:425
  83.4 1.8 %shard_map.104 = bf16[1024,128]{1,0:T(8,128)(2,1)} custom-call(f32[1024,128]{1,0:T(8,128)S(1)} %get-tuple-element.101.kept, bf16[1024,128]{1,0:T(8,128)(2,1)} %collective-permute-done.12.refs_0_, bf16[1024,128]{1,0:T(8,128)(2,1)} %collective-permute-done.14.refs_1_), custom_call_target="tpu_custom_call" | custom-call | flops 131072 | bytes 524288 | tf_op jit(solution)/shard_map/pallas_call | solution.py:352
  85.2 0.7 collective-permute-start.19
  85.8 1.1 %collective-permute-start.18 = (bf16[1024,128]{1,0:T(8,128)(2,1)}, bf16[1024,128]{1,0:T(8,128)(2,1)S(1)}, u32[]{:S(2)}, u32[]{:S(2)}) collective-permute-start(bf16[1024,128]{1,0:T(8,128)(2,1)} %get-tuple-element.108), channel_id=1, source_target_pairs={{0,2},{2,0},{1,3},{3,1},{4,6},{6,4},{5,7},{7,5},{8,10},{10,8},{9,1... | collective-permute-start | bytes 786440 | tf_op jit(solution)/shard_map/ppermute | solution.py:516
  87.0 2.3 %shard_map.106 = (f32[1024,128]{1,0:T(8,128)S(1)}, bf16[1024,128]{1,0:T(8,128)(2,1)S(1)}) custom-call(s32[1]{0:T(128)} %bitcast.16.meta, bf16[53248,512]{1,0:T(8,128)(2,1)} %get-tuple-element.80.work, bf16[512,256]{1,0:T(8,128)(2,1)S(1)} %get-tuple-element.96.flipped_own, bf16[512,256]{1,0:T(8,128)(2,1)S(1)} %get-tuple-element.97.flipped_far), custom_call_target="tpu_custom_call" | custom-call | flops 536870912 | bytes 2097152 | tf_op jit(solution)/shard_map/pallas_call | solution.py:267
  89.4 3.1 %collective-permute-done.18.refs_0_ = bf16[1024,128]{1,0:T(8,128)(2,1)S(1)} collective-permute-done((bf16[1024,128]{1,0:T(8,128)(2,1)}, bf16[1024,128]{1,0:T(8,128)(2,1)S(1)}, u32[]{:S(2)}, u32[]{:S(2)}) %collective-permute-start.18) | collective-permute-done | bytes 262176 | tf_op jit(solution)/shard_map/ppermute | solution.py:516
  92.6 1.1 %shard_map.108 = bf16[1024,128]{1,0:T(8,128)(2,1)S(1)} custom-call(f32[1024,128]{1,0:T(8,128)S(1)} %get-tuple-element.110.kept, bf16[1024,128]{1,0:T(8,128)(2,1)} %collective-permute-done.13.refs_0_, bf16[1024,128]{1,0:T(8,128)(2,1)} %collective-permute-done.20.refs_1_), custom_call_target="tpu_custom_call" | custom-call | flops 131072 | bytes 524288 | tf_op jit(solution)/shard_map/pallas_call | solution.py:352
  93.7 0.7 collective-permute-start.23
  94.4 3.7 %collective-permute-start.22 = (bf16[1024,128]{1,0:T(8,128)(2,1)S(1)}, bf16[1024,128]{1,0:T(8,128)(2,1)S(1)}, u32[]{:S(2)}, u32[]{:S(2)}) collective-permute-start(bf16[1024,128]{1,0:T(8,128)(2,1)S(1)} %shard_map.107), channel_id=1, source_target_pairs={{0,4},{4,0},{8,12},{12,8},{1,5},{5,1},{9,13},{13,9},{2,6},{6,2},{1... | collective-permute-start | bytes 786440 | tf_op jit(solution)/shard_map/ppermute | solution.py:425
  98.1 0.8 collective-permute-start.21
  98.9 0.5 bitcast_select_fusion
  99.4 5.7 %shard_map.109 = bf16[4096,512]{1,0:T(8,128)(2,1)} custom-call(s32[6]{0:T(128)S(1)} %stack.60.meta, bf16[2,128,512]{2,1,0:T(8,128)(2,1)S(1)} %copy-done.9, bf16[2,128,512]{2,1,0:T(8,128)(2,1)} %collective-permute-done.15.refs_1_, bf16[7,128,1024]{2,1,0:T(8,128)(2,1)S(1)} %shard_map.97.refs_2_, bf16[1,128,1024]{2,1,0:T(8,128)(2,1)} %bitcast.15.refs_3_, ...), custom_call_target="tpu_custom_call" | custom-call | flops 2147483648 | bytes 8388608 | tf_op jit(solution)/shard_map/pallas_call | solution.py:393
  105.2 0.9 shard_map.110
  (47 shorter events, 0.4 us)
Async XLA Ops:
  0.6 20.8 %collective-permute-start.4 = (bf16[4096,512]{1,0:T(8,128)(2,1)}, bf16[4096,512]{1,0:T(8,128)(2,1)}, u32[]{:S(2)}, u32[]{:S(2)}) collective-permute-start(bf16[4096,512]{1,0:T(8,128)(2,1)} %w.1), channel_id=1, source_target_pairs={{0,1},{1,0},{2,3},{3,2},{4,5},{5,4},{6,7},{7,6},{8,9},{9,8},{10,11... | collective-permute-start | bytes 12582920 | tf_op jit(solution)/shard_map/ppermute | solution.py:424
  1.1 12.1 %collective-permute-start = (bf16[128,1024]{1,0:T(8,128)(2,1)}, bf16[128,1024]{1,0:T(8,128)(2,1)S(1)}, u32[]{:S(2)}, u32[]{:S(2)}) collective-permute-start(bf16[128,1024]{1,0:T(8,128)(2,1)} %bitcast.24), channel_id=1, source_target_pairs={{0,4},{4,8},{8,12},{12,0},{1,5},{5,9},{9,13},{13,1},{2,6},{6,10},{... | collective-permute-start | bytes 786440 | tf_op jit(solution)/shard_map/ppermute | solution.py:425
  3.8 14.2 %collective-permute-start.1 = (bf16[128,1024]{1,0:T(8,128)(2,1)}, bf16[128,1024]{1,0:T(8,128)(2,1)S(1)}, u32[]{:S(2)}, u32[]{:S(2)}) collective-permute-start(bf16[128,1024]{1,0:T(8,128)(2,1)} %bitcast.25), channel_id=1, source_target_pairs={{0,12},{4,0},{8,4},{12,8},{1,13},{5,1},{9,5},{13,9},{2,14},{6,2},{... | collective-permute-start | bytes 786440 | tf_op jit(solution)/shard_map/ppermute | solution.py:425
  5.9 12.1 %collective-permute-start.2 = (bf16[128,1024]{1,0:T(8,128)(2,1)}, bf16[128,1024]{1,0:T(8,128)(2,1)S(1)}, u32[]{:S(2)}, u32[]{:S(2)}) collective-permute-start(bf16[128,1024]{1,0:T(8,128)(2,1)} %bitcast.26), channel_id=1, source_target_pairs={{0,2},{2,0},{1,3},{3,1},{4,6},{6,4},{5,7},{7,5},{8,10},{10,8},{9,1... | collective-permute-start | bytes 786440 | tf_op jit(solution)/shard_map/ppermute | solution.py:455
  8.3 2.2 %copy-start = (bf16[4096,512]{1,0:T(8,128)(2,1)S(1)}, bf16[4096,512]{1,0:T(8,128)(2,1)}, u32[]{:S(2)}) copy-start(bf16[4096,512]{1,0:T(8,128)(2,1)} %w.1) | copy-start | bytes 12582916
  10.5 7.5 %copy-start.1 = (bf16[1024,1,2,64]{0,3,2,1:T(8,128)(2,1)S(1)}, bf16[1024,1,2,64]{0,3,2,1:T(8,128)(2,1)}, u32[]{:S(2)}) copy-start(bf16[1024,1,2,64]{0,3,2,1:T(8,128)(2,1)} %param.7) | copy-start | bytes 786436
  12.9 14.1 %copy-start.12 = (s32[2]{0:T(128)S(1)}, s32[2]{0:T(128)}, u32[]{:S(2)}) copy-start(s32[2]{0:T(128)} %param.10) | copy-start | bytes 28
  12.9 14.7 %copy-start.10 = (f32[2,2]{1,0:T(2,128)S(1)}, f32[2,2]{1,0:T(2,128)}, u32[]{:S(2)}) copy-start(f32[2,2]{1,0:T(2,128)} %param.12) | copy-start | bytes 52
  12.9 14.7 %copy-start.11 = (f32[2,2]{1,0:T(2,128)S(1)}, f32[2,2]{1,0:T(2,128)}, u32[]{:S(2)}) copy-start(f32[2,2]{1,0:T(2,128)} %param.11) | copy-start | bytes 52
  12.9 17.4 %copy-start.13 = (f32[2]{0:T(128)S(1)}, f32[2]{0:T(128)}, u32[]{:S(2)}) copy-start(f32[2]{0:T(128)} %param.13) | copy-start | bytes 28
  18.0 14.3 %collective-permute-start.3 = (bf16[128,1024]{1,0:T(8,128)(2,1)S(1)}, bf16[128,1024]{1,0:T(8,128)(2,1)}, u32[]{:S(2)}, u32[]{:S(2)}) collective-permute-start(bf16[128,1024]{1,0:T(8,128)(2,1)S(1)} %bitcast.27), channel_id=1, source_target_pairs={{0,8},{4,12},{8,0},{12,4},{1,9},{5,13},{9,1},{13,5},{2,10},{6,14},... | collective-permute-start | bytes 786440 | tf_op jit(solution)/shard_map/ppermute | solution.py:425
  19.4 13.0 %collective-permute-start.5 = (bf16[128,1024]{1,0:T(8,128)(2,1)S(1)}, bf16[128,1024]{1,0:T(8,128)(2,1)S(1)}, u32[]{:S(2)}, u32[]{:S(2)}) collective-permute-start(bf16[128,1024]{1,0:T(8,128)(2,1)S(1)} %collective-permute-done.refs_2_), channel_id=1, source_target_pairs={{0,2},{2,0},{1,3},{3,1},{4,6},{6,4},{5,7},{7,5},{8,10},{10,8},{9,1... | collective-permute-start | bytes 786440 | tf_op jit(solution)/shard_map/ppermute | solution.py:455
  20.9 11.7 %collective-permute-start.6 = (bf16[128,1024]{1,0:T(8,128)(2,1)S(1)}, bf16[128,1024]{1,0:T(8,128)(2,1)S(1)}, u32[]{:S(2)}, u32[]{:S(2)}) collective-permute-start(bf16[128,1024]{1,0:T(8,128)(2,1)S(1)} %collective-permute-done.1.refs_3_.refs_4_), channel_id=1, source_target_pairs={{0,2},{2,0},{1,3},{3,1},{4,6},{6,4},{5,7},{7,5},{8,10},{10,8},{9,1... | collective-permute-start | bytes 786440 | tf_op jit(solution)/shard_map/ppermute | solution.py:455
  26.2 0.8 copy-start.4
  32.6 7.7 %collective-permute-start.7 = (bf16[128,1024]{1,0:T(8,128)(2,1)}, bf16[128,1024]{1,0:T(8,128)(2,1)}, u32[]{:S(2)}, u32[]{:S(2)}) collective-permute-start(bf16[128,1024]{1,0:T(8,128)(2,1)} %collective-permute-done.3.refs_0_.refs_6_), channel_id=1, source_target_pairs={{0,2},{2,0},{1,3},{3,1},{4,6},{6,4},{5,7},{7,5},{8,10},{10,8},{9,1... | collective-permute-start | bytes 786440 | tf_op jit(solution)/shard_map/ppermute | solution.py:455
  35.2 1.0 copy-start.5
  39.4 0.8 copy-start.2
  40.2 59.2 %collective-permute-start.24 = (bf16[7,128,1024]{2,1,0:T(8,128)(2,1)S(1)}, bf16[7,128,1024]{2,1,0:T(8,128)(2,1)}, u32[]{:S(2)}, u32[]{:S(2)}) collective-permute-start(bf16[7,128,1024]{2,1,0:T(8,128)(2,1)S(1)} %shard_map.97.refs_2_), channel_id=1, source_target_pairs={{0,1},{1,0},{2,3},{3,2},{4,5},{5,4},{6,7},{7,6},{8,9},{9,8},{10,11... | collective-permute-start | bytes 5505032 | tf_op jit(solution)/shard_map/ppermute | solution.py:424
  40.4 16.5 %copy-start.3 = (f32[128,1024]{1,0:T(8,128)S(1)}, f32[128,1024]{1,0:T(8,128)}, u32[]{:S(2)}) copy-start(f32[128,1024]{1,0:T(8,128)} %copy-done.2) | copy-start | bytes 1572868
  45.6 4.6 %collective-permute-start.10 = (f32[2,8,128]{2,1,0:T(8,128)S(1)}, f32[2,8,128]{2,1,0:T(8,128)S(1)}, u32[]{:S(2)}, u32[]{:S(2)}) collective-permute-start(f32[2,8,128]{2,1,0:T(8,128)S(1)} %get-tuple-element.94.refs_0_), channel_id=1, source_target_pairs={{0,6},{2,4},{4,2},{6,0},{8,14},{10,12},{12,10},{14,8},{1,7},{3,5},... | collective-permute-start | bytes 24584 | tf_op jit(solution)/shard_map/ppermute | solution.py:502
  47.0 3.7 %collective-permute-start.8 = (f32[2,8,128]{2,1,0:T(8,128)S(1)}, f32[2,8,128]{2,1,0:T(8,128)S(1)}, u32[]{:S(2)}, u32[]{:S(2)}) collective-permute-start(f32[2,8,128]{2,1,0:T(8,128)S(1)} %get-tuple-element.94.refs_0_), channel_id=1, source_target_pairs={{0,2},{2,0},{1,3},{3,1},{4,6},{6,4},{5,7},{7,5},{8,10},{10,8},{9,1... | collective-permute-start | bytes 24584 | tf_op jit(solution)/shard_map/ppermute | solution.py:455
  48.5 3.7 %collective-permute-start.9 = (f32[2,8,128]{2,1,0:T(8,128)S(1)}, f32[2,8,128]{2,1,0:T(8,128)S(1)}, u32[]{:S(2)}, u32[]{:S(2)}) collective-permute-start(f32[2,8,128]{2,1,0:T(8,128)S(1)} %get-tuple-element.94.refs_0_), channel_id=1, source_target_pairs={{0,4},{4,0},{8,12},{12,8},{1,5},{5,1},{9,13},{13,9},{2,6},{6,2},{1... | collective-permute-start | bytes 24584 | tf_op jit(solution)/shard_map/ppermute | solution.py:425
  52.2 4.6 %collective-permute-start.11 = (f32[8,256]{1,0:T(8,128)S(1)}, f32[8,256]{1,0:T(8,128)S(1)}, u32[]{:S(2)}, u32[]{:S(2)}) collective-permute-start(f32[8,256]{1,0:T(8,128)S(1)} %shard_map.99.refs_4_), channel_id=1, source_target_pairs={{0,8},{8,0},{4,12},{12,4},{1,9},{9,1},{5,13},{13,5},{2,10},{10,2},... | collective-permute-start | bytes 24584 | tf_op jit(solution)/shard_map/ppermute | solution.py:425
  60.6 0.7 copy-start.8
  61.3 6.7 %collective-permute-start.12 = (bf16[1024,128]{1,0:T(8,128)(2,1)}, bf16[1024,128]{1,0:T(8,128)(2,1)}, u32[]{:S(2)}, u32[]{:S(2)}) collective-permute-start(bf16[1024,128]{1,0:T(8,128)(2,1)} %get-tuple-element.95), channel_id=1, source_target_pairs={{0,2},{2,0},{1,3},{3,1},{4,6},{6,4},{5,7},{7,5},{8,10},{10,8},{9,1... | collective-permute-start | bytes 786440 | tf_op jit(solution)/shard_map/ppermute | solution.py:516
  61.9 14.9 %collective-permute-start.17 = (bf16[1,128,1024]{2,1,0:T(8,128)(2,1)}, bf16[1,128,1024]{2,1,0:T(8,128)(2,1)}, u32[]{:S(2)}, u32[]{:S(2)}) collective-permute-start(bf16[1,128,1024]{2,1,0:T(8,128)(2,1)} %bitcast.15.refs_3_), channel_id=1, source_target_pairs={{0,1},{1,0},{2,3},{3,2},{4,5},{5,4},{6,7},{7,6},{8,9},{9,8},{10,11... | collective-permute-start | bytes 786440 | tf_op jit(solution)/shard_map/ppermute | solution.py:424
  61.9 14.9 %collective-permute-start.15 = (bf16[2,128,512]{2,1,0:T(8,128)(2,1)}, bf16[2,128,512]{2,1,0:T(8,128)(2,1)}, u32[]{:S(2)}, u32[]{:S(2)}) collective-permute-start(bf16[2,128,512]{2,1,0:T(8,128)(2,1)} %get-tuple-element.105), channel_id=1, source_target_pairs={{0,1},{1,0},{2,3},{3,2},{4,5},{5,4},{6,7},{7,6},{8,9},{9,8},{10,11... | collective-permute-start | bytes 786440 | tf_op jit(solution)/shard_map/ppermute | solution.py:424
  62.4 10.6 %collective-permute-start.16 = (f32[1,128]{1,0:T(1,128)S(1)}, f32[1,128]{1,0:T(1,128)S(1)}, u32[]{:S(2)}, u32[]{:S(2)}) collective-permute-start(f32[1,128]{1,0:T(1,128)S(1)} %get-tuple-element.106), channel_id=1, source_target_pairs={{0,1},{1,0},{2,3},{3,2},{4,5},{5,4},{6,7},{7,6},{8,9},{9,8},{10,11... | collective-permute-start | bytes 1544 | tf_op jit(solution)/shard_map/ppermute | solution.py:424
  69.7 7.1 %collective-permute-start.14 = (bf16[1024,128]{1,0:T(8,128)(2,1)}, bf16[1024,128]{1,0:T(8,128)(2,1)}, u32[]{:S(2)}, u32[]{:S(2)}) collective-permute-start(bf16[1024,128]{1,0:T(8,128)(2,1)} %shard_map.102), channel_id=1, source_target_pairs={{0,4},{12,8},{1,5},{13,9},{2,6},{14,10},{3,7},{15,11},{16,20},{28,... | collective-permute-start | bytes 786440 | tf_op jit(solution)/shard_map/ppermute | solution.py:425
  73.0 6.7 %collective-permute-start.13 = (bf16[1024,128]{1,0:T(8,128)(2,1)}, bf16[1024,128]{1,0:T(8,128)(2,1)}, u32[]{:S(2)}, u32[]{:S(2)}) collective-permute-start(bf16[1024,128]{1,0:T(8,128)(2,1)} %get-tuple-element.100), channel_id=1, source_target_pairs={{0,2},{2,0},{1,3},{3,1},{4,6},{6,4},{5,7},{7,5},{8,10},{10,8},{9,1... | collective-permute-start | bytes 786440 | tf_op jit(solution)/shard_map/ppermute | solution.py:516
  76.8 8.4 %copy-start.6 = (f32[1024,128]{1,0:T(8,128)}, f32[1024,128]{1,0:T(8,128)S(1)}, u32[]{:S(2)}) copy-start(f32[1024,128]{1,0:T(8,128)S(1)} %get-tuple-element.116.kept) | copy-start | bytes 1572868
  81.4 8.0 %collective-permute-start.20 = (bf16[1024,128]{1,0:T(8,128)(2,1)}, bf16[1024,128]{1,0:T(8,128)(2,1)}, u32[]{:S(2)}, u32[]{:S(2)}) collective-permute-start(bf16[1024,128]{1,0:T(8,128)(2,1)} %shard_map.105), channel_id=1, source_target_pairs={{0,4},{12,8},{1,5},{13,9},{2,6},{14,10},{3,7},{15,11},{16,20},{28,... | collective-permute-start | bytes 786440 | tf_op jit(solution)/shard_map/ppermute | solution.py:425
  85.2 4.2 %collective-permute-start.19 = (bf16[1024,128]{1,0:T(8,128)(2,1)}, bf16[1024,128]{1,0:T(8,128)(2,1)S(1)}, u32[]{:S(2)}, u32[]{:S(2)}) collective-permute-start(bf16[1024,128]{1,0:T(8,128)(2,1)} %shard_map.104), channel_id=1, source_target_pairs={{4,8},{8,4},{5,9},{9,5},{6,10},{10,6},{7,11},{11,7},{20,24},{24,20... | collective-permute-start | bytes 786440 | tf_op jit(solution)/shard_map/ppermute | solution.py:425
  85.8 6.6 %collective-permute-start.18 = (bf16[1024,128]{1,0:T(8,128)(2,1)}, bf16[1024,128]{1,0:T(8,128)(2,1)S(1)}, u32[]{:S(2)}, u32[]{:S(2)}) collective-permute-start(bf16[1024,128]{1,0:T(8,128)(2,1)} %get-tuple-element.108), channel_id=1, source_target_pairs={{0,2},{2,0},{1,3},{3,1},{4,6},{6,4},{5,7},{7,5},{8,10},{10,8},{9,1... | collective-permute-start | bytes 786440 | tf_op jit(solution)/shard_map/ppermute | solution.py:516
  87.0 5.5 %copy-start.7 = (f32[1024,128]{1,0:T(8,128)S(1)}, f32[1024,128]{1,0:T(8,128)}, u32[]{:S(2)}) copy-start(f32[1024,128]{1,0:T(8,128)} %copy-done.6) | copy-start | bytes 1572868
  87.0 12.4 %copy-start.9 = (bf16[2,128,512]{2,1,0:T(8,128)(2,1)S(1)}, bf16[2,128,512]{2,1,0:T(8,128)(2,1)}, u32[]{:S(2)}) copy-start(bf16[2,128,512]{2,1,0:T(8,128)(2,1)} %copy-done.8) | copy-start | bytes 786436
  93.7 11.5 %collective-permute-start.23 = (bf16[1024,128]{1,0:T(8,128)(2,1)S(1)}, bf16[1024,128]{1,0:T(8,128)(2,1)S(1)}, u32[]{:S(2)}, u32[]{:S(2)}) collective-permute-start(bf16[1024,128]{1,0:T(8,128)(2,1)S(1)} %shard_map.108), channel_id=1, source_target_pairs={{4,8},{8,4},{5,9},{9,5},{6,10},{10,6},{7,11},{11,7},{20,24},{24,20... | collective-permute-start | bytes 786440 | tf_op jit(solution)/shard_map/ppermute | solution.py:425
  94.4 10.8 %collective-permute-start.22 = (bf16[1024,128]{1,0:T(8,128)(2,1)S(1)}, bf16[1024,128]{1,0:T(8,128)(2,1)S(1)}, u32[]{:S(2)}, u32[]{:S(2)}) collective-permute-start(bf16[1024,128]{1,0:T(8,128)(2,1)S(1)} %shard_map.107), channel_id=1, source_target_pairs={{0,4},{4,0},{8,12},{12,8},{1,5},{5,1},{9,13},{13,9},{2,6},{6,2},{1... | collective-permute-start | bytes 786440 | tf_op jit(solution)/shard_map/ppermute | solution.py:425
  98.1 7.1 %collective-permute-start.21 = (bf16[1024,128]{1,0:T(8,128)(2,1)S(1)}, bf16[1024,128]{1,0:T(8,128)(2,1)S(1)}, u32[]{:S(2)}, u32[]{:S(2)}) collective-permute-start(bf16[1024,128]{1,0:T(8,128)(2,1)S(1)} %get-tuple-element.115), channel_id=1, source_target_pairs={{0,2},{2,0},{1,3},{3,1},{4,6},{6,4},{5,7},{7,5},{8,10},{10,8},{9,1... | collective-permute-start | bytes 786440 | tf_op jit(solution)/shard_map/ppermute | solution.py:516

commit v12 on v4

--- a/solution.py
+++ b/solution.py
@@ -15,8 +15,8 @@
 IN_PLACE = pl.BlockSpec(memory_space=pl.ANY)
 PAIRS_OUT = [(0, 1), (1, 0), (2, 3), (3, 2)]
 PAIR_IN = [(1, 2), (2, 1)]
-TO_ENDS = [(1, 0), (2, 3)]
 FROM_ENDS = [(0, 1), (3, 2)]
+SWAP_HALVES = [(0, 2), (2, 0), (1, 3), (3, 1)]
 
 
 def ring(count, shift):
@@ -313,86 +313,84 @@
     firsts = [
         ((me_voc * n_ctx + me_ctx) * n_dp + owner) * columns for owner in (me_dp, (me_dp + 1) % n_dp)
     ]
-    meta = jnp.stack(part_of + firsts).astype(jnp.int32)
+    came_from = [(me_voc - i) % n_voc for i in range(n_voc)]
+    meta = jnp.stack(came_from + firsts).astype(jnp.int32)
 
     weights = (head_weight, dp_swap(head_weight))
 
     own = hidden.transpose(1, 2, 3, 0).reshape(rows, part)
     chunk = {(0, 0): own}
-    logits = [None] * n_ctx
-    stats = [None] * n_ctx
     call = functools.partial(logits_call, meta=meta, weights=weights, part=part, n_voc=n_voc)
     cross = lambda a: [lax.ppermute(a, "ctx", ring(n_ctx, t)) for t in beyond]
-    inner = last = None
-    for step in range(n_voc):
-        over = cross(chunk[0, step])
-        came = []
-        if line:
-            if step == 0:
-                came = [along(own, PAIRS_OUT), along(own, PAIR_IN)]
-            elif step == 1:
-                came = [along(inner, TO_ENDS), along(chunk[0, 1], PAIR_IN)]
-            elif step == 2:
-                came = [along(last, TO_ENDS)]
-        elif step + 1 < n_voc:
-            came = [along(own, ring(n_voc, step + 1))]
-        if step:
-            plan = [(0, {i: chunk[0, i] for i in ([0, 1] if step == 1 else [step])}, logits[0], None)]
-            plan += [(t, {step - 1: chunk[t, step - 1]}, logits[t], None) for t in beyond]
-            if step == n_voc - 1:
-                plan[0] = plan[0][:3] + (wanted[0],)
-            done = list(call(plan))
-            if step == n_voc - 1:
-                stats[0] = done.pop(1)
-            logits = list(done)
-        else:
-            held, raw = together(came[:1], [targets])
-            pair = lax.broadcasted_iota(jnp.int32, targets.shape, 0)
-            mine = jnp.sum(jnp.where(pair == me_dp, raw[0], 0), axis=0)
-            blocks = [mine[:, b * window:(b + 1) * window].reshape(rows) for b in range(n_ctx)]
-            wanted = []
-            for t in range(n_ctx):
-                at = (me_ctx - t) % n_ctx
-                wanted.append(sum(jnp.where(at == b, blocks[b], 0) for b in range(n_ctx))[:, None])
-            target = jnp.concatenate(wanted)
-        ready = [a for a in logits if a is not None]
-        over, came, ready = together(over, came, ready)
-        if ready:
-            logits = ready
-        for t, a in zip(beyond, over):
-            chunk[t, step] = a
-        if not line:
-            if came:
-                chunk[0, step + 1] = came[0]
-        elif step == 0:
-            chunk[0, 1], inner = came
-        elif step == 1:
-            chunk[0, 2] = inner + came[0]
-            last = came[1]
-        elif step == 2:
-            chunk[0, 3] = last + came[0]
-
+    near = sorted({1, n_voc - 1})
+    rest = [i for i in range(1, n_voc) if i not in near]
+
+    def arrive(i, c, over):
+        chunk[0, i] = c
+        for t, o in zip(beyond, over):
+            chunk[t, i] = o
+
+    came, over, (again,) = together([along(own, ring(n_voc, i)) for i in near], cross(own), [own])
+    arrive(0, own, over)
+    over = [cross(c) for c in came]
+    for i, c, o in zip(near, came, over):
+        arrive(i, c, o)
+    came = [along(again, ring(n_voc, i)) for i in rest]
+    (again,), (raw,) = together([again], [targets])
+    pair = lax.broadcasted_iota(jnp.int32, targets.shape, 0)
+    mine = jnp.sum(jnp.where(pair == me_dp, raw, 0), axis=0)
+    blocks = [mine[:, b * window:(b + 1) * window].reshape(rows) for b in range(n_ctx)]
+    wanted = []
+    for t in range(n_ctx):
+        at = (me_ctx - t) % n_ctx
+        wanted.append(sum(jnp.where(at == b, blocks[b], 0) for b in range(n_ctx))[:, None])
+    target = jnp.concatenate(wanted)
+    logits = call(
+        [(0, {i: chunk[0, i] for i in [0] + near}, None, None)] + [(t, {0: chunk[t, 0]}, None, None) for t in beyond]
+    )
+    came, logits, *over = together(came, list(logits), *over)
+    for i, o in zip(near, over):
+        arrive(i, chunk[0, i], o)
+    for i, c in zip(rest, came):
+        arrive(i, c, cross(c))
+    late = [(t, i) for i in rest for t in beyond]
+    soon = [k for k in chunk if k not in late]
+    done = list(call(
+        [(0, {i: chunk[0, i] for i in rest}, logits[0], wanted[0])]
+        + [(t, {i: chunk[t, i] for i in near}, logits[t], None) for t in beyond]
+    ))
+    last, done = together([chunk[k] for k in late], done)
+    chunk.update(zip(late, last))
+    stats = [done.pop(1)]
+    logits = done
     final = n_voc - 1
-    done = call([(t, {final: chunk[t, final]}, logits[t], wanted[t]) for t in beyond])
+    done = call([(t, {i: chunk[t, i] for i in rest}, logits[t], wanted[t]) for t in beyond])
     logits = [logits[0]] + list(done[0::2])
-    stats = [stats[0]] + list(done[1::2])
-
-    late = [(t, final) for t in beyond]
-    soon = [k for k in chunk if k not in late]
+    stats = stats + list(done[1::2])
+
     far_soon = dp_swap(jnp.stack([chunk[k] for k in soon]))
 
-    others = cross(jnp.stack(stats))
-    merged = []
-    for b in range(n_ctx):
-        seen = [stats[b]] + [o[(b - t) % n_ctx] for t, o in zip(beyond, others)]
-        top = seen[0][0]
-        for o in seen[1:]:
-            top = jnp.maximum(top, o[0])
-        total = sum(o[1] * jnp.exp(o[0] - top) for o in seen)
-        picked = sum(o[2] for o in seen)
-        merged.append(jnp.pad(jnp.stack([top, total, picked]), ((0, 5), (0, 0))))
-    merged = jnp.concatenate(merged, axis=1)
-    all_stats = [merged] + [along(merged, ring(n_voc, s)) for s in range(1, n_voc)]
+    def merge(seen):
+        merged = []
+        for b in range(n_ctx):
+            these = [a[(b - t) % n_ctx] for t, a in seen]
+            top = these[0][0]
+            for a in these[1:]:
+                top = jnp.maximum(top, a[0])
+            total = sum(a[1] * jnp.exp(a[0] - top) for a in these)
+            picked = sum(a[2] for a in these)
+            merged.append(jnp.pad(jnp.stack([top, total, picked]), ((0, 5), (0, 0))))
+        return jnp.concatenate(merged, axis=1)
+
+    stats = jnp.stack(stats)
+    if line and n_ctx == 2:
+        corner = [(2 * a + c, 2 * b + (1 - c)) for a, b in PAIRS_OUT for c in range(2)]
+        diagonal = lax.ppermute(stats, ("vocab", "ctx"), corner)
+        merged = merge([(0, stats), (1, cross(stats)[0]), (0, along(stats, PAIRS_OUT)), (1, diagonal)])
+        all_stats = [merged, along(merged, SWAP_HALVES)]
+    else:
+        merged = merge([(0, stats)] + list(zip(beyond, cross(stats))))
+        all_stats = [merged] + [along(merged, ring(n_voc, i)) for i in range(1, n_voc)]
 
     meta_grads = jnp.stack([part_of[final]] + firsts + [me_dp, me_ctx]).astype(jnp.int32)
     small = (response_start, other_sums, ref_logp, loss_cotangent)

time: 100 us -> 111 us (1.11)
  local copies, waits for them, and re-layouts: 11.4 us -> 23.9 us
  waiting for transfers between devices: 29.5 us -> 18.4 us
  Pallas kernels: 27 us -> 33.8 us
  starting transfers between devices: 28.7 us -> 31.1 us
    unnamed x31 -> x50, local copies, waits for them, and re-layouts: 10.7 us -> 22.4 us
    pallas_call x6, Pallas kernels: 1.22 us -> 8.25 us  [add_call(): pl.pallas_call(functools.partial(add_kernel, turned), out_shape=shape_of(...]
    ppermute x4, waiting for transfers between devices: 6.85 us -> 1.69 us  [shards(): lax.ppermute(c, 'ctx', ring(n_ctx, -t))]
    ppermute x5, waiting for transfers between devices: 5.34 us -> 1.42 us  [shards(): cross = lambda a: [lax.ppermute(a, 'ctx', ring(n_ctx, t)) for t in beyond]]
    ppermute x13 -> x10, waiting for transfers between devices: 17.3 us -> 14.9 us  [shards(): along = lambda a, by: lax.ppermute(a, 'vocab', by)]
    pallas_call x4 -> x3, Pallas kernels: 11.4 us -> 9.15 us  [logits_call(): pl.pallas_call(functools.partial(logits_kernel, kernel_plan, columns, par...]
    ppermute x0 -> x1, starting transfers between devices: none -> 1.89 us  [shards(): diagonal = lax.ppermute(stats, ('vocab', 'ctx'), corner)]
    pallas_call x3, Pallas kernels: 6.21 us -> 7.56 us  [spread_call(): pl.pallas_call(functools.partial(spread_kernel, part), out_shape=out_shap...]
  transfers between devices with their start and end apart: 27 -> 25, of which waited for: 15 -> 11; matrix products, arithmetic and copies ran while one was open for 2% -> 7% of each run, Pallas kernels for 27% -> 28%
where the time goes in v12:
time: 111 us; the launch traced here: 110 us
  Pallas kernels  33.8 us (30%)
  starting transfers between devices  31.1 us (28%)
  local copies, waits for them, and re-layouts  23.9 us (22%)
  waiting for transfers between devices  18.4 us (17%)
  other arithmetic  1.41 us (1%)
    unnamed x50, local copies, waits for them, and re-layouts  22.4 us
    ppermute x10, starting transfers between devices, shards(): along = lambda a, by: lax.ppermute(a, 'vocab', by)  19.5 us
    ppermute x10, waiting for transfers between devices, shards(): along = lambda a, by: lax.ppermute(a, 'vocab', by)  14.9 us
    pallas_call x3, Pallas kernels, logits_call(): pl.pallas_call(functools.partial(logits_kernel, kernel_plan, columns, par...  9.15 us
    pallas_call x6, Pallas kernels, add_call(): pl.pallas_call(functools.partial(add_kernel, turned), out_shape=shape_of(...  8.25 us
    pallas_call x3, Pallas kernels, spread_call(): pl.pallas_call(functools.partial(spread_kernel, part), out_shape=out_shap...  7.56 us
    ppermute x5, starting transfers between devices, shards(): cross = lambda a: [lax.ppermute(a, 'ctx', ring(n_ctx, t)) for t in beyond]  5.55 us
    pallas_call x1, Pallas kernels, head_call(): pl.pallas_call(functools.partial(head_kernel, list(near), [keys for keys,...  5.53 us
  transfers between devices with their start and end apart: 25, of which 11 were waited for; matrix products, arithmetic and copies ran while one was open for 7% of the time, Pallas kernels for 28%

profile of v12, /device:TPU:0, one launch (start us, length us, event | category | flops | bytes accessed | tf_op | source)
XLA Modules:
  0.0 109.5 jit_solution(12958397318564612233)
XLA Ops:
  0.6 0.5 collective-permute-start
  1.2 2.6 %collective-permute-start.1 = (bf16[128,1024]{1,0:T(8,128)(2,1)}, bf16[128,1024]{1,0:T(8,128)(2,1)S(1)}, u32[]{:S(2)}, u32[]{:S(2)}) collective-permute-start(bf16[128,1024]{1,0:T(8,128)(2,1)} %bitcast.157), channel_id=1, source_target_pairs={{0,4},{4,8},{8,12},{12,0},{1,5},{5,9},{9,13},{13,1},{2,6},{6,10},{... | collective-permute-start | bytes 786440 | tf_op jit(solution)/shard_map/ppermute | solution.py:306
  3.8 2.1 %collective-permute-start.2 = (bf16[128,1024]{1,0:T(8,128)(2,1)}, bf16[128,1024]{1,0:T(8,128)(2,1)S(1)}, u32[]{:S(2)}, u32[]{:S(2)}) collective-permute-start(bf16[128,1024]{1,0:T(8,128)(2,1)} %bitcast.158), channel_id=1, source_target_pairs={{0,12},{4,0},{8,4},{12,8},{1,13},{5,1},{9,5},{13,9},{2,14},{6,2},{... | collective-permute-start | bytes 786440 | tf_op jit(solution)/shard_map/ppermute | solution.py:306
  5.9 1.6 %collective-permute-start.3 = (bf16[128,1024]{1,0:T(8,128)(2,1)}, bf16[128,1024]{1,0:T(8,128)(2,1)S(1)}, u32[]{:S(2)}, u32[]{:S(2)}) collective-permute-start(bf16[128,1024]{1,0:T(8,128)(2,1)} %bitcast.159), channel_id=1, source_target_pairs={{0,2},{2,0},{1,3},{3,1},{4,6},{6,4},{5,7},{7,5},{8,10},{10,8},{9,1... | collective-permute-start | bytes 786440 | tf_op jit(solution)/shard_map/ppermute | solution.py:324
  7.7 1.7 %constant_dynamic-update-slice_fusion = bf16[7,128,1024]{2,1,0:T(8,128)(2,1)} fusion(bf16[1,128,1024]{2,1,0:T(8,128)(2,1)} %bitcast.160), kind=kLoop, calls=%fused_computation.6 | loop fusion | bytes 524288
  9.4 3.9 %collective-permute-done.1.refs_1_.refs_4_ = bf16[128,1024]{1,0:T(8,128)(2,1)S(1)} collective-permute-done((bf16[128,1024]{1,0:T(8,128)(2,1)}, bf16[128,1024]{1,0:T(8,128)(2,1)S(1)}, u32[]{:S(2)}, u32[]{:S(2)}) %collective-permute-start.1) | collective-permute-done | bytes 262176 | tf_op jit(solution)/shard_map/ppermute | solution.py:306
  13.2 4.8 %collective-permute-done.2.refs_2_.refs_6_ = bf16[128,1024]{1,0:T(8,128)(2,1)S(1)} collective-permute-done((bf16[128,1024]{1,0:T(8,128)(2,1)}, bf16[128,1024]{1,0:T(8,128)(2,1)S(1)}, u32[]{:S(2)}, u32[]{:S(2)}) %collective-permute-start.2) | collective-permute-done | bytes 262176 | tf_op jit(solution)/shard_map/ppermute | solution.py:306
  18.0 1.3 %collective-permute-start.4 = (bf16[128,1024]{1,0:T(8,128)(2,1)}, bf16[128,1024]{1,0:T(8,128)(2,1)S(1)}, u32[]{:S(2)}, u32[]{:S(2)}) collective-permute-start(bf16[128,1024]{1,0:T(8,128)(2,1)} %bitcast.161), channel_id=1, source_target_pairs={{0,8},{4,12},{8,0},{12,4},{1,9},{5,13},{9,1},{13,5},{2,10},{6,14},... | collective-permute-start | bytes 786440 | tf_op jit(solution)/shard_map/ppermute | solution.py:306
  19.3 1.5 %collective-permute-start.5 = (bf16[128,1024]{1,0:T(8,128)(2,1)S(1)}, bf16[128,1024]{1,0:T(8,128)(2,1)S(1)}, u32[]{:S(2)}, u32[]{:S(2)}) collective-permute-start(bf16[128,1024]{1,0:T(8,128)(2,1)S(1)} %collective-permute-done.1.refs_1_.refs_4_), channel_id=1, source_target_pairs={{0,2},{2,0},{1,3},{3,1},{4,6},{6,4},{5,7},{7,5},{8,10},{10,8},{9,1... | collective-permute-start | bytes 786440 | tf_op jit(solution)/shard_map/ppermute | solution.py:324
  20.8 0.5 collective-permute-start.6
  21.3 0.8 select_reduce_fusion
  22.6 0.7 bitcast_dynamic-update-slice_fusion.5
  23.3 0.7 bitcast_dynamic-update-slice_fusion.4
  24.0 2.2 %copy-done = bf16[4096,512]{1,0:T(8,128)(2,1)S(1)} copy-done((bf16[4096,512]{1,0:T(8,128)(2,1)S(1)}, bf16[4096,512]{1,0:T(8,128)(2,1)}, u32[]{:S(2)}) %copy-start) | copy-done | bytes 4194328
  26.2 3.4 %shard_map.94 = (f32[128,1024]{1,0:T(8,128)S(1)}, f32[128,1024]{1,0:T(8,128)S(1)}) custom-call(s32[6]{0:T(128)S(1)} %stack.90.meta, bf16[4096,512]{1,0:T(8,128)(2,1)S(1)} %copy-done, bf16[4096,512]{1,0:T(8,128)(2,1)} %collective-permute-done.w_far, bf16[128,1024]{1,0:T(8,128)(2,1)S(1)} %bitcast.162, ...), custom_call_target="tpu_custom_call" | custom-call | flops 1073741824 | bytes 6291456 | tf_op jit(solution)/shard_map/pallas_call | solution.py:109
  29.6 2.8 %collective-permute-done.4.refs_0_.refs_8_ = bf16[128,1024]{1,0:T(8,128)(2,1)S(1)} collective-permute-done((bf16[128,1024]{1,0:T(8,128)(2,1)}, bf16[128,1024]{1,0:T(8,128)(2,1)S(1)}, u32[]{:S(2)}, u32[]{:S(2)}) %collective-permute-start.4) | collective-permute-done | bytes 262176 | tf_op jit(solution)/shard_map/ppermute | solution.py:306
  32.6 1.4 %collective-permute-start.7 = (bf16[128,1024]{1,0:T(8,128)(2,1)S(1)}, bf16[128,1024]{1,0:T(8,128)(2,1)S(1)}, u32[]{:S(2)}, u32[]{:S(2)}) collective-permute-start(bf16[128,1024]{1,0:T(8,128)(2,1)S(1)} %collective-permute-done.4.refs_0_.refs_8_), channel_id=1, source_target_pairs={{0,2},{2,0},{1,3},{3,1},{4,6},{6,4},{5,7},{7,5},{8,10},{10,8},{9,1... | collective-permute-start | bytes 786440 | tf_op jit(solution)/shard_map/ppermute | solution.py:324
  33.9 0.7 bitcast_dynamic-update-slice_fusion.3
  34.7 0.7 bitcast_dynamic-update-slice_fusion.2
  35.4 3.2 %shard_map.95 = (f32[128,1024]{1,0:T(8,128)S(1)}, f32[8,128]{1,0:T(8,128)S(1)}, f32[128,1024]{1,0:T(8,128)S(1)}) custom-call(s32[6]{0:T(128)S(1)} %stack.90.meta, bf16[4096,512]{1,0:T(8,128)(2,1)S(1)} %copy-done, bf16[4096,512]{1,0:T(8,128)(2,1)} %collective-permute-done.w_far, bf16[128,1024]{1,0:T(8,128)(2,1)S(1)} %collective-permute-done.4.refs_0_.refs_8_, ...), custom_call_target="tpu_custom_call" | custom-call | flops 805306368 | bytes 6291456 | tf_op jit(solution)/shard_map/pallas_call | solution.py:109
  38.6 0.7 bitcast_dynamic-update-slice_fusion.1
  39.5 2.5 %shard_map.96 = (f32[128,1024]{1,0:T(8,128)S(1)}, f32[8,128]{1,0:T(8,128)S(1)}) custom-call(s32[6]{0:T(128)S(1)} %stack.90.meta, bf16[4096,512]{1,0:T(8,128)(2,1)S(1)} %copy-done, bf16[4096,512]{1,0:T(8,128)(2,1)} %collective-permute-done.w_far, bf16[128,1024]{1,0:T(8,128)(2,1)S(1)} %collective-permute-done.7.refs_0_.refs_9_, ...), custom_call_target="tpu_custom_call" | custom-call | flops 268435456 | bytes 2097152 | tf_op jit(solution)/shard_map/pallas_call | solution.py:109
  42.1 1.9 %collective-permute-start.10 = (f32[2,8,128]{2,1,0:T(8,128)S(1)}, f32[2,8,128]{2,1,0:T(8,128)S(1)}, u32[]{:S(2)}, u32[]{:S(2)}) collective-permute-start(f32[2,8,128]{2,1,0:T(8,128)S(1)} %pad_maximum_fusion), channel_id=1, source_target_pairs={{0,6},{2,4},{4,2},{6,0},{8,14},{10,12},{12,10},{14,8},{1,7},{3,5},... | collective-permute-start | bytes 24584 | tf_op jit(solution)/shard_map/ppermute | solution.py:388
  43.9 1.1 %collective-permute-start.9 = (f32[2,8,128]{2,1,0:T(8,128)S(1)}, f32[2,8,128]{2,1,0:T(8,128)S(1)}, u32[]{:S(2)}, u32[]{:S(2)}) collective-permute-start(f32[2,8,128]{2,1,0:T(8,128)S(1)} %pad_maximum_fusion), channel_id=1, source_target_pairs={{0,4},{4,0},{8,12},{12,8},{1,5},{5,1},{9,13},{13,9},{2,6},{6,2},{1... | collective-permute-start | bytes 24584 | tf_op jit(solution)/shard_map/ppermute | solution.py:306
  45.1 0.5 collective-permute-start.8
  45.6 0.7 bitcast_dynamic-update-slice_fusion
  46.7 0.9 collective-permute-done.9
  47.6 1.1 %collective-permute-done.8 = f32[2,8,128]{2,1,0:T(8,128)S(1)} collective-permute-done((f32[2,8,128]{2,1,0:T(8,128)S(1)}, f32[2,8,128]{2,1,0:T(8,128)S(1)}, u32[]{:S(2)}, u32[]{:S(2)}) %collective-permute-start.8) | collective-permute-done | bytes 8224 | tf_op jit(solution)/shard_map/ppermute | solution.py:324
  48.8 2.1 %collective-permute-start.11 = (f32[8,256]{1,0:T(8,128)S(1)}, f32[8,256]{1,0:T(8,128)S(1)}, u32[]{:S(2)}, u32[]{:S(2)}) collective-permute-start(f32[8,256]{1,0:T(8,128)S(1)} %pad_maximum_fusion.1.refs_3_), channel_id=1, source_target_pairs={{0,8},{8,0},{4,12},{12,4},{1,9},{9,1},{5,13},{13,5},{2,10},{10,2},... | collective-permute-start | bytes 24584 | tf_op jit(solution)/shard_map/ppermute | solution.py:306
  51.0 2.4 %collective-permute-done.11.refs_4_ = f32[8,256]{1,0:T(8,128)S(1)} collective-permute-done((f32[8,256]{1,0:T(8,128)S(1)}, f32[8,256]{1,0:T(8,128)S(1)}, u32[]{:S(2)}, u32[]{:S(2)}) %collective-permute-start.11) | collective-permute-done | bytes 8224 | tf_op jit(solution)/shard_map/ppermute | solution.py:306
  53.4 0.6 copy-done.14
  54.0 2.2 %copy-done.1 = bf16[4096,512]{1,0:T(8,128)(2,1)S(1)} copy-done((bf16[4096,512]{1,0:T(8,128)(2,1)S(1)}, bf16[4096,512]{1,0:T(8,128)(2,1)}, u32[]{:S(2)}) %copy-start.1) | copy-done | bytes 4194328
  56.2 1.0 copy-done.9
  57.2 0.7 copy-done.15
  57.9 0.7 copy-done.16
  58.6 0.7 copy-done.17
  59.3 0.7 copy-done.18
  60.0 0.7 copy-done.19
  60.6 3.3 %shard_map.97 = (bf16[2,128,512]{2,1,0:T(8,128)(2,1)S(1)}, bf16[2,128,512]{2,1,0:T(8,128)(2,1)}, bf16[512,256]{1,0:T(8,128)(2,1)S(1)}, bf16[512,256]{1,0:T(8,128...) custom-call(s32[5]{0:T(128)S(1)} %stack.85.meta, s32[2]{0:T(128)S(1)} %copy-done.18, ...), custom_call_target="tpu_custom_call" | custom-call | flops 536870912 | bytes 4194304 | tf_op jit(solution)/shard_map/pallas_call | solution.py:202
  64.0 0.7 copy-done.12
  64.6 0.5 copy-done.20
  65.2 0.5 collective-permute-start.12
  65.7 2.2 %copy-done.2 = bf16[4096,512]{1,0:T(8,128)(2,1)S(1)} copy-done((bf16[4096,512]{1,0:T(8,128)(2,1)S(1)}, bf16[4096,512]{1,0:T(8,128)(2,1)}, u32[]{:S(2)}) %copy-start.2) | copy-done | bytes 4194328
  67.9 2.8 %shard_map.99 = (f32[1024,128]{1,0:T(8,128)S(1)}, bf16[1024,128]{1,0:T(8,128)(2,1)}) custom-call(s32[1]{0:T(128)} %bitcast.33.meta, bf16[4096,512]{1,0:T(8,128)(2,1)S(1)} %copy-done.2, bf16[4096,512]{1,0:T(8,128)(2,1)} %collective-permute-done.w_far, bf16[512,256]{1,0:T(8,128)(2,1)S(1)} %get-tuple-element.72.flipped_own, ...), custom_call_target="tpu_custom_call" | custom-call | flops 536870912 | bytes 2097152 | tf_op jit(solution)/shard_map/pallas_call | solution.py:216
  70.7 1.7 %collective-permute-done.12.refs_0_ = bf16[1024,128]{1,0:T(8,128)(2,1)} collective-permute-done((bf16[1024,128]{1,0:T(8,128)(2,1)}, bf16[1024,128]{1,0:T(8,128)(2,1)}, u32[]{:S(2)}, u32[]{:S(2)}) %collective-permute-start.12) | collective-permute-done | bytes 262176 | tf_op jit(solution)/shard_map/ppermute | solution.py:402
  72.6 1.7 %shard_map.100 = bf16[1024,128]{1,0:T(8,128)(2,1)} custom-call(f32[1024,128]{1,0:T(8,128)S(1)} %get-tuple-element.78.kept, bf16[1024,128]{1,0:T(8,128)(2,1)} %collective-permute-done.12.refs_0_), custom_call_target="tpu_custom_call" | custom-call | flops 131072 | bytes 524288 | tf_op jit(solution)/shard_map/pallas_call | solution.py:236
  74.3 3.9 %collective-permute-start.14 = (bf16[1024,128]{1,0:T(8,128)(2,1)}, bf16[1024,128]{1,0:T(8,128)(2,1)}, u32[]{:S(2)}, u32[]{:S(2)}) collective-permute-start(bf16[1024,128]{1,0:T(8,128)(2,1)} %shard_map.100), channel_id=1, source_target_pairs={{0,4},{12,8},{1,5},{13,9},{2,6},{14,10},{3,7},{15,11},{16,20},{28,... | collective-permute-start | bytes 786440 | tf_op jit(solution)/shard_map/ppermute | solution.py:306
  78.2 2.2 %copy-done.3 = bf16[4096,512]{1,0:T(8,128)(2,1)S(1)} copy-done((bf16[4096,512]{1,0:T(8,128)(2,1)S(1)}, bf16[4096,512]{1,0:T(8,128)(2,1)}, u32[]{:S(2)}) %copy-start.3) | copy-done | bytes 4194328
  80.4 2.7 %shard_map.101 = (f32[1024,128]{1,0:T(8,128)S(1)}, bf16[1024,128]{1,0:T(8,128)(2,1)}) custom-call(s32[1]{0:T(128)} %bitcast.34.meta, bf16[4096,512]{1,0:T(8,128)(2,1)S(1)} %copy-done.3, bf16[4096,512]{1,0:T(8,128)(2,1)} %collective-permute-done.w_far, bf16[512,256]{1,0:T(8,128)(2,1)S(1)} %get-tuple-element.72.flipped_own, ...), custom_call_target="tpu_custom_call" | custom-call | flops 536870912 | bytes 2097152 | tf_op jit(solution)/shard_map/pallas_call | solution.py:216
  83.1 1.4 %collective-permute-start.15 = (bf16[1024,128]{1,0:T(8,128)(2,1)}, bf16[1024,128]{1,0:T(8,128)(2,1)}, u32[]{:S(2)}, u32[]{:S(2)}) collective-permute-start(bf16[1024,128]{1,0:T(8,128)(2,1)} %get-tuple-element.81), channel_id=1, source_target_pairs={{0,2},{2,0},{1,3},{3,1},{4,6},{6,4},{5,7},{7,5},{8,10},{10,8},{9,1... | collective-permute-start | bytes 786440 | tf_op jit(solution)/shard_map/ppermute | solution.py:402
  84.5 1.7 %shard_map.102 = bf16[1024,128]{1,0:T(8,128)(2,1)} custom-call(f32[1024,128]{1,0:T(8,128)S(1)} %get-tuple-element.82.kept, bf16[1024,128]{1,0:T(8,128)(2,1)} %collective-permute-done.13.refs_0_), custom_call_target="tpu_custom_call" | custom-call | flops 131072 | bytes 524288 | tf_op jit(solution)/shard_map/pallas_call | solution.py:236
  86.2 3.6 %collective-permute-start.16 = (bf16[1024,128]{1,0:T(8,128)(2,1)}, bf16[1024,128]{1,0:T(8,128)(2,1)}, u32[]{:S(2)}, u32[]{:S(2)}) collective-permute-start(bf16[1024,128]{1,0:T(8,128)(2,1)} %shard_map.102), channel_id=1, source_target_pairs={{0,4},{12,8},{1,5},{13,9},{2,6},{14,10},{3,7},{15,11},{16,20},{28,... | collective-permute-start | bytes 786440 | tf_op jit(solution)/shard_map/ppermute | solution.py:306
  89.8 1.8 %shard_map.103 = bf16[1024,128]{1,0:T(8,128)(2,1)} custom-call(f32[1024,128]{1,0:T(8,128)S(1)} %get-tuple-element.78.kept, bf16[1024,128]{1,0:T(8,128)(2,1)} %collective-permute-done.12.refs_0_, bf16[1024,128]{1,0:T(8,128)(2,1)} %collective-permute-done.14.refs_1_), custom_call_target="tpu_custom_call" | custom-call | flops 131072 | bytes 524288 | tf_op jit(solution)/shard_map/pallas_call | solution.py:236
  91.6 0.7 collective-permute-start.17
  92.8 2.2 %copy-done.4 = bf16[4096,512]{1,0:T(8,128)(2,1)S(1)} copy-done((bf16[4096,512]{1,0:T(8,128)(2,1)S(1)}, bf16[4096,512]{1,0:T(8,128)(2,1)}, u32[]{:S(2)}) %copy-start.4) | copy-done | bytes 4194328
  95.0 2.1 %shard_map.98 = (f32[1024,128]{1,0:T(8,128)S(1)}, bf16[1024,128]{1,0:T(8,128)(2,1)S(1)}) custom-call(s32[1]{0:T(128)} %bitcast.meta, bf16[4096,512]{1,0:T(8,128)(2,1)S(1)} %copy-done.4, bf16[4096,512]{1,0:T(8,128)(2,1)} %collective-permute-done.w_far, bf16[512,256]{1,0:T(8,128)(2,1)S(1)} %get-tuple-element.72.flipped_own, ...), custom_call_target="tpu_custom_call" | custom-call | flops 536870912 | bytes 2097152 | tf_op jit(solution)/shard_map/pallas_call | solution.py:216
  97.3 0.7 collective-permute-start.18
  98.0 1.1 %shard_map.105 = bf16[1024,128]{1,0:T(8,128)(2,1)S(1)} custom-call(f32[1024,128]{1,0:T(8,128)S(1)} %get-tuple-element.82.kept, bf16[1024,128]{1,0:T(8,128)(2,1)} %collective-permute-done.13.refs_0_, bf16[1024,128]{1,0:T(8,128)(2,1)} %collective-permute-done.16.refs_1_), custom_call_target="tpu_custom_call" | custom-call | flops 131072 | bytes 524288 | tf_op jit(solution)/shard_map/pallas_call | solution.py:236
  99.1 1.1 shard_map.104
  100.2 1.5 %collective-permute-start.19 = (bf16[1024,128]{1,0:T(8,128)(2,1)S(1)}, bf16[1024,128]{1,0:T(8,128)(2,1)S(1)}, u32[]{:S(2)}, u32[]{:S(2)}) collective-permute-start(bf16[1024,128]{1,0:T(8,128)(2,1)S(1)} %shard_map.104), channel_id=1, source_target_pairs={{0,4},{4,0},{8,12},{12,8},{1,5},{5,1},{9,13},{13,9},{2,6},{6,2},{1... | collective-permute-start | bytes 786440 | tf_op jit(solution)/shard_map/ppermute | solution.py:306
  101.7 0.7 collective-permute-start.20
  102.4 0.5 bitcast_select_fusion
  102.9 5.5 %shard_map.106 = bf16[4096,512]{1,0:T(8,128)(2,1)} custom-call(s32[6]{0:T(128)S(1)} %stack.90.meta, bf16[2,128,512]{2,1,0:T(8,128)(2,1)S(1)} %copy-done.13, bf16[2,128,512]{2,1,0:T(8,128)(2,1)S(1)} %collective-permute-done.21.refs_1_, bf16[128,1024]{1,0:T(8,128)(2,1)S(1)} %bitcast.163, bf16[128,1024]{1,0:T(8,128)(2,1)S(1)} %collective-permute-done.3.refs_3_, ...), custom_call_target="tpu_custom_call" | custom-call | flops 2147483648 | bytes 8388608 | tf_op jit(solution)/shard_map/pallas_call | solution.py:274
  108.6 0.9 shard_map.107
  (68 shorter events, 2.7 us)
Async XLA Ops:
  0.6 23.4 %copy-start.5 = (bf16[1024,1,2,64]{0,3,2,1:T(8,128)(2,1)S(1)}, bf16[1024,1,2,64]{0,3,2,1:T(8,128)(2,1)}, u32[]{:S(2)}) copy-start(bf16[1024,1,2,64]{0,3,2,1:T(8,128)(2,1)} %param.7) | copy-start | bytes 786436
  0.6 23.4 %collective-permute-start = (bf16[4096,512]{1,0:T(8,128)(2,1)}, bf16[4096,512]{1,0:T(8,128)(2,1)}, u32[]{:S(2)}, u32[]{:S(2)}) collective-permute-start(bf16[4096,512]{1,0:T(8,128)(2,1)} %w_own.13), channel_id=1, source_target_pairs={{0,1},{1,0},{2,3},{3,2},{4,5},{5,4},{6,7},{7,6},{8,9},{9,8},{10,11... | collective-permute-start | bytes 12582920 | tf_op jit(solution)/shard_map/ppermute | solution.py:305
  1.2 12.1 %collective-permute-start.1 = (bf16[128,1024]{1,0:T(8,128)(2,1)}, bf16[128,1024]{1,0:T(8,128)(2,1)S(1)}, u32[]{:S(2)}, u32[]{:S(2)}) collective-permute-start(bf16[128,1024]{1,0:T(8,128)(2,1)} %bitcast.157), channel_id=1, source_target_pairs={{0,4},{4,8},{8,12},{12,0},{1,5},{5,9},{9,13},{13,1},{2,6},{6,10},{... | collective-permute-start | bytes 786440 | tf_op jit(solution)/shard_map/ppermute | solution.py:306
  3.8 14.2 %collective-permute-start.2 = (bf16[128,1024]{1,0:T(8,128)(2,1)}, bf16[128,1024]{1,0:T(8,128)(2,1)S(1)}, u32[]{:S(2)}, u32[]{:S(2)}) collective-permute-start(bf16[128,1024]{1,0:T(8,128)(2,1)} %bitcast.158), channel_id=1, source_target_pairs={{0,12},{4,0},{8,4},{12,8},{1,13},{5,1},{9,5},{13,9},{2,14},{6,2},{... | collective-permute-start | bytes 786440 | tf_op jit(solution)/shard_map/ppermute | solution.py:306
  5.9 12.1 %collective-permute-start.3 = (bf16[128,1024]{1,0:T(8,128)(2,1)}, bf16[128,1024]{1,0:T(8,128)(2,1)S(1)}, u32[]{:S(2)}, u32[]{:S(2)}) collective-permute-start(bf16[128,1024]{1,0:T(8,128)(2,1)} %bitcast.159), channel_id=1, source_target_pairs={{0,2},{2,0},{1,3},{3,1},{4,6},{6,4},{5,7},{7,5},{8,10},{10,8},{9,1... | collective-permute-start | bytes 786440 | tf_op jit(solution)/shard_map/ppermute | solution.py:324
  18.0 14.4 %collective-permute-start.4 = (bf16[128,1024]{1,0:T(8,128)(2,1)}, bf16[128,1024]{1,0:T(8,128)(2,1)S(1)}, u32[]{:S(2)}, u32[]{:S(2)}) collective-permute-start(bf16[128,1024]{1,0:T(8,128)(2,1)} %bitcast.161), channel_id=1, source_target_pairs={{0,8},{4,12},{8,0},{12,4},{1,9},{5,13},{9,1},{13,5},{2,10},{6,14},... | collective-permute-start | bytes 786440 | tf_op jit(solution)/shard_map/ppermute | solution.py:306
  19.3 13.1 %collective-permute-start.5 = (bf16[128,1024]{1,0:T(8,128)(2,1)S(1)}, bf16[128,1024]{1,0:T(8,128)(2,1)S(1)}, u32[]{:S(2)}, u32[]{:S(2)}) collective-permute-start(bf16[128,1024]{1,0:T(8,128)(2,1)S(1)} %collective-permute-done.1.refs_1_.refs_4_), channel_id=1, source_target_pairs={{0,2},{2,0},{1,3},{3,1},{4,6},{6,4},{5,7},{7,5},{8,10},{10,8},{9,1... | collective-permute-start | bytes 786440 | tf_op jit(solution)/shard_map/ppermute | solution.py:324
  20.8 11.8 %collective-permute-start.6 = (bf16[128,1024]{1,0:T(8,128)(2,1)S(1)}, bf16[128,1024]{1,0:T(8,128)(2,1)S(1)}, u32[]{:S(2)}, u32[]{:S(2)}) collective-permute-start(bf16[128,1024]{1,0:T(8,128)(2,1)S(1)} %collective-permute-done.2.refs_2_.refs_6_), channel_id=1, source_target_pairs={{0,2},{2,0},{1,3},{3,1},{4,6},{6,4},{5,7},{7,5},{8,10},{10,8},{9,1... | collective-permute-start | bytes 786440 | tf_op jit(solution)/shard_map/ppermute | solution.py:324
  24.0 2.2 %copy-start = (bf16[4096,512]{1,0:T(8,128)(2,1)S(1)}, bf16[4096,512]{1,0:T(8,128)(2,1)}, u32[]{:S(2)}) copy-start(bf16[4096,512]{1,0:T(8,128)(2,1)} %w_own.13) | copy-start | bytes 12582916
  32.6 6.9 %collective-permute-start.7 = (bf16[128,1024]{1,0:T(8,128)(2,1)S(1)}, bf16[128,1024]{1,0:T(8,128)(2,1)S(1)}, u32[]{:S(2)}, u32[]{:S(2)}) collective-permute-start(bf16[128,1024]{1,0:T(8,128)(2,1)S(1)} %collective-permute-done.4.refs_0_.refs_8_), channel_id=1, source_target_pairs={{0,2},{2,0},{1,3},{3,1},{4,6},{6,4},{5,7},{7,5},{8,10},{10,8},{9,1... | collective-permute-start | bytes 786440 | tf_op jit(solution)/shard_map/ppermute | solution.py:324
  39.5 2.6 %copy-start.6 = (bf16[128,1024]{1,0:T(8,128)(2,1)}, bf16[128,1024]{1,0:T(8,128)(2,1)S(1)}, u32[]{:S(2)}) copy-start(bf16[128,1024]{1,0:T(8,128)(2,1)S(1)} %collective-permute-done.7.refs_0_.refs_9_) | copy-start | bytes 786436
  42.0 11.4 %copy-start.8 = (f32[128,1024]{1,0:T(8,128)}, f32[128,1024]{1,0:T(8,128)S(1)}, u32[]{:S(2)}) copy-start(f32[128,1024]{1,0:T(8,128)S(1)} %get-tuple-element.69.refs_1_) | copy-start | bytes 1572868
  42.1 4.6 %collective-permute-start.10 = (f32[2,8,128]{2,1,0:T(8,128)S(1)}, f32[2,8,128]{2,1,0:T(8,128)S(1)}, u32[]{:S(2)}, u32[]{:S(2)}) collective-permute-start(f32[2,8,128]{2,1,0:T(8,128)S(1)} %pad_maximum_fusion), channel_id=1, source_target_pairs={{0,6},{2,4},{4,2},{6,0},{8,14},{10,12},{12,10},{14,8},{1,7},{3,5},... | collective-permute-start | bytes 24584 | tf_op jit(solution)/shard_map/ppermute | solution.py:388
  43.9 3.7 %collective-permute-start.9 = (f32[2,8,128]{2,1,0:T(8,128)S(1)}, f32[2,8,128]{2,1,0:T(8,128)S(1)}, u32[]{:S(2)}, u32[]{:S(2)}) collective-permute-start(f32[2,8,128]{2,1,0:T(8,128)S(1)} %pad_maximum_fusion), channel_id=1, source_target_pairs={{0,4},{4,0},{8,12},{12,8},{1,5},{5,1},{9,13},{13,9},{2,6},{6,2},{1... | collective-permute-start | bytes 24584 | tf_op jit(solution)/shard_map/ppermute | solution.py:306
  45.1 3.7 %collective-permute-start.8 = (f32[2,8,128]{2,1,0:T(8,128)S(1)}, f32[2,8,128]{2,1,0:T(8,128)S(1)}, u32[]{:S(2)}, u32[]{:S(2)}) collective-permute-start(f32[2,8,128]{2,1,0:T(8,128)S(1)} %pad_maximum_fusion), channel_id=1, source_target_pairs={{0,2},{2,0},{1,3},{3,1},{4,6},{6,4},{5,7},{7,5},{8,10},{10,8},{9,1... | collective-permute-start | bytes 24584 | tf_op jit(solution)/shard_map/ppermute | solution.py:324
  46.3 56.6 %collective-permute-start.22 = (bf16[7,128,1024]{2,1,0:T(8,128)(2,1)}, bf16[7,128,1024]{2,1,0:T(8,128)(2,1)}, u32[]{:S(2)}, u32[]{:S(2)}) collective-permute-start(bf16[7,128,1024]{2,1,0:T(8,128)(2,1)} %bitcast_dynamic-update-slice_fusion), channel_id=1, source_target_pairs={{0,1},{1,0},{2,3},{3,2},{4,5},{5,4},{6,7},{7,6},{8,9},{9,8},{10,11... | collective-permute-start | bytes 5505032 | tf_op jit(solution)/shard_map/ppermute | solution.py:305
  48.8 4.6 %collective-permute-start.11 = (f32[8,256]{1,0:T(8,128)S(1)}, f32[8,256]{1,0:T(8,128)S(1)}, u32[]{:S(2)}, u32[]{:S(2)}) collective-permute-start(f32[8,256]{1,0:T(8,128)S(1)} %pad_maximum_fusion.1.refs_3_), channel_id=1, source_target_pairs={{0,8},{8,0},{4,12},{12,4},{1,9},{9,1},{5,13},{13,5},{2,10},{10,2},... | collective-permute-start | bytes 24584 | tf_op jit(solution)/shard_map/ppermute | solution.py:306
  53.4 0.6 copy-start.14
  54.0 2.2 %copy-start.1 = (bf16[4096,512]{1,0:T(8,128)(2,1)S(1)}, bf16[4096,512]{1,0:T(8,128)(2,1)}, u32[]{:S(2)}) copy-start(bf16[4096,512]{1,0:T(8,128)(2,1)} %w_own.13) | copy-start | bytes 12582916
  56.2 1.0 copy-start.9
  57.2 0.7 copy-start.15
  57.9 0.7 copy-start.16
  58.6 0.7 copy-start.17
  59.3 0.7 copy-start.18
  60.0 0.7 copy-start.19
  64.0 0.7 copy-start.12
  64.6 0.5 copy-start.20
  65.2 7.2 %collective-permute-start.12 = (bf16[1024,128]{1,0:T(8,128)(2,1)}, bf16[1024,128]{1,0:T(8,128)(2,1)}, u32[]{:S(2)}, u32[]{:S(2)}) collective-permute-start(bf16[1024,128]{1,0:T(8,128)(2,1)} %get-tuple-element.75), channel_id=1, source_target_pairs={{0,2},{2,0},{1,3},{3,1},{4,6},{6,4},{5,7},{7,5},{8,10},{10,8},{9,1... | collective-permute-start | bytes 786440 | tf_op jit(solution)/shard_map/ppermute | solution.py:402
  65.7 2.2 %copy-start.2 = (bf16[4096,512]{1,0:T(8,128)(2,1)S(1)}, bf16[4096,512]{1,0:T(8,128)(2,1)}, u32[]{:S(2)}) copy-start(bf16[4096,512]{1,0:T(8,128)(2,1)} %w_own.13) | copy-start | bytes 12582916
  72.3 10.8 %collective-permute-start.13 = (bf16[1024,128]{1,0:T(8,128)(2,1)}, bf16[1024,128]{1,0:T(8,128)(2,1)}, u32[]{:S(2)}, u32[]{:S(2)}) collective-permute-start(bf16[1024,128]{1,0:T(8,128)(2,1)} %get-tuple-element.77), channel_id=1, source_target_pairs={{0,2},{2,0},{1,3},{3,1},{4,6},{6,4},{5,7},{7,5},{8,10},{10,8},{9,1... | collective-permute-start | bytes 786440 | tf_op jit(solution)/shard_map/ppermute | solution.py:402
  74.3 8.8 %collective-permute-start.14 = (bf16[1024,128]{1,0:T(8,128)(2,1)}, bf16[1024,128]{1,0:T(8,128)(2,1)}, u32[]{:S(2)}, u32[]{:S(2)}) collective-permute-start(bf16[1024,128]{1,0:T(8,128)(2,1)} %shard_map.100), channel_id=1, source_target_pairs={{0,4},{12,8},{1,5},{13,9},{2,6},{14,10},{3,7},{15,11},{16,20},{28,... | collective-permute-start | bytes 786440 | tf_op jit(solution)/shard_map/ppermute | solution.py:306
  78.2 2.2 %copy-start.3 = (bf16[4096,512]{1,0:T(8,128)(2,1)S(1)}, bf16[4096,512]{1,0:T(8,128)(2,1)}, u32[]{:S(2)}) copy-start(bf16[4096,512]{1,0:T(8,128)(2,1)} %w_own.13) | copy-start | bytes 12582916
  83.1 8.5 %copy-start.10 = (f32[1024,128]{1,0:T(8,128)}, f32[1024,128]{1,0:T(8,128)S(1)}, u32[]{:S(2)}) copy-start(f32[1024,128]{1,0:T(8,128)S(1)} %get-tuple-element.87.kept) | copy-start | bytes 1572868
  83.1 9.2 %collective-permute-start.15 = (bf16[1024,128]{1,0:T(8,128)(2,1)}, bf16[1024,128]{1,0:T(8,128)(2,1)}, u32[]{:S(2)}, u32[]{:S(2)}) collective-permute-start(bf16[1024,128]{1,0:T(8,128)(2,1)} %get-tuple-element.81), channel_id=1, source_target_pairs={{0,2},{2,0},{1,3},{3,1},{4,6},{6,4},{5,7},{7,5},{8,10},{10,8},{9,1... | collective-permute-start | bytes 786440 | tf_op jit(solution)/shard_map/ppermute | solution.py:402
  86.2 10.9 %collective-permute-start.16 = (bf16[1024,128]{1,0:T(8,128)(2,1)}, bf16[1024,128]{1,0:T(8,128)(2,1)}, u32[]{:S(2)}, u32[]{:S(2)}) collective-permute-start(bf16[1024,128]{1,0:T(8,128)(2,1)} %shard_map.102), channel_id=1, source_target_pairs={{0,4},{12,8},{1,5},{13,9},{2,6},{14,10},{3,7},{15,11},{16,20},{28,... | collective-permute-start | bytes 786440 | tf_op jit(solution)/shard_map/ppermute | solution.py:306
  91.6 5.7 %collective-permute-start.17 = (bf16[1024,128]{1,0:T(8,128)(2,1)}, bf16[1024,128]{1,0:T(8,128)(2,1)S(1)}, u32[]{:S(2)}, u32[]{:S(2)}) collective-permute-start(bf16[1024,128]{1,0:T(8,128)(2,1)} %shard_map.103), channel_id=1, source_target_pairs={{4,8},{8,4},{5,9},{9,5},{6,10},{10,6},{7,11},{11,7},{20,24},{24,20... | collective-permute-start | bytes 786440 | tf_op jit(solution)/shard_map/ppermute | solution.py:306
  92.3 9.5 %collective-permute-start.21 = (bf16[2,128,512]{2,1,0:T(8,128)(2,1)}, bf16[2,128,512]{2,1,0:T(8,128)(2,1)S(1)}, u32[]{:S(2)}, u32[]{:S(2)}) collective-permute-start(bf16[2,128,512]{2,1,0:T(8,128)(2,1)} %get-tuple-element.92), channel_id=1, source_target_pairs={{0,1},{1,0},{2,3},{3,2},{4,5},{5,4},{6,7},{7,6},{8,9},{9,8},{10,11... | collective-permute-start | bytes 786440 | tf_op jit(solution)/shard_map/ppermute | solution.py:305
  92.4 10.5 %collective-permute-start.23 = (bf16[1,128,1024]{2,1,0:T(8,128)(2,1)}, bf16[1,128,1024]{2,1,0:T(8,128)(2,1)S(1)}, u32[]{:S(2)}, u32[]{:S(2)}) collective-permute-start(bf16[1,128,1024]{2,1,0:T(8,128)(2,1)} %bitcast.164), channel_id=1, source_target_pairs={{0,1},{1,0},{2,3},{3,2},{4,5},{5,4},{6,7},{7,6},{8,9},{9,8},{10,11... | collective-permute-start | bytes 786440 | tf_op jit(solution)/shard_map/ppermute | solution.py:305
  92.8 2.2 %copy-start.4 = (bf16[4096,512]{1,0:T(8,128)(2,1)S(1)}, bf16[4096,512]{1,0:T(8,128)(2,1)}, u32[]{:S(2)}) copy-start(bf16[4096,512]{1,0:T(8,128)(2,1)} %w_own.13) | copy-start | bytes 12582916
  95.0 2.1 %copy-start.21 = (f32[1,128]{1,0:T(1,128)S(1)}, f32[1,128]{1,0:T(1,128)}, u32[]{:S(2)}) copy-start(f32[1,128]{1,0:T(1,128)} %copy-done.20) | copy-start | bytes 1540
  95.0 4.1 %copy-start.11 = (f32[1024,128]{1,0:T(8,128)S(1)}, f32[1024,128]{1,0:T(8,128)}, u32[]{:S(2)}) copy-start(f32[1024,128]{1,0:T(8,128)} %copy-done.10) | copy-start | bytes 1572868
  97.1 5.8 %copy-start.7 = (bf16[128,1024]{1,0:T(8,128)(2,1)S(1)}, bf16[128,1024]{1,0:T(8,128)(2,1)}, u32[]{:S(2)}) copy-start(bf16[128,1024]{1,0:T(8,128)(2,1)} %copy-done.6) | copy-start | bytes 786436
  97.1 5.8 %copy-start.13 = (bf16[2,128,512]{2,1,0:T(8,128)(2,1)S(1)}, bf16[2,128,512]{2,1,0:T(8,128)(2,1)}, u32[]{:S(2)}) copy-start(bf16[2,128,512]{2,1,0:T(8,128)(2,1)} %copy-done.12) | copy-start | bytes 786436
  97.1 3.0 %collective-permute-start.24 = (f32[1,128]{1,0:T(1,128)S(1)}, f32[1,128]{1,0:T(1,128)S(1)}, u32[]{:S(2)}, u32[]{:S(2)}) collective-permute-start(f32[1,128]{1,0:T(1,128)S(1)} %copy-done.21), channel_id=1, source_target_pairs={{0,1},{1,0},{2,3},{3,2},{4,5},{5,4},{6,7},{7,6},{8,9},{9,8},{10,11... | collective-permute-start | bytes 1544 | tf_op jit(solution)/shard_map/ppermute | solution.py:305
  97.3 11.2 %collective-permute-start.18 = (bf16[1024,128]{1,0:T(8,128)(2,1)S(1)}, bf16[1024,128]{1,0:T(8,128)(2,1)S(1)}, u32[]{:S(2)}, u32[]{:S(2)}) collective-permute-start(bf16[1024,128]{1,0:T(8,128)(2,1)S(1)} %get-tuple-element.86), channel_id=1, source_target_pairs={{0,2},{2,0},{1,3},{3,1},{4,6},{6,4},{5,7},{7,5},{8,10},{10,8},{9,1... | collective-permute-start | bytes 786440 | tf_op jit(solution)/shard_map/ppermute | solution.py:402
  100.2 8.4 %collective-permute-start.19 = (bf16[1024,128]{1,0:T(8,128)(2,1)S(1)}, bf16[1024,128]{1,0:T(8,128)(2,1)S(1)}, u32[]{:S(2)}, u32[]{:S(2)}) collective-permute-start(bf16[1024,128]{1,0:T(8,128)(2,1)S(1)} %shard_map.104), channel_id=1, source_target_pairs={{0,4},{4,0},{8,12},{12,8},{1,5},{5,1},{9,13},{13,9},{2,6},{6,2},{1... | collective-permute-start | bytes 786440 | tf_op jit(solution)/shard_map/ppermute | solution.py:306
  101.7 6.9 %collective-permute-start.20 = (bf16[1024,128]{1,0:T(8,128)(2,1)S(1)}, bf16[1024,128]{1,0:T(8,128)(2,1)S(1)}, u32[]{:S(2)}, u32[]{:S(2)}) collective-permute-start(bf16[1024,128]{1,0:T(8,128)(2,1)S(1)} %shard_map.105), channel_id=1, source_target_pairs={{4,8},{8,4},{5,9},{9,5},{6,10},{10,6},{7,11},{11,7},{20,24},{24,20... | collective-permute-start | bytes 786440 | tf_op jit(solution)/shard_map/ppermute | solution.py:306
